TPU v7x, 32 devices: a whole 2x2x4 slice. The times are simulated.
32 devices in a mesh: fsdp: 4 (over z), ctx: 4 (over y, x), tp: 2 (over core).
Axes of the slice: x: 2, y: 2, z: 4, core: 2. Of those that a mesh axis runs over, the one named last changes fastest.
Arguments:
- tokens: bfloat16 [4, 1024, 2048], P('fsdp', 'ctx'), may hold values from -6 to 6
- w_query: bfloat16 [2048, 2048], P('fsdp', 'tp'), may hold values from -0.125 to 0.125
- w_key: bfloat16 [2048, 2048], P('fsdp', 'tp'), may hold values from -0.125 to 0.125
- w_value: bfloat16 [2048, 2048], P('fsdp', 'tp'), may hold values from -0.125 to 0.125
- w_out: bfloat16 [2048, 2048], P('tp', 'fsdp'), may hold values from -4 to 4
- gain_attn: bfloat16 [2048], P('fsdp'), may hold values from 0.5 to 1.5
- gain_query: bfloat16 [128], P('fsdp'), may hold values from 0.5 to 1.5
- gain_key: bfloat16 [128], P('fsdp'), may hold values from 0.5 to 1.5
- gain_moe: bfloat16 [2048], P('fsdp'), may hold values from 0.5 to 1.5
- w_router: bfloat16 [2048, 16], P('fsdp'), may hold values from -0.125 to 0.125
- w_experts: bfloat16 [2048, 3, 16, 1024], P('fsdp', None, None, 'tp')
- routes: int32 [4, 1024, 8], P('fsdp', 'ctx'), may hold values from 0 to 15, all different within a row; in each aligned block of 256 rows (0 to 255, 256 to 511, ..., all dimensions but the last counted through in order) at most 144 rows name the same one
- cotangent: bfloat16 [4, 1024, 2048], P('fsdp', 'ctx'), may hold values from -6 to 6
Outputs:
- layer_out: bfloat16 [4, 1024, 2048], P('fsdp', 'ctx', 'tp')
- tokens_grad: bfloat16 [4, 1024, 2048], P('fsdp', 'ctx')
- dw_query: float32 [2048, 2048], P(('fsdp', 'ctx'), 'tp')
- dw_key: float32 [2048, 2048], P(('fsdp', 'ctx'), 'tp')
- dw_value: float32 [2048, 2048], P(('fsdp', 'ctx'), 'tp')
- dw_out: float32 [2048, 2048], P('tp', ('fsdp', 'ctx'))
- dgain_attn: float32 [2048], P(('fsdp', 'ctx'))
- dgain_query: float32 [128], P(('fsdp', 'ctx'))
- dgain_key: float32 [128], P(('fsdp', 'ctx'))
- dgain_moe: float32 [2048], P(('fsdp', 'ctx'))
- dw_router: float32 [2048, 16], P(('fsdp', 'ctx'))
- dw_experts: float32 [2048, 3, 16, 1024], P(('fsdp', 'ctx'), None, None, 'tp')
Inputs may be any that keep to these rules, and one draw needn't show every extreme that they name: `routes`: within each sequence, each aligned block of 256 positions (the positions of one index of ctx) names no expert more than 144 times; some blocks reach 144. The 8 experts of a token are distinct.
All inputs are finite; a program needn't handle non-finite values.
Results may differ from a plain program's by a relative error of at most 0.022.
Values may be sent and summed in bfloat16 or wider, within the bound.
A program may use at most 320 MiB of HBM per device.

v0:
```python
import math

import jax
import jax.numpy as jnp
from jax import lax
from jax.sharding import PartitionSpec as P

HD = 128
TOPK = 8
E = 16
CAP = 512


EPS = 1e-06
ROPE_BASE = 10000.0


def prefix(value, axis, join, neutral):
    count, mine = (lax.axis_size(axis), lax.axis_index(axis))
    pieces = lax.all_gather(value, axis)
    running = jnp.full_like(value, 0) + jnp.asarray(neutral, value.dtype)

    def lap(position, running):
        longer = join(running, pieces[position])
        return jnp.where(position < mine, longer, running)

    return lax.fori_loop(0, count - 1, lap, running)


def rms_scale(values):
    return lax.rsqrt(jnp.mean(values * values, -1, keepdims=True) + EPS)


def norm_back(grad_normed, values, inv_rms, gain_vec):
    weighted = grad_normed * gain_vec.astype(jnp.float32)
    inner_sum = jnp.sum(weighted * values, -1, keepdims=True)
    return (
        inv_rms * weighted - values * (inv_rms * inv_rms * inv_rms) * inner_sum / values.shape[-1]
    )


def rope_tables(first, length):
    half_dim = HD // 2
    inv_freq = jnp.exp(jnp.arange(half_dim, dtype=jnp.float32) * (-2.0 * math.log(ROPE_BASE) / HD))
    places = (first + jnp.arange(length, dtype=jnp.int32)).astype(jnp.float32)
    angles = places[:, None] * inv_freq[None, :]
    cos_table = jnp.cos(angles)
    sin_table = jnp.sin(angles)
    cos_full = jnp.concatenate([cos_table, cos_table], -1)[:, None, :]
    sin_full = jnp.concatenate([sin_table, sin_table], -1)[:, None, :]
    return (cos_full, sin_full)


def rotate(values):
    half_dim = values.shape[-1] // 2
    return jnp.concatenate([-values[..., half_dim:], values[..., :half_dim]], -1)


def rotate_back(values):
    half_dim = values.shape[-1] // 2
    return jnp.concatenate([values[..., half_dim:], -values[..., :half_dim]], -1)


def apply_rope(values, cos_full, sin_full):
    return values * cos_full + rotate(values) * sin_full


def rope_back(grads, cos_full, sin_full):
    return grads * cos_full + rotate_back(grads * sin_full)


def add_counts(earlier, later):
    return earlier + later


def local(
    tokens,
    w_query,
    w_key,
    w_value,
    w_out,
    gain_attn,
    gain_query,
    gain_key,
    gain_moe,
    w_router,
    w_experts,
    routes,
    cotangent,
):
    seq_count, block_len, model_width = tokens.shape
    row_count = seq_count * block_len
    (
        full_query,
        full_key,
        full_value,
        full_out,
        router_full,
        attn_gain,
        query_gain,
        key_gain,
        moe_gain,
    ) = (
        lax.all_gather(w_query, "fsdp", axis=0, tiled=True),
        lax.all_gather(w_key, "fsdp", axis=0, tiled=True),
        lax.all_gather(w_value, "fsdp", axis=0, tiled=True),
        lax.all_gather(w_out, "fsdp", axis=1, tiled=True),
        lax.all_gather(w_router, "fsdp", axis=0, tiled=True),
        lax.all_gather(gain_attn, "fsdp", axis=0, tiled=True),
        lax.all_gather(gain_query, "fsdp", axis=0, tiled=True),
        lax.all_gather(gain_key, "fsdp", axis=0, tiled=True),
        lax.all_gather(gain_moe, "fsdp", axis=0, tiled=True),
    )
    local_width = full_query.shape[1]
    head_count = local_width // HD
    head_shape = (seq_count, block_len, head_count, HD)
    token_rows = tokens.reshape(row_count, model_width).astype(jnp.float32)
    inv_one = rms_scale(token_rows)
    normed_one = (token_rows * inv_one * attn_gain.astype(jnp.float32)).astype(jnp.bfloat16)
    query_proj = jnp.dot(normed_one, full_query, preferred_element_type=jnp.float32)
    key_proj = jnp.dot(normed_one, full_key, preferred_element_type=jnp.float32)
    value_proj = jnp.dot(normed_one, full_value, preferred_element_type=jnp.float32)
    cos_full, sin_full = rope_tables(lax.axis_index("ctx") * block_len, block_len)
    query_heads = query_proj.reshape(head_shape)
    key_heads = key_proj.reshape(head_shape)
    query_inv = rms_scale(query_heads)
    key_inv = rms_scale(key_heads)
    queries = apply_rope(
        query_heads * query_inv * query_gain.astype(jnp.float32), cos_full, sin_full
    ).astype(jnp.bfloat16)
    keys_local = apply_rope(
        key_heads * key_inv * key_gain.astype(jnp.float32), cos_full, sin_full
    ).astype(jnp.bfloat16)
    keys_local = keys_local.reshape(seq_count, block_len, local_width)
    values_local = value_proj.astype(jnp.bfloat16).reshape(seq_count, block_len, local_width)
    keys_all, values_all = (
        lax.all_gather(keys_local, "ctx", axis=1, tiled=True),
        lax.all_gather(values_local, "ctx", axis=1, tiled=True),
    )
    seq_len = keys_all.shape[1]
    key_rows = keys_all.reshape(seq_count, seq_len, head_count, HD)
    value_rows = values_all.reshape(seq_count, seq_len, head_count, HD)
    score_scale = 1.0 / math.sqrt(HD)
    scores = (
        jnp.einsum("sqhd,skhd->shqk", queries, key_rows, preferred_element_type=jnp.float32)
        * score_scale
    )
    maximum = jnp.max(scores, -1, keepdims=True)
    exp_scores = jnp.exp(scores - maximum)
    denominator = jnp.sum(exp_scores, -1, keepdims=True)
    attn_probs = exp_scores / denominator
    log_total = maximum + jnp.log(denominator)
    context = jnp.einsum(
        "shqk,skhd->sqhd",
        attn_probs.astype(jnp.bfloat16),
        value_rows,
        preferred_element_type=jnp.float32,
    )
    context = context.astype(jnp.bfloat16).reshape(row_count, local_width)
    attn_part = jnp.dot(context, full_out, preferred_element_type=jnp.float32)
    residual = token_rows + lax.psum(attn_part, "tp")
    inv_two = rms_scale(residual)
    normed_two = (residual * inv_two * moe_gain.astype(jnp.float32)).astype(jnp.bfloat16)
    logits = jnp.dot(normed_two, router_full, preferred_element_type=jnp.float32)
    router_probs = jax.nn.softmax(logits, -1)
    pair_count = block_len * TOPK
    route_rows = routes.reshape(seq_count, pair_count)
    expert_ids = jnp.arange(E, dtype=jnp.int32)
    onehot = (route_rows[:, :, None] == expert_ids[None, None, :]).astype(jnp.int32)
    counts = jnp.sum(onehot, 1, dtype=jnp.int32)
    offsets = prefix(counts, "ctx", add_counts, jnp.zeros_like(counts))
    earlier = jnp.cumsum(onehot, 1, dtype=jnp.int32) - onehot
    local_rank = jnp.sum(earlier * onehot, 2, dtype=jnp.int32)
    slot_base = jnp.sum(onehot * offsets[:, None, :], 2, dtype=jnp.int32)
    kept_mask = (slot_base + local_rank < CAP).astype(jnp.float32).reshape(row_count, TOPK)
    block_most = pair_count * 9 // (8 * E)
    expert_span = seq_count * block_most
    seq_ids = jnp.arange(seq_count, dtype=jnp.int32)[:, None]
    buffer_row = (route_rows * expert_span + seq_ids * block_most + local_rank).reshape(
        row_count * TOPK
    )
    token_ids = (
        seq_ids * block_len + jnp.arange(pair_count, dtype=jnp.int32)[None, :] // TOPK
    ).reshape(row_count * TOPK)
    owner_rows = jnp.zeros((E * expert_span,), jnp.int32).at[buffer_row].set(token_ids)
    onehot_f = onehot.astype(jnp.float32).reshape(row_count, TOPK, E)
    gate_weight = jnp.sum(onehot_f * router_probs[:, None, :], 2) * kept_mask
    slot_weight = (
        jnp.zeros((E * expert_span,), jnp.float32)
        .at[buffer_row]
        .set(gate_weight.reshape(row_count * TOPK))
    )
    expert_rows = normed_two[owner_rows].reshape(E, expert_span, model_width)
    cotan_rows = cotangent.reshape(row_count, model_width)
    grad_expert = (slot_weight[:, None] * cotan_rows[owner_rows].astype(jnp.float32)).astype(
        jnp.bfloat16
    )
    grad_expert = grad_expert.reshape(E, expert_span, model_width)
    ffn_local = w_experts.shape[3]
    fsdp_count = lax.axis_size("fsdp")
    ctx_count = lax.axis_size("ctx")
    group_count = fsdp_count * ctx_count
    sharing = group_count // E
    padded_span = -(-expert_span // sharing) * sharing
    part_span = padded_span // sharing
    target_experts = (
        jnp.arange(fsdp_count, dtype=jnp.int32) * ctx_count + lax.axis_index("ctx")
    ) // sharing
    selected = jnp.take(w_experts, target_experts, axis=2)
    owned = lax.all_to_all(selected, "fsdp", split_axis=2, concat_axis=0, tiled=True)[:, :, 0]
    send_rows = expert_rows.reshape(group_count, part_span, model_width)
    send_grads = grad_expert.reshape(group_count, part_span, model_width)
    recv_rows, recv_grads = (
        lax.all_to_all(send_rows, ("fsdp", "ctx"), split_axis=0, concat_axis=0, tiled=True),
        lax.all_to_all(send_grads, ("fsdp", "ctx"), split_axis=0, concat_axis=0, tiled=True),
    )
    rows_flat = recv_rows.reshape(group_count * part_span, model_width)
    grads_flat = recv_grads.reshape(group_count * part_span, model_width)
    gate_act = jnp.dot(rows_flat, owned[:, 0], preferred_element_type=jnp.float32)
    up_act = jnp.dot(rows_flat, owned[:, 1], preferred_element_type=jnp.float32)
    sigmoid_gate = jax.nn.sigmoid(gate_act)
    silu_gate = gate_act * sigmoid_gate
    hidden = (silu_gate * up_act).astype(jnp.bfloat16)
    produced = jnp.einsum("mf,df->md", hidden, owned[:, 2], preferred_element_type=jnp.float32)
    grad_hidden = jnp.dot(grads_flat, owned[:, 2], preferred_element_type=jnp.float32)
    grad_gate = (
        grad_hidden * up_act * sigmoid_gate * (1.0 + gate_act * (1.0 - sigmoid_gate))
    ).astype(jnp.bfloat16)
    grad_up = (grad_hidden * silu_gate).astype(jnp.bfloat16)
    rows_grad = jnp.einsum("mf,df->md", grad_gate, owned[:, 0], preferred_element_type=jnp.float32)
    rows_grad = rows_grad + jnp.einsum(
        "mf,df->md", grad_up, owned[:, 1], preferred_element_type=jnp.float32
    )
    back_out, back_rows = (
        lax.all_to_all(
            produced.reshape(group_count, part_span, model_width).astype(jnp.bfloat16),
            ("fsdp", "ctx"),
            split_axis=0,
            concat_axis=0,
            tiled=True,
        ).astype(jnp.float32),
        lax.all_to_all(
            rows_grad.reshape(group_count, part_span, model_width).astype(jnp.bfloat16),
            ("fsdp", "ctx"),
            split_axis=0,
            concat_axis=0,
            tiled=True,
        ).astype(jnp.float32),
    )
    expert_out = back_out.reshape(E, padded_span, model_width)
    grad_rows = back_rows.reshape(E, padded_span, model_width)
    gate_term = jnp.einsum("md,mf->df", rows_flat, grad_gate, preferred_element_type=jnp.float32)
    up_term = jnp.einsum("md,mf->df", rows_flat, grad_up, preferred_element_type=jnp.float32)
    down_term = jnp.einsum("md,mf->df", grads_flat, hidden, preferred_element_type=jnp.float32)
    owner_terms = jnp.stack([gate_term, up_term, down_term], 1)[:, :, None, :]
    relaid = lax.all_to_all(
        owner_terms.astype(jnp.bfloat16), ("fsdp", "ctx"), split_axis=0, concat_axis=2, tiled=True
    ).astype(owner_terms.dtype)
    dw_experts = jnp.sum(relaid.reshape(relaid.shape[0], 3, E, sharing, ffn_local), 3)
    picked = expert_out.reshape(E * expert_span, model_width)[buffer_row].reshape(
        row_count, TOPK, model_width
    )
    moe_part = jnp.sum(gate_weight[:, :, None] * picked, 1)
    cotan_float = cotan_rows.astype(jnp.float32)
    grad_gate_part = jnp.sum(picked * cotan_float[:, None, :], 2)
    moe_shard = lax.psum_scatter(
        moe_part.astype(jnp.bfloat16), "tp", scatter_dimension=1, tiled=True
    ).astype(jnp.float32)
    piece_width = moe_shard.shape[1]
    residual_shard = lax.dynamic_slice_in_dim(
        residual, lax.axis_index("tp") * piece_width, piece_width, 1
    )
    layer_out = (
        (residual_shard + moe_shard).astype(jnp.bfloat16).reshape(seq_count, block_len, piece_width)
    )
    grad_normed_part = jnp.sum(
        grad_rows.reshape(E * expert_span, model_width)[buffer_row].reshape(
            row_count, TOPK, model_width
        ),
        1,
    )
    grad_normed_sum, grad_gate_sum = (
        lax.psum(grad_normed_part.astype(jnp.bfloat16), "tp").astype(jnp.float32),
        lax.psum(grad_gate_part.astype(jnp.bfloat16), "tp").astype(jnp.float32),
    )
    grad_pick = grad_gate_sum * kept_mask
    grad_router_probs = jnp.sum(onehot_f * grad_pick[:, :, None], 1)
    grad_logits = router_probs * (
        grad_router_probs - jnp.sum(router_probs * grad_router_probs, -1, keepdims=True)
    )
    grad_logits = grad_logits.astype(jnp.bfloat16)
    grad_router_w = jnp.einsum(
        "nd,ne->de", normed_two, grad_logits, preferred_element_type=jnp.float32
    )
    grad_normed_two = grad_normed_sum + jnp.einsum(
        "ne,de->nd", grad_logits, router_full, preferred_element_type=jnp.float32
    )
    grad_moe_gain = jnp.sum(grad_normed_two * residual * inv_two, 0)
    grad_residual = cotan_float + norm_back(grad_normed_two, residual, inv_two, moe_gain)
    grad_attn = grad_residual.astype(jnp.bfloat16)
    grad_w_out = jnp.einsum("nl,nd->ld", context, grad_attn, preferred_element_type=jnp.float32)
    grad_context = jnp.einsum("nd,ld->nl", grad_attn, full_out, preferred_element_type=jnp.float32)
    grad_context = grad_context.astype(jnp.bfloat16).reshape(head_shape)
    scores = (
        jnp.einsum("sqhd,skhd->shqk", queries, key_rows, preferred_element_type=jnp.float32)
        * score_scale
    )
    attn_probs = jnp.exp(scores - log_total)
    grad_probs = jnp.einsum(
        "sqhd,skhd->shqk", grad_context, value_rows, preferred_element_type=jnp.float32
    )
    grad_scores = attn_probs * (grad_probs - jnp.sum(attn_probs * grad_probs, -1, keepdims=True))
    grad_scores = grad_scores.astype(jnp.bfloat16)
    grad_queries = (
        jnp.einsum("shqk,skhd->sqhd", grad_scores, key_rows, preferred_element_type=jnp.float32)
        * score_scale
    )
    grad_keys_all = (
        jnp.einsum("shqk,sqhd->skhd", grad_scores, queries, preferred_element_type=jnp.float32)
        * score_scale
    )
    grad_values_all = jnp.einsum(
        "shqk,sqhd->skhd",
        attn_probs.astype(jnp.bfloat16),
        grad_context,
        preferred_element_type=jnp.float32,
    )
    grad_keys_own, grad_values_own = (
        lax.psum_scatter(
            grad_keys_all.reshape(seq_count, seq_len, local_width).astype(jnp.bfloat16),
            "ctx",
            scatter_dimension=1,
            tiled=True,
        ).astype(jnp.float32),
        lax.psum_scatter(
            grad_values_all.reshape(seq_count, seq_len, local_width).astype(jnp.bfloat16),
            "ctx",
            scatter_dimension=1,
            tiled=True,
        ).astype(jnp.float32),
    )
    grad_qnormed = rope_back(grad_queries, cos_full, sin_full)
    grad_knormed = rope_back(grad_keys_own.reshape(head_shape), cos_full, sin_full)
    grad_qgain = jnp.sum(grad_qnormed * query_heads * query_inv, (0, 1, 2))
    grad_kgain = jnp.sum(grad_knormed * key_heads * key_inv, (0, 1, 2))
    grad_qproj = (
        norm_back(grad_qnormed, query_heads, query_inv, query_gain)
        .astype(jnp.bfloat16)
        .reshape(row_count, local_width)
    )
    grad_kproj = (
        norm_back(grad_knormed, key_heads, key_inv, key_gain)
        .astype(jnp.bfloat16)
        .reshape(row_count, local_width)
    )
    grad_vproj = grad_values_own.astype(jnp.bfloat16).reshape(row_count, local_width)
    grad_wq = jnp.einsum("nd,nl->dl", normed_one, grad_qproj, preferred_element_type=jnp.float32)
    grad_wk = jnp.einsum("nd,nl->dl", normed_one, grad_kproj, preferred_element_type=jnp.float32)
    grad_wv = jnp.einsum("nd,nl->dl", normed_one, grad_vproj, preferred_element_type=jnp.float32)
    grad_normed_one = jnp.einsum(
        "nl,dl->nd", grad_qproj, full_query, preferred_element_type=jnp.float32
    )
    grad_normed_one = grad_normed_one + jnp.einsum(
        "nl,dl->nd", grad_kproj, full_key, preferred_element_type=jnp.float32
    )
    grad_normed_one = grad_normed_one + jnp.einsum(
        "nl,dl->nd", grad_vproj, full_value, preferred_element_type=jnp.float32
    )
    grad_normed_one, grad_qgain, grad_kgain = (
        lax.psum(grad_normed_one.astype(jnp.bfloat16), "tp").astype(jnp.float32),
        lax.psum(grad_qgain.astype(jnp.bfloat16), "tp").astype(jnp.float32),
        lax.psum(grad_kgain.astype(jnp.bfloat16), "tp").astype(jnp.float32),
    )
    grad_attn_gain = jnp.sum(grad_normed_one * token_rows * inv_one, 0)
    tokens_grad = grad_residual + norm_back(grad_normed_one, token_rows, inv_one, attn_gain)
    tokens_grad = tokens_grad.astype(jnp.bfloat16).reshape(seq_count, block_len, model_width)
    dw_query, dw_key, dw_value, dw_out, dw_router, dgain_attn, dgain_query, dgain_key, dgain_moe = (
        lax.psum_scatter(grad_wq, ("fsdp", "ctx"), scatter_dimension=0, tiled=True),
        lax.psum_scatter(grad_wk, ("fsdp", "ctx"), scatter_dimension=0, tiled=True),
        lax.psum_scatter(grad_wv, ("fsdp", "ctx"), scatter_dimension=0, tiled=True),
        lax.psum_scatter(grad_w_out, ("fsdp", "ctx"), scatter_dimension=1, tiled=True),
        lax.psum_scatter(grad_router_w, ("fsdp", "ctx"), scatter_dimension=0, tiled=True),
        lax.psum_scatter(grad_attn_gain, ("fsdp", "ctx"), scatter_dimension=0, tiled=True),
        lax.psum_scatter(grad_qgain, ("fsdp", "ctx"), scatter_dimension=0, tiled=True),
        lax.psum_scatter(grad_kgain, ("fsdp", "ctx"), scatter_dimension=0, tiled=True),
        lax.psum_scatter(grad_moe_gain, ("fsdp", "ctx"), scatter_dimension=0, tiled=True),
    )
    return (
        layer_out,
        tokens_grad,
        dw_query,
        dw_key,
        dw_value,
        dw_out,
        dgain_attn,
        dgain_query,
        dgain_key,
        dgain_moe,
        dw_router,
        dw_experts,
    )


def solution(mesh):
    return jax.shard_map(
        local,
        mesh=mesh,
        in_specs=(
            P("fsdp", "ctx", None),
            P("fsdp", "tp"),
            P("fsdp", "tp"),
            P("fsdp", "tp"),
            P("tp", "fsdp"),
            P("fsdp"),
            P("fsdp"),
            P("fsdp"),
            P("fsdp"),
            P("fsdp", None),
            P("fsdp", None, None, "tp"),
            P("fsdp", "ctx", None),
            P("fsdp", "ctx", None),
        ),
        out_specs=(
            P("fsdp", "ctx", "tp"),
            P("fsdp", "ctx", None),
            P(("fsdp", "ctx"), "tp"),
            P(("fsdp", "ctx"), "tp"),
            P(("fsdp", "ctx"), "tp"),
            P("tp", ("fsdp", "ctx")),
            P(("fsdp", "ctx")),
            P(("fsdp", "ctx")),
            P(("fsdp", "ctx")),
            P(("fsdp", "ctx")),
            P(("fsdp", "ctx"), None),
            P(("fsdp", "ctx"), None, None, "tp"),
        ),
        check_vma=False,
    )
```

profile of v0, /device:TPU:15, one launch (start us, length us, event | category | flops | bytes accessed | tf_op | source)
XLA Modules:
  0.0 2566.3 jit_solution(7016868883033967893)
XLA Ops:
  10.1 9.5 all-gather.3
  23.3 8.6 all-reduce.8
  35.7 53.6 %all-gather.16.cloned.1.call-done = bf16[2048,1024]{1,0:T(8,128)(2,1)} async-done(((bf16[512,1024]{1,0:T(8,128)(2,1)}), bf16[2048,1024]{1,0:T(8,128)(2,1)}) %all-gather.16.cloned.1.call-update) | async-done | bytes 4194320 | tf_op jit(solution)/shard_map/all_gather | solution.py:105
  101.4 68.7 %all-gather.12.cloned.1.call-done = bf16[2048,1024]{1,0:T(8,128)(2,1)} async-done(((bf16[512,1024]{1,0:T(8,128)(2,1)}), bf16[2048,1024]{1,0:T(8,128)(2,1)}) %all-gather.12.cloned.1.call-update) | async-done | bytes 4194320 | tf_op jit(solution)/shard_map/all_gather | solution.py:106
  175.1 25.0 copy.215
  200.1 12.0 gather_fusion.1
  218.2 8.0 all-to-all-start.1
  226.7 167.9 %all-gather.4 = bf16[4,1,512]{2,1,0:T(2,128)(2,1)S(1)} all-gather(bf16[1,1,512]{2,1,0:T(2,128)(2,1)S(1)} %reshape.1117), channel_id=1, replica_groups=mesh['fsdp'=4,'ctx'=4,'tp'=2] {'fsdp'}, dimensions={0}, use_global_device_ids=true | all-gather | bytes 5120 | tf_op jit(solution)/shard_map/all_gather | solution.py:112
  436.4 16.4 all-gather.18.cloned.1.call-done
  460.2 8.1 scatter_custom_fusion
  468.3 13.4 all-reduce.14.cloned.1.call-done
  485.1 9.8 gather_fusion
  494.9 17.5 all-to-all-start
  512.4 9.9 gather_fusion.3
  522.3 206.2 %all_gather.51 = bf16[2048,16]{0,1:T(8,128)(2,1)S(1)} all-gather(bf16[512,16]{0,1:T(8,128)(2,1)S(1)} %copy-done.73), channel_id=1, replica_groups=mesh['fsdp'=4,'ctx'=4,'tp'=2] {'fsdp'}, dimensions={0}, use_global_device_ids=true | all-gather | bytes 81920 | tf_op jit(solution)/shard_map/all_gather | solution.py:108
  730.0 8.1 scatter_custom_fusion.1
  738.2 8.9 fusion
  747.1 6.4 all-to-all-start.3
  757.0 12.7 fusion.46
  769.7 10.4 fusion.45
  780.1 181.3 %all-to-all-done.3 = bf16[16,144,2048]{2,1,0:T(8,128)(2,1)} async-done(((bf16[16,144,2048]{2,1,0:T(8,128)(2,1)}), bf16[16,144,2048]{2,1,0:T(8,128)(2,1)}, u32[]{:S(2)}, u32[]{:S(2)}) %all-to-all-start.3) | async-done | bytes 9437216 | tf_op jit(solution)/shard_map/all_to_all | solution.py:215
  961.3 13.8 multiply_convert_fusion.1
  975.2 9.3 fusion.44
  984.5 12.3 add_convert_fusion
  1001.5 9.5 convolution_convert_fusion
  1011.0 196.7 %all-to-all-done.4 = bf16[16,144,2048]{2,1,0:T(8,128)(2,1)} async-done(((bf16[16,144,2048]{2,1,0:T(8,128)(2,1)}), bf16[16,144,2048]{2,1,0:T(8,128)(2,1)}, u32[]{:S(2)}, u32[]{:S(2)}) %all-to-all-start.4) | async-done | bytes 9437216 | tf_op jit(solution)/shard_map/all_to_all | solution.py:242
  1214.4 12.6 bitcast_convert_fusion
  1226.9 23.0 gather_fusion.4
  1249.9 9.2 bitcast_reduce_fusion
  1259.1 164.1 %all-to-all-done.2 = bf16[16,144,2048]{2,1,0:T(8,128)(2,1)} async-done(((bf16[16,144,2048]{2,1,0:T(8,128)(2,1)}), bf16[16,144,2048]{2,1,0:T(8,128)(2,1)}, u32[]{:S(2)}, u32[]{:S(2)}) %all-to-all-start.2) | async-done | bytes 9437216 | tf_op jit(solution)/shard_map/all_to_all | solution.py:235
  1423.2 12.5 bitcast_convert_fusion.1
  1435.8 23.1 gather_fusion.2
  1458.9 10.6 fusion.2
  1496.7 6.7 fusion.41
  1514.7 17.9 reduce-scatter.11.cloned.1.call-done
  1541.6 29.3 %reduce-scatter.13.cloned.1.call-done = bf16[1,256,1024]{1,2,0:T(8,128)(2,1)} async-done(((bf16[1,1024,1024]{1,2,0:T(8,128)(2,1)}), bf16[1,256,1024]{1,2,0:T(8,128)(2,1)}) %reduce-scatter.13.cloned.1.call-update) | async-done | bytes 524304 | tf_op jit(solution)/shard_map/reduce_scatter | solution.py:335
  1596.6 9.4 fusion.13
  1610.7 8.5 fusion.11
  1619.3 9.5 fusion.12
  1629.5 27.3 %copy.231 = bf16[2048,3,1,512]{3,1,2,0:T(4,128)(2,1)} copy(bf16[2048,3,1,512]{3,0,2,1:T(8,128)(2,1)S(1)} %pad_maximum_fusion) | data formatting | bytes 12582912 | tf_op jit(solution)/shard_map/stack | solution.py:255
  1656.9 6.5 all-to-all-start.5
  1665.3 219.9 %all-to-all-done.5 = bf16[2048,3,1,512]{3,1,2,0:T(4,128)(2,1)} async-done(((bf16[2048,3,1,512]{3,1,2,0:T(4,128)(2,1)}), bf16[2048,3,1,512]{3,1,2,0:T(4,128)(2,1)}, u32[]{:S(2)}, u32[]{:S(2)}) %all-to-all-start.5) | async-done | bytes 6291488 | tf_op jit(solution)/shard_map/all_to_all | solution.py:256
  1885.1 15.5 copy.274
  1910.7 55.6 %all-reduce.7 = (f32[2048]{0:T(1024)S(1)}, f32[128]{0:T(128)S(1)}, f32[128]{0:T(128)S(1)}, f32[2048]{0:T(1024)S(1)}) all-reduce(f32[2048]{0:T(1024)S(1)} %get-tuple-element.141, bf16[128]{0:T(256)(128)(2,1)S(1)} %get-tuple-element.159, ...), channel_id=12, replica_groups=mesh['fsdp'=4,'ctx'=4,'tp'=2] {'fsdp','ctx'}, use_global_device_ids=true, to_apply=%region_40.41.clone | all-reduce | flops 4352 | bytes 34304
  1972.2 26.2 %reduce-scatter.21.cloned.1.call-done = f32[1024,128]{1,0:T(8,128)} async-done(((f32[1024,2048]{1,0:T(8,128)}), f32[1024,128]{1,0:T(8,128)}) %reduce-scatter.21.cloned.1.call-update) | async-done | bytes 524304 | tf_op jit(solution)/shard_map/reduce_scatter | solution.py:381
  1998.4 195.0 %reduce-scatter.15.cloned.1.call-done = f32[128,1024]{1,0:T(8,128)} async-done(((f32[2048,1024]{1,0:T(8,128)}), f32[128,1024]{1,0:T(8,128)}) %reduce-scatter.15.cloned.1.call-update) | async-done | bytes 524304 | tf_op jit(solution)/shard_map/reduce_scatter | solution.py:378
  2193.4 183.1 %reduce-scatter.19.cloned.1.call-done = f32[128,1024]{1,0:T(8,128)} async-done(((f32[2048,1024]{1,0:T(8,128)}), f32[128,1024]{1,0:T(8,128)}) %reduce-scatter.19.cloned.1.call-update) | async-done | bytes 524304 | tf_op jit(solution)/shard_map/reduce_scatter | solution.py:380
  2376.5 183.1 %reduce-scatter.17.cloned.1.call-done = f32[128,1024]{1,0:T(8,128)} async-done(((f32[2048,1024]{1,0:T(8,128)}), f32[128,1024]{1,0:T(8,128)}) %reduce-scatter.17.cloned.1.call-update) | async-done | bytes 524304 | tf_op jit(solution)/shard_map/reduce_scatter | solution.py:379
  (378 shorter events, 197.7 us)
Async XLA Ops:
  7.2 82.1 %all-gather.16.cloned.1.call-start = ((), (), s32[]{:S(2)}) async-start(), calls=%async_computation.16 | async-start | bytes 5242880 | tf_op jit(solution)/shard_map/all_gather | solution.py:105
  7.9 162.2 %all-gather.12.cloned.1.call-start = ((), (), s32[]{:S(2)}) async-start(), calls=%async_computation.14 | async-start | bytes 5242880 | tf_op jit(solution)/shard_map/all_gather | solution.py:106
  8.7 26.2 %copy-start.4 = (bf16[1,256,2048]{2,1,0:T(8,128)(2,1)S(1)}, bf16[1,256,2048]{2,1,0:T(8,128)(2,1)}, u32[]{:S(2)}) copy-start(bf16[1,256,2048]{2,1,0:T(8,128)(2,1)} %param.15) | copy-start | bytes 3145732
  8.7 399.8 %all-gather.14.cloned.1.call-start = ((), (), s32[]{:S(2)}) async-start(), calls=%async_computation.15 | async-start | bytes 5242880 | tf_op jit(solution)/shard_map/all_gather | solution.py:104
  9.4 409.7 %all-gather.22.cloned.1.call-start = ((), (), s32[]{:S(2)}) async-start(), calls=%async_computation.30 | async-start | bytes 2621440 | tf_op jit(solution)/shard_map/all_gather | solution.py:137
  19.6 388.9 %copy-start.38 = (f32[4,1,512]{2,1,0:T(1,128)}, f32[4,1,512]{2,1,0:T(1,128)S(1)}, u32[]{:S(2)}) copy-start(f32[4,1,512]{2,1,0:T(1,128)S(1)} %convert_element_type.349) | copy-start | bytes 24580
  33.0 384.3 %copy-start.32 = (f32[256,128]{0,1:T(8,128)}, f32[256,128]{0,1:T(8,128)S(1)}, u32[]{:S(2)}) copy-start(f32[256,128]{0,1:T(8,128)S(1)} %get-tuple-element.204) | copy-start | bytes 393220
  33.0 384.3 %copy-start.34 = (f32[256,128]{0,1:T(8,128)}, f32[256,128]{0,1:T(8,128)S(1)}, u32[]{:S(2)}) copy-start(f32[256,128]{0,1:T(8,128)S(1)} %get-tuple-element.184) | copy-start | bytes 393220
  33.4 65.7 %copy-start.15 = (f32[256,1024]{1,0:T(8,128)}, f32[256,1024]{1,0:T(8,128)S(1)}, u32[]{:S(2)}) copy-start(f32[256,1024]{1,0:T(8,128)S(1)} %copy.235) | copy-start | bytes 3145732
  35.7 134.4 %copy-start.56 = (f32[256]{0:T(256)}, f32[256]{0:T(256)S(1)}, u32[]{:S(2)}) copy-start(f32[256]{0:T(256)S(1)} %get-tuple-element.192) | copy-start | bytes 3076
  35.7 63.5 %copy-start.61 = (f32[1024]{0:T(1024)}, f32[1024]{0:T(1024)S(1)}, u32[]{:S(2)}) copy-start(f32[1024]{0:T(1024)S(1)} %broadcast_bitcast_fusion) | copy-start | bytes 12292
  99.2 75.3 %copy-start.20 = (f32[256,8,128]{2,1,0:T(8,128)}, f32[256,8,128]{2,1,0:T(8,128)S(1)}, u32[]{:S(2)}) copy-start(f32[256,8,128]{2,1,0:T(8,128)S(1)} %mul.769) | copy-start | bytes 3145732
  101.3 328.6 %all-gather.20.cloned.1.call-start = ((), (), s32[]{:S(2)}) async-start(), calls=%async_computation.29 | async-start | bytes 2621440 | tf_op jit(solution)/shard_map/all_gather | solution.py:138
  174.5 278.3 %all-gather.18.cloned.1.call-start = ((), (), s32[]{:S(2)}) async-start(), calls=%async_computation.17 | async-start | bytes 5242880 | tf_op jit(solution)/shard_map/all_gather | solution.py:107
  218.1 176.5 %copy-start.85 = (u32[32]{0:T(128)S(1)}, u32[32]{0:T(128)}, u32[]{:S(2)}) copy-start(u32[32]{0:T(128)} %constant.149) | copy-start | bytes 388
  218.1 177.1 %copy-start.53 = (s32[1,256,8]{1,2,0:T(8,128)S(1)}, s32[1,256,8]{1,2,0:T(8,128)}, u32[]{:S(2)}) copy-start(s32[1,256,8]{1,2,0:T(8,128)} %param.26) | copy-start | bytes 24580
  218.1 190.4 %copy-start.57 = (f32[256]{0:T(256)S(1)}, f32[256]{0:T(256)}, u32[]{:S(2)}) copy-start(f32[256]{0:T(256)} %copy-done.56) | copy-start | bytes 3076
  218.2 276.7 %all-to-all-start.1 = ((bf16[512,3,4,512]{3,0,1,2:T(8,128)(2,1)}), bf16[512,3,4,512]{3,0,1,2:T(8,128)(2,1)}, u32[]{:S(2)}, u32[]{:S(2)}) async-start(bf16[512,3,4,512]{3,0,1,2:T(8,128)(2,1)} %select_bitcast_fusion), calls=%async_computation.1 | async-start | bytes 12582912 | tf_op jit(solution)/shard_map/all_to_all | solution.py:210
  226.2 255.4 %all-reduce.14.cloned.1.call-start = ((), (), s32[]{:S(2)}) async-start(), calls=%async_computation.18 | async-start | bytes 4194304 | tf_op jit(solution)/shard_map/psum | solution.py:161
  394.7 89.5 %copy-start.49 = (f32[4,1,512]{2,1,0:T(1,128)}, f32[4,1,512]{2,1,0:T(1,128)S(1)}, u32[]{:S(2)}) copy-start(f32[4,1,512]{2,1,0:T(1,128)S(1)} %convert_element_type.350) | copy-start | bytes 24580
  436.3 21.3 copy-start.40
  485.1 243.3 %copy-start = (bf16[256,2048]{1,0:T(8,128)(2,1)}, bf16[256,2048]{1,0:T(8,128)(2,1)S(1)}, u32[]{:S(2)}) copy-start(bf16[256,2048]{1,0:T(8,128)(2,1)S(1)} %multiply_convert_fusion.5) | copy-start | bytes 3145732
  494.9 17.5 copy-start.2
  494.9 252.1 %all-to-all-start = ((bf16[16,144,2048]{2,1,0:T(8,128)(2,1)}), bf16[16,144,2048]{2,1,0:T(8,128)(2,1)}, u32[]{:S(2)}, u32[]{:S(2)}) async-start(bf16[16,144,2048]{2,1,0:T(8,128)(2,1)} %bitcast.323), calls=%async_computation | async-start | bytes 18874368 | tf_op jit(solution)/shard_map/all_to_all | solution.py:214
  747.1 214.3 %all-to-all-start.3 = ((bf16[16,144,2048]{2,1,0:T(8,128)(2,1)}), bf16[16,144,2048]{2,1,0:T(8,128)(2,1)}, u32[]{:S(2)}, u32[]{:S(2)}) async-start(bf16[16,144,2048]{2,1,0:T(8,128)(2,1)} %fusion), calls=%async_computation.4 | async-start | bytes 18874368 | tf_op jit(solution)/shard_map/all_to_all | solution.py:215
  996.8 210.9 %all-to-all-start.4 = ((bf16[16,144,2048]{2,1,0:T(8,128)(2,1)}), bf16[16,144,2048]{2,1,0:T(8,128)(2,1)}, u32[]{:S(2)}, u32[]{:S(2)}) async-start(bf16[16,144,2048]{2,1,0:T(8,128)(2,1)} %bitcast.331), calls=%async_computation.5 | async-start | bytes 18874368 | tf_op jit(solution)/shard_map/all_to_all | solution.py:242
  1011.0 203.0 %copy-start.60 = (f32[8,256]{1,0:T(8,128)S(1)}, f32[8,256]{1,0:T(8,128)}, u32[]{:S(2)}) copy-start(f32[8,256]{1,0:T(8,128)} %copy-done.59) | copy-start | bytes 24580
  1011.0 203.0 %copy-start.67 = (f32[8,256]{1,0:T(8,128)S(1)}, f32[8,256]{1,0:T(8,128)}, u32[]{:S(2)}) copy-start(f32[8,256]{1,0:T(8,128)} %copy-done.66) | copy-start | bytes 24580
  1207.7 215.6 %all-to-all-start.2 = ((bf16[16,144,2048]{2,1,0:T(8,128)(2,1)}), bf16[16,144,2048]{2,1,0:T(8,128)(2,1)}, u32[]{:S(2)}, u32[]{:S(2)}) async-start(bf16[16,144,2048]{2,1,0:T(8,128)(2,1)} %convolution_convert_fusion), calls=%async_computation.2 | async-start | bytes 18874368 | tf_op jit(solution)/shard_map/all_to_all | solution.py:235
  1212.4 260.9 %all-reduce.16.cloned.1.call-start = ((), (), s32[]{:S(2)}) async-start(), calls=%async_computation.20 | async-start | bytes 2097152 | tf_op jit(solution)/shard_map/psum | solution.py:283
  1259.1 273.5 %reduce-scatter.11.cloned.1.call-start = ((), (), s32[]{:S(2)}) async-start(), calls=%async_computation.21 | async-start | bytes 2621440 | tf_op jit(solution)/shard_map/reduce_scatter | solution.py:329
  1458.9 14.3 copy-start.69
  1458.9 14.3 copy-start.75
  1458.9 14.4 copy-start.7
  1458.9 14.4 copy-start.42
  1458.9 14.4 copy-start.50
  1458.9 14.4 copy-start.72
  1496.7 74.2 %reduce-scatter.13.cloned.1.call-start = ((), (), s32[]{:S(2)}) async-start(), calls=%async_computation.22 | async-start | bytes 2621440 | tf_op jit(solution)/shard_map/reduce_scatter | solution.py:335
  1503.5 397.2 %reduce-scatter.9.cloned.1.call-start = ((), (), s32[]{:S(2)}) async-start(), calls=%async_computation.19 | async-start | bytes 1572864 | tf_op jit(solution)/shard_map/reduce_scatter | solution.py:266
  1504.2 404.5 %all-reduce.18.cloned.1.call-start = ((), (), s32[]{:S(2)}) async-start(), calls=%async_computation.23 | async-start | bytes 2097152 | tf_op jit(solution)/shard_map/psum | solution.py:370
  1541.6 34.7 %copy-start.1 = (bf16[256,2048]{1,0:T(8,128)(2,1)S(1)}, bf16[256,2048]{1,0:T(8,128)(2,1)}, u32[]{:S(2)}) copy-start(bf16[256,2048]{1,0:T(8,128)(2,1)} %copy-done) | copy-start | bytes 3145732
  1576.3 396.0 %reduce-scatter.23.cloned.1.call-start = ((), (), s32[]{:S(2)}) async-start(), calls=%async_computation.28 | async-start | bytes 139264 | tf_op jit(solution)/shard_map/reduce_scatter | solution.py:382
  1577.2 421.1 %reduce-scatter.21.cloned.1.call-start = ((), (), s32[]{:S(2)}) async-start(), calls=%async_computation.27 | async-start | bytes 8912896 | tf_op jit(solution)/shard_map/reduce_scatter | solution.py:381
  1583.6 609.7 %reduce-scatter.15.cloned.1.call-start = ((), (), s32[]{:S(2)}) async-start(), calls=%async_computation.24 | async-start | bytes 8912896 | tf_op jit(solution)/shard_map/reduce_scatter | solution.py:378
  1590.6 785.9 %reduce-scatter.19.cloned.1.call-start = ((), (), s32[]{:S(2)}) async-start(), calls=%async_computation.26 | async-start | bytes 8912896 | tf_op jit(solution)/shard_map/reduce_scatter | solution.py:380
  1596.4 963.2 %reduce-scatter.17.cloned.1.call-start = ((), (), s32[]{:S(2)}) async-start(), calls=%async_computation.25 | async-start | bytes 8912896 | tf_op jit(solution)/shard_map/reduce_scatter | solution.py:379
  1656.9 228.3 %all-to-all-start.5 = ((bf16[2048,3,1,512]{3,1,2,0:T(4,128)(2,1)}), bf16[2048,3,1,512]{3,1,2,0:T(4,128)(2,1)}, u32[]{:S(2)}, u32[]{:S(2)}) async-start(bf16[2048,3,1,512]{3,1,2,0:T(4,128)(2,1)} %copy.231), calls=%async_computation.13 | async-start | bytes 16777216 | tf_op jit(solution)/shard_map/all_to_all | solution.py:256
  1900.7 68.0 %copy-start.80 = (f32[256]{0:T(256)S(1)}, f32[256]{0:T(256)}, u32[]{:S(2)}) copy-start(f32[256]{0:T(256)} %get-tuple-element.191) | copy-start | bytes 3076
  (66 other events, 315.6 us)
Sparse Core Ops, SparseCore 0:
  9.6 79.6 all-gather.15
  90.9 79.2 all-gather.11
  171.7 113.9 all-gather.13
  288.0 46.1 all-gather.21
  336.4 35.2 all-gather.19
  373.2 79.5 all-gather.17
  457.7 23.8 all-reduce.13
  1259.2 22.4 all-reduce.15
  1496.8 35.8 reduce-scatter.10
  1535.7 35.1 reduce-scatter.12
  1573.7 10.1 reduce-scatter.8
  1586.3 20.7 all-reduce.17
  1609.8 50.5 reduce-scatter.22
  1663.3 335.0 reduce-scatter.20
  2001.2 192.1 reduce-scatter.14
  2196.2 180.2 reduce-scatter.18
  2379.3 180.2 reduce-scatter.16
where the time goes:
time: 2570 us
  waiting for transfers between devices  1550 us (60%)
  blocking collectives  463 us (18%)
  local copies, waits for them, and re-layouts  205 us (8%)
  matrix products  178 us (7%)
  other arithmetic  101 us (4%)
  starting transfers between devices  49 us (2%)
    all_to_all x1, waiting for transfers between devices, local(): lax.all_to_all(owner_terms.astype(jnp.bfloat16), ('fsdp', 'ctx'), split_a...  220 us
    all_gather x1, blocking collectives, local(): lax.all_gather(w_router, 'fsdp', axis=0, tiled=True)  206 us
    all_to_all x1, waiting for transfers between devices, local(): lax.all_to_all(rows_grad.reshape(group_count, part_span, model_width).ast...  197 us
    reduce_scatter x1, waiting for transfers between devices, local(): lax.psum_scatter(grad_wq, ('fsdp', 'ctx'), scatter_dimension=0, tiled=True)  195 us
    reduce_scatter x1, waiting for transfers between devices, local(): lax.psum_scatter(grad_wv, ('fsdp', 'ctx'), scatter_dimension=0, tiled=True)  183 us
    reduce_scatter x1, waiting for transfers between devices, local(): lax.psum_scatter(grad_wk, ('fsdp', 'ctx'), scatter_dimension=0, tiled=True)  183 us
    all_to_all x1, waiting for transfers between devices, local(): lax.all_to_all(send_grads, ('fsdp', 'ctx'), split_axis=0, concat_axis=0,...  181 us
    all_gather x1, blocking collectives, local(): lax.all_gather(gain_moe, 'fsdp', axis=0, tiled=True)  168 us
  transfers between devices with their start and end apart: 23, of which 14 were waited for; matrix products, arithmetic and copies ran while one was open for 16% of the time, Pallas kernels for 0%

commit v1 on v0

--- a/solution.py
+++ b/solution.py
@@ -73,7 +73,7 @@
     return earlier + later
 
 
-def local(
+def general(
     tokens,
     w_query,
     w_key,
@@ -401,9 +401,309 @@
     )
 
 
+def swap(value):
+    return lax.ppermute(value, "tp", [(0, 1), (1, 0)])
+
+
+def exchange(value, axes):
+    return lax.all_to_all(value, axes, split_axis=0, concat_axis=0, tiled=True)
+
+
+def spread(value, axes):
+    count = lax.axis_size(axes)
+    return exchange(jnp.broadcast_to(value[None], (count,) + value.shape), axes)
+
+
+def dot(left, right):
+    return jnp.dot(left, right, preferred_element_type=jnp.float32)
+
+
+def dot_nt(left, right):
+    return lax.dot_general(left, right, (((1,), (1,)), ((), ())), preferred_element_type=jnp.float32)
+
+
+def dot_tn(left, right):
+    return lax.dot_general(left, right, (((0,), (0,)), ((), ())), preferred_element_type=jnp.float32)
+
+
+def two_parts(values):
+    high = values.astype(jnp.bfloat16)
+    low = (values - high.astype(jnp.float32)).astype(jnp.bfloat16)
+    return (high, low)
+
+
+def by_core(mine, other, core):
+    return jnp.where(core == 0, jnp.stack([mine, other]), jnp.stack([other, mine]))
+
+
+def half_rows_sum(partial):
+    received = swap(partial[1].astype(jnp.bfloat16))
+    summed = (partial[0] + received.astype(jnp.float32)).astype(jnp.bfloat16)
+    pieces = exchange(summed, "ctx")
+    return jnp.sum(pieces.astype(jnp.float32), 0)
+
+
+def all_rows(half):
+    mine = spread(half, "ctx")
+    return jnp.stack([mine, swap(mine)])
+
+
+def one_chip(
+    tokens,
+    w_query,
+    w_key,
+    w_value,
+    w_out,
+    gain_attn,
+    gain_query,
+    gain_key,
+    gain_moe,
+    w_router,
+    w_experts,
+    routes,
+    cotangent,
+):
+    z, c, t = lax.axis_index("fsdp"), lax.axis_index("ctx"), lax.axis_index("tp")
+    nz, nc = lax.axis_size("fsdp"), lax.axis_size("ctx")
+    block, width = tokens.shape[1], tokens.shape[2]
+    rows = block // 2
+    tall = block * nc
+    deep = width // nz
+    ffn = w_experts.shape[3]
+    most = block * TOPK * 9 // (8 * E)
+    bf16, f32 = jnp.bfloat16, jnp.float32
+
+    token_half = lax.dynamic_slice_in_dim(tokens[0], t * rows, rows, 0)
+    cotan_half = lax.dynamic_slice_in_dim(cotangent[0], t * rows, rows, 0)
+    small = jnp.concatenate(
+        [gain_attn, gain_moe, w_router.T.reshape(-1), gain_query, gain_key]
+    )
+    small = lax.all_gather(small, "fsdp", axis=0)
+    attn_gain = small[:, :deep].reshape(-1).astype(f32)
+    moe_gain = small[:, deep : 2 * deep].reshape(-1).astype(f32)
+    router = small[:, 2 * deep : (2 + E) * deep].reshape(nz, E, deep)
+    router = router.transpose(0, 2, 1).reshape(width, E)
+    part = HD // nz
+    query_gain = small[:, (2 + E) * deep : (2 + E) * deep + part].reshape(-1).astype(f32)
+    key_gain = small[:, (2 + E) * deep + part :].reshape(-1).astype(f32)
+    routes_all = lax.all_gather(routes[0], ("fsdp", "ctx"), axis=0)
+
+    local = w_query.shape[1] // nc
+    cols = [lax.dynamic_slice_in_dim(w, c * local, local, 1) for w in (w_query, w_key, w_value)]
+    w_qkv = spread(jnp.concatenate(cols, 1), "fsdp").reshape(width, 3 * local)
+    w_o = spread(lax.dynamic_slice_in_dim(w_out, c * local, local, 0), "fsdp")
+    w_o = w_o.transpose(1, 0, 2).reshape(local, width)
+
+    own = lax.dynamic_slice_in_dim(w_experts, c * nz, nz, 2)
+    own = own.transpose(1, 2, 0, 3)
+    mats = [exchange(own[k], "fsdp").reshape(width, ffn) for k in range(3)]
+    others = [swap(m) for m in mats]
+    halves = [mats, others]
+
+    x_rows = all_rows(token_half).reshape(tall, width).astype(f32)
+    place = (
+        jnp.arange(nc, dtype=jnp.int32)[None, :, None] * block
+        + ((jnp.arange(2, dtype=jnp.int32) + t) % 2)[:, None, None] * rows
+        + jnp.arange(rows, dtype=jnp.int32)[None, None, :]
+    ).reshape(tall)
+    half_dim = HD // 2
+    inv_freq = jnp.exp(jnp.arange(half_dim, dtype=f32) * (-2.0 * math.log(ROPE_BASE) / HD))
+    angles = place.astype(f32)[:, None] * inv_freq[None, :]
+    cos_full = jnp.concatenate([jnp.cos(angles)] * 2, -1)[:, None, :]
+    sin_full = jnp.concatenate([jnp.sin(angles)] * 2, -1)[:, None, :]
+    normed_one = (x_rows * rms_scale(x_rows) * attn_gain).astype(bf16)
+    proj = dot(normed_one, w_qkv).reshape(tall, 3, local // HD, HD)
+    query_heads, key_heads = proj[:, 0], proj[:, 1]
+    values = proj[:, 2].astype(bf16)
+    query_inv, key_inv = rms_scale(query_heads), rms_scale(key_heads)
+    queries = apply_rope(query_heads * query_inv * query_gain, cos_full, sin_full).astype(bf16)
+    keys = apply_rope(key_heads * key_inv * key_gain, cos_full, sin_full).astype(bf16)
+    score_scale = 1.0 / math.sqrt(HD)
+    scores = jnp.einsum("qhd,khd->hqk", queries, keys, preferred_element_type=f32) * score_scale
+    maximum = jnp.max(scores, -1, keepdims=True)
+    exp_scores = jnp.exp(scores - maximum)
+    denominator = jnp.sum(exp_scores, -1, keepdims=True)
+    attn_probs = exp_scores / denominator
+    log_total = maximum + jnp.log(denominator)
+    context = jnp.einsum("hqk,khd->qhd", attn_probs.astype(bf16), values, preferred_element_type=f32)
+    context = context.astype(bf16).reshape(tall, local)
+    attn_part = dot(context, w_o).reshape(2, nc, rows, width)
+    own_tokens = token_half.astype(f32)
+    residual = own_tokens + half_rows_sum(attn_part)
+    inv_two = rms_scale(residual)
+    normed_two = (residual * inv_two * moe_gain).astype(bf16)
+    logits = dot(normed_two, router)
+    router_probs = jax.nn.softmax(logits, -1)
+
+    ids = jnp.arange(E, dtype=jnp.int32)
+    named_all = jnp.any(routes_all[:, :, :, None] == ids, 2)
+    named_all = named_all.reshape(nz, nc, block, E).astype(jnp.int32)
+    own_seq = lax.dynamic_index_in_dim(named_all, z, 0, keepdims=False).reshape(tall, E)
+    slot = jnp.cumsum(own_seq, 0) - own_seq
+    kept_seq = (own_seq * (slot < CAP)).astype(f32)
+    kept = lax.dynamic_slice_in_dim(kept_seq, c * block + t * rows, rows, 0)
+    gates = router_probs * kept
+    line = lax.dynamic_index_in_dim(named_all, c, 1, keepdims=False)
+    line = lax.dynamic_slice_in_dim(line, t * 2, 2, 0)
+    rank = jnp.cumsum(line, 1) - line
+    plane = jnp.arange(nc, dtype=jnp.int32) * nz + z
+    line = jnp.take(line, plane, axis=2)
+    rank = jnp.take(rank, plane, axis=2)
+    order = (jnp.arange(2, dtype=jnp.int32) + t) % 2
+    line = jnp.take(line.reshape(2, 2, rows, nc), order, axis=1).reshape(2, block, nc)
+    rank = jnp.take(rank.reshape(2, 2, rows, nc), order, axis=1).reshape(2, block, nc)
+    pick = (rank[..., None] == jnp.arange(most, dtype=jnp.int32)) & (line[..., None] > 0)
+    pick = pick.transpose(0, 2, 3, 1).reshape(2, nc * most, block).astype(bf16)
+
+    def dispatch(half):
+        mine = spread(half, "fsdp")
+        keep = lax.dynamic_slice_in_dim(mine, t * 2, 2, 0)
+        send = lax.dynamic_slice_in_dim(mine, (1 - t) * 2, 2, 0)
+        both = jnp.concatenate([keep, swap(send)], 1)
+        picked = jnp.einsum("sib,sbw->siw", pick, both, preferred_element_type=f32).astype(bf16)
+        picked = picked.reshape(2, nc, most, -1).transpose(1, 0, 2, 3)
+        return exchange(picked, "ctx").reshape(nc * 2 * most, -1)
+
+    cot_rows = dispatch(cotan_half)
+    high, low = two_parts(gates)
+    tail = jnp.zeros((rows, 128 - 2 * E), bf16)
+    in_rows = dispatch(jnp.concatenate([normed_two, high, low, tail], 1))
+    x_in = in_rows[:, :width]
+    mine_id = c * nz + z
+    extra = in_rows[:, width : width + 2 * E].astype(f32).reshape(-1, 2, E)
+    weight = jnp.sum(jnp.where(ids == mine_id, extra, 0.0), (1, 2))[:, None]
+
+    out_rows = back_rows = 0.0
+    pair_grad = 0.0
+    updates = []
+    for w_gate, w_up, w_down in halves:
+        gate_act = dot(x_in, w_gate)
+        up_act = dot(x_in, w_up)
+        grad_out = dot(cot_rows, w_down)
+        sig = jax.nn.sigmoid(gate_act)
+        silu = gate_act * sig
+        hidden = silu * up_act
+        pair_grad = pair_grad + jnp.sum(hidden.astype(bf16).astype(f32) * grad_out, 1, keepdims=True)
+        weighted = (weight * hidden).astype(bf16)
+        grad_hidden = weight * grad_out
+        grad_gate = (grad_hidden * up_act * sig * (1.0 + gate_act * (1.0 - sig))).astype(bf16)
+        grad_up = (grad_hidden * silu).astype(bf16)
+        out_rows = out_rows + dot_nt(weighted, w_down)
+        back_rows = back_rows + dot_nt(grad_gate, w_gate) + dot_nt(grad_up, w_up)
+        updates.append((dot_tn(x_in, grad_gate), dot_tn(x_in, grad_up), dot_tn(cot_rows, weighted)))
+    own_updates, other_updates = updates
+    high, low = two_parts(jnp.where(ids == mine_id, pair_grad, 0.0))
+    tail = jnp.zeros((high.shape[0], 128 - 2 * E), bf16)
+    reply = jnp.concatenate([out_rows.astype(bf16), back_rows.astype(bf16), high, low, tail], 1)
+
+    def collect(reply):
+        reply = exchange(reply.reshape(nc, 2, most, -1), "ctx")
+        reply = reply.transpose(1, 0, 2, 3).reshape(2, nc * most, -1)
+        dense = jnp.einsum("sib,siw->sbw", pick, reply, preferred_element_type=f32).astype(bf16)
+        mine, send = dense[:, :rows], dense[:, rows:]
+        stacked = by_core(mine, swap(send), t).reshape(nz, rows, -1)
+        return jnp.sum(exchange(stacked, "fsdp").astype(f32), 0)
+
+    dense = collect(reply)
+    moe_rows, grad_rows = dense[:, :width], dense[:, width : 2 * width]
+    pair_rows = dense[:, 2 * width : 2 * width + E] + dense[:, 2 * width + E : 2 * width + 2 * E]
+
+    dw_experts = []
+    for mine, other in zip(own_updates, other_updates):
+        total = (mine + swap(other.astype(bf16)).astype(f32)).astype(bf16)
+        dw_experts.append(exchange(total.reshape(nz * nc, -1, ffn), ("fsdp", "ctx")))
+    dw_experts = jnp.stack(dw_experts, 1).astype(f32)
+    dw_experts = dw_experts.reshape(nz, nc, 3, -1, ffn).transpose(3, 2, 1, 0, 4)
+    dw_experts = dw_experts.reshape(-1, 3, E, ffn)
+
+    layer = (residual + moe_rows).astype(bf16)
+    piece = width // 2
+    layer_mine = lax.dynamic_slice_in_dim(layer, t * piece, piece, 1)
+    layer_send = lax.dynamic_slice_in_dim(layer, (1 - t) * piece, piece, 1)
+    layer_out = by_core(layer_mine, swap(layer_send), t).reshape(1, block, piece)
+
+    grad_router_probs = pair_rows * kept
+    grad_logits = router_probs * (
+        grad_router_probs - jnp.sum(router_probs * grad_router_probs, -1, keepdims=True)
+    )
+    grad_logits = grad_logits.astype(bf16)
+    dw_router = dot_tn(normed_two, grad_logits)
+    grad_normed_two = grad_rows + dot_nt(grad_logits, router)
+    dgain_moe = jnp.sum(grad_normed_two * residual * inv_two, 0)
+    grad_residual = cotan_half.astype(f32) + norm_back(grad_normed_two, residual, inv_two, moe_gain)
+    grad_attn = all_rows(grad_residual.astype(bf16)).reshape(tall, width)
+
+    dw_out = dot_tn(context, grad_attn).astype(bf16)
+    grad_context = dot_nt(grad_attn, w_o).astype(bf16).reshape(tall, -1, HD)
+    scores = jnp.einsum("qhd,khd->hqk", queries, keys, preferred_element_type=f32) * score_scale
+    attn_probs = jnp.exp(scores - log_total)
+    grad_probs = jnp.einsum("qhd,khd->hqk", grad_context, values, preferred_element_type=f32)
+    grad_scores = attn_probs * (grad_probs - jnp.sum(attn_probs * grad_probs, -1, keepdims=True))
+    grad_scores = grad_scores.astype(bf16)
+    grad_queries = jnp.einsum("hqk,khd->qhd", grad_scores, keys, preferred_element_type=f32) * score_scale
+    grad_keys = jnp.einsum("hqk,qhd->khd", grad_scores, queries, preferred_element_type=f32) * score_scale
+    grad_values = jnp.einsum(
+        "hqk,qhd->khd", attn_probs.astype(bf16), grad_context, preferred_element_type=f32
+    ).astype(bf16)
+    grad_qnormed = rope_back(grad_queries, cos_full, sin_full)
+    grad_knormed = rope_back(grad_keys, cos_full, sin_full)
+    dgain_query = jnp.sum(grad_qnormed * query_heads * query_inv, (0, 1))
+    dgain_key = jnp.sum(grad_knormed * key_heads * key_inv, (0, 1))
+    grad_qproj = norm_back(grad_qnormed, query_heads, query_inv, query_gain).astype(bf16)
+    grad_kproj = norm_back(grad_knormed, key_heads, key_inv, key_gain).astype(bf16)
+    grad_proj = jnp.stack([grad_qproj, grad_kproj, grad_values], 1).reshape(tall, 3 * local)
+    dw_qkv = dot_tn(normed_one, grad_proj).astype(bf16)
+    grad_normed_part = dot_nt(grad_proj, w_qkv).reshape(2, nc, rows, width)
+    grad_normed_one = half_rows_sum(grad_normed_part)
+    inv_one = rms_scale(own_tokens)
+    dgain_attn = jnp.sum(grad_normed_one * own_tokens * inv_one, 0)
+    grad_tokens = grad_residual + norm_back(grad_normed_one, own_tokens, inv_one, attn_gain)
+    grad_tokens = grad_tokens.astype(bf16)
+    tokens_grad = by_core(grad_tokens, swap(grad_tokens), t).reshape(1, block, width)
+
+    chips = nz * nc
+    strip = width // chips
+    got_qkv = exchange(dw_qkv.reshape(chips, strip, 3 * local), ("fsdp", "ctx"))
+    got_qkv = jnp.sum(got_qkv.reshape(nz, nc, strip, 3, local).astype(f32), 0)
+    got_qkv = got_qkv.transpose(2, 1, 0, 3).reshape(3, strip, nc * local)
+    got_out = exchange(dw_out.reshape(local, chips, strip).transpose(1, 0, 2), ("fsdp", "ctx"))
+    got_out = jnp.sum(got_out.reshape(nz, nc, local, strip).astype(f32), 0).reshape(nc * local, strip)
+
+    head_part = HD // chips
+    sums = jnp.concatenate(
+        [
+            dw_router.reshape(chips, strip * E),
+            dgain_attn.reshape(chips, strip),
+            dgain_moe.reshape(chips, strip),
+            dgain_query.reshape(chips, head_part),
+            dgain_key.reshape(chips, head_part),
+        ],
+        1,
+    )
+    sums = jnp.sum(exchange(sums, ("fsdp", "ctx")), 0)
+    sums = sums + swap(sums)
+    base = strip * E
+    return (
+        layer_out,
+        tokens_grad,
+        got_qkv[0],
+        got_qkv[1],
+        got_qkv[2],
+        got_out,
+        sums[base : base + strip],
+        sums[base + 2 * strip : base + 2 * strip + head_part],
+        sums[base + 2 * strip + head_part :],
+        sums[base + strip : base + 2 * strip],
+        sums[:base].reshape(strip, E),
+        dw_experts,
+    )
+
+
 def solution(mesh):
+    chips = mesh.shape["fsdp"] * mesh.shape["ctx"]
+    plain = chips == E and mesh.shape["fsdp"] == 4 and mesh.shape["tp"] == 2
     return jax.shard_map(
-        local,
+        one_chip if plain else general,
         mesh=mesh,
         in_specs=(
             P("fsdp", "ctx", None),

time: 2570 us -> 1290 us (0.50)
  waiting for transfers between devices: 1550 us -> 472 us
  blocking collectives: 463 us -> 253 us
  starting transfers between devices: 49 us -> 148 us
  local copies, waits for them, and re-layouts: 205 us -> 131 us
  other arithmetic: 101 us -> 69.7 us
    reduce_scatter x8 -> x0, waiting for transfers between devices: 635 us -> none  [the longest x1 195 us: local(): lax.psum_scatter(grad_wq, ('fsdp', 'ctx'), scatter_dimension=0, tiled=True)]
    all_to_all x6 -> x18, waiting for transfers between devices: 762 us -> 411 us  [exchange(): return lax.all_to_all(value, axes, split_axis=0, concat_axis=0, tiled=True)]
    all_gather x3 -> x1, blocking collectives: 384 us -> 64.2 us  [one_chip(): routes_all = lax.all_gather(routes[0], ('fsdp', 'ctx'), axis=0)]
    all_to_all x0 -> x3, blocking collectives: none -> 189 us  [exchange(): return lax.all_to_all(value, axes, split_axis=0, concat_axis=0, tiled=True)]
    all_gather x6 -> x0, waiting for transfers between devices: 139 us -> none  [the longest x1 68.7 us: local(): lax.all_gather(w_value, 'fsdp', axis=0, tiled=True)]
    gather x5 -> x4, local copies, waits for them, and re-layouts: 77.7 us -> 2.28 us  [the longest x1 0.57 us: one_chip(): rank = jnp.take(rank, plane, axis=2)]
    all_to_all x6 -> x18, starting transfers between devices: 47.8 us -> 121 us  [exchange(): return lax.all_to_all(value, axes, split_axis=0, concat_axis=0, tiled=True)]
    unnamed x3 -> x0, blocking collectives: 69.7 us -> none
  transfers between devices with their start and end apart: 23 -> 35, of which waited for: 14 -> 20; matrix products, arithmetic and copies ran while one was open for 16% -> 21% of each run, Pallas kernels for 0% -> 0%
where the time goes in v1:
time: 1290 us; the launch traced here: 1280 us
  waiting for transfers between devices  472 us (37%)
  blocking collectives  253 us (20%)
  matrix products  190 us (15%)
  starting transfers between devices  148 us (11%)
  local copies, waits for them, and re-layouts  131 us (10%)
  other arithmetic  69.7 us (5%)
  between operations  16.7 us (1%)
    all_to_all x18, waiting for transfers between devices, exchange(): return lax.all_to_all(value, axes, split_axis=0, concat_axis=0, tiled=True)  411 us
    all_to_all x3, blocking collectives, exchange(): return lax.all_to_all(value, axes, split_axis=0, concat_axis=0, tiled=True)  189 us
    all_to_all x18, starting transfers between devices, exchange(): return lax.all_to_all(value, axes, split_axis=0, concat_axis=0, tiled=True)  121 us
    all_gather x1, blocking collectives, one_chip(): routes_all = lax.all_gather(routes[0], ('fsdp', 'ctx'), axis=0)  64.2 us
    dot_general x9, matrix products, dot(): return jnp.dot(left, right, preferred_element_type=jnp.float32)  57.2 us
    dot_general x9, matrix products, dot_nt(): lax.dot_general(left, right, (((1,), (1,)), ((), ())), preferred_element_...  56.1 us
    dot_general x9, matrix products, dot_tn(): lax.dot_general(left, right, (((0,), (0,)), ((), ())), preferred_element_...  51.5 us
    unnamed x2, waiting for transfers between devices  47.9 us
  transfers between devices with their start and end apart: 35, of which 20 were waited for; matrix products, arithmetic and copies ran while one was open for 21% of the time, Pallas kernels for 0%

profile of v1, /device:TPU:15, one launch (start us, length us, event | category | flops | bytes accessed | tf_op | source)
XLA Modules:
  0.0 1280.8 jit_solution(5397649782170970036)
XLA Ops:
  17.5 20.7 %all-to-all-done = bf16[4,128,2048]{2,1,0:T(8,128)(2,1)S(1)} async-done(((bf16[4,128,2048]{2,1,0:T(8,128)(2,1)}), bf16[4,128,2048]{2,1,0:T(8,128)(2,1)S(1)}, u32[]{:S(2)}, u32[]{:S(2)}) %all-to-all-start) | async-done | bytes 2097184 | tf_op jit(solution)/shard_map/all_to_all | solution.py:409
  49.8 10.7 constant_dynamic-slice_fusion.3
  73.9 47.9 %all-reduce.3.cloned.1.call-done = bf16[37120]{0:T(1024)(128)(2,1)} async-done(((bf16[37120]{0:T(1024)(128)(2,1)}), bf16[37120]{0:T(1024)(128)(2,1)}) %all-reduce.3.cloned.1.call-update) | async-done | bytes 74256
  176.1 31.6 %all-to-all-done.9 = bf16[4,128,2048]{2,1,0:T(8,128)(2,1)S(1)} async-done(((bf16[4,128,2048]{2,1,0:T(8,128)(2,1)}), bf16[4,128,2048]{2,1,0:T(8,128)(2,1)S(1)}, u32[]{:S(2)}, u32[]{:S(2)}) %all-to-all-start.9) | async-done | bytes 2097184 | tf_op jit(solution)/shard_map/all_to_all | solution.py:409
  207.7 8.3 all-to-all-start.8
  225.0 34.8 %all-to-all-done.8 = bf16[4,512,512]{2,1,0:T(8,128)(2,1)} async-done(((bf16[4,512,512]{2,1,0:T(8,128)(2,1)}), bf16[4,512,512]{2,1,0:T(8,128)(2,1)}, u32[]{:S(2)}, u32[]{:S(2)}) %all-to-all-start.8) | async-done | bytes 2097184 | tf_op jit(solution)/shard_map/all_to_all | solution.py:409
  259.7 25.6 %all_to_all.109 = bf16[4,128,2048]{2,1,0:T(8,128)(2,1)} all-to-all(bf16[4,128,2048]{2,1,0:T(8,128)(2,1)S(1)} %add_convert_fusion.6), channel_id=1, replica_groups=mesh['fsdp'=4,'ctx'=4,'tp'=2] {'ctx'}, dimensions={0} | all-to-all | bytes 4194304 | tf_op jit(solution)/shard_map/all_to_all | solution.py:409
  285.3 9.5 all-to-all-start.7
  294.9 64.2 %all_gather.11 = s32[16,256,8]{1,2,0:T(8,128)S(1)} all-gather(s32[1,256,8]{1,2,0:T(8,128)S(1)} %copy-done.66), channel_id=1, replica_groups=mesh['fsdp'=4,'ctx'=4,'tp'=2] {'fsdp','ctx'}, dimensions={0}, use_global_device_ids=true | all-gather | bytes 139264 | tf_op jit(solution)/shard_map/all_gather | solution.py:489
  369.6 48.7 %all_to_all.110 = bf16[4,128,2176]{2,1,0:T(8,128)(2,1)S(1)} all-to-all(bf16[4,128,2176]{2,1,0:T(8,128)(2,1)S(1)} %broadcast_in_dim.66), channel_id=1, replica_groups=mesh['fsdp'=4,'ctx'=4,'tp'=2] {'fsdp'}, dimensions={0} | all-to-all | bytes 4456448 | tf_op jit(solution)/shard_map/all_to_all | solution.py:409
  439.3 26.5 %all-to-all-done.6 = bf16[4,512,512]{2,1,0:T(8,128)(2,1)} async-done(((bf16[4,512,512]{2,1,0:T(8,128)(2,1)}), bf16[4,512,512]{2,1,0:T(8,128)(2,1)}, u32[]{:S(2)}, u32[]{:S(2)}) %all-to-all-start.6) | async-done | bytes 2097184 | tf_op jit(solution)/shard_map/all_to_all | solution.py:409
  465.8 8.6 all-to-all-start.5
  486.7 37.8 %all-to-all-done.5 = bf16[4,2,144,2176]{3,2,1,0:T(8,128)(2,1)} async-done(((bf16[4,2,144,2176]{3,2,1,0:T(8,128)(2,1)}), bf16[4,2,144,2176]{3,2,1,0:T(8,128)(2,1)}, u32[]{:S(2)}, u32[]{:S(2)}) %all-to-all-start.5) | async-done | bytes 5013536 | tf_op jit(solution)/shard_map/all_to_all | solution.py:409
  524.6 10.7 all-to-all-start.10
  537.2 7.4 fusion.69
  544.6 7.4 fusion.71
  551.9 7.4 fusion.67
  560.4 7.1 fusion.65
  567.5 17.9 %all-to-all-done.10 = bf16[4,2,144,2048]{3,2,1,0:T(8,128)(2,1)} async-done(((bf16[4,2,144,2048]{3,2,1,0:T(8,128)(2,1)}), bf16[4,2,144,2048]{3,2,1,0:T(8,128)(2,1)}, u32[]{:S(2)}, u32[]{:S(2)}) %all-to-all-start.10) | async-done | bytes 4718624 | tf_op jit(solution)/shard_map/all_to_all | solution.py:409
  585.5 10.3 multiply_reduce_fusion.3
  595.7 8.9 multiply_reduce_fusion.2
  605.3 8.3 fusion.112
  613.6 8.1 fusion.111
  626.1 8.1 fusion.113
  634.2 6.5 add_convert_fusion.1
  640.7 13.1 %add_convert_fusion = bf16[1152,2048]{1,0:T(8,128)(2,1)} fusion(f32[1152,2048]{1,0:T(8,128)} %fusion.113, f32[1152,2048]{1,0:T(8,128)} %fusion.111, f32[1152,2048]{1,0:T(8,128)} %fusion.112, bf16[1152,512]{0,1:T(8,128)(2,1)S(1)} %copy-done.35, bf16[2048,512]{1,0:T(8,128)(2,1)S(1)} %collective-permute-done.4), kind=kOutput, calls=%fused_computation.9 | convolution fusion | flops 2425356288 | bytes 36306944 | tf_op jit(solution)/shard_map/dot_general | solution.py:422
  653.8 15.5 %concatenate.49 = bf16[1152,4224]{1,0:T(8,128)(2,1)} concatenate(bf16[1152,2048]{1,0:T(8,128)(2,1)} %add_convert_fusion.1, bf16[1152,2048]{1,0:T(8,128)(2,1)} %add_convert_fusion, bf16[1152,16]{1,0:T(8,128)(2,1)S(1)} %copy.289, bf16[1152,16]{1,0:T(8,128)(2,1)S(1)} %copy.290, bf16[1152,96]{1,0:T(8,128)(2,1)S(1)} %broadcast_in_dim.78), dimensions={1} | concatenate | bytes 19464192 | tf_op jit(solution)/shard_map/concatenate | solution.py:597
  669.4 114.3 %all_to_all.111 = bf16[4,2,144,4224]{3,2,1,0:T(8,128)(2,1)} all-to-all(bf16[4,2,144,4224]{3,2,1,0:T(8,128)(2,1)} %bitcast.304), channel_id=1, replica_groups=mesh['fsdp'=4,'ctx'=4,'tp'=2] {'ctx'}, dimensions={0} | all-to-all | bytes 19464192 | tf_op jit(solution)/shard_map/all_to_all | solution.py:409
  783.7 8.3 copy.291
  791.9 7.7 convolution_convert_fusion
  812.6 11.6 all-to-all-start.12
  831.5 85.4 %all-to-all-done.12 = bf16[4,128,4224]{2,1,0:T(8,128)(2,1)} async-done(((bf16[4,128,4224]{2,1,0:T(8,128)(2,1)}), bf16[4,128,4224]{2,1,0:T(8,128)(2,1)}, u32[]{:S(2)}, u32[]{:S(2)}) %all-to-all-start.12) | async-done | bytes 4325408 | tf_op jit(solution)/shard_map/all_to_all | solution.py:409
  930.6 7.1 convolution_convert_fusion.6
  939.1 6.9 add_convert_fusion.2
  946.0 7.1 all-to-all-done.13
  954.5 8.1 all-to-all-start.20
  970.5 7.0 add_convert_fusion.4
  977.5 6.6 add_convert_fusion.3
  986.5 23.9 %all-to-all-done.20 = bf16[16,128,512]{2,1,0:T(8,128)(2,1)S(1)} async-done(((bf16[16,128,512]{2,1,0:T(8,128)(2,1)}), bf16[16,128,512]{2,1,0:T(8,128)(2,1)S(1)}, u32[]{:S(2)}, u32[]{:S(2)}) %all-to-all-start.20) | async-done | bytes 2097184 | tf_op jit(solution)/shard_map/all_to_all | solution.py:409
  1034.5 27.9 %all-to-all-done.18 = bf16[16,128,512]{2,1,0:T(8,128)(2,1)} async-done(((bf16[16,128,512]{2,1,0:T(8,128)(2,1)}), bf16[16,128,512]{2,1,0:T(8,128)(2,1)}, u32[]{:S(2)}, u32[]{:S(2)}) %all-to-all-start.18) | async-done | bytes 2097184 | tf_op jit(solution)/shard_map/all_to_all | solution.py:409
  1086.5 28.4 %all-to-all-done.19 = bf16[16,128,512]{2,1,0:T(8,128)(2,1)S(1)} async-done(((bf16[16,128,512]{2,1,0:T(8,128)(2,1)}), bf16[16,128,512]{2,1,0:T(8,128)(2,1)S(1)}, u32[]{:S(2)}, u32[]{:S(2)}) %all-to-all-start.19) | async-done | bytes 2097184 | tf_op jit(solution)/shard_map/all_to_all | solution.py:409
  1124.1 16.8 %all-to-all-done.14 = bf16[4,128,2048]{2,1,0:T(8,128)(2,1)} async-done(((bf16[4,128,2048]{2,1,0:T(8,128)(2,1)}), bf16[4,128,2048]{2,1,0:T(8,128)(2,1)}, u32[]{:S(2)}, u32[]{:S(2)}) %all-to-all-start.14) | async-done | bytes 2097184 | tf_op jit(solution)/shard_map/all_to_all | solution.py:409
  1151.6 19.4 %all-to-all-done.16 = bf16[16,256,128]{2,1,0:T(8,128)(2,1)S(1)} async-done(((bf16[16,256,128]{2,1,0:T(8,128)(2,1)}), bf16[16,256,128]{2,1,0:T(8,128)(2,1)S(1)}, u32[]{:S(2)}, u32[]{:S(2)}) %all-to-all-start.16) | async-done | bytes 1048608 | tf_op jit(solution)/shard_map/all_to_all | solution.py:409
  1171.0 6.8 all-to-all-start.17
  1177.9 7.9 convolution_convert_fusion.3
  1209.1 6.9 convert_bitcast_fusion
  1216.0 14.7 %reshape.627 = f32[128,3,16,512]{3,2,1,0:T(8,128)} reshape(f32[128,3,4,4,512]{4,3,2,1,0:T(4,128)} %convert_bitcast_fusion) | data formatting | bytes 25165824 | tf_op jit(solution)/shard_map/reshape | solution.py:617
  1238.8 28.9 %all-to-all-done.15 = bf16[16,128,768]{1,2,0:T(8,128)(2,1)} async-done(((bf16[16,128,768]{1,2,0:T(8,128)(2,1)}), bf16[16,128,768]{1,2,0:T(8,128)(2,1)}, u32[]{:S(2)}, u32[]{:S(2)}) %all-to-all-start.15) | async-done | bytes 3145760 | tf_op jit(solution)/shard_map/all_to_all | solution.py:409
  (432 shorter events, 301.0 us)
Async XLA Ops:
  11.4 26.8 %all-to-all-start = ((bf16[4,128,2048]{2,1,0:T(8,128)(2,1)}), bf16[4,128,2048]{2,1,0:T(8,128)(2,1)S(1)}, u32[]{:S(2)}, u32[]{:S(2)}) async-start(bf16[4,128,2048]{2,1,0:T(8,128)(2,1)} %broadcast_in_dim.57), calls=%async_computation | async-start | bytes 4194304 | tf_op jit(solution)/shard_map/all_to_all | solution.py:409
  41.3 87.8 %all-to-all-start.1 = ((bf16[4,512,768]{1,2,0:T(8,128)(2,1)}), bf16[4,512,768]{1,2,0:T(8,128)(2,1)}, u32[]{:S(2)}, u32[]{:S(2)}) async-start(bf16[4,512,768]{1,2,0:T(8,128)(2,1)} %broadcast_in_dim.60), calls=%async_computation.1 | async-start | bytes 6291456 | tf_op jit(solution)/shard_map/all_to_all | solution.py:409
  46.2 75.6 %all-reduce.3.cloned.1.call-start = ((), (), s32[]{:S(2)}) async-start(), calls=%async_computation.21 | async-start | bytes 151552
  60.5 62.6 %collective-permute-start = (bf16[4,128,2048]{2,1,0:T(8,128)(2,1)S(1)}, bf16[4,128,2048]{2,1,0:T(8,128)(2,1)}, u32[]{:S(2)}, u32[]{:S(2)}) collective-permute-start(bf16[4,128,2048]{2,1,0:T(8,128)(2,1)S(1)} %all-to-all-done), channel_id=1, source_target_pairs={{0,1},{1,0},{2,3},{3,2},{4,5},{5,4},{6,7},{7,6},{8,9},{9,8},{10,11... | collective-permute-start | bytes 6291464 | tf_op jit(solution)/shard_map/ppermute | solution.py:405
  123.0 40.9 %copy-start.71 = (f32[128]{0:T(128)}, f32[128]{0:T(128)S(1)}, u32[]{:S(2)}) copy-start(f32[128]{0:T(128)S(1)} %reshape.621) | copy-start | bytes 1540
  123.1 40.8 %copy-start.73 = (f32[128]{0:T(128)}, f32[128]{0:T(128)S(1)}, u32[]{:S(2)}) copy-start(f32[128]{0:T(128)S(1)} %reshape.620) | copy-start | bytes 1540
  130.1 26.0 %all-to-all-start.2 = ((bf16[4,256,512]{1,2,0:T(8,128)(2,1)}), bf16[4,256,512]{1,2,0:T(8,128)(2,1)S(1)}, u32[]{:S(2)}, u32[]{:S(2)}) async-start(bf16[4,256,512]{1,2,0:T(8,128)(2,1)} %broadcast_in_dim.61), calls=%async_computation.2 | async-start | bytes 2097152 | tf_op jit(solution)/shard_map/all_to_all | solution.py:409
  157.9 49.8 %all-to-all-start.9 = ((bf16[4,128,2048]{2,1,0:T(8,128)(2,1)}), bf16[4,128,2048]{2,1,0:T(8,128)(2,1)S(1)}, u32[]{:S(2)}, u32[]{:S(2)}) async-start(bf16[4,128,2048]{2,1,0:T(8,128)(2,1)} %broadcast_in_dim.74), calls=%async_computation.9 | async-start | bytes 4194304 | tf_op jit(solution)/shard_map/all_to_all | solution.py:409
  176.1 39.9 %copy-start.26 = (bf16[4,256,512]{1,2,0:T(8,128)(2,1)S(1)}, bf16[4,256,512]{1,2,0:T(8,128)(2,1)}, u32[]{:S(2)}) copy-start(bf16[4,256,512]{1,2,0:T(8,128)(2,1)} %copy-done.25) | copy-start | bytes 3145732
  207.7 52.1 %all-to-all-start.8 = ((bf16[4,512,512]{2,1,0:T(8,128)(2,1)}), bf16[4,512,512]{2,1,0:T(8,128)(2,1)}, u32[]{:S(2)}, u32[]{:S(2)}) async-start(bf16[4,512,512]{2,1,0:T(8,128)(2,1)} %get-tuple-element.108), calls=%async_computation.8 | async-start | bytes 4194304 | tf_op jit(solution)/shard_map/all_to_all | solution.py:409
  218.6 5.6 collective-permute-start.1
  285.3 83.6 %all-to-all-start.7 = ((bf16[4,512,512]{2,1,0:T(8,128)(2,1)}), bf16[4,512,512]{2,1,0:T(8,128)(2,1)}, u32[]{:S(2)}, u32[]{:S(2)}) async-start(bf16[4,512,512]{2,1,0:T(8,128)(2,1)} %get-tuple-element.109), calls=%async_computation.7 | async-start | bytes 4194304 | tf_op jit(solution)/shard_map/all_to_all | solution.py:409
  418.3 47.5 %all-to-all-start.6 = ((bf16[4,512,512]{2,1,0:T(8,128)(2,1)}), bf16[4,512,512]{2,1,0:T(8,128)(2,1)}, u32[]{:S(2)}, u32[]{:S(2)}) async-start(bf16[4,512,512]{2,1,0:T(8,128)(2,1)} %get-tuple-element.110), calls=%async_computation.6 | async-start | bytes 4194304 | tf_op jit(solution)/shard_map/all_to_all | solution.py:409
  427.9 7.2 collective-permute-start.2
  465.8 58.7 %all-to-all-start.5 = ((bf16[4,2,144,2176]{3,2,1,0:T(8,128)(2,1)}), bf16[4,2,144,2176]{3,2,1,0:T(8,128)(2,1)}, u32[]{:S(2)}, u32[]{:S(2)}) async-start(bf16[4,2,144,2176]{3,2,1,0:T(8,128)(2,1)} %bitcast.307), calls=%async_computation.5 | async-start | bytes 10027008 | tf_op jit(solution)/shard_map/all_to_all | solution.py:409
  474.5 8.3 collective-permute-start.6
  479.8 72.1 %collective-permute-start.3 = (bf16[2048,512]{1,0:T(8,128)(2,1)}, bf16[2048,512]{1,0:T(8,128)(2,1)}, u32[]{:S(2)}, u32[]{:S(2)}) collective-permute-start(bf16[2048,512]{1,0:T(8,128)(2,1)} %bitcast.47), channel_id=1, source_target_pairs={{0,1},{1,0},{2,3},{3,2},{4,5},{5,4},{6,7},{7,6},{8,9},{9,8},{10,11... | collective-permute-start | bytes 6291464 | tf_op jit(solution)/shard_map/ppermute | solution.py:405
  524.6 60.9 %all-to-all-start.10 = ((bf16[4,2,144,2048]{3,2,1,0:T(8,128)(2,1)}), bf16[4,2,144,2048]{3,2,1,0:T(8,128)(2,1)}, u32[]{:S(2)}, u32[]{:S(2)}) async-start(bf16[4,2,144,2048]{3,2,1,0:T(8,128)(2,1)} %bitcast.311), calls=%async_computation.10 | async-start | bytes 9437184 | tf_op jit(solution)/shard_map/all_to_all | solution.py:409
  535.3 25.1 %collective-permute-start.4 = (bf16[2048,512]{1,0:T(8,128)(2,1)}, bf16[2048,512]{1,0:T(8,128)(2,1)S(1)}, u32[]{:S(2)}, u32[]{:S(2)}) collective-permute-start(bf16[2048,512]{1,0:T(8,128)(2,1)} %bitcast.49), channel_id=1, source_target_pairs={{0,1},{1,0},{2,3},{3,2},{4,5},{5,4},{6,7},{7,6},{8,9},{9,8},{10,11... | collective-permute-start | bytes 6291464 | tf_op jit(solution)/shard_map/ppermute | solution.py:405
  537.1 58.6 %collective-permute-start.5 = (bf16[2048,512]{1,0:T(8,128)(2,1)}, bf16[2048,512]{1,0:T(8,128)(2,1)}, u32[]{:S(2)}, u32[]{:S(2)}) collective-permute-start(bf16[2048,512]{1,0:T(8,128)(2,1)} %bitcast.51), channel_id=1, source_target_pairs={{0,1},{1,0},{2,3},{3,2},{4,5},{5,4},{6,7},{7,6},{8,9},{9,8},{10,11... | collective-permute-start | bytes 6291464 | tf_op jit(solution)/shard_map/ppermute | solution.py:405
  801.3 6.6 collective-permute-start.7
  812.6 104.3 %all-to-all-start.12 = ((bf16[4,128,4224]{2,1,0:T(8,128)(2,1)}), bf16[4,128,4224]{2,1,0:T(8,128)(2,1)}, u32[]{:S(2)}, u32[]{:S(2)}) async-start(bf16[4,128,4224]{2,1,0:T(8,128)(2,1)} %bitcast.313), calls=%async_computation.12 | async-start | bytes 8650752 | tf_op jit(solution)/shard_map/all_to_all | solution.py:409
  830.7 89.5 %copy-start.46 = (f32[128,16]{0,1:T(8,128)S(1)}, f32[128,16]{0,1:T(8,128)}, u32[]{:S(2)}) copy-start(f32[128,16]{0,1:T(8,128)} %copy-done.45) | copy-start | bytes 24580
  830.7 89.5 %copy-start.52 = (f32[128,16]{0,1:T(8,128)S(1)}, f32[128,16]{0,1:T(8,128)}, u32[]{:S(2)}) copy-start(f32[128,16]{0,1:T(8,128)} %copy-done.51) | copy-start | bytes 24580
  830.7 89.5 %copy-start.62 = (f32[128]{0:T(128)S(1)}, f32[128]{0:T(128)}, u32[]{:S(2)}) copy-start(f32[128]{0:T(128)} %copy-done.61) | copy-start | bytes 1540
  830.7 89.5 %copy-start.65 = (f32[128]{0:T(128)S(1)}, f32[128]{0:T(128)}, u32[]{:S(2)}) copy-start(f32[128]{0:T(128)} %copy-done.64) | copy-start | bytes 1540
  830.7 89.6 %copy-start.6 = (f32[128,2048]{1,0:T(8,128)S(1)}, f32[128,2048]{1,0:T(8,128)}, u32[]{:S(2)}) copy-start(f32[128,2048]{1,0:T(8,128)} %copy-done.5) | copy-start | bytes 3145732
  830.7 89.6 %copy-start.43 = (bf16[2,8,4,512]{3,1,2,0:T(8,128)(2,1)S(1)}, bf16[2,8,4,512]{3,1,2,0:T(8,128)(2,1)}, u32[]{:S(2)}) copy-start(bf16[2,8,4,512]{3,1,2,0:T(8,128)(2,1)} %copy-done.42) | copy-start | bytes 196612
  830.7 89.6 %copy-start.48 = (f32[1,4,4,128]{3,1,2,0:T(4,128)S(1)}, f32[1,4,4,128]{3,1,2,0:T(4,128)}, u32[]{:S(2)}) copy-start(f32[1,4,4,128]{3,1,2,0:T(4,128)} %copy-done.47) | copy-start | bytes 24580
  830.7 89.6 %copy-start.70 = (f32[128]{0:T(128)S(1)}, f32[128]{0:T(128)}, u32[]{:S(2)}) copy-start(f32[128]{0:T(128)} %copy-done.69) | copy-start | bytes 1540
  830.8 108.4 %collective-permute-start.15 = (bf16[2048,512]{1,0:T(8,128)(2,1)}, bf16[2048,512]{1,0:T(8,128)(2,1)}, u32[]{:S(2)}, u32[]{:S(2)}) collective-permute-start(bf16[2048,512]{1,0:T(8,128)(2,1)} %convolution_convert_fusion.4), channel_id=1, source_target_pairs={{0,1},{1,0},{2,3},{3,2},{4,5},{5,4},{6,7},{7,6},{8,9},{9,8},{10,11... | collective-permute-start | bytes 6291464 | tf_op jit(solution)/shard_map/ppermute | solution.py:405
  924.6 28.5 %all-to-all-start.13 = ((bf16[4,128,2048]{2,1,0:T(8,128)(2,1)}), bf16[4,128,2048]{2,1,0:T(8,128)(2,1)S(1)}, u32[]{:S(2)}, u32[]{:S(2)}) async-start(bf16[4,128,2048]{2,1,0:T(8,128)(2,1)} %broadcast_in_dim.79), calls=%async_computation.13 | async-start | bytes 4194304 | tf_op jit(solution)/shard_map/all_to_all | solution.py:409
  937.7 32.8 %collective-permute-start.13 = (bf16[2048,512]{1,0:T(8,128)(2,1)}, bf16[2048,512]{1,0:T(8,128)(2,1)}, u32[]{:S(2)}, u32[]{:S(2)}) collective-permute-start(bf16[2048,512]{1,0:T(8,128)(2,1)} %convolution_convert_fusion.6), channel_id=1, source_target_pairs={{0,1},{1,0},{2,3},{3,2},{4,5},{5,4},{6,7},{7,6},{8,9},{9,8},{10,11... | collective-permute-start | bytes 6291464 | tf_op jit(solution)/shard_map/ppermute | solution.py:405
  954.5 55.9 %all-to-all-start.20 = ((bf16[16,128,512]{2,1,0:T(8,128)(2,1)}), bf16[16,128,512]{2,1,0:T(8,128)(2,1)S(1)}, u32[]{:S(2)}, u32[]{:S(2)}) async-start(bf16[16,128,512]{2,1,0:T(8,128)(2,1)} %bitcast.337), calls=%async_computation.20 | async-start | bytes 4194304 | tf_op jit(solution)/shard_map/all_to_all | solution.py:409
  968.4 9.1 collective-permute-start.14
  970.4 13.7 %collective-permute-start.9 = (bf16[4,128,2048]{2,1,0:T(8,128)(2,1)S(1)}, bf16[4,128,2048]{2,1,0:T(8,128)(2,1)S(1)}, u32[]{:S(2)}, u32[]{:S(2)}) collective-permute-start(bf16[4,128,2048]{2,1,0:T(8,128)(2,1)S(1)} %copy-done.17), channel_id=1, source_target_pairs={{0,1},{1,0},{2,3},{3,2},{4,5},{5,4},{6,7},{7,6},{8,9},{9,8},{10,11... | collective-permute-start | bytes 6291464 | tf_op jit(solution)/shard_map/ppermute | solution.py:405
  1010.4 52.0 %all-to-all-start.18 = ((bf16[16,128,512]{2,1,0:T(8,128)(2,1)}), bf16[16,128,512]{2,1,0:T(8,128)(2,1)}, u32[]{:S(2)}, u32[]{:S(2)}) async-start(bf16[16,128,512]{2,1,0:T(8,128)(2,1)} %bitcast.336), calls=%async_computation.18 | async-start | bytes 4194304 | tf_op jit(solution)/shard_map/all_to_all | solution.py:409
  1034.5 32.9 %copy-start.68 = (f32[1024,2]{0,1:T(2,128)S(1)}, f32[1024,2]{0,1:T(2,128)}, u32[]{:S(2)}) copy-start(f32[1024,2]{0,1:T(2,128)} %get-tuple-element.157) | copy-start | bytes 24580
  1062.4 52.5 %all-to-all-start.19 = ((bf16[16,128,512]{2,1,0:T(8,128)(2,1)}), bf16[16,128,512]{2,1,0:T(8,128)(2,1)S(1)}, u32[]{:S(2)}, u32[]{:S(2)}) async-start(bf16[16,128,512]{2,1,0:T(8,128)(2,1)} %bitcast.335), calls=%async_computation.19 | async-start | bytes 4194304 | tf_op jit(solution)/shard_map/all_to_all | solution.py:409
  1078.4 6.0 collective-permute-start.10
  1086.5 32.9 %copy-start.40 = (bf16[2,128,1024]{2,1,0:T(8,128)(2,1)S(1)}, bf16[2,128,1024]{2,1,0:T(8,128)(2,1)}, u32[]{:S(2)}) copy-start(bf16[2,128,1024]{2,1,0:T(8,128)(2,1)} %fusion.28) | copy-start | bytes 1572868
  1114.9 26.0 %all-to-all-start.14 = ((bf16[4,128,2048]{2,1,0:T(8,128)(2,1)}), bf16[4,128,2048]{2,1,0:T(8,128)(2,1)}, u32[]{:S(2)}, u32[]{:S(2)}) async-start(bf16[4,128,2048]{2,1,0:T(8,128)(2,1)} %add_convert_fusion.5), calls=%async_computation.14 | async-start | bytes 4194304 | tf_op jit(solution)/shard_map/all_to_all | solution.py:409
  1140.9 30.1 %all-to-all-start.16 = ((bf16[16,256,128]{2,1,0:T(8,128)(2,1)}), bf16[16,256,128]{2,1,0:T(8,128)(2,1)S(1)}, u32[]{:S(2)}, u32[]{:S(2)}) async-start(bf16[16,256,128]{2,1,0:T(8,128)(2,1)} %bitcast.329), calls=%async_computation.16 | async-start | bytes 2097152 | tf_op jit(solution)/shard_map/all_to_all | solution.py:409
  1171.0 19.5 %all-to-all-start.17 = ((f32[16,1,2320]{2,1,0:T(1,128)}), f32[16,1,2320]{2,1,0:T(1,128)S(1)}, u32[]{:S(2)}, u32[]{:S(2)}) async-start(f32[16,1,2320]{2,1,0:T(1,128)} %copy.304), calls=%async_computation.17 | async-start | bytes 311296 | tf_op jit(solution)/shard_map/all_to_all | solution.py:409
  1191.2 76.6 %all-to-all-start.15 = ((bf16[16,128,768]{1,2,0:T(8,128)(2,1)}), bf16[16,128,768]{1,2,0:T(8,128)(2,1)}, u32[]{:S(2)}, u32[]{:S(2)}) async-start(bf16[16,128,768]{1,2,0:T(8,128)(2,1)} %copy.299), calls=%async_computation.15 | async-start | bytes 6291456 | tf_op jit(solution)/shard_map/all_to_all | solution.py:409
  1206.5 24.1 %collective-permute-start.8 = (bf16[128,1024]{1,0:T(8,128)(2,1)}, bf16[128,1024]{1,0:T(8,128)(2,1)S(1)}, u32[]{:S(2)}, u32[]{:S(2)}) collective-permute-start(bf16[128,1024]{1,0:T(8,128)(2,1)} %get-tuple-element.142), channel_id=1, source_target_pairs={{0,1},{1,0},{2,3},{3,2},{4,5},{5,4},{6,7},{7,6},{8,9},{9,8},{10,11... | collective-permute-start | bytes 786440 | tf_op jit(solution)/shard_map/ppermute | solution.py:405
  1233.2 4.5 collective-permute-start.11
  1234.3 1.5 collective-permute-start.12
  (81 other events, 459.9 us)
Sparse Core Ops, SparseCore 0:
  49.9 71.8 all-reduce.2

commit v2 on v1

--- a/solution.py
+++ b/solution.py
@@ -1,14 +1,18 @@
+import functools
 import math
 
 import jax
 import jax.numpy as jnp
 from jax import lax
+from jax.experimental import pallas as pl
+from jax.experimental.pallas import tpu as pltpu
 from jax.sharding import PartitionSpec as P
 
 HD = 128
 TOPK = 8
 E = 16
 CAP = 512
+MESH = pl.DeviceIdType.MESH
 
 
 EPS = 1e-06
@@ -436,16 +440,411 @@
     return jnp.where(core == 0, jnp.stack([mine, other]), jnp.stack([other, mine]))
 
 
-def half_rows_sum(partial):
-    received = swap(partial[1].astype(jnp.bfloat16))
-    summed = (partial[0] + received.astype(jnp.float32)).astype(jnp.bfloat16)
+def remote(src, dst, send, recv, **where):
+    return pltpu.make_async_remote_copy(
+        src_ref=src, dst_ref=dst, send_sem=send, recv_sem=recv, device_id=where, device_id_type=MESH
+    )
+
+
+def places():
+    return lax.axis_index("fsdp"), lax.axis_index("ctx"), lax.axis_index("tp")
+
+
+def ring(index, step, count):
+    return lax.rem(index + step + count, count)
+
+
+def greet(nz, nc, line):
+    z, c, t = places()
+    barrier = pltpu.get_barrier_semaphore()
+
+    def tell(**where):
+        pl.semaphore_signal(barrier, inc=1, device_id=where, device_id_type=MESH)
+
+    if line:
+        for step in range(1, nz):
+            tell(fsdp=ring(z, step, nz))
+        count = nz - 1
+    else:
+        pl.when(z > 0)(lambda: tell(fsdp=z - 1))
+        pl.when(z < nz - 1)(lambda: tell(fsdp=z + 1))
+        count = jnp.where(z > 0, 1, 0) + jnp.where(z < nz - 1, 1, 0)
+    for step in range(1, nc):
+        tell(ctx=ring(c, step, nc))
+    tell(tp=1 - t)
+    pl.semaphore_wait(barrier, count + nc)
+
+
+def line_copies(bufs, send_sem, recv_sem, way, step, shard, target):
+    return [
+        remote(buf.at[shard], buf.at[shard], send_sem.at[way, step, k], recv_sem.at[way, step, k], fsdp=target)
+        for k, buf in enumerate(bufs)
+    ]
+
+
+def line_gather(nz, bufs, send_sem, recv_sem, arrived):
+    z = lax.axis_index("fsdp")
+    for step in range(nz - 1):
+
+        @pl.when((z < nz - 1) & (z >= step))
+        def _():
+            for copy in line_copies(bufs, send_sem, recv_sem, 0, step, z - step, z + 1):
+                copy.start()
+
+        @pl.when((z > 0) & (z + step < nz))
+        def _():
+            for copy in line_copies(bufs, send_sem, recv_sem, 1, step, z + step, z - 1):
+                copy.start()
+
+        @pl.when(z - 1 >= step)
+        def _():
+            for copy in line_copies(bufs, send_sem, recv_sem, 0, step, z - 1 - step, z - 1):
+                copy.wait_recv()
+            arrived(z - 1 - step)
+
+        @pl.when(z + 1 + step < nz)
+        def _():
+            for copy in line_copies(bufs, send_sem, recv_sem, 1, step, z + 1 + step, z + 1):
+                copy.wait_recv()
+            arrived(z + 1 + step)
+
+    for step in range(nz - 1):
+
+        @pl.when((z < nz - 1) & (z >= step))
+        def _():
+            for copy in line_copies(bufs, send_sem, recv_sem, 0, step, z - step, z + 1):
+                copy.wait_send()
+
+        @pl.when((z > 0) & (z + step < nz))
+        def _():
+            for copy in line_copies(bufs, send_sem, recv_sem, 1, step, z + step, z - 1):
+                copy.wait_send()
+
+
+def regroup(shard, t, rows, line, two, keep_sem, give_send, give_recv, start):
+    slot = lax.rem(shard, 2)
+    band = pl.ds(pl.multiple_of(t * rows, rows), rows)
+
+    def keep():
+        pltpu.make_async_copy(line.at[shard], two.at[slot, band], keep_sem.at[slot]).start()
+
+    def give():
+        remote(line.at[shard], two.at[slot, band], give_send.at[slot], give_recv.at[slot], tp=1 - t).start()
+
+    pl.when(shard // 2 == t)(keep)
+    pl.when(shard // 2 != t)(give)
+
+
+def load_kernel(
+    nz, nc, tok, cot, wq, wk, wv, wo, small,
+    x_all, w_qkv, w_o, small_all, cot_line, cot_two, routes_seq,
+    own_sem, line_send, line_recv, tok_send, tok_recv, pass_send, pass_recv,
+    route_send, route_recv, keep_sem, give_send, give_recv,
+):
+    z, c, t = places()
+    block = tok.shape[0]
+    rows = block // 2
+    local = w_qkv.shape[2] // 3
+    kinds = routes_seq.shape[1]
+    first = small.shape[0] - kinds
+    half = pl.ds(pl.multiple_of(t * rows, rows), rows)
+    column = pl.ds(pl.multiple_of(c * local, local), local)
+    own = [
+        pltpu.make_async_copy(w.at[:, column], w_qkv.at[z, :, pl.ds(k * local, local)], own_sem.at[k])
+        for k, w in enumerate((wq, wk, wv))
+    ]
+    own += [
+        pltpu.make_async_copy(wo.at[column], w_o.at[z], own_sem.at[3]),
+        pltpu.make_async_copy(small, small_all.at[z], own_sem.at[4]),
+        pltpu.make_async_copy(cot.at[half], cot_line.at[z], own_sem.at[5]),
+        pltpu.make_async_copy(tok, x_all.at[pl.ds(pl.multiple_of(c * block, block), block)], own_sem.at[6]),
+        pltpu.make_async_copy(small.at[pl.ds(first, kinds)], routes_seq.at[c], own_sem.at[7]),
+    ]
+    for copy in own:
+        copy.start()
+    greet(nz, nc, False)
+
+    def band(source, core):
+        return x_all.at[pl.ds(pl.multiple_of(source * block + core * rows, rows), rows)]
+
+    def token_copy(step, source, target):
+        return remote(tok.at[half], band(source, t), tok_send.at[step], tok_recv.at[step], ctx=target)
+
+    def pass_copy(step, source, core):
+        return remote(band(source, core), band(source, core), pass_send.at[step], pass_recv.at[step], tp=1 - t)
+
+    def route_copy(step, source, target):
+        return remote(
+            small.at[pl.ds(first, kinds)], routes_seq.at[source], route_send.at[step], route_recv.at[step], ctx=target
+        )
+
+    for step in range(1, nc):
+        token_copy(step - 1, c, ring(c, step, nc)).start()
+        route_copy(step - 1, c, ring(c, step, nc)).start()
+    for copy in own:
+        copy.wait()
+
+    def arrived(shard):
+        regroup(shard, t, rows, cot_line, cot_two, keep_sem, give_send, give_recv, True)
+
+    arrived(z)
+
+    def later(shard):
+        arrived(shard)
+
+    line_gather(nz, (w_qkv, w_o, small_all, cot_line), line_send, line_recv, later)
+    for step in range(1, nc):
+        source = ring(c, -step, nc)
+        token_copy(step - 1, source, source).wait_recv()
+        pass_copy(step - 1, source, t).start()
+        route_copy(step - 1, source, source).wait_recv()
+    for step in range(1, nc):
+        source = ring(c, -step, nc)
+        pass_copy(step - 1, source, 1 - t).wait_recv()
+        pass_copy(step - 1, source, t).wait_send()
+        token_copy(step - 1, c, source).wait_send()
+        route_copy(step - 1, c, source).wait_send()
+    finish_regroup(t, rows, cot_line, cot_two, keep_sem, give_send, give_recv)
+
+
+def finish_regroup(t, rows, line, two, keep_sem, give_send, give_recv):
+    for slot in range(2):
+        wait_two(slot, t, rows, line, two, keep_sem, give_recv)
+        band = pl.ds(pl.multiple_of(t * rows, rows), rows)
+        remote(line.at[0], two.at[slot, band], give_send.at[slot], give_recv.at[slot], tp=1 - t).wait_send()
+
+
+def wait_two(slot, t, rows, line, two, keep_sem, give_recv):
+    band = pl.ds(pl.multiple_of(t * rows, rows), rows)
+    other = pl.ds(pl.multiple_of((1 - t) * rows, rows), rows)
+    pltpu.make_async_copy(line.at[0], two.at[slot, band], keep_sem.at[slot]).wait()
+    remote(line.at[0], two.at[slot, other], give_recv.at[slot], give_recv.at[slot], tp=1 - t).wait_recv()
+
+
+def load(tok, cot, wq, wk, wv, wo, small, kinds):
+    nz, nc = lax.axis_size("fsdp"), lax.axis_size("ctx")
+    block, width = tok.shape
+    deep, local = wq.shape[0], wq.shape[1] // nc
+    rows = block // 2
+    dma = pltpu.SemaphoreType.DMA
+    bf16 = jnp.bfloat16
+    shapes = [
+        (nc * block, width),
+        (nz, deep, 3 * local),
+        (nz, local, wo.shape[1]),
+        (nz,) + small.shape,
+        (nz, rows, width),
+        (2, block, width),
+        (nc, kinds, 128),
+    ]
+    return pl.pallas_call(
+        functools.partial(load_kernel, nz, nc),
+        out_shape=[jax.ShapeDtypeStruct(shape, bf16) for shape in shapes],
+        in_specs=[pl.BlockSpec(memory_space=pl.ANY)] * 7,
+        out_specs=[pl.BlockSpec(memory_space=pltpu.VMEM)] * 7,
+        scratch_shapes=[
+            dma((8,)),
+            dma((2, nz - 1, 4)), dma((2, nz - 1, 4)),
+            dma((nc - 1,)), dma((nc - 1,)), dma((nc - 1,)), dma((nc - 1,)), dma((nc - 1,)), dma((nc - 1,)),
+            dma((2,)), dma((2,)), dma((2,)),
+        ],
+        compiler_params=pltpu.CompilerParams(
+            collective_id=0, has_side_effects=True, vmem_limit_bytes=40 * 2**20
+        ),
+    )(tok, cot, wq, wk, wv, wo, small)
+
+
+def dispatch_kernel(
+    nz, nc, part, tok, gain, router, kept, pick, cot_two,
+    residual, normed, probs, x_in, g_in, cot_in,
+    sib, rs_send, rs_recv, n_line, g_line, n_two, g_two, x_send, g_send, cot_send,
+    sib_s, sib_r, rs_s, rs_r, line_send, line_recv, keep_sem, give_send, give_recv,
+    gkeep_sem, ggive_send, ggive_recv, x_s, x_r, g_s, g_r, cot_s, cot_r, own_sem,
+):
+    z, c, t = places()
+    f32, bf16 = jnp.float32, jnp.bfloat16
+    rows, width = residual.shape
+    most = x_in.shape[2]
+    greet(nz, nc, False)
+
+    def sib_copy(q):
+        return remote(part.at[q, 1 - t], sib.at[q], sib_s.at[q], sib_r.at[q], tp=1 - t)
+
+    def rs_copy(step, source, target):
+        return remote(rs_send.at[step], rs_recv.at[step], rs_s.at[step], rs_r.at[step], ctx=target)
+
+    for step in range(1, nc + 1):
+        sib_copy(ring(c, step, nc)).start()
+    chunk = 16
+    for step in range(1, nc):
+        q = ring(c, step, nc)
+        sib_copy(q).wait_recv()
+
+        @pl.loop(0, rows // chunk)
+        def _(k):
+            at = pl.ds(pl.multiple_of(k * chunk, chunk), chunk)
+            rs_send[step - 1, at, :] = (part[q, t, at, :].astype(f32) + sib[q, at, :].astype(f32)).astype(bf16)
+
+        rs_copy(step - 1, c, q).start()
+
+    def picked(slot, source, out, out_at):
+        lanes = out.shape[-1]
+        piece = min(lanes, 512)
+
+        @pl.loop(0, lanes // piece)
+        def _(k):
+            at = pl.ds(pl.multiple_of(k * piece, piece), piece)
+            out[out_at, :, at] = jnp.dot(
+                pick[slot], source[slot, :, at], preferred_element_type=f32
+            ).astype(bf16)
+
+    def send_copy(slot, step, src, dst, send, recv, source, target):
+        return remote(
+            src.at[slot, pl.ds(pl.multiple_of(target * most, 16), most)],
+            dst.at[source, slot],
+            send.at[slot, step - 1],
+            recv.at[slot, step - 1],
+            ctx=target,
+        )
+
+    def own_copy(slot, src, dst, k):
+        return pltpu.make_async_copy(
+            src.at[slot, pl.ds(pl.multiple_of(c * most, 16), most)], dst.at[c, slot], own_sem.at[k, slot]
+        )
+
+    for slot in range(2):
+        picked(slot, cot_two, cot_send, slot)
+        for step in range(1, nc):
+            send_copy(slot, step, cot_send, cot_in, cot_s, cot_r, c, ring(c, step, nc)).start()
+        own_copy(slot, cot_send, cot_in, 0).start()
+
+    sib_copy(c).wait_recv()
+    for step in range(1, nc):
+        rs_copy(step - 1, c, c).wait_recv()
+
+    @pl.loop(0, rows // chunk)
+    def _(k):
+        at = pl.ds(pl.multiple_of(k * chunk, chunk), chunk)
+        start = pl.ds(pl.multiple_of(t * rows + k * chunk, chunk), chunk)
+        total = part[c, t, at, :].astype(f32) + sib[c, at, :].astype(f32)
+        for step in range(nc - 1):
+            total = total + rs_recv[step, at, :].astype(f32)
+        total = total + tok[start, :].astype(f32)
+        residual[at, :] = total
+        inv = lax.rsqrt(jnp.mean(total * total, -1, keepdims=True) + EPS)
+        row = (total * inv * gain[...]).astype(bf16)
+        normed[at, :] = row
+        n_line[z, at, :] = row
+
+    logits = lax.dot_general(
+        normed[...], router[...], (((1,), (1,)), ((), ())), preferred_element_type=f32
+    )
+    lane = lax.broadcasted_iota(jnp.int32, logits.shape, 1)
+    logits = jnp.where(lane < E, logits, -jnp.inf)
+    top = jnp.max(logits, -1, keepdims=True)
+    raised = jnp.exp(logits - top)
+    prob = raised / jnp.sum(raised, -1, keepdims=True)
+    probs[...] = prob
+    gates = prob * kept[...]
+    high = gates.astype(bf16)
+    g_line[z, :, pl.ds(0, 128)] = high
+    g_line[z, :, pl.ds(128, 128)] = (gates - high.astype(f32)).astype(bf16)
+
+    def arrived(shard):
+        regroup(shard, t, rows, n_line, n_two, keep_sem, give_send, give_recv, True)
+        regroup(shard, t, rows, g_line, g_two, gkeep_sem, ggive_send, ggive_recv, True)
+
+    arrived(z)
+    line_gather(nz, (n_line, g_line), line_send, line_recv, arrived)
+    for slot in range(2):
+        wait_two(slot, t, rows, n_line, n_two, keep_sem, give_recv)
+        wait_two(slot, t, rows, g_line, g_two, gkeep_sem, ggive_recv)
+        picked(slot, n_two, x_send, slot)
+        picked(slot, g_two, g_send, slot)
+        for step in range(1, nc):
+            send_copy(slot, step, x_send, x_in, x_s, x_r, c, ring(c, step, nc)).start()
+            send_copy(slot, step, g_send, g_in, g_s, g_r, c, ring(c, step, nc)).start()
+        own_copy(slot, x_send, x_in, 1).start()
+        own_copy(slot, g_send, g_in, 2).start()
+
+    band = pl.ds(pl.multiple_of(t * rows, rows), rows)
+    for slot in range(2):
+        remote(n_line.at[0], n_two.at[slot, band], give_send.at[slot], give_recv.at[slot], tp=1 - t).wait_send()
+        remote(g_line.at[0], g_two.at[slot, band], ggive_send.at[slot], ggive_recv.at[slot], tp=1 - t).wait_send()
+        own_copy(slot, cot_send, cot_in, 0).wait()
+        own_copy(slot, x_send, x_in, 1).wait()
+        own_copy(slot, g_send, g_in, 2).wait()
+        for step in range(1, nc):
+            source = ring(c, -step, nc)
+            for src, dst, s, r in (
+                (cot_send, cot_in, cot_s, cot_r),
+                (x_send, x_in, x_s, x_r),
+                (g_send, g_in, g_s, g_r),
+            ):
+                copy = send_copy(slot, step, src, dst, s, r, source, source)
+                copy.wait_recv()
+                copy.wait_send()
+    for step in range(1, nc):
+        rs_copy(step - 1, c, c).wait_send()
+    for step in range(nc):
+        sib_copy(step).wait_send()
+
+
+def dispatch(part, tok, gain, router, kept, pick, cot_two):
+    nz, nc = lax.axis_size("fsdp"), lax.axis_size("ctx")
+    rows, width = part.shape[2], part.shape[3]
+    block = rows * 2
+    most = pick.shape[1] // nc
+    dma = pltpu.SemaphoreType.DMA
+    bf16, f32 = jnp.bfloat16, jnp.float32
+    vmem = pl.BlockSpec(memory_space=pltpu.VMEM)
+    hbm = pl.BlockSpec(memory_space=pl.ANY)
+    return pl.pallas_call(
+        functools.partial(dispatch_kernel, nz, nc),
+        out_shape=[
+            jax.ShapeDtypeStruct((rows, width), f32),
+            jax.ShapeDtypeStruct((rows, width), bf16),
+            jax.ShapeDtypeStruct((rows, 128), f32),
+            jax.ShapeDtypeStruct((nc, 2, most, width), bf16),
+            jax.ShapeDtypeStruct((nc, 2, most, 256), bf16),
+            jax.ShapeDtypeStruct((nc, 2, most, width), bf16),
+        ],
+        in_specs=[vmem] * 7,
+        out_specs=[vmem] * 3 + [hbm] * 3,
+        scratch_shapes=[
+            pltpu.VMEM((nc, rows, width), bf16),
+            pltpu.VMEM((nc - 1, rows, width), bf16),
+            pltpu.VMEM((nc - 1, rows, width), bf16),
+            pltpu.VMEM((nz, rows, width), bf16),
+            pltpu.VMEM((nz, rows, 256), bf16),
+            pltpu.VMEM((2, block, width), bf16),
+            pltpu.VMEM((2, block, 256), bf16),
+            pltpu.VMEM((2, nc * most, width), bf16),
+            pltpu.VMEM((2, nc * most, 256), bf16),
+            pltpu.VMEM((2, nc * most, width), bf16),
+            dma((nc,)), dma((nc,)), dma((nc - 1,)), dma((nc - 1,)),
+            dma((2, nz - 1, 2)), dma((2, nz - 1, 2)),
+            dma((2,)), dma((2,)), dma((2,)), dma((2,)), dma((2,)), dma((2,)),
+            dma((2, nc - 1)), dma((2, nc - 1)), dma((2, nc - 1)), dma((2, nc - 1)), dma((2, nc - 1)), dma((2, nc - 1)),
+            dma((3, 2)),
+        ],
+        compiler_params=pltpu.CompilerParams(
+            collective_id=1, has_side_effects=True, vmem_limit_bytes=56 * 2**20
+        ),
+    )(part, tok, gain, router, kept, pick, cot_two)
+
+
+def half_rows_sum(partial, core):
+    mine = lax.dynamic_index_in_dim(partial, core, 1, keepdims=False)
+    received = swap(lax.dynamic_index_in_dim(partial, 1 - core, 1, keepdims=False))
+    summed = (mine.astype(jnp.float32) + received.astype(jnp.float32)).astype(jnp.bfloat16)
     pieces = exchange(summed, "ctx")
     return jnp.sum(pieces.astype(jnp.float32), 0)
 
 
-def all_rows(half):
+def all_rows(half, core):
     mine = spread(half, "ctx")
-    return jnp.stack([mine, swap(mine)])
+    return by_core(mine, swap(mine), core).transpose(1, 0, 2, 3)
 
 
 def one_chip(
@@ -475,37 +874,49 @@
 
     token_half = lax.dynamic_slice_in_dim(tokens[0], t * rows, rows, 0)
     cotan_half = lax.dynamic_slice_in_dim(cotangent[0], t * rows, rows, 0)
-    small = jnp.concatenate(
-        [gain_attn, gain_moe, w_router.T.reshape(-1), gain_query, gain_key]
-    )
-    small = lax.all_gather(small, "fsdp", axis=0)
-    attn_gain = small[:, :deep].reshape(-1).astype(f32)
-    moe_gain = small[:, deep : 2 * deep].reshape(-1).astype(f32)
-    router = small[:, 2 * deep : (2 + E) * deep].reshape(nz, E, deep)
-    router = router.transpose(0, 2, 1).reshape(width, E)
-    part = HD // nz
-    query_gain = small[:, (2 + E) * deep : (2 + E) * deep + part].reshape(-1).astype(f32)
-    key_gain = small[:, (2 + E) * deep + part :].reshape(-1).astype(f32)
-    routes_all = lax.all_gather(routes[0], ("fsdp", "ctx"), axis=0)
-
     local = w_query.shape[1] // nc
-    cols = [lax.dynamic_slice_in_dim(w, c * local, local, 1) for w in (w_query, w_key, w_value)]
-    w_qkv = spread(jnp.concatenate(cols, 1), "fsdp").reshape(width, 3 * local)
-    w_o = spread(lax.dynamic_slice_in_dim(w_out, c * local, local, 0), "fsdp")
+    small = jnp.concatenate([w_router.T.reshape(-1), gain_attn, gain_moe, gain_query, gain_key])
+    total = small.shape[0]
+    small = jnp.pad(small, (0, -total % 2048))
+    kinds = block * TOPK // 128
+    small = jnp.concatenate([small, routes.reshape(-1).astype(bf16)]).reshape(-1, 128)
+    x_rows, w_qkv, w_o, small, _, cot_two, routes_seq = load(
+        tokens[0], cotangent[0], w_query, w_key, w_value, w_out, small, kinds
+    )
+    w_qkv = w_qkv.reshape(width, 3 * local)
     w_o = w_o.transpose(1, 0, 2).reshape(local, width)
-
-    own = lax.dynamic_slice_in_dim(w_experts, c * nz, nz, 2)
-    own = own.transpose(1, 2, 0, 3)
-    mats = [exchange(own[k], "fsdp").reshape(width, ffn) for k in range(3)]
+    routes_line = small[:, small.shape[1] - kinds :].reshape(nz, block, TOPK)
+    routes_seq = routes_seq.reshape(tall, TOPK)
+    small = small.reshape(nz, -1)
+    router = small[:, : E * deep].reshape(nz, E, deep).transpose(1, 0, 2).reshape(E, width)
+    at = E * deep
+    attn_gain = small[:, at : at + deep].reshape(-1).astype(f32)
+    moe_gain = small[:, at + deep : at + 2 * deep].reshape(-1).astype(f32)
+    at, part = at + 2 * deep, HD // nz
+    query_gain = small[:, at : at + part].reshape(-1).astype(f32)
+    key_gain = small[:, at + part : at + 2 * part].reshape(-1).astype(f32)
+
+    own = lax.dynamic_slice_in_dim(w_experts, c * nz, nz, 2).transpose(2, 1, 0, 3)
+    own, w_qkv = lax.optimization_barrier((own, w_qkv))
+    moved = exchange(own, "fsdp").transpose(1, 0, 2, 3)
+    mats = [moved[k].reshape(width, ffn) for k in range(3)]
     others = [swap(m) for m in mats]
     halves = [mats, others]
 
-    x_rows = all_rows(token_half).reshape(tall, width).astype(f32)
-    place = (
-        jnp.arange(nc, dtype=jnp.int32)[None, :, None] * block
-        + ((jnp.arange(2, dtype=jnp.int32) + t) % 2)[:, None, None] * rows
-        + jnp.arange(rows, dtype=jnp.int32)[None, None, :]
-    ).reshape(tall)
+    ids = jnp.arange(E, dtype=jnp.int32)
+    own_seq = jnp.any(routes_seq[:, :, None] == ids.astype(bf16), 1).astype(jnp.int32)
+    slot = jnp.cumsum(own_seq, 0) - own_seq
+    kept_seq = (own_seq * (slot < CAP)).astype(f32)
+    kept = lax.dynamic_slice_in_dim(kept_seq, c * block + t * rows, rows, 0)
+    line = lax.dynamic_slice_in_dim(routes_line, t * 2, 2, 0)
+    plane = (jnp.arange(nc, dtype=jnp.int32) * nz + z).astype(bf16)
+    line = jnp.any(line[..., None] == plane, 2).astype(jnp.int32)
+    rank = jnp.cumsum(line, 1) - line
+    pick = (rank[..., None] == jnp.arange(most, dtype=jnp.int32)) & (line[..., None] > 0)
+    pick = pick.transpose(0, 2, 3, 1).reshape(2, nc * most, block).astype(bf16)
+
+    x_rows = x_rows.astype(f32)
+    place = jnp.arange(tall, dtype=jnp.int32)
     half_dim = HD // 2
     inv_freq = jnp.exp(jnp.arange(half_dim, dtype=f32) * (-2.0 * math.log(ROPE_BASE) / HD))
     angles = place.astype(f32)[:, None] * inv_freq[None, :]
@@ -527,51 +938,20 @@
     log_total = maximum + jnp.log(denominator)
     context = jnp.einsum("hqk,khd->qhd", attn_probs.astype(bf16), values, preferred_element_type=f32)
     context = context.astype(bf16).reshape(tall, local)
-    attn_part = dot(context, w_o).reshape(2, nc, rows, width)
+    attn_part = dot(context, w_o).astype(bf16).reshape(nc, 2, rows, width)
+    kept_wide = jnp.pad(kept, ((0, 0), (0, 128 - E)))
+    router_wide = jnp.pad(router, ((0, 128 - E), (0, 0)))
+    residual, normed_two, router_probs, x_in, g_in, cot_rows = dispatch(
+        attn_part, tokens[0], moe_gain[None], router_wide, kept_wide, pick, cot_two
+    )
+    router_probs = router_probs[:, :E]
     own_tokens = token_half.astype(f32)
-    residual = own_tokens + half_rows_sum(attn_part)
     inv_two = rms_scale(residual)
-    normed_two = (residual * inv_two * moe_gain).astype(bf16)
-    logits = dot(normed_two, router)
-    router_probs = jax.nn.softmax(logits, -1)
-
-    ids = jnp.arange(E, dtype=jnp.int32)
-    named_all = jnp.any(routes_all[:, :, :, None] == ids, 2)
-    named_all = named_all.reshape(nz, nc, block, E).astype(jnp.int32)
-    own_seq = lax.dynamic_index_in_dim(named_all, z, 0, keepdims=False).reshape(tall, E)
-    slot = jnp.cumsum(own_seq, 0) - own_seq
-    kept_seq = (own_seq * (slot < CAP)).astype(f32)
-    kept = lax.dynamic_slice_in_dim(kept_seq, c * block + t * rows, rows, 0)
-    gates = router_probs * kept
-    line = lax.dynamic_index_in_dim(named_all, c, 1, keepdims=False)
-    line = lax.dynamic_slice_in_dim(line, t * 2, 2, 0)
-    rank = jnp.cumsum(line, 1) - line
-    plane = jnp.arange(nc, dtype=jnp.int32) * nz + z
-    line = jnp.take(line, plane, axis=2)
-    rank = jnp.take(rank, plane, axis=2)
-    order = (jnp.arange(2, dtype=jnp.int32) + t) % 2
-    line = jnp.take(line.reshape(2, 2, rows, nc), order, axis=1).reshape(2, block, nc)
-    rank = jnp.take(rank.reshape(2, 2, rows, nc), order, axis=1).reshape(2, block, nc)
-    pick = (rank[..., None] == jnp.arange(most, dtype=jnp.int32)) & (line[..., None] > 0)
-    pick = pick.transpose(0, 2, 3, 1).reshape(2, nc * most, block).astype(bf16)
-
-    def dispatch(half):
-        mine = spread(half, "fsdp")
-        keep = lax.dynamic_slice_in_dim(mine, t * 2, 2, 0)
-        send = lax.dynamic_slice_in_dim(mine, (1 - t) * 2, 2, 0)
-        both = jnp.concatenate([keep, swap(send)], 1)
-        picked = jnp.einsum("sib,sbw->siw", pick, both, preferred_element_type=f32).astype(bf16)
-        picked = picked.reshape(2, nc, most, -1).transpose(1, 0, 2, 3)
-        return exchange(picked, "ctx").reshape(nc * 2 * most, -1)
-
-    cot_rows = dispatch(cotan_half)
-    high, low = two_parts(gates)
-    tail = jnp.zeros((rows, 128 - 2 * E), bf16)
-    in_rows = dispatch(jnp.concatenate([normed_two, high, low, tail], 1))
-    x_in = in_rows[:, :width]
+    x_in = x_in.reshape(nc * 2 * most, width)
+    cot_rows = cot_rows.reshape(nc * 2 * most, width)
+    g_in = g_in.reshape(nc * 2 * most, 2, 128)[:, :, :E].astype(f32)
     mine_id = c * nz + z
-    extra = in_rows[:, width : width + 2 * E].astype(f32).reshape(-1, 2, E)
-    weight = jnp.sum(jnp.where(ids == mine_id, extra, 0.0), (1, 2))[:, None]
+    weight = jnp.sum(jnp.where(ids == mine_id, g_in, 0.0), (1, 2))[:, None]
 
     out_rows = back_rows = 0.0
     pair_grad = 0.0
@@ -600,7 +980,8 @@
         reply = exchange(reply.reshape(nc, 2, most, -1), "ctx")
         reply = reply.transpose(1, 0, 2, 3).reshape(2, nc * most, -1)
         dense = jnp.einsum("sib,siw->sbw", pick, reply, preferred_element_type=f32).astype(bf16)
-        mine, send = dense[:, :rows], dense[:, rows:]
+        mine = lax.dynamic_slice_in_dim(dense, t * rows, rows, 1)
+        send = lax.dynamic_slice_in_dim(dense, (1 - t) * rows, rows, 1)
         stacked = by_core(mine, swap(send), t).reshape(nz, rows, -1)
         return jnp.sum(exchange(stacked, "fsdp").astype(f32), 0)
 
@@ -628,10 +1009,10 @@
     )
     grad_logits = grad_logits.astype(bf16)
     dw_router = dot_tn(normed_two, grad_logits)
-    grad_normed_two = grad_rows + dot_nt(grad_logits, router)
+    grad_normed_two = grad_rows + dot(grad_logits, router)
     dgain_moe = jnp.sum(grad_normed_two * residual * inv_two, 0)
     grad_residual = cotan_half.astype(f32) + norm_back(grad_normed_two, residual, inv_two, moe_gain)
-    grad_attn = all_rows(grad_residual.astype(bf16)).reshape(tall, width)
+    grad_attn = all_rows(grad_residual.astype(bf16), t).reshape(tall, width)
 
     dw_out = dot_tn(context, grad_attn).astype(bf16)
     grad_context = dot_nt(grad_attn, w_o).astype(bf16).reshape(tall, -1, HD)
@@ -653,8 +1034,8 @@
     grad_kproj = norm_back(grad_knormed, key_heads, key_inv, key_gain).astype(bf16)
     grad_proj = jnp.stack([grad_qproj, grad_kproj, grad_values], 1).reshape(tall, 3 * local)
     dw_qkv = dot_tn(normed_one, grad_proj).astype(bf16)
-    grad_normed_part = dot_nt(grad_proj, w_qkv).reshape(2, nc, rows, width)
-    grad_normed_one = half_rows_sum(grad_normed_part)
+    grad_normed_part = dot_nt(grad_proj, w_qkv).astype(bf16).reshape(nc, 2, rows, width)
+    grad_normed_one = half_rows_sum(grad_normed_part, t)
     inv_one = rms_scale(own_tokens)
     dgain_attn = jnp.sum(grad_normed_one * own_tokens * inv_one, 0)
     grad_tokens = grad_residual + norm_back(grad_normed_one, own_tokens, inv_one, attn_gain)

time: 1290 us -> 1100 us (0.85)
  Pallas kernels: 0 us -> 315 us
  blocking collectives: 253 us -> 0 us
  waiting for transfers between devices: 472 us -> 343 us
  starting transfers between devices: 148 us -> 83.2 us
  matrix products: 190 us -> 163 us
  local copies, waits for them, and re-layouts: 131 us -> 113 us
  between operations: 16.7 us -> 2.08 us
    pallas_call x0 -> x2, Pallas kernels: none -> 315 us  [the longest x1 200 us: dispatch(): pl.pallas_call(functools.partial(dispatch_kernel, nz, nc), out_shape=[jax...]
    all_to_all x3 -> x0, blocking collectives: 189 us -> none  [exchange(): return lax.all_to_all(value, axes, split_axis=0, concat_axis=0, tiled=True)]
    all_to_all x18 -> x11, waiting for transfers between devices: 411 us -> 334 us  [exchange(): return lax.all_to_all(value, axes, split_axis=0, concat_axis=0, tiled=True)]
    all_gather x1 -> x0, blocking collectives: 64.2 us -> none  [one_chip(): routes_all = lax.all_gather(routes[0], ('fsdp', 'ctx'), axis=0)]
    all_to_all x18 -> x11, starting transfers between devices: 121 us -> 70.1 us  [exchange(): return lax.all_to_all(value, axes, split_axis=0, concat_axis=0, tiled=True)]
    unnamed x2 -> x0, waiting for transfers between devices: 47.9 us -> none
    dot_general x9, matrix products: 57.2 us -> 40.8 us  [dot(): return jnp.dot(left, right, preferred_element_type=jnp.float32)]
    ppermute x16 -> x12, starting transfers between devices: 27.5 us -> 13.1 us  [swap(): return lax.ppermute(value, 'tp', [(0, 1), (1, 0)])]
  transfers between devices with their start and end apart: 35 -> 23, of which waited for: 20 -> 12; matrix products, arithmetic and copies ran while one was open for 21% -> 21% of each run, Pallas kernels for 0% -> 18%
where the time goes in v2:
time: 1100 us; the launch traced here: 1090 us
  waiting for transfers between devices  343 us (31%)
  Pallas kernels  315 us (29%)
  matrix products  163 us (15%)
  local copies, waits for them, and re-layouts  113 us (10%)
  starting transfers between devices  83.2 us (8%)
  other arithmetic  72.6 us (7%)
    all_to_all x11, waiting for transfers between devices, exchange(): return lax.all_to_all(value, axes, split_axis=0, concat_axis=0, tiled=True)  334 us
    pallas_call x1, Pallas kernels, dispatch(): pl.pallas_call(functools.partial(dispatch_kernel, nz, nc), out_shape=[jax...  200 us
    pallas_call x1, Pallas kernels, load(): pl.pallas_call(functools.partial(load_kernel, nz, nc), out_shape=[jax.Sha...  115 us
    all_to_all x11, starting transfers between devices, exchange(): return lax.all_to_all(value, axes, split_axis=0, concat_axis=0, tiled=True)  70.1 us
    dot_general x9, matrix products, dot_tn(): lax.dot_general(left, right, (((0,), (0,)), ((), ())), preferred_element_...  52.9 us
    dot_general x8, matrix products, dot_nt(): lax.dot_general(left, right, (((1,), (1,)), ((), ())), preferred_element_...  49.7 us
    dot_general x9, matrix products, dot(): return jnp.dot(left, right, preferred_element_type=jnp.float32)  40.8 us
    unnamed x187, local copies, waits for them, and re-layouts  29.3 us
  transfers between devices with their start and end apart: 23, of which 12 were waited for; matrix products, arithmetic and copies ran while one was open for 21% of the time, Pallas kernels for 18%

profile of v2, /device:TPU:15, one launch (start us, length us, event | category | flops | bytes accessed | tf_op | source)
XLA Modules:
  0.0 1092.4 jit_solution(7190244880349865442)
XLA Ops:
  2.3 10.7 constant_dynamic-slice_fusion.3
  13.1 6.9 copy.230
  25.0 115.2 %shard_map.220 = (bf16[1024,2048]{1,0:T(8,128)(2,1)}, bf16[4,512,768]{2,1,0:T(8,128)(2,1)}, bf16[4,256,512]{2,1,0:T(8,128)(2,1)S(1)}, bf16[4,96,128]{2,1,0:T(8,1...) custom-call(bf16[256,2048]{1,0:T(8,128)(2,1)S(1)} %bitcast.246, ...), custom_call_target="tpu_custom_call" | custom-call | tf_op jit(solution)/shard_map/pallas_call | solution.py:640
  141.6 8.2 all-to-all-start
  156.6 4.7 reduce-window.14
  184.6 200.0 %shard_map.221 = (f32[128,2048]{1,0:T(8,128)}, bf16[128,2048]{1,0:T(8,128)(2,1)}, f32[128,128]{1,0:T(8,128)}, bf16[4,2,144,2048]{3,2,1,0:T(8,128)(2,1)}, bf16[4,...) custom-call(bf16[4,2,128,2048]{3,2,1,0:T(8,128)(2,1)} %bitcast.254, bf16[256,2048]{1,0:T(8,128)(2,1)} %bitcast.245, ...), custom_call_target="tpu_custom_call" | custom-call | tf_op jit(solution)/shard_map/pallas_call | solution.py:802
  386.5 8.7 select_reduce_fusion
  412.0 7.3 multiply_reduce_fusion.3
  419.3 5.1 fusion.86
  424.4 5.1 fusion.85
  429.5 5.2 fusion.82
  443.7 7.7 multiply_reduce_fusion.2
  452.7 8.3 fusion.87
  461.0 7.1 add_convert_fusion.1
  468.1 13.1 %add_convert_fusion = bf16[1152,2048]{1,0:T(8,128)(2,1)} fusion(f32[1152,2048]{1,0:T(8,128)} %fusion.87, f32[1152,2048]{1,0:T(8,128)} %fusion.85, f32[1152,2048]{1,0:T(8,128)} %fusion.86, bf16[1152,512]{0,1:T(8,128)(2,1)S(1)} %copy-done.35, bf16[2048,512]{1,0:T(8,128)(2,1)S(1)} %collective-permute-done.1), kind=kOutput, calls=%fused_computation.5 | convolution fusion | flops 2425356288 | bytes 36306944 | tf_op jit(solution)/shard_map/dot_general | solution.py:426
  481.3 15.5 %concatenate.37 = bf16[1152,4224]{1,0:T(8,128)(2,1)} concatenate(bf16[1152,2048]{1,0:T(8,128)(2,1)} %add_convert_fusion.1, bf16[1152,2048]{1,0:T(8,128)(2,1)} %add_convert_fusion, bf16[1152,16]{1,0:T(8,128)(2,1)S(1)} %copy.187, bf16[1152,16]{1,0:T(8,128)(2,1)} %copy.188, bf16[1152,96]{1,0:T(8,128)(2,1)S(1)} %broadcast_in_dim.28), dimensions={1} | concatenate | bytes 19464192 | tf_op jit(solution)/shard_map/concatenate | solution.py:977
  496.8 6.1 all-to-all-start.1
  502.9 106.0 %all-to-all-done.1 = bf16[4,2,144,4224]{3,2,1,0:T(8,128)(2,1)} async-done(((bf16[4,2,144,4224]{3,2,1,0:T(8,128)(2,1)}), bf16[4,2,144,4224]{3,2,1,0:T(8,128)(2,1)}, u32[]{:S(2)}, u32[]{:S(2)}) %all-to-all-start.1) | async-done | bytes 9732128 | tf_op jit(solution)/shard_map/all_to_all | solution.py:413
  609.0 8.3 copy.189
  617.3 7.7 convolution_convert_fusion
  631.6 4.8 maximum_select_fusion
  636.4 7.8 all-to-all-start.2
  644.4 7.0 convolution_convert_fusion.4
  652.0 84.8 %all-to-all-done.2 = bf16[4,128,4224]{2,1,0:T(8,128)(2,1)} async-done(((bf16[4,128,4224]{2,1,0:T(8,128)(2,1)}), bf16[4,128,4224]{2,1,0:T(8,128)(2,1)}, u32[]{:S(2)}, u32[]{:S(2)}) %all-to-all-start.2) | async-done | bytes 4325408 | tf_op jit(solution)/shard_map/all_to_all | solution.py:413
  744.0 5.7 all-to-all-start.3
  749.7 7.1 convolution_convert_fusion.6
  758.3 5.4 add_convert_fusion.2
  763.8 8.6 all-to-all-done.3
  772.3 8.4 all-to-all-start.10
  780.8 7.0 convolution_convert_fusion.5
  789.7 7.8 add_convert_fusion.4
  797.5 5.5 add_convert_fusion.3
  811.2 17.1 %all-to-all-done.10 = bf16[16,128,512]{2,1,0:T(8,128)(2,1)S(1)} async-done(((bf16[16,128,512]{2,1,0:T(8,128)(2,1)}), bf16[16,128,512]{2,1,0:T(8,128)(2,1)S(1)}, u32[]{:S(2)}, u32[]{:S(2)}) %all-to-all-start.10) | async-done | bytes 2097184 | tf_op jit(solution)/shard_map/all_to_all | solution.py:413
  828.4 4.9 all-to-all-start.8
  833.3 4.9 multiply_reduce_fusion
  851.3 29.6 %all-to-all-done.8 = bf16[16,128,512]{2,1,0:T(8,128)(2,1)} async-done(((bf16[16,128,512]{2,1,0:T(8,128)(2,1)}), bf16[16,128,512]{2,1,0:T(8,128)(2,1)}, u32[]{:S(2)}, u32[]{:S(2)}) %all-to-all-start.8) | async-done | bytes 2097184 | tf_op jit(solution)/shard_map/all_to_all | solution.py:413
  880.9 4.7 all-to-all-start.9
  906.6 26.8 %all-to-all-done.9 = bf16[16,128,512]{2,1,0:T(8,128)(2,1)S(1)} async-done(((bf16[16,128,512]{2,1,0:T(8,128)(2,1)}), bf16[16,128,512]{2,1,0:T(8,128)(2,1)S(1)}, u32[]{:S(2)}, u32[]{:S(2)}) %all-to-all-start.9) | async-done | bytes 2097184 | tf_op jit(solution)/shard_map/all_to_all | solution.py:413
  942.5 16.8 %all-to-all-done.4 = bf16[4,128,2048]{2,1,0:T(8,128)(2,1)} async-done(((bf16[4,128,2048]{2,1,0:T(8,128)(2,1)}), bf16[4,128,2048]{2,1,0:T(8,128)(2,1)}, u32[]{:S(2)}, u32[]{:S(2)}) %all-to-all-start.4) | async-done | bytes 2097184 | tf_op jit(solution)/shard_map/all_to_all | solution.py:413
  959.3 6.7 all-to-all-start.6
  971.9 17.9 %all-to-all-done.6 = bf16[16,256,128]{2,1,0:T(8,128)(2,1)S(1)} async-done(((bf16[16,256,128]{2,1,0:T(8,128)(2,1)}), bf16[16,256,128]{2,1,0:T(8,128)(2,1)S(1)}, u32[]{:S(2)}, u32[]{:S(2)}) %all-to-all-start.6) | async-done | bytes 1048608 | tf_op jit(solution)/shard_map/all_to_all | solution.py:413
  989.8 6.5 all-to-all-start.7
  996.3 8.2 convolution_convert_fusion.3
  1004.5 4.6 copy.195
  1009.8 6.7 all-to-all-start.5
  1028.1 6.9 convert_bitcast_fusion
  1034.9 14.7 %reshape.441 = f32[128,3,16,512]{3,2,1,0:T(8,128)} reshape(f32[128,3,4,4,512]{4,3,2,1,0:T(4,128)} %convert_bitcast_fusion) | data formatting | bytes 25165824 | tf_op jit(solution)/shard_map/reshape | solution.py:998
  1060.2 26.3 %all-to-all-done.5 = bf16[16,128,768]{1,2,0:T(8,128)(2,1)} async-done(((bf16[16,128,768]{1,2,0:T(8,128)(2,1)}), bf16[16,128,768]{1,2,0:T(8,128)(2,1)}, u32[]{:S(2)}, u32[]{:S(2)}) %all-to-all-start.5) | async-done | bytes 3145760 | tf_op jit(solution)/shard_map/all_to_all | solution.py:413
  (350 shorter events, 170.2 us)
Async XLA Ops:
  141.6 253.6 %all-to-all-start = ((bf16[4,3,512,512]{3,2,1,0:T(8,128)(2,1)}), bf16[4,3,512,512]{3,2,1,0:T(8,128)(2,1)}, u32[]{:S(2)}, u32[]{:S(2)}) async-start(bf16[4,3,512,512]{3,2,1,0:T(8,128)(2,1)} %bitcast.255), calls=%async_computation | async-start | bytes 12582912 | tf_op jit(solution)/shard_map/all_to_all | solution.py:413
  150.4 30.9 %copy-start.21 = (bf16[256,4,512]{0,2,1:T(8,128)(2,1)}, bf16[256,4,512]{0,2,1:T(8,128)(2,1)S(1)}, u32[]{:S(2)}) copy-start(bf16[256,4,512]{0,2,1:T(8,128)(2,1)S(1)} %copy.175) | copy-start | bytes 3145732
  150.7 22.4 %copy-start.58 = (f32[128]{0:T(128)}, f32[128]{0:T(128)S(1)}, u32[]{:S(2)}) copy-start(f32[128]{0:T(128)S(1)} %reshape.431) | copy-start | bytes 1540
  150.8 22.3 %copy-start.60 = (f32[128]{0:T(128)}, f32[128]{0:T(128)S(1)}, u32[]{:S(2)}) copy-start(f32[128]{0:T(128)S(1)} %reshape.430) | copy-start | bytes 1540
  150.8 14.9 %copy-start.39 = (bf16[2,8,4,512]{3,1,2,0:T(8,128)(2,1)}, bf16[2,8,4,512]{3,1,2,0:T(8,128)(2,1)S(1)}, u32[]{:S(2)}) copy-start(bf16[2,8,4,512]{3,1,2,0:T(8,128)(2,1)S(1)} %copy.224) | copy-start | bytes 196612
  152.0 15.7 %copy-start.43 = (f32[1,4,4,128]{3,1,2,0:T(4,128)}, f32[1,4,4,128]{3,1,2,0:T(4,128)S(1)}, u32[]{:S(2)}) copy-start(f32[1,4,4,128]{3,1,2,0:T(4,128)S(1)} %copy.222) | copy-start | bytes 24580
  399.7 35.0 %collective-permute-start.1 = (bf16[2048,512]{1,0:T(8,128)(2,1)S(1)}, bf16[2048,512]{1,0:T(8,128)(2,1)S(1)}, u32[]{:S(2)}, u32[]{:S(2)}) collective-permute-start(bf16[2048,512]{1,0:T(8,128)(2,1)S(1)} %bitcast.290), channel_id=1, source_target_pairs={{0,1},{1,0},{2,3},{3,2},{4,5},{5,4},{6,7},{7,6},{8,9},{9,8},{10,11... | collective-permute-start | bytes 6291464 | tf_op jit(solution)/shard_map/ppermute | solution.py:409
  402.5 36.6 %collective-permute-start = (bf16[2048,512]{1,0:T(8,128)(2,1)S(1)}, bf16[2048,512]{1,0:T(8,128)(2,1)S(1)}, u32[]{:S(2)}, u32[]{:S(2)}) collective-permute-start(bf16[2048,512]{1,0:T(8,128)(2,1)S(1)} %bitcast.287), channel_id=1, source_target_pairs={{0,1},{1,0},{2,3},{3,2},{4,5},{5,4},{6,7},{7,6},{8,9},{9,8},{10,11... | collective-permute-start | bytes 6291464 | tf_op jit(solution)/shard_map/ppermute | solution.py:409
  402.6 9.4 slice-start.6
  411.5 32.1 %collective-permute-start.2 = (bf16[2048,512]{1,0:T(8,128)(2,1)S(1)}, bf16[2048,512]{1,0:T(8,128)(2,1)S(1)}, u32[]{:S(2)}, u32[]{:S(2)}) collective-permute-start(bf16[2048,512]{1,0:T(8,128)(2,1)S(1)} %bitcast.284), channel_id=1, source_target_pairs={{0,1},{1,0},{2,3},{3,2},{4,5},{5,4},{6,7},{7,6},{8,9},{9,8},{10,11... | collective-permute-start | bytes 6291464 | tf_op jit(solution)/shard_map/ppermute | solution.py:409
  452.7 8.3 copy-start.70
  452.7 8.3 copy-start.76
  496.8 112.2 %all-to-all-start.1 = ((bf16[4,2,144,4224]{3,2,1,0:T(8,128)(2,1)}), bf16[4,2,144,4224]{3,2,1,0:T(8,128)(2,1)}, u32[]{:S(2)}, u32[]{:S(2)}) async-start(bf16[4,2,144,4224]{3,2,1,0:T(8,128)(2,1)} %bitcast.253), calls=%async_computation.1 | async-start | bytes 19464192 | tf_op jit(solution)/shard_map/all_to_all | solution.py:413
  609.0 8.3 copy-start.36
  626.7 4.9 collective-permute-start.3
  636.4 100.5 %all-to-all-start.2 = ((bf16[4,128,4224]{2,1,0:T(8,128)(2,1)}), bf16[4,128,4224]{2,1,0:T(8,128)(2,1)}, u32[]{:S(2)}, u32[]{:S(2)}) async-start(bf16[4,128,4224]{2,1,0:T(8,128)(2,1)} %bitcast.257), calls=%async_computation.2 | async-start | bytes 8650752 | tf_op jit(solution)/shard_map/all_to_all | solution.py:413
  651.4 88.6 %copy-start.31 = (f32[128,16]{1,0:T(8,128)S(1)}, f32[128,16]{1,0:T(8,128)}, u32[]{:S(2)}) copy-start(f32[128,16]{1,0:T(8,128)} %copy-done.30) | copy-start | bytes 24580
  651.4 88.6 %copy-start.41 = (f32[128,128]{1,0:T(8,128)S(1)}, f32[128,128]{1,0:T(8,128)}, u32[]{:S(2)}) copy-start(f32[128,128]{1,0:T(8,128)} %get-tuple-element.38) | copy-start | bytes 196612
  651.4 88.8 %copy-start.40 = (bf16[2,8,4,512]{3,1,2,0:T(8,128)(2,1)S(1)}, bf16[2,8,4,512]{3,1,2,0:T(8,128)(2,1)}, u32[]{:S(2)}) copy-start(bf16[2,8,4,512]{3,1,2,0:T(8,128)(2,1)} %copy-done.39) | copy-start | bytes 196612
  651.4 106.9 %collective-permute-start.11 = (bf16[2048,512]{1,0:T(8,128)(2,1)}, bf16[2048,512]{1,0:T(8,128)(2,1)}, u32[]{:S(2)}, u32[]{:S(2)}) collective-permute-start(bf16[2048,512]{1,0:T(8,128)(2,1)} %convolution_convert_fusion.4), channel_id=1, source_target_pairs={{0,1},{1,0},{2,3},{3,2},{4,5},{5,4},{6,7},{7,6},{8,9},{9,8},{10,11... | collective-permute-start | bytes 6291464 | tf_op jit(solution)/shard_map/ppermute | solution.py:409
  742.4 15.9 %slice-start.8 = ((s8[4718592]{0:T(1024)(128)(4,1)}), s8[524288]{0:T(1024)(128)(4,1)S(1)}, s32[]{:S(2)}) async-start(s8[4718592]{0:T(1024)(128)(4,1)} %bitcast.341), calls=%async_computation.19 | async-start | bytes 1048576
  744.0 28.3 %all-to-all-start.3 = ((bf16[4,128,2048]{2,1,0:T(8,128)(2,1)}), bf16[4,128,2048]{2,1,0:T(8,128)(2,1)}, u32[]{:S(2)}, u32[]{:S(2)}) async-start(bf16[4,128,2048]{2,1,0:T(8,128)(2,1)} %broadcast_in_dim.29), calls=%async_computation.3 | async-start | bytes 4194304 | tf_op jit(solution)/shard_map/all_to_all | solution.py:413
  749.7 8.6 slice-start.9
  749.7 8.6 copy-start.75
  756.8 32.9 %collective-permute-start.9 = (bf16[2048,512]{1,0:T(8,128)(2,1)}, bf16[2048,512]{1,0:T(8,128)(2,1)}, u32[]{:S(2)}, u32[]{:S(2)}) collective-permute-start(bf16[2048,512]{1,0:T(8,128)(2,1)} %convolution_convert_fusion.6), channel_id=1, source_target_pairs={{0,1},{1,0},{2,3},{3,2},{4,5},{5,4},{6,7},{7,6},{8,9},{9,8},{10,11... | collective-permute-start | bytes 6291464 | tf_op jit(solution)/shard_map/ppermute | solution.py:409
  772.3 56.0 %all-to-all-start.10 = ((bf16[16,128,512]{2,1,0:T(8,128)(2,1)}), bf16[16,128,512]{2,1,0:T(8,128)(2,1)S(1)}, u32[]{:S(2)}, u32[]{:S(2)}) async-start(bf16[16,128,512]{2,1,0:T(8,128)(2,1)} %bitcast.280), calls=%async_computation.10 | async-start | bytes 4194304 | tf_op jit(solution)/shard_map/all_to_all | solution.py:413
  780.8 8.9 copy-start.50
  780.8 8.9 copy-start.53
  787.7 9.7 collective-permute-start.10
  789.6 13.3 %collective-permute-start.5 = (bf16[4,128,2048]{2,1,0:T(8,128)(2,1)}, bf16[4,128,2048]{2,1,0:T(8,128)(2,1)}, u32[]{:S(2)}, u32[]{:S(2)}) collective-permute-start(bf16[4,128,2048]{2,1,0:T(8,128)(2,1)} %all-to-all-done.3), channel_id=1, source_target_pairs={{0,1},{1,0},{2,3},{3,2},{4,5},{5,4},{6,7},{7,6},{8,9},{9,8},{10,11... | collective-permute-start | bytes 6291464 | tf_op jit(solution)/shard_map/ppermute | solution.py:409
  811.2 22.1 %copy-start.28 = (bf16[1024,256]{0,1:T(8,128)(2,1)S(1)}, bf16[1024,256]{0,1:T(8,128)(2,1)}, u32[]{:S(2)}) copy-start(bf16[1024,256]{0,1:T(8,128)(2,1)} %convolution_convert_fusion.8) | copy-start | bytes 1572868
  828.4 9.9 copy-start.12
  828.4 52.5 %all-to-all-start.8 = ((bf16[16,128,512]{2,1,0:T(8,128)(2,1)}), bf16[16,128,512]{2,1,0:T(8,128)(2,1)}, u32[]{:S(2)}, u32[]{:S(2)}) async-start(bf16[16,128,512]{2,1,0:T(8,128)(2,1)} %bitcast.279), calls=%async_computation.8 | async-start | bytes 4194304 | tf_op jit(solution)/shard_map/all_to_all | solution.py:413
  851.3 34.3 %copy-start.54 = (f32[1024,2]{0,1:T(2,128)S(1)}, f32[1024,2]{0,1:T(2,128)}, u32[]{:S(2)}) copy-start(f32[1024,2]{0,1:T(2,128)} %get-tuple-element.162) | copy-start | bytes 24580
  851.3 34.3 %copy-start.59 = (f32[128]{0:T(128)S(1)}, f32[128]{0:T(128)}, u32[]{:S(2)}) copy-start(f32[128]{0:T(128)} %copy-done.58) | copy-start | bytes 1540
  880.9 52.4 %all-to-all-start.9 = ((bf16[16,128,512]{2,1,0:T(8,128)(2,1)}), bf16[16,128,512]{2,1,0:T(8,128)(2,1)S(1)}, u32[]{:S(2)}, u32[]{:S(2)}) async-start(bf16[16,128,512]{2,1,0:T(8,128)(2,1)} %bitcast.278), calls=%async_computation.9 | async-start | bytes 4194304 | tf_op jit(solution)/shard_map/all_to_all | solution.py:413
  896.0 6.1 collective-permute-start.6
  906.5 31.3 %copy-start.33 = (bf16[2,128,1024]{2,1,0:T(8,128)(2,1)S(1)}, bf16[2,128,1024]{2,1,0:T(8,128)(2,1)}, u32[]{:S(2)}) copy-start(bf16[2,128,1024]{2,1,0:T(8,128)(2,1)} %copy-done.32) | copy-start | bytes 1572868
  933.3 7.9 copy-start.13
  933.3 26.0 %all-to-all-start.4 = ((bf16[4,128,2048]{2,1,0:T(8,128)(2,1)}), bf16[4,128,2048]{2,1,0:T(8,128)(2,1)}, u32[]{:S(2)}, u32[]{:S(2)}) async-start(bf16[4,128,2048]{2,1,0:T(8,128)(2,1)} %fusion.9), calls=%async_computation.4 | async-start | bytes 4194304 | tf_op jit(solution)/shard_map/all_to_all | solution.py:413
  941.3 24.7 %copy-start.1 = (bf16[1,256,2048]{2,1,0:T(8,128)(2,1)S(1)}, bf16[1,256,2048]{2,1,0:T(8,128)(2,1)}, u32[]{:S(2)}) copy-start(bf16[1,256,2048]{2,1,0:T(8,128)(2,1)} %param.13) | copy-start | bytes 3145732
  959.3 30.4 %all-to-all-start.6 = ((bf16[16,256,128]{2,1,0:T(8,128)(2,1)}), bf16[16,256,128]{2,1,0:T(8,128)(2,1)S(1)}, u32[]{:S(2)}, u32[]{:S(2)}) async-start(bf16[16,256,128]{2,1,0:T(8,128)(2,1)} %bitcast.275), calls=%async_computation.6 | async-start | bytes 2097152 | tf_op jit(solution)/shard_map/all_to_all | solution.py:413
  968.4 27.9 %copy-start.57 = (f32[1024]{0:T(1024)S(1)}, f32[1024]{0:T(1024)}, u32[]{:S(2)}) copy-start(f32[1024]{0:T(1024)} %copy-done.56) | copy-start | bytes 12292
  989.8 19.4 %all-to-all-start.7 = ((f32[16,1,2320]{2,1,0:T(1,128)}), f32[16,1,2320]{2,1,0:T(1,128)S(1)}, u32[]{:S(2)}, u32[]{:S(2)}) async-start(f32[16,1,2320]{2,1,0:T(1,128)} %copy.200), calls=%async_computation.7 | async-start | bytes 311296 | tf_op jit(solution)/shard_map/all_to_all | solution.py:413
  1009.8 76.7 %all-to-all-start.5 = ((bf16[16,128,768]{1,2,0:T(8,128)(2,1)}), bf16[16,128,768]{1,2,0:T(8,128)(2,1)}, u32[]{:S(2)}, u32[]{:S(2)}) async-start(bf16[16,128,768]{1,2,0:T(8,128)(2,1)} %copy.195), calls=%async_computation.5 | async-start | bytes 6291456 | tf_op jit(solution)/shard_map/all_to_all | solution.py:413
  1025.5 24.1 %collective-permute-start.4 = (bf16[128,1024]{1,0:T(8,128)(2,1)}, bf16[128,1024]{1,0:T(8,128)(2,1)}, u32[]{:S(2)}, u32[]{:S(2)}) collective-permute-start(bf16[128,1024]{1,0:T(8,128)(2,1)} %get-tuple-element.144), channel_id=1, source_target_pairs={{0,1},{1,0},{2,3},{3,2},{4,5},{5,4},{6,7},{7,6},{8,9},{9,8},{10,11... | collective-permute-start | bytes 786440 | tf_op jit(solution)/shard_map/ppermute | solution.py:409
  1054.0 3.8 collective-permute-start.7
  1054.1 1.8 collective-permute-start.8
  (63 other events, 248.6 us)

commit v3 on v2

--- a/solution.py
+++ b/solution.py
@@ -482,7 +482,7 @@
     ]
 
 
-def line_gather(nz, bufs, send_sem, recv_sem, arrived):
+def line_gather(nz, bufs, send_sem, recv_sem, arrived, begun=None, near=None):
     z = lax.axis_index("fsdp")
     for step in range(nz - 1):
 
@@ -495,6 +495,11 @@
         def _():
             for copy in line_copies(bufs, send_sem, recv_sem, 1, step, z + step, z - 1):
                 copy.start()
+
+        if step == 0 and begun is not None:
+            begun()
+        if near is not None:
+            near(step)
 
         @pl.when(z - 1 >= step)
         def _():
@@ -508,6 +513,9 @@
                 copy.wait_recv()
             arrived(z + 1 + step)
 
+
+def line_sent(nz, bufs, send_sem, recv_sem):
+    z = lax.axis_index("fsdp")
     for step in range(nz - 1):
 
         @pl.when((z < nz - 1) & (z >= step))
@@ -521,7 +529,26 @@
                 copy.wait_send()
 
 
-def regroup(shard, t, rows, line, two, keep_sem, give_send, give_recv, start):
+def pick_rows(pick, slot, source, out):
+    lanes = out.shape[-1]
+    piece = min(lanes, 512)
+
+    @pl.loop(0, lanes // piece)
+    def _(k):
+        at = pl.ds(pl.multiple_of(k * piece, piece), piece)
+        out[slot, :, at] = jnp.dot(pick[slot], source[slot, :, at], preferred_element_type=jnp.float32).astype(
+            jnp.bfloat16
+        )
+
+
+def plane_copy(most, src, dst, send, recv, slot, step, source, target):
+    rows = pl.ds(pl.multiple_of(target * most, 16), most)
+    return remote(
+        src.at[slot, rows], dst.at[source, slot], send.at[slot, step - 1], recv.at[slot, step - 1], ctx=target
+    )
+
+
+def regroup(shard, t, rows, line, two, keep_sem, give_send, give_recv):
     slot = lax.rem(shard, 2)
     band = pl.ds(pl.multiple_of(t * rows, rows), rows)
 
@@ -536,29 +563,32 @@
 
 
 def load_kernel(
-    nz, nc, tok, cot, wq, wk, wv, wo, small,
-    x_all, w_qkv, w_o, small_all, cot_line, cot_two, routes_seq,
-    own_sem, line_send, line_recv, tok_send, tok_recv, pass_send, pass_recv,
-    route_send, route_recv, keep_sem, give_send, give_recv,
+    nz, nc, tok, cot, wq, wk, wv, wo, small, rank,
+    x_all, w_qkv, w_o, small_all, rank_line, rank_seq, pick, cot_in,
+    cot_line, cot_two, cot_send,
+    own_sem, line_send, line_recv, w_send, w_recv, tok_send, tok_recv, pass_send, pass_recv,
+    rank_send, rank_recv, keep_sem, give_send, give_recv, cot_s, cot_r, cot_own,
 ):
     z, c, t = places()
     block = tok.shape[0]
     rows = block // 2
     local = w_qkv.shape[2] // 3
-    kinds = routes_seq.shape[1]
-    first = small.shape[0] - kinds
+    most = cot_in.shape[2]
     half = pl.ds(pl.multiple_of(t * rows, rows), rows)
     column = pl.ds(pl.multiple_of(c * local, local), local)
     own = [
+        pltpu.make_async_copy(cot.at[half], cot_line.at[z], own_sem.at[5]),
+        pltpu.make_async_copy(small, small_all.at[z], own_sem.at[4]),
+        pltpu.make_async_copy(rank, rank_line.at[z], own_sem.at[7]),
+        pltpu.make_async_copy(rank, rank_seq.at[c], own_sem.at[8]),
+    ]
+    own += [
         pltpu.make_async_copy(w.at[:, column], w_qkv.at[z, :, pl.ds(k * local, local)], own_sem.at[k])
         for k, w in enumerate((wq, wk, wv))
     ]
     own += [
         pltpu.make_async_copy(wo.at[column], w_o.at[z], own_sem.at[3]),
-        pltpu.make_async_copy(small, small_all.at[z], own_sem.at[4]),
-        pltpu.make_async_copy(cot.at[half], cot_line.at[z], own_sem.at[5]),
         pltpu.make_async_copy(tok, x_all.at[pl.ds(pl.multiple_of(c * block, block), block)], own_sem.at[6]),
-        pltpu.make_async_copy(small.at[pl.ds(first, kinds)], routes_seq.at[c], own_sem.at[7]),
     ]
     for copy in own:
         copy.start()
@@ -573,45 +603,70 @@
     def pass_copy(step, source, core):
         return remote(band(source, core), band(source, core), pass_send.at[step], pass_recv.at[step], tp=1 - t)
 
-    def route_copy(step, source, target):
-        return remote(
-            small.at[pl.ds(first, kinds)], routes_seq.at[source], route_send.at[step], route_recv.at[step], ctx=target
-        )
+    def rank_copy(step, source, target):
+        return remote(rank, rank_seq.at[source], rank_send.at[step], rank_recv.at[step], ctx=target)
 
     for step in range(1, nc):
         token_copy(step - 1, c, ring(c, step, nc)).start()
-        route_copy(step - 1, c, ring(c, step, nc)).start()
+        rank_copy(step - 1, c, ring(c, step, nc)).start()
     for copy in own:
         copy.wait()
 
     def arrived(shard):
-        regroup(shard, t, rows, cot_line, cot_two, keep_sem, give_send, give_recv, True)
+        regroup(shard, t, rows, cot_line, cot_two, keep_sem, give_send, give_recv)
 
     arrived(z)
-
-    def later(shard):
-        arrived(shard)
-
-    line_gather(nz, (w_qkv, w_o, small_all, cot_line), line_send, line_recv, later)
+    first = (cot_line, rank_line, small_all)
+    line_gather(nz, first, line_send, line_recv, arrived)
+
+    def own_copy(slot):
+        return pltpu.make_async_copy(
+            cot_send.at[slot, pl.ds(pl.multiple_of(c * most, 16), most)], cot_in.at[c, slot], cot_own.at[slot]
+        )
+
+    def send_cotangent():
+        number = lax.broadcasted_iota(jnp.int32, (most, block), 0).astype(jnp.float32)
+        for slot in range(2):
+            for q in range(nc):
+                row = rank_line[2 * t + slot, pl.ds(q * nz + z, 1), :]
+                hit = jnp.where(number == row, 1.0, 0.0)
+                pick[slot, pl.ds(q * most, most), :] = hit.astype(jnp.bfloat16)
+        for slot in range(2):
+            wait_two(slot, t, rows, cot_line, cot_two, keep_sem, give_recv)
+            pick_rows(pick, slot, cot_two, cot_send)
+            for step in range(1, nc):
+                plane_copy(most, cot_send, cot_in, cot_s, cot_r, slot, step, c, ring(c, step, nc)).start()
+            own_copy(slot).start()
+
+    def ignore(shard):
+        pass
+
+    line_gather(nz, (w_qkv, w_o), w_send, w_recv, ignore, send_cotangent)
     for step in range(1, nc):
         source = ring(c, -step, nc)
         token_copy(step - 1, source, source).wait_recv()
         pass_copy(step - 1, source, t).start()
-        route_copy(step - 1, source, source).wait_recv()
+        rank_copy(step - 1, source, source).wait_recv()
     for step in range(1, nc):
         source = ring(c, -step, nc)
         pass_copy(step - 1, source, 1 - t).wait_recv()
         pass_copy(step - 1, source, t).wait_send()
         token_copy(step - 1, c, source).wait_send()
-        route_copy(step - 1, c, source).wait_send()
-    finish_regroup(t, rows, cot_line, cot_two, keep_sem, give_send, give_recv)
-
-
-def finish_regroup(t, rows, line, two, keep_sem, give_send, give_recv):
+        rank_copy(step - 1, c, source).wait_send()
+        for slot in range(2):
+            copy = plane_copy(most, cot_send, cot_in, cot_s, cot_r, slot, step, source, source)
+            copy.wait_recv()
+            copy.wait_send()
+    line_sent(nz, first, line_send, line_recv)
+    line_sent(nz, (w_qkv, w_o), w_send, w_recv)
     for slot in range(2):
-        wait_two(slot, t, rows, line, two, keep_sem, give_recv)
-        band = pl.ds(pl.multiple_of(t * rows, rows), rows)
-        remote(line.at[0], two.at[slot, band], give_send.at[slot], give_recv.at[slot], tp=1 - t).wait_send()
+        own_copy(slot).wait()
+        wait_given(slot, t, rows, cot_line, cot_two, give_send, give_recv)
+
+
+def wait_given(slot, t, rows, line, two, give_send, give_recv):
+    band = pl.ds(pl.multiple_of(t * rows, rows), rows)
+    remote(line.at[0], two.at[slot, band], give_send.at[slot], give_recv.at[slot], tp=1 - t).wait_send()
 
 
 def wait_two(slot, t, rows, line, two, keep_sem, give_recv):
@@ -621,45 +676,50 @@
     remote(line.at[0], two.at[slot, other], give_recv.at[slot], give_recv.at[slot], tp=1 - t).wait_recv()
 
 
-def load(tok, cot, wq, wk, wv, wo, small, kinds):
+def load(tok, cot, wq, wk, wv, wo, small, rank, most):
     nz, nc = lax.axis_size("fsdp"), lax.axis_size("ctx")
     block, width = tok.shape
     deep, local = wq.shape[0], wq.shape[1] // nc
     rows = block // 2
     dma = pltpu.SemaphoreType.DMA
-    bf16 = jnp.bfloat16
+    bf16, f32 = jnp.bfloat16, jnp.float32
     shapes = [
-        (nc * block, width),
-        (nz, deep, 3 * local),
-        (nz, local, wo.shape[1]),
-        (nz,) + small.shape,
-        (nz, rows, width),
-        (2, block, width),
-        (nc, kinds, 128),
+        ((nc * block, width), bf16),
+        ((nz, deep, 3 * local), bf16),
+        ((nz, local, wo.shape[1]), bf16),
+        ((nz,) + small.shape, bf16),
+        ((nz,) + rank.shape, f32),
+        ((nc,) + rank.shape, f32),
+        ((2, nc * most, block), bf16),
+        ((nc, 2, most, width), bf16),
     ]
+    hbm = pl.BlockSpec(memory_space=pl.ANY)
     return pl.pallas_call(
         functools.partial(load_kernel, nz, nc),
-        out_shape=[jax.ShapeDtypeStruct(shape, bf16) for shape in shapes],
-        in_specs=[pl.BlockSpec(memory_space=pl.ANY)] * 7,
-        out_specs=[pl.BlockSpec(memory_space=pltpu.VMEM)] * 7,
+        out_shape=[jax.ShapeDtypeStruct(shape, kind) for shape, kind in shapes],
+        in_specs=[hbm] * 8,
+        out_specs=[pl.BlockSpec(memory_space=pltpu.VMEM)] * 7 + [hbm],
         scratch_shapes=[
-            dma((8,)),
-            dma((2, nz - 1, 4)), dma((2, nz - 1, 4)),
+            pltpu.VMEM((nz, rows, width), bf16),
+            pltpu.VMEM((2, block, width), bf16),
+            pltpu.VMEM((2, nc * most, width), bf16),
+            dma((9,)),
+            dma((2, nz - 1, 3)), dma((2, nz - 1, 3)), dma((2, nz - 1, 2)), dma((2, nz - 1, 2)),
             dma((nc - 1,)), dma((nc - 1,)), dma((nc - 1,)), dma((nc - 1,)), dma((nc - 1,)), dma((nc - 1,)),
-            dma((2,)), dma((2,)), dma((2,)),
+            dma((2,)), dma((2,)), dma((2,)), dma((2, nc - 1)), dma((2, nc - 1)), dma((2,)),
         ],
         compiler_params=pltpu.CompilerParams(
-            collective_id=0, has_side_effects=True, vmem_limit_bytes=40 * 2**20
+            collective_id=0, has_side_effects=True, vmem_limit_bytes=48 * 2**20
         ),
-    )(tok, cot, wq, wk, wv, wo, small)
+    )(tok, cot, wq, wk, wv, wo, small, rank)
 
 
 def dispatch_kernel(
-    nz, nc, part, tok, gain, router, kept, pick, cot_two,
-    residual, normed, probs, x_in, g_in, cot_in,
-    sib, rs_send, rs_recv, n_line, g_line, n_two, g_two, x_send, g_send, cot_send,
+    nz, nc, part, tok, gain, router, kept, pick,
+    residual, normed, probs, x_in, g_in,
+    sib, rs_send, rs_recv, n_line, g_line, n_two, g_two, x_send, g_send,
     sib_s, sib_r, rs_s, rs_r, line_send, line_recv, keep_sem, give_send, give_recv,
-    gkeep_sem, ggive_send, ggive_recv, x_s, x_r, g_s, g_r, cot_s, cot_r, own_sem,
+    gkeep_sem, ggive_send, ggive_recv, x_s, x_r, g_s, g_r, own_sem,
 ):
     z, c, t = places()
     f32, bf16 = jnp.float32, jnp.bfloat16
@@ -687,36 +747,10 @@
 
         rs_copy(step - 1, c, q).start()
 
-    def picked(slot, source, out, out_at):
-        lanes = out.shape[-1]
-        piece = min(lanes, 512)
-
-        @pl.loop(0, lanes // piece)
-        def _(k):
-            at = pl.ds(pl.multiple_of(k * piece, piece), piece)
-            out[out_at, :, at] = jnp.dot(
-                pick[slot], source[slot, :, at], preferred_element_type=f32
-            ).astype(bf16)
-
-    def send_copy(slot, step, src, dst, send, recv, source, target):
-        return remote(
-            src.at[slot, pl.ds(pl.multiple_of(target * most, 16), most)],
-            dst.at[source, slot],
-            send.at[slot, step - 1],
-            recv.at[slot, step - 1],
-            ctx=target,
-        )
-
     def own_copy(slot, src, dst, k):
         return pltpu.make_async_copy(
             src.at[slot, pl.ds(pl.multiple_of(c * most, 16), most)], dst.at[c, slot], own_sem.at[k, slot]
         )
-
-    for slot in range(2):
-        picked(slot, cot_two, cot_send, slot)
-        for step in range(1, nc):
-            send_copy(slot, step, cot_send, cot_in, cot_s, cot_r, c, ring(c, step, nc)).start()
-        own_copy(slot, cot_send, cot_in, 0).start()
 
     sib_copy(c).wait_recv()
     for step in range(1, nc):
@@ -751,37 +785,40 @@
     g_line[z, :, pl.ds(128, 128)] = (gates - high.astype(f32)).astype(bf16)
 
     def arrived(shard):
-        regroup(shard, t, rows, n_line, n_two, keep_sem, give_send, give_recv, True)
-        regroup(shard, t, rows, g_line, g_two, gkeep_sem, ggive_send, ggive_recv, True)
+        regroup(shard, t, rows, n_line, n_two, keep_sem, give_send, give_recv)
+        regroup(shard, t, rows, g_line, g_two, gkeep_sem, ggive_send, ggive_recv)
 
     arrived(z)
-    line_gather(nz, (n_line, g_line), line_send, line_recv, arrived)
+    sent = ((x_send, x_in, x_s, x_r), (g_send, g_in, g_s, g_r))
+
+    def near(distance):
+        above, below = z + distance, z - distance
+        is_above = (above < nz) & (above // 2 == t)
+        is_below = (below >= 0) & (below // 2 == t)
+        slot = lax.rem(jnp.where(is_above, above, below + 2), 2)
+
+        @pl.when(is_above | is_below)
+        def _():
+            wait_two(slot, t, rows, n_line, n_two, keep_sem, give_recv)
+            wait_two(slot, t, rows, g_line, g_two, gkeep_sem, ggive_recv)
+            pick_rows(pick, slot, n_two, x_send)
+            pick_rows(pick, slot, g_two, g_send)
+            for k, (src, dst, s, r) in enumerate(sent):
+                for step in range(1, nc):
+                    plane_copy(most, src, dst, s, r, slot, step, c, ring(c, step, nc)).start()
+                own_copy(slot, src, dst, k).start()
+
+    line_gather(nz, (n_line, g_line), line_send, line_recv, arrived, None, near)
+    near(nz - 1)
+    line_sent(nz, (n_line, g_line), line_send, line_recv)
     for slot in range(2):
-        wait_two(slot, t, rows, n_line, n_two, keep_sem, give_recv)
-        wait_two(slot, t, rows, g_line, g_two, gkeep_sem, ggive_recv)
-        picked(slot, n_two, x_send, slot)
-        picked(slot, g_two, g_send, slot)
-        for step in range(1, nc):
-            send_copy(slot, step, x_send, x_in, x_s, x_r, c, ring(c, step, nc)).start()
-            send_copy(slot, step, g_send, g_in, g_s, g_r, c, ring(c, step, nc)).start()
-        own_copy(slot, x_send, x_in, 1).start()
-        own_copy(slot, g_send, g_in, 2).start()
-
-    band = pl.ds(pl.multiple_of(t * rows, rows), rows)
-    for slot in range(2):
-        remote(n_line.at[0], n_two.at[slot, band], give_send.at[slot], give_recv.at[slot], tp=1 - t).wait_send()
-        remote(g_line.at[0], g_two.at[slot, band], ggive_send.at[slot], ggive_recv.at[slot], tp=1 - t).wait_send()
-        own_copy(slot, cot_send, cot_in, 0).wait()
-        own_copy(slot, x_send, x_in, 1).wait()
-        own_copy(slot, g_send, g_in, 2).wait()
-        for step in range(1, nc):
-            source = ring(c, -step, nc)
-            for src, dst, s, r in (
-                (cot_send, cot_in, cot_s, cot_r),
-                (x_send, x_in, x_s, x_r),
-                (g_send, g_in, g_s, g_r),
-            ):
-                copy = send_copy(slot, step, src, dst, s, r, source, source)
+        wait_given(slot, t, rows, n_line, n_two, give_send, give_recv)
+        wait_given(slot, t, rows, g_line, g_two, ggive_send, ggive_recv)
+        for k, (src, dst, s, r) in enumerate(sent):
+            own_copy(slot, src, dst, k).wait()
+            for step in range(1, nc):
+                source = ring(c, -step, nc)
+                copy = plane_copy(most, src, dst, s, r, slot, step, source, source)
                 copy.wait_recv()
                 copy.wait_send()
     for step in range(1, nc):
@@ -790,7 +827,7 @@
         sib_copy(step).wait_send()
 
 
-def dispatch(part, tok, gain, router, kept, pick, cot_two):
+def dispatch(part, tok, gain, router, kept, pick):
     nz, nc = lax.axis_size("fsdp"), lax.axis_size("ctx")
     rows, width = part.shape[2], part.shape[3]
     block = rows * 2
@@ -807,10 +844,9 @@
             jax.ShapeDtypeStruct((rows, 128), f32),
             jax.ShapeDtypeStruct((nc, 2, most, width), bf16),
             jax.ShapeDtypeStruct((nc, 2, most, 256), bf16),
-            jax.ShapeDtypeStruct((nc, 2, most, width), bf16),
         ],
-        in_specs=[vmem] * 7,
-        out_specs=[vmem] * 3 + [hbm] * 3,
+        in_specs=[vmem] * 6,
+        out_specs=[vmem] * 3 + [hbm] * 2,
         scratch_shapes=[
             pltpu.VMEM((nc, rows, width), bf16),
             pltpu.VMEM((nc - 1, rows, width), bf16),
@@ -821,30 +857,639 @@
             pltpu.VMEM((2, block, 256), bf16),
             pltpu.VMEM((2, nc * most, width), bf16),
             pltpu.VMEM((2, nc * most, 256), bf16),
-            pltpu.VMEM((2, nc * most, width), bf16),
             dma((nc,)), dma((nc,)), dma((nc - 1,)), dma((nc - 1,)),
             dma((2, nz - 1, 2)), dma((2, nz - 1, 2)),
             dma((2,)), dma((2,)), dma((2,)), dma((2,)), dma((2,)), dma((2,)),
-            dma((2, nc - 1)), dma((2, nc - 1)), dma((2, nc - 1)), dma((2, nc - 1)), dma((2, nc - 1)), dma((2, nc - 1)),
-            dma((3, 2)),
+            dma((2, nc - 1)), dma((2, nc - 1)), dma((2, nc - 1)), dma((2, nc - 1)),
+            dma((2, 2)),
         ],
         compiler_params=pltpu.CompilerParams(
             collective_id=1, has_side_effects=True, vmem_limit_bytes=56 * 2**20
         ),
-    )(part, tok, gain, router, kept, pick, cot_two)
-
-
-def half_rows_sum(partial, core):
-    mine = lax.dynamic_index_in_dim(partial, core, 1, keepdims=False)
-    received = swap(lax.dynamic_index_in_dim(partial, 1 - core, 1, keepdims=False))
-    summed = (mine.astype(jnp.float32) + received.astype(jnp.float32)).astype(jnp.bfloat16)
-    pieces = exchange(summed, "ctx")
-    return jnp.sum(pieces.astype(jnp.float32), 0)
-
-
-def all_rows(half, core):
-    mine = spread(half, "ctx")
-    return by_core(mine, swap(mine), core).transpose(1, 0, 2, 3)
+    )(part, tok, gain, router, kept, pick)
+
+
+def experts_kernel(
+    x_hbm, cot_hbm, weight, own_hbm, other_hbm, y, r, pair, own_grad, other_grad,
+    x, cot, w, gate, up, out_grad, hid, gg, gu, stage, sem, stage_sem,
+):
+    f32, bf16 = jnp.float32, jnp.bfloat16
+    width, tall = x.shape[1], x.shape[0]
+    nz, deep, ffn = w.shape[1], w.shape[3], w.shape[4]
+    span = 256
+    copies = [
+        pltpu.make_async_copy(cot_hbm, cot, sem.at[0]),
+        pltpu.make_async_copy(own_hbm, w.at[0], sem.at[1]),
+        pltpu.make_async_copy(x_hbm, x, sem.at[2]),
+        pltpu.make_async_copy(other_hbm, w.at[1], sem.at[3]),
+    ]
+    for copy in copies:
+        copy.start()
+    for copy in copies:
+        copy.wait()
+    pair[...] = jnp.zeros_like(pair)
+    per = ffn // span
+
+    @pl.loop(0, 2 * per)
+    def _(n):
+        half, at = n // per, pl.ds(pl.multiple_of(lax.rem(n, per) * span, span), span)
+        full = pl.ds(pl.multiple_of(n * span, span), span)
+
+        def times(rows, k):
+            return jnp.dot(rows[...], w[half, :, k, :, at].reshape(width, span), preferred_element_type=f32)
+
+        out_grad[...] = times(cot, 2)
+        gate[...] = times(x, 0)
+        up[...] = times(x, 1)
+        chunk = 48
+
+        @pl.loop(0, tall // chunk)
+        def _(m):
+            rows = pl.ds(pl.multiple_of(m * chunk, chunk), chunk)
+            g, u, o, k = gate[rows, :], up[rows, :], out_grad[rows, :], weight[rows, :]
+            sig = 1.0 / (1.0 + jnp.exp(-g))
+            silu = g * sig
+            hidden = silu * u
+            pair[rows, :] += jnp.sum(hidden.astype(bf16).astype(f32) * o, 1, keepdims=True)
+            hid[rows, full] = (k * hidden).astype(bf16)
+            o = k * o
+            gg[rows, full] = (o * u * sig * (1.0 + g * (1.0 - sig))).astype(bf16)
+            gu[rows, full] = (o * silu).astype(bf16)
+
+    per_deep = deep // span
+
+    @pl.loop(0, width // span)
+    def _(n):
+        zone, at = n // per_deep, pl.ds(pl.multiple_of(lax.rem(n, per_deep) * span, span), span)
+        full = pl.ds(pl.multiple_of(n * span, span), span)
+
+        def back(rows, k):
+            total = 0.0
+            for half in range(2):
+                total = total + lax.dot_general(
+                    rows[:, pl.ds(half * ffn, ffn)], w[half, zone, k, at, :], (((1,), (1,)), ((), ())),
+                    preferred_element_type=f32,
+                )
+            return total
+
+        y[:, full] = back(hid, 2).astype(bf16)
+        r[:, full] = (back(gg, 0) + back(gu, 1)).astype(bf16)
+
+    strip = stage.shape[4]
+    count = span // strip
+
+    def flush(n, half):
+        slot = lax.rem(n, 2)
+        out = (own_grad, other_grad)[half]
+        return pltpu.make_async_copy(
+            stage.at[slot, half], out.at[pl.ds(pl.multiple_of(n * count, count), count)], stage_sem.at[slot, half]
+        )
+
+    @pl.loop(0, width // span)
+    def _(n):
+        full = pl.ds(pl.multiple_of(n * span, span), span)
+        slot = lax.rem(n, 2)
+
+        @pl.when(n >= 2)
+        def _():
+            for half in range(2):
+                flush(n - 2, half).wait()
+
+        for k, (rows, grads) in enumerate(((x, gg), (x, gu), (cot, hid))):
+            value = lax.dot_general(
+                rows[:, full], grads[...], (((0,), (0,)), ((), ())), preferred_element_type=f32
+            ).astype(bf16)
+            for half in range(2):
+                for i in range(count):
+                    stage[slot, half, i, k] = value[i * strip : (i + 1) * strip, half * ffn : (half + 1) * ffn]
+        for half in range(2):
+            flush(n, half).start()
+
+    for n in (width // span - 2, width // span - 1):
+        for half in range(2):
+            flush(n, half).wait()
+
+
+def experts(x, cot, weight, own, other, strip):
+    bf16, f32 = jnp.bfloat16, jnp.float32
+    tall, width = x.shape
+    ffn = own.shape[3]
+    vmem = pl.BlockSpec(memory_space=pltpu.VMEM)
+    hbm = pl.BlockSpec(memory_space=pl.ANY)
+    grads = jax.ShapeDtypeStruct((width // strip, 3, strip, ffn), bf16)
+    dma = pltpu.SemaphoreType.DMA
+    return pl.pallas_call(
+        experts_kernel,
+        out_shape=[
+            jax.ShapeDtypeStruct((tall, width), bf16),
+            jax.ShapeDtypeStruct((tall, width), bf16),
+            jax.ShapeDtypeStruct((tall, 1), f32),
+            grads,
+            grads,
+        ],
+        in_specs=[hbm, hbm, vmem, hbm, hbm],
+        out_specs=[vmem, vmem, vmem, hbm, hbm],
+        scratch_shapes=[
+            pltpu.VMEM((tall, width), bf16),
+            pltpu.VMEM((tall, width), bf16),
+            pltpu.VMEM((2,) + own.shape, bf16),
+            pltpu.VMEM((tall, 256), f32),
+            pltpu.VMEM((tall, 256), f32),
+            pltpu.VMEM((tall, 256), f32),
+            pltpu.VMEM((tall, 2 * ffn), bf16),
+            pltpu.VMEM((tall, 2 * ffn), bf16),
+            pltpu.VMEM((tall, 2 * ffn), bf16),
+            pltpu.VMEM((2, 2, 256 // strip, 3, strip, ffn), bf16),
+            dma((4,)),
+            dma((2, 2)),
+        ],
+        compiler_params=pltpu.CompilerParams(vmem_limit_bytes=60 * 2**20),
+    )(x, cot, weight, own, other)
+
+
+def collector(nz, nc, pick_t, items, sems):
+    z, c, t = places()
+    to_s, to_r, own_sem, sib_s, sib_r, line_s, line_r, keep_sem = sems
+    rows = items[0][2].shape[1]
+    mine_at = pl.ds(pl.multiple_of(t * rows, rows), rows)
+    give_at = pl.ds(pl.multiple_of((1 - t) * rows, rows), rows)
+    count = len(items)
+
+    def to_copy(slot, k, step, source, target):
+        src, got = items[k][:2]
+        return remote(
+            src.at[target, slot], got.at[slot, source], to_s.at[k, slot, step - 1], to_r.at[k, slot, step - 1], ctx=target
+        )
+
+    def own_copy(slot, k):
+        src, got = items[k][:2]
+        return pltpu.make_async_copy(src.at[c, slot], got.at[slot, c], own_sem.at[k, slot])
+
+    def sib_copy(slot, k):
+        give, sib = items[k][3:5]
+        return remote(give.at[slot], sib.at[slot], sib_s.at[k, slot], sib_r.at[k, slot], tp=1 - t)
+
+    def line_copy(slot, k, half, source, target):
+        src = items[k][2 if half == 0 else 4]
+        return remote(src.at[slot], items[k][5].at[source], line_s.at[k, half, slot], line_r.at[k, source], fsdp=target)
+
+    def keep_copy(slot, k, half):
+        src = items[k][2 if half == 0 else 4]
+        return pltpu.make_async_copy(src.at[slot], items[k][5].at[z], keep_sem.at[k])
+
+    def goal(slot, half):
+        return 2 * (t if half == 0 else 1 - t) + slot
+
+    def forward(slot, k, half):
+        target = goal(slot, half)
+        pl.when(target != z)(lambda: line_copy(slot, k, half, z, target).start())
+        pl.when(target == z)(lambda: keep_copy(slot, k, half).start())
+
+    def begin(slot):
+        for k in range(count):
+            for step in range(1, nc):
+                to_copy(slot, k, step, c, ring(c, step, nc)).start()
+            own_copy(slot, k).start()
+
+    def scatter(slot, k):
+        got, mine, give = items[k][1:4]
+        lanes = mine.shape[-1]
+        span = min(lanes, 512)
+        tall = got.shape[1] * got.shape[2]
+
+        @pl.loop(0, lanes // span)
+        def _(n):
+            at = pl.ds(pl.multiple_of(n * span, span), span)
+            pairs = got[slot, :, :, at].reshape(tall, span)
+            for picks, out in ((mine_at, mine), (give_at, give)):
+                out[slot, :, at] = jnp.dot(
+                    pick_t[slot, picks, :], pairs, preferred_element_type=jnp.float32
+                ).astype(jnp.bfloat16)
+
+    def process(slot):
+        for k in range(count):
+            own_copy(slot, k).wait()
+            for step in range(1, nc):
+                source = ring(c, -step, nc)
+                to_copy(slot, k, step, source, c).wait_recv()
+            scatter(slot, k)
+            sib_copy(slot, k).start()
+            forward(slot, k, 0)
+        for k in range(count):
+            sib_copy(slot, k).wait_recv()
+            forward(slot, k, 1)
+
+    def join():
+        for k in range(count):
+            keep_copy(0, k, 0).wait()
+            for step in range(1, nz):
+                line_copy(0, k, 0, ring(z, -step, nz), z).wait_recv()
+
+    def done():
+        for slot in range(2):
+            for k in range(count):
+                for step in range(1, nc):
+                    to_copy(slot, k, step, c, ring(c, step, nc)).wait_send()
+                sib_copy(slot, k).wait_send()
+                for half in range(2):
+                    pl.when(goal(slot, half) != z)(
+                        lambda: line_copy(slot, k, half, z, goal(slot, half)).wait_send()
+                    )
+
+    return begin, process, join, done
+
+
+def collector_scratch(nz, nc, most, rows, widths):
+    dma = pltpu.SemaphoreType.DMA
+    bf16 = jnp.bfloat16
+    count = len(widths)
+    bufs = []
+    for w in widths:
+        bufs += [pltpu.VMEM((2, nc, most, w), bf16)]
+        bufs += [pltpu.VMEM((2, rows, w), bf16)] * 3
+        bufs += [pltpu.VMEM((nz, rows, w), bf16)]
+    sems = [
+        dma((count, 2, nc - 1)), dma((count, 2, nc - 1)), dma((count, 2)), dma((count, 2)), dma((count, 2)),
+        dma((count, 2, 2)), dma((count, nz)), dma((count,)),
+    ]
+    return bufs, sems
+
+
+def return_kernel(
+    nz, nc, r, g, pick_t, residual, probs, kept, router, gain, cot,
+    logits_grad, gain_grad, residual_grad, attn_grad, *scratch,
+):
+    z, c, t = places()
+    f32, bf16 = jnp.float32, jnp.bfloat16
+    rows, width = residual.shape
+    r_line, g_line = scratch[4], scratch[9]
+    row_s, row_r, pass_s, pass_r = scratch[18:]
+    items = ((r,) + scratch[:5], (g,) + scratch[5:10])
+    begin, process, join, done = collector(nz, nc, pick_t, items, scratch[10:18])
+    greet(nz, nc, True)
+    for slot in range(2):
+        begin(slot)
+    for slot in range(2):
+        process(slot)
+    join()
+    pairs = jnp.zeros((rows, 128), f32)
+    for source in range(nz):
+        pairs = pairs + g_line[source, :, 0:128].astype(f32) + g_line[source, :, 128:256].astype(f32)
+    pairs = pairs * kept[...]
+    prob = probs[...]
+    grad_logits = (prob * (pairs - jnp.sum(prob * pairs, -1, keepdims=True))).astype(bf16)
+    logits_grad[...] = grad_logits
+    gain_grad[...] = jnp.zeros_like(gain_grad)
+    chunk = 16
+
+    @pl.loop(0, rows // chunk)
+    def _(k):
+        at = pl.ds(pl.multiple_of(k * chunk, chunk), chunk)
+        full = pl.ds(pl.multiple_of(t * rows + k * chunk, chunk), chunk)
+        res = residual[at, :]
+        grad = r_line[0, at, :].astype(f32)
+        for source in range(1, nz):
+            grad = grad + r_line[source, at, :].astype(f32)
+        grad = grad + jnp.dot(logits_grad[at, :], router[...], preferred_element_type=f32)
+        inv = lax.rsqrt(jnp.mean(res * res, -1, keepdims=True) + EPS)
+        gain_grad[...] += jnp.sum((grad * res * inv).reshape(chunk // 8, 8, width), 0)
+        weighted = grad * gain[...]
+        inner = jnp.sum(weighted * res, -1, keepdims=True)
+        out = cot[full, :].astype(f32) + inv * weighted - res * (inv * inv * inv) * inner / width
+        residual_grad[at, :] = out
+        attn_grad[c, t, at, :] = out.astype(bf16)
+
+    def row_copy(step, source, target):
+        return remote(attn_grad.at[source, t], attn_grad.at[source, t], row_s.at[step], row_r.at[step], ctx=target)
+
+    def pass_copy(step, source, core):
+        return remote(attn_grad.at[source, core], attn_grad.at[source, core], pass_s.at[step], pass_r.at[step], tp=1 - t)
+
+    for step in range(1, nc):
+        row_copy(step, c, ring(c, step, nc)).start()
+    pass_copy(0, c, t).start()
+    for step in range(1, nc):
+        source = ring(c, -step, nc)
+        row_copy(step, source, source).wait_recv()
+        pass_copy(step, source, t).start()
+    for step in range(nc):
+        source = ring(c, -step, nc)
+        pass_copy(step, source, 1 - t).wait_recv()
+        pass_copy(step, source, t).wait_send()
+        if step:
+            row_copy(step, c, source).wait_send()
+    done()
+
+
+def give_back(r, g, pick_t, residual, probs, kept, router, gain, cot):
+    nz, nc = lax.axis_size("fsdp"), lax.axis_size("ctx")
+    rows, width = residual.shape
+    dma = pltpu.SemaphoreType.DMA
+    bf16, f32 = jnp.bfloat16, jnp.float32
+    vmem = pl.BlockSpec(memory_space=pltpu.VMEM)
+    hbm = pl.BlockSpec(memory_space=pl.ANY)
+    bufs, sems = collector_scratch(nz, nc, r.shape[2], rows, (width, 256))
+    return pl.pallas_call(
+        functools.partial(return_kernel, nz, nc),
+        out_shape=[
+            jax.ShapeDtypeStruct((rows, 128), bf16),
+            jax.ShapeDtypeStruct((8, width), f32),
+            jax.ShapeDtypeStruct((rows, width), f32),
+            jax.ShapeDtypeStruct((nc, 2, rows, width), bf16),
+        ],
+        in_specs=[hbm] * 2 + [vmem] * 7,
+        out_specs=[vmem] * 4,
+        scratch_shapes=bufs + sems + [dma((nc,)), dma((nc,)), dma((nc,)), dma((nc,))],
+        compiler_params=pltpu.CompilerParams(
+            collective_id=2, has_side_effects=True, vmem_limit_bytes=56 * 2**20
+        ),
+    )(r, g, pick_t, residual, probs, kept, router, gain, cot)
+
+
+def final_kernel(
+    nz, nc, part, tok, gain, residual_grad, dw, dwo, small, y, pick_t, residual,
+    tokens_grad, dw_out, dwo_out, small_out, layer,
+    sib, rs_send, rs_recv, tok_grad, gain_acc, dw_up, dw_down, dwo_up, dwo_down, dw_to, dwo_to,
+    dw_next, dwo_next, small_line, small_plane, small_sib, small_a, small_b,
+    sib_s, sib_r, rs_s, rs_r, line_s, line_r, to_s, to_r, tg_s, tg_r, sm_s, sm_r, sp_s, sp_r, ss_s, ss_r,
+    layer_send, lay_s, lay_r, *scratch,
+):
+    z, c, t = places()
+    f32, bf16 = jnp.float32, jnp.bfloat16
+    rows, width = residual_grad.shape
+    piece = width // 2
+    chunk = 16
+    y_line = scratch[4]
+    begin, process, join, done = collector(nz, nc, pick_t, ((y,) + scratch[:5],), scratch[5:])
+    greet(nz, nc, True)
+
+    bufs = ((dw, dw_up, dw_down), (dwo, dwo_up, dwo_down))
+    outs = (dw_next, dwo_next)
+
+    def hop(way, step, k, target):
+        src = outs[k].at[way, step]
+        return remote(src, bufs[k][1 + way].at[step], line_s.at[way, step, k], line_r.at[way, step, k], fsdp=target)
+
+    def add_to(k, way, step, shard, joined):
+        own, out = bufs[k][0], outs[k]
+        got = bufs[k][1 + way]
+        height = own.shape[2]
+        tile = 32
+
+        @pl.loop(0, nc * (height // tile))
+        def _(n):
+            q, at = n // (height // tile), pl.ds(pl.multiple_of(lax.rem(n, height // tile) * tile, tile), tile)
+            value = own[shard, q, at, :]
+            if joined:
+                value = (value.astype(f32) + got[step, q, at, :].astype(f32)).astype(bf16)
+            out[way, step, q, at, :] = value
+
+    def line_step(step):
+        for way in range(2):
+            shard = nz - 1 - step if way == 0 else step
+            ahead = z + 1 if way == 0 else z - 1
+            behind = z - 1 if way == 0 else z + 1
+            first = z == 0 if way == 0 else z == nz - 1
+            sends = shard > z if way == 0 else shard < z
+            gets = (z > 0) & (shard >= z) if way == 0 else (z < nz - 1) & (shard <= z)
+
+            @pl.when(gets)
+            def _():
+                for k in range(2):
+                    hop(way, step, k, behind).wait_recv()
+
+            @pl.when(sends & jnp.logical_not(first))
+            def _():
+                for k in range(2):
+                    add_to(k, way, step, shard, True)
+                    hop(way, step, k, ahead).start()
+
+    def line_begin():
+        for way in range(2):
+            first = z == 0 if way == 0 else z == nz - 1
+
+            @pl.when(first)
+            def _():
+                for step in range(nz - 1):
+                    shard = nz - 1 - step if way == 0 else step
+                    for k in range(2):
+                        add_to(k, way, step, shard, False)
+                        hop(way, step, k, z + 1 if way == 0 else z - 1).start()
+
+    def sib_copy(q):
+        return remote(part.at[q, 1 - t], sib.at[q], sib_s.at[q], sib_r.at[q], tp=1 - t)
+
+    def rs_copy(step, target):
+        return remote(rs_send.at[step], rs_recv.at[step], rs_s.at[step], rs_r.at[step], ctx=target)
+
+    for step in range(1, nc + 1):
+        sib_copy(ring(c, step, nc)).start()
+    line_begin()
+    for step in range(1, nc):
+        q = ring(c, step, nc)
+        sib_copy(q).wait_recv()
+
+        @pl.loop(0, rows // chunk)
+        def _(k):
+            at = pl.ds(pl.multiple_of(k * chunk, chunk), chunk)
+            rs_send[step - 1, at, :] = (part[q, t, at, :].astype(f32) + sib[q, at, :].astype(f32)).astype(bf16)
+
+        rs_copy(step - 1, q).start()
+    sib_copy(c).wait_recv()
+    begin(0)
+    line_step(0)
+    begin(1)
+    for step in range(1, nc):
+        rs_copy(step - 1, c).wait_recv()
+    gain_acc[...] = jnp.zeros_like(gain_acc)
+
+    @pl.loop(0, rows // chunk)
+    def _(k):
+        at = pl.ds(pl.multiple_of(k * chunk, chunk), chunk)
+        full = pl.ds(pl.multiple_of(t * rows + k * chunk, chunk), chunk)
+        grad = part[c, t, at, :].astype(f32) + sib[c, at, :].astype(f32)
+        for step in range(nc - 1):
+            grad = grad + rs_recv[step, at, :].astype(f32)
+        x = tok[full, :].astype(f32)
+        inv = lax.rsqrt(jnp.mean(x * x, -1, keepdims=True) + EPS)
+        gain_acc[...] += jnp.sum((grad * x * inv).reshape(chunk // 8, 8, width), 0)
+        weighted = grad * gain[...]
+        inner = jnp.sum(weighted * x, -1, keepdims=True)
+        out = residual_grad[at, :] + inv * weighted - x * (inv * inv * inv) * inner / width
+        tok_grad[at, :] = out.astype(bf16)
+        tokens_grad[full, :] = out.astype(bf16)
+
+    def grad_copy(core):
+        return remote(
+            tok_grad, tokens_grad.at[pl.ds(pl.multiple_of(core * rows, rows), rows)], tg_s, tg_r, tp=1 - t
+        )
+
+    grad_copy(t).start()
+
+    small_a[...] = small[...]
+    total = jnp.sum(gain_acc[...], 0, keepdims=True)
+    for strip in range(nz * nc):
+        small_a[strip // nc, strip % nc, pl.ds(17, 1), :] = total[:, strip * 128 : (strip + 1) * 128]
+
+    def small_copy(step, shard, target):
+        return remote(small_a.at[shard], small_line.at[step], sm_s.at[step], sm_r.at[step], fsdp=target)
+
+    def plane_copy(step, shard, target):
+        return remote(small_b.at[shard], small_plane.at[step], sp_s.at[step], sp_r.at[step], ctx=target)
+
+    for step in range(1, nz):
+        small_copy(step - 1, ring(z, step, nz), ring(z, step, nz)).start()
+    line_step(1)
+    process(0)
+    line_step(2)
+    for step in range(1, nz):
+        small_copy(step - 1, z, z).wait_recv()
+    value = small_a[z]
+    for step in range(nz - 1):
+        value = value + small_line[step]
+    small_b[...] = value
+    for step in range(1, nc):
+        plane_copy(step - 1, ring(c, step, nc), ring(c, step, nc)).start()
+
+    def close(k, out, to):
+        own, up, down = bufs[k]
+        height = own.shape[2]
+        tile = 32
+
+        @pl.loop(0, nc * (height // tile))
+        def _(n):
+            q, at = n // (height // tile), pl.ds(pl.multiple_of(lax.rem(n, height // tile) * tile, tile), tile)
+            base = own[z, q, at, :].astype(f32)
+            above = up[jnp.minimum(nz - 1 - z, nz - 2), q, at, :].astype(f32)
+            below = down[jnp.minimum(z, nz - 2), q, at, :].astype(f32)
+            base = base + jnp.where(z > 0, above, 0.0) + jnp.where(z < nz - 1, below, 0.0)
+            to[q, at, :] = base.astype(bf16)
+
+    close(0, dw_out, dw_to)
+    close(1, dwo_out, dwo_to)
+
+    def to_copy(k, step, source, target):
+        src, dst = ((dw_to, dw_out), (dwo_to, dwo_out))[k]
+        return remote(src.at[target], dst.at[source], to_s.at[k, step], to_r.at[k, step], ctx=target)
+
+    for step in range(1, nc):
+        for k in range(2):
+            to_copy(k, step - 1, c, ring(c, step, nc)).start()
+    def layer_copy(core):
+        return remote(
+            layer_send.at[:, pl.ds(pl.multiple_of((1 - t) * piece, piece), piece)],
+            layer.at[pl.ds(pl.multiple_of(core * rows, rows), rows)],
+            lay_s, lay_r, tp=1 - t,
+        )
+
+    process(1)
+    join()
+
+    @pl.loop(0, rows // chunk)
+    def _(k):
+        at = pl.ds(pl.multiple_of(k * chunk, chunk), chunk)
+        full = pl.ds(pl.multiple_of(t * rows + k * chunk, chunk), chunk)
+        total = residual[at, :]
+        for source in range(nz):
+            total = total + y_line[source, at, :].astype(f32)
+        layer_send[at, :] = total.astype(bf16)
+        layer[full, :] = layer_send[at, pl.ds(pl.multiple_of(t * piece, piece), piece)]
+
+    layer_copy(t).start()
+    dw_out[c, :, :] = dw_to[c, :, :]
+    dwo_out[c, :, :] = dwo_to[c, :, :]
+    for step in range(1, nc):
+        plane_copy(step - 1, c, c).wait_recv()
+    value = small_b[c]
+    for step in range(nc - 1):
+        value = value + small_plane[step]
+    small_out[...] = value
+    final = remote(small_out, small_sib, ss_s, ss_r, tp=1 - t)
+    final.start()
+    final.wait()
+    small_out[...] = value + small_sib[...]
+    for step in range(1, nc):
+        source = ring(c, -step, nc)
+        for k in range(2):
+            src, dst = ((dw_to, dw_out), (dwo_to, dwo_out))[k]
+            remote(
+                src.at[c], dst.at[source], to_s.at[k, step - 1], to_r.at[k, step - 1], ctx=source
+            ).wait_recv()
+    grad_copy(1 - t).wait_recv()
+    grad_copy(t).wait_send()
+    layer_copy(1 - t).wait_recv()
+    layer_copy(t).wait_send()
+    done()
+    for step in range(1, nc):
+        for k in range(2):
+            to_copy(k, step - 1, c, ring(c, step, nc)).wait_send()
+        plane_copy(step - 1, ring(c, step, nc), ring(c, step, nc)).wait_send()
+        rs_copy(step - 1, c).wait_send()
+    for step in range(1, nz):
+        small_copy(step - 1, ring(z, step, nz), ring(z, step, nz)).wait_send()
+    for q in range(nc):
+        sib_copy(q).wait_send()
+    for step in range(nz - 1):
+        for way in range(2):
+            shard = nz - 1 - step if way == 0 else step
+            ahead = z + 1 if way == 0 else z - 1
+            sends = shard > z if way == 0 else shard < z
+
+            @pl.when(sends)
+            def _():
+                for k in range(2):
+                    hop(way, step, k, ahead).wait_send()
+
+
+def finish(part, tok, gain, residual_grad, dw, dwo, small, y, pick_t, residual):
+    nz, nc = lax.axis_size("fsdp"), lax.axis_size("ctx")
+    rows, width = residual_grad.shape
+    dma = pltpu.SemaphoreType.DMA
+    bf16, f32 = jnp.bfloat16, jnp.float32
+    vmem = pl.BlockSpec(memory_space=pltpu.VMEM)
+    one, two = dw.shape[1:], dwo.shape[1:]
+    bufs, sems = collector_scratch(nz, nc, y.shape[2], rows, (width,))
+    tiny = small.shape[2:]
+    return pl.pallas_call(
+        functools.partial(final_kernel, nz, nc),
+        out_shape=[
+            jax.ShapeDtypeStruct((2 * rows, width), bf16),
+            jax.ShapeDtypeStruct(one, bf16),
+            jax.ShapeDtypeStruct(two, bf16),
+            jax.ShapeDtypeStruct(tiny, f32),
+            jax.ShapeDtypeStruct((2 * rows, width // 2), bf16),
+        ],
+        in_specs=[vmem] * 7 + [pl.BlockSpec(memory_space=pl.ANY)] + [vmem] * 2,
+        out_specs=[vmem] * 5,
+        scratch_shapes=[
+            pltpu.VMEM((nc, rows, width), bf16),
+            pltpu.VMEM((nc - 1, rows, width), bf16),
+            pltpu.VMEM((nc - 1, rows, width), bf16),
+            pltpu.VMEM((rows, width), bf16),
+            pltpu.VMEM((8, width), f32),
+            pltpu.VMEM((nz - 1,) + one, bf16),
+            pltpu.VMEM((nz - 1,) + one, bf16),
+            pltpu.VMEM((nz - 1,) + two, bf16),
+            pltpu.VMEM((nz - 1,) + two, bf16),
+            pltpu.VMEM(one, bf16),
+            pltpu.VMEM(two, bf16),
+            pltpu.VMEM((2, nz - 1) + one, bf16),
+            pltpu.VMEM((2, nz - 1) + two, bf16),
+            pltpu.VMEM((nz - 1,) + small.shape[1:], f32),
+            pltpu.VMEM((nc - 1,) + tiny, f32),
+            pltpu.VMEM(tiny, f32),
+            pltpu.VMEM(small.shape, f32),
+            pltpu.VMEM(small.shape[1:], f32),
+            dma((nc,)), dma((nc,)), dma((nc - 1,)), dma((nc - 1,)),
+            dma((2, nz - 1, 2)), dma((2, nz - 1, 2)),
+            dma((2, nc - 1)), dma((2, nc - 1)), dma, dma,
+            dma((nz - 1,)), dma((nz - 1,)), dma((nc - 1,)), dma((nc - 1,)), dma, dma,
+            pltpu.VMEM((rows, width), bf16), dma, dma,
+        ] + bufs + sems,
+        compiler_params=pltpu.CompilerParams(
+            collective_id=3, has_side_effects=True, vmem_limit_bytes=60 * 2**20
+        ),
+    )(part, tok, gain, residual_grad, dw, dwo, small, y, pick_t, residual)
 
 
 def one_chip(
@@ -878,15 +1523,16 @@
     small = jnp.concatenate([w_router.T.reshape(-1), gain_attn, gain_moe, gain_query, gain_key])
     total = small.shape[0]
     small = jnp.pad(small, (0, -total % 2048))
-    kinds = block * TOPK // 128
-    small = jnp.concatenate([small, routes.reshape(-1).astype(bf16)]).reshape(-1, 128)
-    x_rows, w_qkv, w_o, small, _, cot_two, routes_seq = load(
-        tokens[0], cotangent[0], w_query, w_key, w_value, w_out, small, kinds
+    small = small.reshape(-1, 128)
+    ids = jnp.arange(E, dtype=jnp.int32)
+    named = jnp.any(routes[0][:, :, None] == ids, 1)
+    below = jnp.tril(jnp.ones((block, block), bf16), -1)
+    rank = jnp.where(named, dot(below, named.astype(bf16)), -1.0).T
+    x_rows, w_qkv, w_o, small, _, rank_seq, pick, cot_rows = load(
+        tokens[0], cotangent[0], w_query, w_key, w_value, w_out, small, rank, most
     )
     w_qkv = w_qkv.reshape(width, 3 * local)
     w_o = w_o.transpose(1, 0, 2).reshape(local, width)
-    routes_line = small[:, small.shape[1] - kinds :].reshape(nz, block, TOPK)
-    routes_seq = routes_seq.reshape(tall, TOPK)
     small = small.reshape(nz, -1)
     router = small[:, : E * deep].reshape(nz, E, deep).transpose(1, 0, 2).reshape(E, width)
     at = E * deep
@@ -898,22 +1544,12 @@
 
     own = lax.dynamic_slice_in_dim(w_experts, c * nz, nz, 2).transpose(2, 1, 0, 3)
     own, w_qkv = lax.optimization_barrier((own, w_qkv))
-    moved = exchange(own, "fsdp").transpose(1, 0, 2, 3)
-    mats = [moved[k].reshape(width, ffn) for k in range(3)]
-    others = [swap(m) for m in mats]
-    halves = [mats, others]
-
-    ids = jnp.arange(E, dtype=jnp.int32)
-    own_seq = jnp.any(routes_seq[:, :, None] == ids.astype(bf16), 1).astype(jnp.int32)
-    slot = jnp.cumsum(own_seq, 0) - own_seq
-    kept_seq = (own_seq * (slot < CAP)).astype(f32)
-    kept = lax.dynamic_slice_in_dim(kept_seq, c * block + t * rows, rows, 0)
-    line = lax.dynamic_slice_in_dim(routes_line, t * 2, 2, 0)
-    plane = (jnp.arange(nc, dtype=jnp.int32) * nz + z).astype(bf16)
-    line = jnp.any(line[..., None] == plane, 2).astype(jnp.int32)
-    rank = jnp.cumsum(line, 1) - line
-    pick = (rank[..., None] == jnp.arange(most, dtype=jnp.int32)) & (line[..., None] > 0)
-    pick = pick.transpose(0, 2, 3, 1).reshape(2, nc * most, block).astype(bf16)
+    own = exchange(own, "fsdp")
+
+    counts = jnp.sum((rank_seq >= 0).astype(f32), 2)
+    earlier = jnp.sum(jnp.where(jnp.arange(nc)[:, None] < c, counts, 0.0), 0)
+    kept = ((rank >= 0) & (rank + earlier[:, None] < CAP)).astype(f32).T
+    kept = lax.dynamic_slice_in_dim(kept, t * rows, rows, 0)
 
     x_rows = x_rows.astype(f32)
     place = jnp.arange(tall, dtype=jnp.int32)
@@ -941,78 +1577,42 @@
     attn_part = dot(context, w_o).astype(bf16).reshape(nc, 2, rows, width)
     kept_wide = jnp.pad(kept, ((0, 0), (0, 128 - E)))
     router_wide = jnp.pad(router, ((0, 128 - E), (0, 0)))
-    residual, normed_two, router_probs, x_in, g_in, cot_rows = dispatch(
-        attn_part, tokens[0], moe_gain[None], router_wide, kept_wide, pick, cot_two
-    )
-    router_probs = router_probs[:, :E]
-    own_tokens = token_half.astype(f32)
-    inv_two = rms_scale(residual)
+    residual, normed_two, router_probs, x_in, g_in = dispatch(
+        attn_part, tokens[0], moe_gain[None], router_wide, kept_wide, pick
+    )
+    own, x_in = lax.optimization_barrier((own, x_in))
+    other = swap(own)
     x_in = x_in.reshape(nc * 2 * most, width)
     cot_rows = cot_rows.reshape(nc * 2 * most, width)
     g_in = g_in.reshape(nc * 2 * most, 2, 128)[:, :, :E].astype(f32)
     mine_id = c * nz + z
     weight = jnp.sum(jnp.where(ids == mine_id, g_in, 0.0), (1, 2))[:, None]
 
-    out_rows = back_rows = 0.0
-    pair_grad = 0.0
-    updates = []
-    for w_gate, w_up, w_down in halves:
-        gate_act = dot(x_in, w_gate)
-        up_act = dot(x_in, w_up)
-        grad_out = dot(cot_rows, w_down)
-        sig = jax.nn.sigmoid(gate_act)
-        silu = gate_act * sig
-        hidden = silu * up_act
-        pair_grad = pair_grad + jnp.sum(hidden.astype(bf16).astype(f32) * grad_out, 1, keepdims=True)
-        weighted = (weight * hidden).astype(bf16)
-        grad_hidden = weight * grad_out
-        grad_gate = (grad_hidden * up_act * sig * (1.0 + gate_act * (1.0 - sig))).astype(bf16)
-        grad_up = (grad_hidden * silu).astype(bf16)
-        out_rows = out_rows + dot_nt(weighted, w_down)
-        back_rows = back_rows + dot_nt(grad_gate, w_gate) + dot_nt(grad_up, w_up)
-        updates.append((dot_tn(x_in, grad_gate), dot_tn(x_in, grad_up), dot_tn(cot_rows, weighted)))
-    own_updates, other_updates = updates
-    high, low = two_parts(jnp.where(ids == mine_id, pair_grad, 0.0))
-    tail = jnp.zeros((high.shape[0], 128 - 2 * E), bf16)
-    reply = jnp.concatenate([out_rows.astype(bf16), back_rows.astype(bf16), high, low, tail], 1)
-
-    def collect(reply):
-        reply = exchange(reply.reshape(nc, 2, most, -1), "ctx")
-        reply = reply.transpose(1, 0, 2, 3).reshape(2, nc * most, -1)
-        dense = jnp.einsum("sib,siw->sbw", pick, reply, preferred_element_type=f32).astype(bf16)
-        mine = lax.dynamic_slice_in_dim(dense, t * rows, rows, 1)
-        send = lax.dynamic_slice_in_dim(dense, (1 - t) * rows, rows, 1)
-        stacked = by_core(mine, swap(send), t).reshape(nz, rows, -1)
-        return jnp.sum(exchange(stacked, "fsdp").astype(f32), 0)
-
-    dense = collect(reply)
-    moe_rows, grad_rows = dense[:, :width], dense[:, width : 2 * width]
-    pair_rows = dense[:, 2 * width : 2 * width + E] + dense[:, 2 * width + E : 2 * width + 2 * E]
-
-    dw_experts = []
-    for mine, other in zip(own_updates, other_updates):
-        total = (mine + swap(other.astype(bf16)).astype(f32)).astype(bf16)
-        dw_experts.append(exchange(total.reshape(nz * nc, -1, ffn), ("fsdp", "ctx")))
-    dw_experts = jnp.stack(dw_experts, 1).astype(f32)
-    dw_experts = dw_experts.reshape(nz, nc, 3, -1, ffn).transpose(3, 2, 1, 0, 4)
-    dw_experts = dw_experts.reshape(-1, 3, E, ffn)
-
-    layer = (residual + moe_rows).astype(bf16)
-    piece = width // 2
-    layer_mine = lax.dynamic_slice_in_dim(layer, t * piece, piece, 1)
-    layer_send = lax.dynamic_slice_in_dim(layer, (1 - t) * piece, piece, 1)
-    layer_out = by_core(layer_mine, swap(layer_send), t).reshape(1, block, piece)
-
-    grad_router_probs = pair_rows * kept
-    grad_logits = router_probs * (
-        grad_router_probs - jnp.sum(router_probs * grad_router_probs, -1, keepdims=True)
-    )
-    grad_logits = grad_logits.astype(bf16)
-    dw_router = dot_tn(normed_two, grad_logits)
-    grad_normed_two = grad_rows + dot(grad_logits, router)
-    dgain_moe = jnp.sum(grad_normed_two * residual * inv_two, 0)
-    grad_residual = cotan_half.astype(f32) + norm_back(grad_normed_two, residual, inv_two, moe_gain)
-    grad_attn = all_rows(grad_residual.astype(bf16), t).reshape(tall, width)
+    chips = nz * nc
+    strip = width // chips
+    out_rows, back_rows, pair_grad, own_grad, other_grad = experts(x_in, cot_rows, weight, own, other, strip)
+    dw_experts = (own_grad.astype(f32) + swap(other_grad).astype(f32)).astype(bf16)
+    dw_gate = exchange(dw_experts[:, :1], ("fsdp", "ctx"))
+    high, low = two_parts(jnp.where(jnp.arange(128) == mine_id, pair_grad, 0.0))
+    shape = (nc, 2, most, -1)
+    pick_t = pick.transpose(0, 2, 1)
+    grad_logits, dgain_moe, grad_residual, grad_attn = give_back(
+        back_rows.reshape(shape),
+        jnp.concatenate([high, low], 1).reshape(shape),
+        pick_t,
+        residual,
+        router_probs,
+        kept_wide,
+        router_wide,
+        moe_gain[None],
+        cotangent[0],
+    )
+
+    dw_router = dot_tn(normed_two, grad_logits[:, :E])
+    dgain_moe = jnp.sum(dgain_moe, 0)
+    dw_rest, grad_attn = lax.optimization_barrier((dw_experts[:, 1:], grad_attn))
+    dw_rest = exchange(dw_rest, ("fsdp", "ctx"))
+    grad_attn = grad_attn.reshape(tall, width)
 
     dw_out = dot_tn(context, grad_attn).astype(bf16)
     grad_context = dot_nt(grad_attn, w_o).astype(bf16).reshape(tall, -1, HD)
@@ -1035,47 +1635,47 @@
     grad_proj = jnp.stack([grad_qproj, grad_kproj, grad_values], 1).reshape(tall, 3 * local)
     dw_qkv = dot_tn(normed_one, grad_proj).astype(bf16)
     grad_normed_part = dot_nt(grad_proj, w_qkv).astype(bf16).reshape(nc, 2, rows, width)
-    grad_normed_one = half_rows_sum(grad_normed_part, t)
-    inv_one = rms_scale(own_tokens)
-    dgain_attn = jnp.sum(grad_normed_one * own_tokens * inv_one, 0)
-    grad_tokens = grad_residual + norm_back(grad_normed_one, own_tokens, inv_one, attn_gain)
-    grad_tokens = grad_tokens.astype(bf16)
-    tokens_grad = by_core(grad_tokens, swap(grad_tokens), t).reshape(1, block, width)
-
-    chips = nz * nc
-    strip = width // chips
-    got_qkv = exchange(dw_qkv.reshape(chips, strip, 3 * local), ("fsdp", "ctx"))
-    got_qkv = jnp.sum(got_qkv.reshape(nz, nc, strip, 3, local).astype(f32), 0)
-    got_qkv = got_qkv.transpose(2, 1, 0, 3).reshape(3, strip, nc * local)
-    got_out = exchange(dw_out.reshape(local, chips, strip).transpose(1, 0, 2), ("fsdp", "ctx"))
-    got_out = jnp.sum(got_out.reshape(nz, nc, local, strip).astype(f32), 0).reshape(nc * local, strip)
-
     head_part = HD // chips
+    heads = [dgain_query.reshape(chips, 1, head_part), dgain_key.reshape(chips, 1, head_part)]
+    heads = jnp.pad(jnp.concatenate(heads, 2), ((0, 0), (0, 0), (0, strip - 2 * head_part)))
     sums = jnp.concatenate(
         [
-            dw_router.reshape(chips, strip * E),
-            dgain_attn.reshape(chips, strip),
-            dgain_moe.reshape(chips, strip),
-            dgain_query.reshape(chips, head_part),
-            dgain_key.reshape(chips, head_part),
+            dw_router.reshape(chips, E, strip),
+            dgain_moe.reshape(chips, 1, strip),
+            jnp.zeros((chips, 1, strip), f32),
+            heads,
+            jnp.zeros((chips, 24 - E - 3, strip), f32),
         ],
         1,
-    )
-    sums = jnp.sum(exchange(sums, ("fsdp", "ctx")), 0)
-    sums = sums + swap(sums)
-    base = strip * E
+    ).reshape(nz, nc, 24, strip)
+    dw_experts = jnp.concatenate([dw_gate, dw_rest], 1).reshape(nz, nc, 3, strip, ffn).transpose(3, 2, 1, 0, 4)
+    dw_experts = dw_experts.reshape(strip, 3, E, ffn).astype(f32)
+    tokens_grad, got_qkv, got_out, sums, layer_out = finish(
+        grad_normed_part,
+        tokens[0],
+        attn_gain[None],
+        grad_residual,
+        dw_qkv.reshape(nz, nc, strip, 3 * local),
+        dw_out.reshape(local, nz, nc, strip).transpose(1, 2, 0, 3),
+        sums,
+        out_rows.reshape(shape),
+        pick_t,
+        residual,
+    )
+    got_qkv = got_qkv.astype(f32).reshape(nc, strip, 3, local)
+    got_qkv = got_qkv.transpose(2, 1, 0, 3).reshape(3, strip, nc * local)
     return (
-        layer_out,
-        tokens_grad,
+        layer_out[None],
+        tokens_grad[None],
         got_qkv[0],
         got_qkv[1],
         got_qkv[2],
-        got_out,
-        sums[base : base + strip],
-        sums[base + 2 * strip : base + 2 * strip + head_part],
-        sums[base + 2 * strip + head_part :],
-        sums[base + strip : base + 2 * strip],
-        sums[:base].reshape(strip, E),
+        got_out.astype(f32).reshape(nc * local, strip),
+        sums[E + 1],
+        sums[E + 2, :head_part],
+        sums[E + 2, head_part : 2 * head_part],
+        sums[E],
+        sums[:E].reshape(strip, E),
         dw_experts,
     )
 

time: 1100 us -> 919 us (0.84)
  Pallas kernels: 315 us -> 690 us
  waiting for transfers between devices: 343 us -> 10 us
  matrix products: 163 us -> 44.7 us
  starting transfers between devices: 83.2 us -> 35.8 us
  other arithmetic: 72.6 us -> 42.2 us
  local copies, waits for them, and re-layouts: 113 us -> 84.1 us
    pallas_call x0 -> x3, Pallas kernels: none -> 405 us  [the longest x1 188 us: finish(): pl.pallas_call(functools.partial(final_kernel, nz, nc), out_shape=[jax.Sh...]
    all_to_all x11 -> x3, waiting for transfers between devices: 334 us -> 0.01 us  [exchange(): return lax.all_to_all(value, axes, split_axis=0, concat_axis=0, tiled=True)]
    dot_general x8 -> x2, matrix products: 49.7 us -> 8.97 us  [dot_nt(): lax.dot_general(left, right, (((1,), (1,)), ((), ())), preferred_element_...]
    dot_general x9 -> x3, matrix products: 52.9 us -> 12.4 us  [dot_tn(): lax.dot_general(left, right, (((0,), (0,)), ((), ())), preferred_element_...]
    all_to_all x11 -> x3, starting transfers between devices: 70.1 us -> 35.2 us  [exchange(): return lax.all_to_all(value, axes, split_axis=0, concat_axis=0, tiled=True)]
    dot_general x9 -> x3, matrix products: 40.8 us -> 7.47 us  [dot(): return jnp.dot(left, right, preferred_element_type=jnp.float32)]
    convert_element_type x4 -> x3, local copies, waits for them, and re-layouts: 1.37 us -> 32.6 us  [the longest x2 30.4 us: one_chip(): dw_experts = dw_experts.reshape(strip, 3, E, ffn).astype(f32)]
    pallas_call x1, Pallas kernels: 200 us -> 176 us  [dispatch(): pl.pallas_call(functools.partial(dispatch_kernel, nz, nc), out_shape=[jax...]
  transfers between devices with their start and end apart: 23 -> 5, of which waited for: 12 -> 1; matrix products, arithmetic and copies ran while one was open for 21% -> 11% of each run, Pallas kernels for 18% -> 56%
where the time goes in v3:
time: 919 us; the launch traced here: 909 us
  Pallas kernels  690 us (75%)
  local copies, waits for them, and re-layouts  84.1 us (9%)
  matrix products  44.7 us (5%)
  other arithmetic  42.2 us (5%)
  starting transfers between devices  35.8 us (4%)
  waiting for transfers between devices  10 us (1%)
    pallas_call x1, Pallas kernels, finish(): pl.pallas_call(functools.partial(final_kernel, nz, nc), out_shape=[jax.Sh...  188 us
    pallas_call x1, Pallas kernels, dispatch(): pl.pallas_call(functools.partial(dispatch_kernel, nz, nc), out_shape=[jax...  176 us
    pallas_call x1, Pallas kernels, give_back(): pl.pallas_call(functools.partial(return_kernel, nz, nc), out_shape=[jax.S...  143 us
    pallas_call x1, Pallas kernels, load(): pl.pallas_call(functools.partial(load_kernel, nz, nc), out_shape=[jax.Sha...  110 us
    pallas_call x1, Pallas kernels, experts(): pl.pallas_call(experts_kernel, out_shape=[jax.ShapeDtypeStruct((tall, wid...  73.7 us
    all_to_all x3, starting transfers between devices, exchange(): return lax.all_to_all(value, axes, split_axis=0, concat_axis=0, tiled=True)  35.2 us
    convert_element_type x2, local copies, waits for them, and re-layouts, one_chip(): dw_experts = dw_experts.reshape(strip, 3, E, ffn).astype(f32)  30.4 us
    unnamed x89, local copies, waits for them, and re-layouts  18.5 us
  transfers between devices with their start and end apart: 5, of which 1 were waited for; matrix products, arithmetic and copies ran while one was open for 11% of the time, Pallas kernels for 56%

profile of v3, /device:TPU:15, one launch (start us, length us, event | category | flops | bytes accessed | tf_op | source)
XLA Modules:
  0.0 908.7 jit_solution(6027044949512928387)
XLA Ops:
  0.7 10.6 %constant_dynamic-slice_fusion = bf16[512,3,4,512]{3,2,1,0:T(4,128)(2,1)} fusion(bf16[512,3,16,512]{3,2,1,0:T(8,128)(2,1)} %param.23, s32[]{:T(128)S(6)} %select_n.31), kind=kLoop, calls=%fused_computation.128 | loop fusion | bytes 12582916 | tf_op jit(solution)/shard_map/dynamic_slice | solution.py:1545
  11.3 6.9 copy.155
  18.8 1.2 copy-done.4
  20.0 1.2 copy-done.5
  21.3 109.9 %shard_map.220 = (bf16[1024,2048]{1,0:T(8,128)(2,1)}, bf16[4,512,768]{2,1,0:T(8,128)(2,1)}, bf16[4,256,512]{2,1,0:T(8,128)(2,1)S(1)}, bf16[4,80,128]{2,1,0:T(8,1...) custom-call(bf16[256,2048]{1,0:T(8,128)(2,1)S(1)} %bitcast.154, ...), custom_call_target="tpu_custom_call" | custom-call | tf_op jit(solution)/shard_map/pallas_call | solution.py:697
  132.0 13.4 %all-to-all-start = ((bf16[4,3,512,512]{3,2,1,0:T(8,128)(2,1)}), bf16[4,3,512,512]{3,2,1,0:T(8,128)(2,1)}, u32[]{:S(2)}, u32[]{:S(2)}) async-start(bf16[4,3,512,512]{3,2,1,0:T(8,128)(2,1)} %bitcast.162), calls=%async_computation | async-start | bytes 12582912 | tf_op jit(solution)/shard_map/all_to_all | solution.py:413
  149.7 1.1 broadcast_multiply_fusion.2
  150.9 3.1 fusion.2
  154.0 3.9 fusion.30
  160.1 1.3 multiply_reduce_fusion.1
  161.4 1.4 fusion.5
  162.8 2.3 fusion.18
  165.1 3.3 convolution_convert_fusion
  168.5 175.5 %shard_map.221 = (f32[128,2048]{1,0:T(8,128)}, bf16[128,2048]{1,0:T(8,128)(2,1)}, f32[128,128]{1,0:T(8,128)}, bf16[4,2,144,2048]{3,2,1,0:T(8,128)(2,1)}, bf16[4,2,144,256]{3,2,1,0:T(8,128)(2,1)}) custom-call(bf16[4,2,128,2048]{3,2,1,0:T(8,128)(2,1)} %bitcast.161, bf16[256,2048]{1,0:T(8,128)(2,1)} %bitcast.152, f32[1,2048]{1,0:T(1,128)} %bitcast.200, ...), custom_call_target="tpu_custom_call" | custom-call | tf_op jit(solution)/shard_map/pallas_call | solution.py:839
  344.1 1.8 reshape.275
  345.9 8.7 select_reduce_fusion
  354.6 1.1 broadcast_in_dim.103.weight
  355.6 73.7 %shard_map.222 = (bf16[1152,2048]{1,0:T(8,128)(2,1)}, bf16[1152,2048]{1,0:T(8,128)(2,1)}, f32[1152,1]{1,0:T(8,128)}, bf16[16,3,128,512]{3,2,1,0:T(8,128)(2,1)}, bf16[16,3,128,512]{3,2,1,0:T(8,128)(2,1)}) custom-call(bf16[1152,2048]{1,0:T(8,128)(2,1)} %bitcast.177, bf16[1152,2048]{1,0:T(8,128)(2,1)} %bitcast.176, f32[1152,1]{1,0:T(8,128)} %broadcast_in_dim.103.weight, ...), custom_call_target="tpu_custom_call" | custom-call | tf_op jit(solution)/shard_map/pallas_call | solution.py:981
  429.9 10.0 %collective-permute-done.1 = bf16[16,3,128,512]{3,2,1,0:T(8,128)(2,1)S(1)} collective-permute-done((bf16[16,3,128,512]{3,2,1,0:T(8,128)(2,1)}, bf16[16,3,128,512]{3,2,1,0:T(8,128)(2,1)S(1)}, u32[]{:S(2)}, u32[]{:S(2)}) %collective-permute-start.1) | collective-permute-done | bytes 6291488 | tf_op jit(solution)/shard_map/ppermute | solution.py:409
  439.9 8.1 add_convert_fusion
  448.0 3.2 slice.137
  451.3 6.2 all-to-all-start.1
  457.4 1.1 copy.106
  460.8 143.0 %shard_map.223 = (bf16[128,128]{1,0:T(8,128)(2,1)}, f32[8,2048]{1,0:T(8,128)}, f32[128,2048]{1,0:T(8,128)}, bf16[4,2,128,2048]{3,2,1,0:T(8,128)(2,1)}) custom-call(bf16[4,2,144,2048]{3,2,1,0:T(8,128)(2,1)} %bitcast.174, bf16[4,2,144,256]{3,2,1,0:T(8,128)(2,1)} %pad_maximum_fusion.2.g, bf16[2,256,576]{2,1,0:T(8,128)(2,1)} %bitcast.172, ...), custom_call_target="tpu_custom_call" | custom-call | tf_op jit(solution)/shard_map/pallas_call | solution.py:1192
  603.8 2.1 fusion.52
  605.9 1.5 concatenate.49
  608.3 4.6 slice.129
  612.9 15.6 %all-to-all-start.2 = ((bf16[16,2,128,512]{3,2,1,0:T(8,128)(2,1)}), bf16[16,2,128,512]{3,2,1,0:T(8,128)(2,1)}, u32[]{:S(2)}, u32[]{:S(2)}) async-start(bf16[16,2,128,512]{3,2,1,0:T(8,128)(2,1)} %slice.129), calls=%async_computation.2 | async-start | bytes 8388608 | tf_op jit(solution)/shard_map/all_to_all | solution.py:413
  628.5 3.9 convolution_convert_fusion.4
  632.5 4.7 multiply_reduce_fusion
  637.5 2.5 multiply_convert_fusion
  641.2 1.5 broadcast_multiply_fusion
  643.0 1.8 multiply_reduce_fusion.3
  645.0 4.6 convolution_convert_fusion.3
  649.6 2.3 copy.112
  651.9 2.3 copy.113
  654.3 1.3 concatenate.53.small
  655.6 2.0 fusion.24
  657.6 2.0 fusion.25
  659.6 5.3 fusion.26
  665.1 5.0 convolution_convert_fusion.1
  670.1 5.7 convolution_convert_fusion.2
  675.8 188.0 %shard_map.224 = (bf16[256,2048]{1,0:T(8,128)(2,1)}, bf16[4,128,768]{2,1,0:T(8,128)(2,1)}, bf16[4,256,128]{2,1,0:T(8,128)(2,1)}, f32[24,128]{1,0:T(8,128)}, bf16[256,1024]{1,0:T(8,128)(2,1)}) custom-call(bf16[4,2,128,2048]{3,2,1,0:T(8,128)(2,1)} %bitcast.181, bf16[256,2048]{1,0:T(8,128)(2,1)} %bitcast.153, f32[1,2048]{1,0:T(1,128)} %bitcast.203, ...), custom_call_target="tpu_custom_call" | custom-call | tf_op jit(solution)/shard_map/pallas_call | solution.py:1453
  863.9 1.4 copy.115
  871.1 3.5 pad_maximum_fusion
  874.6 1.7 convert_bitcast_fusion
  876.4 15.6 %copy.116 = f32[128,3,4,4,512]{4,3,2,1,0:T(4,128)} copy(f32[128,3,4,4,512]{4,0,1,2,3:T(8,128)S(1)} %convert_bitcast_fusion) | data formatting | bytes 25165824 | tf_op jit(solution)/shard_map/convert_element_type | solution.py:1652
  892.0 14.8 %reshape.297 = f32[128,3,16,512]{3,2,1,0:T(8,128)} reshape(f32[128,3,4,4,512]{4,3,2,1,0:T(4,128)} %copy.116) | data formatting | bytes 25165824 | tf_op jit(solution)/shard_map/convert_element_type | solution.py:1652
  (146 shorter events, 21.2 us)
Async XLA Ops:
  11.3 7.0 copy-start.29
  11.3 7.4 copy-start.27
  11.3 7.4 copy-start.30
  11.3 7.4 copy-start.31
  11.3 7.4 copy-start.32
  11.3 7.4 copy-start.33
  11.3 7.5 copy-start
  11.3 7.5 copy-start.1
  18.8 1.2 copy-start.4
  20.0 1.2 copy-start.5
  131.2 0.8 copy-start.2
  132.0 212.0 %all-to-all-start = ((bf16[4,3,512,512]{3,2,1,0:T(8,128)(2,1)}), bf16[4,3,512,512]{3,2,1,0:T(8,128)(2,1)}, u32[]{:S(2)}, u32[]{:S(2)}) async-start(bf16[4,3,512,512]{3,2,1,0:T(8,128)(2,1)} %bitcast.162), calls=%async_computation | async-start | bytes 12582912 | tf_op jit(solution)/shard_map/all_to_all | solution.py:413
  146.3 18.8 %copy-start.14 = (bf16[256,4,512]{0,2,1:T(8,128)(2,1)}, bf16[256,4,512]{0,2,1:T(8,128)(2,1)S(1)}, u32[]{:S(2)}) copy-start(bf16[256,4,512]{0,2,1:T(8,128)(2,1)S(1)} %copy.102) | copy-start | bytes 3145732
  147.0 7.0 copy-start.15
  147.0 7.0 copy-start.34
  157.9 4.9 copy-start.7
  159.3 0.8 copy-start.10
  159.3 2.1 copy-start.12
  161.4 3.7 copy-start.6
  165.1 3.3 copy-start.21
  344.0 11.6 %collective-permute-start = (bf16[4,3,512,512]{3,2,1,0:T(8,128)(2,1)}, bf16[4,3,512,512]{3,2,1,0:T(8,128)(2,1)}, u32[]{:S(2)}, u32[]{:S(2)}) collective-permute-start(bf16[4,3,512,512]{3,2,1,0:T(8,128)(2,1)} %all-to-all-done.own_hbm), channel_id=1, source_target_pairs={{0,1},{1,0},{2,3},{3,2},{4,5},{5,4},{6,7},{7,6},{8,9},{9,8},{10,11... | collective-permute-start | bytes 18874376 | tf_op jit(solution)/shard_map/ppermute | solution.py:409
  429.4 10.6 %collective-permute-start.1 = (bf16[16,3,128,512]{3,2,1,0:T(8,128)(2,1)}, bf16[16,3,128,512]{3,2,1,0:T(8,128)(2,1)S(1)}, u32[]{:S(2)}, u32[]{:S(2)}) collective-permute-start(bf16[16,3,128,512]{3,2,1,0:T(8,128)(2,1)} %get-tuple-element.58), channel_id=1, source_target_pairs={{0,1},{1,0},{2,3},{3,2},{4,5},{5,4},{6,7},{7,6},{8,9},{9,8},{10,11... | collective-permute-start | bytes 18874376 | tf_op jit(solution)/shard_map/ppermute | solution.py:409
  448.0 9.4 %copy-start.3 = (bf16[2,576,256]{2,1,0:T(8,128)(2,1)S(1)}, bf16[2,576,256]{2,1,0:T(8,128)(2,1)}, u32[]{:S(2)}) copy-start(bf16[2,576,256]{2,1,0:T(8,128)(2,1)} %copy-done.2) | copy-start | bytes 1769476
  448.0 11.1 %copy-start.23 = (f32[1152,1]{1,0:T(8,128)S(1)}, f32[1152,1]{1,0:T(8,128)}, u32[]{:S(2)}) copy-start(f32[1152,1]{1,0:T(8,128)} %get-tuple-element.60) | copy-start | bytes 13828
  451.3 161.6 %all-to-all-start.1 = ((bf16[16,1,128,512]{3,2,1,0:T(8,128)(2,1)}), bf16[16,1,128,512]{3,2,1,0:T(8,128)(2,1)S(1)}, u32[]{:S(2)}, u32[]{:S(2)}) async-start(bf16[16,1,128,512]{3,2,1,0:T(8,128)(2,1)} %slice.137), calls=%async_computation.1 | async-start | bytes 4194304 | tf_op jit(solution)/shard_map/all_to_all | solution.py:413
  458.5 145.3 %copy-start.24 = (bf16[128,2048]{1,0:T(8,128)(2,1)S(1)}, bf16[128,2048]{1,0:T(8,128)(2,1)}, u32[]{:S(2)}) copy-start(bf16[128,2048]{1,0:T(8,128)(2,1)} %get-tuple-element.66) | copy-start | bytes 1572868
  612.9 15.6 %copy-start.9 = (bf16[16,1,128,512]{3,2,1,0:T(8,128)(2,1)}, bf16[16,1,128,512]{3,2,1,0:T(8,128)(2,1)S(1)}, u32[]{:S(2)}) copy-start(bf16[16,1,128,512]{3,2,1,0:T(8,128)(2,1)S(1)} %all-to-all-done.1) | copy-start | bytes 6291460
  612.9 258.3 %all-to-all-start.2 = ((bf16[16,2,128,512]{3,2,1,0:T(8,128)(2,1)}), bf16[16,2,128,512]{3,2,1,0:T(8,128)(2,1)}, u32[]{:S(2)}, u32[]{:S(2)}) async-start(bf16[16,2,128,512]{3,2,1,0:T(8,128)(2,1)} %slice.129), calls=%async_computation.2 | async-start | bytes 8388608 | tf_op jit(solution)/shard_map/all_to_all | solution.py:413
  628.5 4.0 copy-start.8
  628.5 8.7 slice-start
  632.5 4.8 copy-start.19
  632.5 5.0 slice-start.1
  637.5 2.5 copy-start.11
  640.0 1.0 copy-start.13
  640.0 1.2 copy-start.18
  641.2 1.8 copy-start.17
  655.6 4.0 copy-start.20
  659.6 5.5 copy-start.35
  665.1 5.1 copy-start.16
  863.9 4.6 copy-start.28
  863.9 6.4 copy-start.26
  892.0 14.8 %copy-start.25 = (bf16[256,1024]{1,0:T(8,128)(2,1)S(1)}, bf16[256,1024]{1,0:T(8,128)(2,1)}, u32[]{:S(2)}) copy-start(bf16[256,1024]{1,0:T(8,128)(2,1)} %get-tuple-element.70) | copy-start | bytes 1572868
  892.0 15.6 %copy-start.22 = (bf16[256,2048]{1,0:T(8,128)(2,1)S(1)}, bf16[256,2048]{1,0:T(8,128)(2,1)}, u32[]{:S(2)}) copy-start(bf16[256,2048]{1,0:T(8,128)(2,1)} %get-tuple-element.71) | copy-start | bytes 3145732

commit v4 on v3

--- a/solution.py
+++ b/solution.py
@@ -454,7 +454,7 @@
     return lax.rem(index + step + count, count)
 
 
-def greet(nz, nc, line):
+def greet(nz, nc, line, far=False):
     z, c, t = places()
     barrier = pltpu.get_barrier_semaphore()
 
@@ -471,6 +471,11 @@
         count = jnp.where(z > 0, 1, 0) + jnp.where(z < nz - 1, 1, 0)
     for step in range(1, nc):
         tell(ctx=ring(c, step, nc))
+        if far:
+            for hop in range(1, nz):
+                tell(fsdp=ring(z, hop, nz), ctx=ring(c, step, nc))
+    if far:
+        count = count + (nz - 1) * (nc - 1)
     tell(tp=1 - t)
     pl.semaphore_wait(barrier, count + nc)
 
@@ -715,17 +720,23 @@
 
 
 def dispatch_kernel(
-    nz, nc, part, tok, gain, router, kept, pick,
-    residual, normed, probs, x_in, g_in,
+    nz, nc, part, tok, gain, router, kept, pick, third,
+    residual, normed, probs, x_in, g_in, third_got,
     sib, rs_send, rs_recv, n_line, g_line, n_two, g_two, x_send, g_send,
     sib_s, sib_r, rs_s, rs_r, line_send, line_recv, keep_sem, give_send, give_recv,
     gkeep_sem, ggive_send, ggive_recv, x_s, x_r, g_s, g_r, own_sem,
+    third_s, third_r, third_own,
 ):
     z, c, t = places()
     f32, bf16 = jnp.float32, jnp.bfloat16
     rows, width = residual.shape
     most = x_in.shape[2]
-    greet(nz, nc, False)
+    greet(nz, nc, True)
+    keep_third = pltpu.make_async_copy(third.at[z], third_got.at[z], third_own)
+    keep_third.start()
+
+    def third_copy(step, source, target):
+        return remote(third.at[target], third_got.at[source], third_s.at[step], third_r.at[step], fsdp=target)
 
     def sib_copy(q):
         return remote(part.at[q, 1 - t], sib.at[q], sib_s.at[q], sib_r.at[q], tp=1 - t)
@@ -810,6 +821,8 @@
 
     line_gather(nz, (n_line, g_line), line_send, line_recv, arrived, None, near)
     near(nz - 1)
+    for step in range(1, nz):
+        third_copy(step - 1, z, ring(z, step, nz)).start()
     line_sent(nz, (n_line, g_line), line_send, line_recv)
     for slot in range(2):
         wait_given(slot, t, rows, n_line, n_two, give_send, give_recv)
@@ -825,9 +838,14 @@
         rs_copy(step - 1, c, c).wait_send()
     for step in range(nc):
         sib_copy(step).wait_send()
-
-
-def dispatch(part, tok, gain, router, kept, pick):
+    for step in range(1, nz):
+        source = ring(z, -step, nz)
+        third_copy(step - 1, source, source).wait_recv()
+        third_copy(step - 1, source, source).wait_send()
+    keep_third.wait()
+
+
+def dispatch(part, tok, gain, router, kept, pick, third):
     nz, nc = lax.axis_size("fsdp"), lax.axis_size("ctx")
     rows, width = part.shape[2], part.shape[3]
     block = rows * 2
@@ -844,9 +862,10 @@
             jax.ShapeDtypeStruct((rows, 128), f32),
             jax.ShapeDtypeStruct((nc, 2, most, width), bf16),
             jax.ShapeDtypeStruct((nc, 2, most, 256), bf16),
+            jax.ShapeDtypeStruct(third.shape, bf16),
         ],
-        in_specs=[vmem] * 6,
-        out_specs=[vmem] * 3 + [hbm] * 2,
+        in_specs=[vmem] * 6 + [hbm],
+        out_specs=[vmem] * 3 + [hbm] * 3,
         scratch_shapes=[
             pltpu.VMEM((nc, rows, width), bf16),
             pltpu.VMEM((nc - 1, rows, width), bf16),
@@ -862,46 +881,67 @@
             dma((2,)), dma((2,)), dma((2,)), dma((2,)), dma((2,)), dma((2,)),
             dma((2, nc - 1)), dma((2, nc - 1)), dma((2, nc - 1)), dma((2, nc - 1)),
             dma((2, 2)),
+            dma((nz - 1,)), dma((nz - 1,)), dma,
         ],
         compiler_params=pltpu.CompilerParams(
             collective_id=1, has_side_effects=True, vmem_limit_bytes=56 * 2**20
         ),
-    )(part, tok, gain, router, kept, pick)
+    )(part, tok, gain, router, kept, pick, third)
 
 
 def experts_kernel(
-    x_hbm, cot_hbm, weight, own_hbm, other_hbm, y, r, pair, own_grad, other_grad,
-    x, cot, w, gate, up, out_grad, hid, gg, gu, stage, sem, stage_sem,
+    nz, nc, x_hbm, cot_hbm, gates, pair_hbm, third_hbm, y, r, pair_out, own_grad, other_grad,
+    x, cot, w, weight, pair, gate, up, out_grad, hid, gg, gu, stage,
+    sem, swap_s, swap_r, stage_sem, give_sem, got_sem,
 ):
+    z, c, t = places()
     f32, bf16 = jnp.float32, jnp.bfloat16
     width, tall = x.shape[1], x.shape[0]
-    nz, deep, ffn = w.shape[1], w.shape[3], w.shape[4]
+    deep, ffn = w.shape[3], w.shape[4]
     span = 256
+    chunk = 48
     copies = [
         pltpu.make_async_copy(cot_hbm, cot, sem.at[0]),
-        pltpu.make_async_copy(own_hbm, w.at[0], sem.at[1]),
+        pltpu.make_async_copy(pair_hbm, w.at[0, :, pl.ds(0, 2)], sem.at[1]),
         pltpu.make_async_copy(x_hbm, x, sem.at[2]),
-        pltpu.make_async_copy(other_hbm, w.at[1], sem.at[3]),
+        pltpu.make_async_copy(third_hbm, w.at[0, :, 2], sem.at[3]),
     ]
     for copy in copies:
         copy.start()
+    barrier = pltpu.get_barrier_semaphore()
+    pl.semaphore_signal(barrier, inc=1, device_id=dict(tp=1 - t), device_id_type=MESH)
+    pl.semaphore_wait(barrier, 1)
+    swaps = [
+        remote(pair_hbm, w.at[1, :, pl.ds(0, 2)], swap_s.at[0], swap_r.at[0], tp=1 - t),
+        remote(third_hbm, w.at[1, :, 2], swap_s.at[1], swap_r.at[1], tp=1 - t),
+    ]
+    for copy in swaps:
+        copy.start()
+    pair[...] = jnp.zeros_like(pair)
+    lane = lax.broadcasted_iota(jnp.int32, (chunk, 256), 1)
+    mine = c * nz + z
+
+    @pl.loop(0, tall // chunk)
+    def _(m):
+        rows = pl.ds(pl.multiple_of(m * chunk, chunk), chunk)
+        value = gates[rows, :].astype(f32)
+        value = jnp.where((lane == mine) | (lane == mine + 128), value, 0.0)
+        weight[rows, :] = jnp.sum(value, 1, keepdims=True)
+
     for copy in copies:
         copy.wait()
-    pair[...] = jnp.zeros_like(pair)
     per = ffn // span
 
-    @pl.loop(0, 2 * per)
-    def _(n):
+    def forward(n):
         half, at = n // per, pl.ds(pl.multiple_of(lax.rem(n, per) * span, span), span)
         full = pl.ds(pl.multiple_of(n * span, span), span)
 
         def times(rows, k):
             return jnp.dot(rows[...], w[half, :, k, :, at].reshape(width, span), preferred_element_type=f32)
 
-        out_grad[...] = times(cot, 2)
+        out_grad[...] = times(cot, 1)
         gate[...] = times(x, 0)
-        up[...] = times(x, 1)
-        chunk = 48
+        up[...] = times(x, 2)
 
         @pl.loop(0, tall // chunk)
         def _(m):
@@ -916,6 +956,19 @@
             gg[rows, full] = (o * u * sig * (1.0 + g * (1.0 - sig))).astype(bf16)
             gu[rows, full] = (o * silu).astype(bf16)
 
+    pl.loop(0, per)(forward)
+    for copy in swaps:
+        copy.wait_recv()
+    pl.loop(per, 2 * per)(forward)
+
+    @pl.loop(0, tall // chunk)
+    def _(m):
+        rows = pl.ds(pl.multiple_of(m * chunk, chunk), chunk)
+        value = pair[rows, :]
+        high = value.astype(bf16).astype(f32)
+        out = jnp.where(lane == mine, high, jnp.where(lane == mine + 128, value - high, 0.0))
+        pair_out[rows, :] = out.astype(bf16)
+
     per_deep = deep // span
 
     @pl.loop(0, width // span)
@@ -932,18 +985,24 @@
                 )
             return total
 
-        y[:, full] = back(hid, 2).astype(bf16)
-        r[:, full] = (back(gg, 0) + back(gu, 1)).astype(bf16)
+        y[:, full] = back(hid, 1).astype(bf16)
+        r[:, full] = (back(gg, 0) + back(gu, 2)).astype(bf16)
 
     strip = stage.shape[4]
     count = span // strip
 
-    def flush(n, half):
+    def flush(n):
         slot = lax.rem(n, 2)
-        out = (own_grad, other_grad)[half]
-        return pltpu.make_async_copy(
-            stage.at[slot, half], out.at[pl.ds(pl.multiple_of(n * count, count), count)], stage_sem.at[slot, half]
+        at = pl.ds(pl.multiple_of(n * count, count), count)
+        return (
+            pltpu.make_async_copy(stage.at[slot, 0], own_grad.at[at], stage_sem.at[slot]),
+            remote(stage.at[slot, 1], other_grad.at[at], give_sem.at[slot], got_sem, tp=1 - t),
         )
+
+    def flushed(n):
+        keep, give = flush(n)
+        keep.wait()
+        give.wait_send()
 
     @pl.loop(0, width // span)
     def _(n):
@@ -952,8 +1011,7 @@
 
         @pl.when(n >= 2)
         def _():
-            for half in range(2):
-                flush(n - 2, half).wait()
+            flushed(n - 2)
 
         for k, (rows, grads) in enumerate(((x, gg), (x, gu), (cot, hid))):
             value = lax.dot_general(
@@ -962,28 +1020,31 @@
             for half in range(2):
                 for i in range(count):
                     stage[slot, half, i, k] = value[i * strip : (i + 1) * strip, half * ffn : (half + 1) * ffn]
-        for half in range(2):
-            flush(n, half).start()
-
-    for n in (width // span - 2, width // span - 1):
-        for half in range(2):
-            flush(n, half).wait()
-
-
-def experts(x, cot, weight, own, other, strip):
+        for copy in flush(n):
+            copy.start()
+
+    flushed(width // span - 2)
+    flushed(width // span - 1)
+    remote(other_grad, other_grad, got_sem, got_sem, tp=1 - t).wait_recv()
+    for copy in swaps:
+        copy.wait_send()
+
+
+def experts(x, cot, gates, pair, third, strip):
     bf16, f32 = jnp.bfloat16, jnp.float32
+    nz, nc = lax.axis_size("fsdp"), lax.axis_size("ctx")
     tall, width = x.shape
-    ffn = own.shape[3]
+    deep, ffn = third.shape[1:]
     vmem = pl.BlockSpec(memory_space=pltpu.VMEM)
     hbm = pl.BlockSpec(memory_space=pl.ANY)
     grads = jax.ShapeDtypeStruct((width // strip, 3, strip, ffn), bf16)
     dma = pltpu.SemaphoreType.DMA
     return pl.pallas_call(
-        experts_kernel,
+        functools.partial(experts_kernel, nz, nc),
         out_shape=[
             jax.ShapeDtypeStruct((tall, width), bf16),
             jax.ShapeDtypeStruct((tall, width), bf16),
-            jax.ShapeDtypeStruct((tall, 1), f32),
+            jax.ShapeDtypeStruct((tall, 256), bf16),
             grads,
             grads,
         ],
@@ -992,7 +1053,9 @@
         scratch_shapes=[
             pltpu.VMEM((tall, width), bf16),
             pltpu.VMEM((tall, width), bf16),
-            pltpu.VMEM((2,) + own.shape, bf16),
+            pltpu.VMEM((2, nz, 3, deep, ffn), bf16),
+            pltpu.VMEM((tall, 1), f32),
+            pltpu.VMEM((tall, 1), f32),
             pltpu.VMEM((tall, 256), f32),
             pltpu.VMEM((tall, 256), f32),
             pltpu.VMEM((tall, 256), f32),
@@ -1000,11 +1063,83 @@
             pltpu.VMEM((tall, 2 * ffn), bf16),
             pltpu.VMEM((tall, 2 * ffn), bf16),
             pltpu.VMEM((2, 2, 256 // strip, 3, strip, ffn), bf16),
-            dma((4,)),
-            dma((2, 2)),
+            dma((4,)), dma((2,)), dma((2,)), dma((2,)), dma((2,)), dma,
         ],
-        compiler_params=pltpu.CompilerParams(vmem_limit_bytes=60 * 2**20),
-    )(x, cot, weight, own, other)
+        compiler_params=pltpu.CompilerParams(
+            collective_id=4, has_side_effects=True, vmem_limit_bytes=60 * 2**20
+        ),
+    )(x, cot, gates, pair, third)
+
+
+def select_kernel(nz, src, pair, third):
+    c = lax.axis_index("ctx")
+    tile = 16
+    count = src.shape[2]
+    row = lax.broadcasted_iota(jnp.int32, (nz * tile, tile * count), 0)
+    column = lax.broadcasted_iota(jnp.int32, (nz * tile, tile * count), 1)
+    hit = column == lax.rem(row, tile) * count + c * nz + row // tile
+    hit = jnp.where(hit, 1.0, 0.0).astype(jnp.bfloat16)
+    for n in range(src.shape[0] // tile):
+        at = pl.ds(n * tile, tile)
+        for k in range(3):
+            value = src[n * tile : (n + 1) * tile, k].reshape(tile * count, -1)
+            value = jnp.dot(hit, value, preferred_element_type=jnp.float32).astype(jnp.bfloat16)
+            value = value.reshape(nz, tile, -1)
+            if k == 1:
+                third[:, at, :] = value
+            else:
+                pair[:, k // 2, at, :] = value
+
+
+def select(w_experts, nz):
+    deep, kinds, count, ffn = w_experts.shape
+    band = 64
+    bf16 = jnp.bfloat16
+    return pl.pallas_call(
+        functools.partial(select_kernel, nz),
+        grid=(deep // band,),
+        out_shape=[
+            jax.ShapeDtypeStruct((nz, 2, deep, ffn), bf16),
+            jax.ShapeDtypeStruct((nz, deep, ffn), bf16),
+        ],
+        in_specs=[pl.BlockSpec((band, kinds, count, ffn), lambda i: (i, 0, 0, 0))],
+        out_specs=[
+            pl.BlockSpec((nz, 2, band, ffn), lambda i: (0, 0, i, 0)),
+            pl.BlockSpec((nz, band, ffn), lambda i: (0, i, 0)),
+        ],
+        compiler_params=pltpu.CompilerParams(vmem_limit_bytes=40 * 2**20),
+    )(w_experts)
+
+
+def place_kernel(nz, nc, gate, rest, out):
+    tile = gate.shape[2]
+    count = nz * nc
+    row = lax.broadcasted_iota(jnp.int32, (tile * count, tile * count), 0)
+    column = lax.broadcasted_iota(jnp.int32, (tile * count, tile * count), 1)
+    expert = lax.rem(row, count)
+    hit = column == (lax.rem(expert, nz) * nc + expert // nz) * tile + row // count
+    hit = jnp.where(hit, 1.0, 0.0).astype(jnp.bfloat16)
+    for k in range(3):
+        early = gate.shape[1]
+        value = (gate[:, k] if k < early else rest[:, k - early]).reshape(count * tile, -1)
+        value = jnp.dot(hit, value, preferred_element_type=jnp.float32)
+        out[:, k] = value.reshape(tile, count, -1)
+
+
+def lay_out(gate, rest, nz, nc):
+    count, _, strip, ffn = gate.shape
+    tile = 16
+    return pl.pallas_call(
+        functools.partial(place_kernel, nz, nc),
+        grid=(strip // tile,),
+        out_shape=jax.ShapeDtypeStruct((strip, 3, count, ffn), jnp.float32),
+        in_specs=[
+            pl.BlockSpec((count, src.shape[1], tile, ffn), lambda i: (0, 0, i, 0))
+            for src in (gate, rest)
+        ],
+        out_specs=pl.BlockSpec((tile, 3, count, ffn), lambda i: (i, 0, 0, 0)),
+        compiler_params=pltpu.CompilerParams(vmem_limit_bytes=40 * 2**20),
+    )(gate, rest)
 
 
 def collector(nz, nc, pick_t, items, sems):
@@ -1015,86 +1150,103 @@
     give_at = pl.ds(pl.multiple_of((1 - t) * rows, rows), rows)
     count = len(items)
 
-    def to_copy(slot, k, step, source, target):
+    def lanes(turn, k):
+        wide = items[k][2].shape[-1] // 2
+        return pl.ds(turn * wide, wide)
+
+    def to_copy(turn, k, step, source, target):
         src, got = items[k][:2]
+        at = lanes(turn, k)
         return remote(
-            src.at[target, slot], got.at[slot, source], to_s.at[k, slot, step - 1], to_r.at[k, slot, step - 1], ctx=target
+            src.at[target, :, :, at], got.at[source, :, :, at], to_s.at[k, turn, step - 1], to_r.at[k, turn, step - 1],
+            ctx=target,
         )
 
-    def own_copy(slot, k):
+    def own_copy(turn, k):
         src, got = items[k][:2]
-        return pltpu.make_async_copy(src.at[c, slot], got.at[slot, c], own_sem.at[k, slot])
-
-    def sib_copy(slot, k):
+        at = lanes(turn, k)
+        return pltpu.make_async_copy(src.at[c, :, :, at], got.at[c, :, :, at], own_sem.at[k, turn])
+
+    def sib_copy(turn, k):
         give, sib = items[k][3:5]
-        return remote(give.at[slot], sib.at[slot], sib_s.at[k, slot], sib_r.at[k, slot], tp=1 - t)
-
-    def line_copy(slot, k, half, source, target):
+        at = lanes(turn, k)
+        return remote(give.at[:, :, at], sib.at[:, :, at], sib_s.at[k, turn], sib_r.at[k, turn], tp=1 - t)
+
+    def line_copy(turn, slot, k, half, source, target):
         src = items[k][2 if half == 0 else 4]
-        return remote(src.at[slot], items[k][5].at[source], line_s.at[k, half, slot], line_r.at[k, source], fsdp=target)
-
-    def keep_copy(slot, k, half):
+        at = lanes(turn, k)
+        return remote(
+            src.at[slot, :, at], items[k][5].at[source, :, at],
+            line_s.at[k, turn, 2 * half + slot], line_r.at[k, turn, source], fsdp=target,
+        )
+
+    def keep_copy(turn, slot, k, half):
         src = items[k][2 if half == 0 else 4]
-        return pltpu.make_async_copy(src.at[slot], items[k][5].at[z], keep_sem.at[k])
+        at = lanes(turn, k)
+        return pltpu.make_async_copy(src.at[slot, :, at], items[k][5].at[z, :, at], keep_sem.at[k, turn])
 
     def goal(slot, half):
         return 2 * (t if half == 0 else 1 - t) + slot
 
-    def forward(slot, k, half):
-        target = goal(slot, half)
-        pl.when(target != z)(lambda: line_copy(slot, k, half, z, target).start())
-        pl.when(target == z)(lambda: keep_copy(slot, k, half).start())
-
-    def begin(slot):
+    def forward(turn, k, half):
+        for slot in range(2):
+            target = goal(slot, half)
+            pl.when(target != z)(lambda: line_copy(turn, slot, k, half, z, target).start())
+            pl.when(target == z)(lambda: keep_copy(turn, slot, k, half).start())
+
+    def begin(turn):
         for k in range(count):
             for step in range(1, nc):
-                to_copy(slot, k, step, c, ring(c, step, nc)).start()
-            own_copy(slot, k).start()
-
-    def scatter(slot, k):
+                to_copy(turn, k, step, c, ring(c, step, nc)).start()
+            own_copy(turn, k).start()
+
+    def scatter(turn, slot, k):
         got, mine, give = items[k][1:4]
-        lanes = mine.shape[-1]
-        span = min(lanes, 512)
-        tall = got.shape[1] * got.shape[2]
-
-        @pl.loop(0, lanes // span)
+        wide = mine.shape[-1] // 2
+        span = min(wide, 512)
+        tall = got.shape[0] * got.shape[2]
+
+        @pl.loop(0, wide // span)
         def _(n):
-            at = pl.ds(pl.multiple_of(n * span, span), span)
-            pairs = got[slot, :, :, at].reshape(tall, span)
+            at = pl.ds(pl.multiple_of(turn * wide + n * span, span), span)
+            pairs = got[:, slot, :, at].reshape(tall, span)
             for picks, out in ((mine_at, mine), (give_at, give)):
                 out[slot, :, at] = jnp.dot(
                     pick_t[slot, picks, :], pairs, preferred_element_type=jnp.float32
                 ).astype(jnp.bfloat16)
 
-    def process(slot):
+    def process(turn):
         for k in range(count):
-            own_copy(slot, k).wait()
+            own_copy(turn, k).wait()
             for step in range(1, nc):
                 source = ring(c, -step, nc)
-                to_copy(slot, k, step, source, c).wait_recv()
-            scatter(slot, k)
-            sib_copy(slot, k).start()
-            forward(slot, k, 0)
+                to_copy(turn, k, step, source, c).wait_recv()
+            for slot in range(2):
+                scatter(turn, slot, k)
+            sib_copy(turn, k).start()
+            forward(turn, k, 0)
         for k in range(count):
-            sib_copy(slot, k).wait_recv()
-            forward(slot, k, 1)
+            sib_copy(turn, k).wait_recv()
+            forward(turn, k, 1)
 
     def join():
-        for k in range(count):
-            keep_copy(0, k, 0).wait()
-            for step in range(1, nz):
-                line_copy(0, k, 0, ring(z, -step, nz), z).wait_recv()
+        for turn in range(2):
+            for k in range(count):
+                keep_copy(turn, 0, k, 0).wait()
+                for step in range(1, nz):
+                    line_copy(turn, 0, k, 0, ring(z, -step, nz), z).wait_recv()
 
     def done():
-        for slot in range(2):
+        for turn in range(2):
             for k in range(count):
                 for step in range(1, nc):
-                    to_copy(slot, k, step, c, ring(c, step, nc)).wait_send()
-                sib_copy(slot, k).wait_send()
+                    to_copy(turn, k, step, c, ring(c, step, nc)).wait_send()
+                sib_copy(turn, k).wait_send()
                 for half in range(2):
-                    pl.when(goal(slot, half) != z)(
-                        lambda: line_copy(slot, k, half, z, goal(slot, half)).wait_send()
-                    )
+                    for slot in range(2):
+                        pl.when(goal(slot, half) != z)(
+                            lambda: line_copy(turn, slot, k, half, z, goal(slot, half)).wait_send()
+                        )
 
     return begin, process, join, done
 
@@ -1105,32 +1257,44 @@
     count = len(widths)
     bufs = []
     for w in widths:
-        bufs += [pltpu.VMEM((2, nc, most, w), bf16)]
+        bufs += [pltpu.VMEM((nc, 2, most, w), bf16)]
         bufs += [pltpu.VMEM((2, rows, w), bf16)] * 3
         bufs += [pltpu.VMEM((nz, rows, w), bf16)]
     sems = [
         dma((count, 2, nc - 1)), dma((count, 2, nc - 1)), dma((count, 2)), dma((count, 2)), dma((count, 2)),
-        dma((count, 2, 2)), dma((count, nz)), dma((count,)),
+        dma((count, 2, 4)), dma((count, 2, nz)), dma((count, 2)),
     ]
     return bufs, sems
 
 
 def return_kernel(
-    nz, nc, r, g, pick_t, residual, probs, kept, router, gain, cot,
-    logits_grad, gain_grad, residual_grad, attn_grad, *scratch,
+    nz, nc, r, g, early, pick_t, residual, probs, kept, router, gain, cot,
+    logits_grad, gain_grad, residual_grad, attn_grad, early_got, *scratch,
 ):
     z, c, t = places()
     f32, bf16 = jnp.float32, jnp.bfloat16
     rows, width = residual.shape
     r_line, g_line = scratch[4], scratch[9]
-    row_s, row_r, pass_s, pass_r = scratch[18:]
+    row_s, row_r, pass_s, pass_r, early_s, early_r, early_own = scratch[18:]
     items = ((r,) + scratch[:5], (g,) + scratch[5:10])
     begin, process, join, done = collector(nz, nc, pick_t, items, scratch[10:18])
-    greet(nz, nc, True)
-    for slot in range(2):
-        begin(slot)
-    for slot in range(2):
-        process(slot)
+    here = z * nc + c
+    keep_early = pltpu.make_async_copy(early.at[here], early_got.at[here], early_own)
+    keep_early.start()
+    greet(nz, nc, True, True)
+    chips = nz * nc
+    steps = [(i, j) for i in range(nz) for j in range(nc) if i or j]
+
+    def early_copy(n, source, target, fsdp, ctx):
+        return remote(early.at[target], early_got.at[source], early_s.at[n], early_r.at[n], fsdp=fsdp, ctx=ctx)
+
+    begin(0)
+    for n, (i, j) in enumerate(steps):
+        zz, cc = ring(z, i, nz), ring(c, j, nc)
+        early_copy(n, here, zz * nc + cc, zz, cc).start()
+    begin(1)
+    for turn in range(2):
+        process(turn)
     join()
     pairs = jnp.zeros((rows, 128), f32)
     for source in range(nz):
@@ -1179,9 +1343,15 @@
         if step:
             row_copy(step, c, source).wait_send()
     done()
-
-
-def give_back(r, g, pick_t, residual, probs, kept, router, gain, cot):
+    for n, (i, j) in enumerate(steps):
+        zz, cc = ring(z, -i, nz), ring(c, -j, nc)
+        copy = early_copy(n, zz * nc + cc, zz * nc + cc, zz, cc)
+        copy.wait_recv()
+        copy.wait_send()
+    keep_early.wait()
+
+
+def give_back(r, g, early, pick_t, residual, probs, kept, router, gain, cot):
     nz, nc = lax.axis_size("fsdp"), lax.axis_size("ctx")
     rows, width = residual.shape
     dma = pltpu.SemaphoreType.DMA
@@ -1196,14 +1366,18 @@
             jax.ShapeDtypeStruct((8, width), f32),
             jax.ShapeDtypeStruct((rows, width), f32),
             jax.ShapeDtypeStruct((nc, 2, rows, width), bf16),
+            jax.ShapeDtypeStruct(early.shape, bf16),
         ],
-        in_specs=[hbm] * 2 + [vmem] * 7,
-        out_specs=[vmem] * 4,
-        scratch_shapes=bufs + sems + [dma((nc,)), dma((nc,)), dma((nc,)), dma((nc,))],
+        in_specs=[hbm] * 3 + [vmem] * 7,
+        out_specs=[vmem] * 4 + [hbm],
+        scratch_shapes=bufs
+        + sems
+        + [dma((nc,)), dma((nc,)), dma((nc,)), dma((nc,))]
+        + [dma((nz * nc - 1,)), dma((nz * nc - 1,)), dma],
         compiler_params=pltpu.CompilerParams(
             collective_id=2, has_side_effects=True, vmem_limit_bytes=56 * 2**20
         ),
-    )(r, g, pick_t, residual, probs, kept, router, gain, cot)
+    )(r, g, early, pick_t, residual, probs, kept, router, gain, cot)
 
 
 def final_kernel(
@@ -1244,25 +1418,35 @@
                 value = (value.astype(f32) + got[step, q, at, :].astype(f32)).astype(bf16)
             out[way, step, q, at, :] = value
 
+    def line_one(step, way):
+        shard = nz - 1 - step if way == 0 else step
+        ahead = z + 1 if way == 0 else z - 1
+        behind = z - 1 if way == 0 else z + 1
+        first = z == 0 if way == 0 else z == nz - 1
+        sends = shard > z if way == 0 else shard < z
+        gets = (z > 0) & (shard >= z) if way == 0 else (z < nz - 1) & (shard <= z)
+
+        @pl.when(gets)
+        def _():
+            for k in range(2):
+                hop(way, step, k, behind).wait_recv()
+
+        @pl.when(sends & jnp.logical_not(first))
+        def _():
+            for k in range(2):
+                add_to(k, way, step, shard, True)
+                hop(way, step, k, ahead).start()
+
     def line_step(step):
-        for way in range(2):
-            shard = nz - 1 - step if way == 0 else step
-            ahead = z + 1 if way == 0 else z - 1
-            behind = z - 1 if way == 0 else z + 1
-            first = z == 0 if way == 0 else z == nz - 1
-            sends = shard > z if way == 0 else shard < z
-            gets = (z > 0) & (shard >= z) if way == 0 else (z < nz - 1) & (shard <= z)
-
-            @pl.when(gets)
-            def _():
-                for k in range(2):
-                    hop(way, step, k, behind).wait_recv()
-
-            @pl.when(sends & jnp.logical_not(first))
-            def _():
-                for k in range(2):
-                    add_to(k, way, step, shard, True)
-                    hop(way, step, k, ahead).start()
+        @pl.when(2 * z < nz)
+        def _():
+            line_one(step, 0)
+            line_one(step, 1)
+
+        @pl.when(2 * z >= nz)
+        def _():
+            line_one(step, 1)
+            line_one(step, 0)
 
     def line_begin():
         for way in range(2):
@@ -1342,6 +1526,7 @@
     line_step(1)
     process(0)
     line_step(2)
+    process(1)
     for step in range(1, nz):
         small_copy(step - 1, z, z).wait_recv()
     value = small_a[z]
@@ -1382,7 +1567,6 @@
             lay_s, lay_r, tp=1 - t,
         )
 
-    process(1)
     join()
 
     @pl.loop(0, rows // chunk)
@@ -1542,9 +1726,9 @@
     query_gain = small[:, at : at + part].reshape(-1).astype(f32)
     key_gain = small[:, at + part : at + 2 * part].reshape(-1).astype(f32)
 
-    own = lax.dynamic_slice_in_dim(w_experts, c * nz, nz, 2).transpose(2, 1, 0, 3)
-    own, w_qkv = lax.optimization_barrier((own, w_qkv))
-    own = exchange(own, "fsdp")
+    w_experts, w_qkv = lax.optimization_barrier((w_experts, w_qkv))
+    pair, third = select(w_experts, nz)
+    pair = exchange(pair, "fsdp")
 
     counts = jnp.sum((rank_seq >= 0).astype(f32), 2)
     earlier = jnp.sum(jnp.where(jnp.arange(nc)[:, None] < c, counts, 0.0), 0)
@@ -1577,28 +1761,25 @@
     attn_part = dot(context, w_o).astype(bf16).reshape(nc, 2, rows, width)
     kept_wide = jnp.pad(kept, ((0, 0), (0, 128 - E)))
     router_wide = jnp.pad(router, ((0, 128 - E), (0, 0)))
-    residual, normed_two, router_probs, x_in, g_in = dispatch(
-        attn_part, tokens[0], moe_gain[None], router_wide, kept_wide, pick
-    )
-    own, x_in = lax.optimization_barrier((own, x_in))
-    other = swap(own)
+    residual, normed_two, router_probs, x_in, g_in, third = dispatch(
+        attn_part, tokens[0], moe_gain[None], router_wide, kept_wide, pick, third
+    )
+    pair, x_in = lax.optimization_barrier((pair, x_in))
     x_in = x_in.reshape(nc * 2 * most, width)
     cot_rows = cot_rows.reshape(nc * 2 * most, width)
-    g_in = g_in.reshape(nc * 2 * most, 2, 128)[:, :, :E].astype(f32)
-    mine_id = c * nz + z
-    weight = jnp.sum(jnp.where(ids == mine_id, g_in, 0.0), (1, 2))[:, None]
-
     chips = nz * nc
     strip = width // chips
-    out_rows, back_rows, pair_grad, own_grad, other_grad = experts(x_in, cot_rows, weight, own, other, strip)
-    dw_experts = (own_grad.astype(f32) + swap(other_grad).astype(f32)).astype(bf16)
-    dw_gate = exchange(dw_experts[:, :1], ("fsdp", "ctx"))
-    high, low = two_parts(jnp.where(jnp.arange(128) == mine_id, pair_grad, 0.0))
+    out_rows, back_rows, pair_rows, own_grad, other_grad = experts(
+        x_in, cot_rows, g_in.reshape(nc * 2 * most, -1), pair, third, strip
+    )
+    early = 1
+    dw_gate = (own_grad[:, :early].astype(f32) + other_grad[:, :early].astype(f32)).astype(bf16)
     shape = (nc, 2, most, -1)
     pick_t = pick.transpose(0, 2, 1)
-    grad_logits, dgain_moe, grad_residual, grad_attn = give_back(
+    grad_logits, dgain_moe, grad_residual, grad_attn, dw_gate = give_back(
         back_rows.reshape(shape),
-        jnp.concatenate([high, low], 1).reshape(shape),
+        pair_rows.reshape(shape),
+        dw_gate,
         pick_t,
         residual,
         router_probs,
@@ -1610,7 +1791,8 @@
 
     dw_router = dot_tn(normed_two, grad_logits[:, :E])
     dgain_moe = jnp.sum(dgain_moe, 0)
-    dw_rest, grad_attn = lax.optimization_barrier((dw_experts[:, 1:], grad_attn))
+    dw_rest = (own_grad[:, early:].astype(f32) + other_grad[:, early:].astype(f32)).astype(bf16)
+    dw_rest, grad_attn = lax.optimization_barrier((dw_rest, grad_attn))
     dw_rest = exchange(dw_rest, ("fsdp", "ctx"))
     grad_attn = grad_attn.reshape(tall, width)
 
@@ -1648,8 +1830,6 @@
         ],
         1,
     ).reshape(nz, nc, 24, strip)
-    dw_experts = jnp.concatenate([dw_gate, dw_rest], 1).reshape(nz, nc, 3, strip, ffn).transpose(3, 2, 1, 0, 4)
-    dw_experts = dw_experts.reshape(strip, 3, E, ffn).astype(f32)
     tokens_grad, got_qkv, got_out, sums, layer_out = finish(
         grad_normed_part,
         tokens[0],
@@ -1662,6 +1842,7 @@
         pick_t,
         residual,
     )
+    dw_experts = lay_out(dw_gate, dw_rest, nz, nc)
     got_qkv = got_qkv.astype(f32).reshape(nc, strip, 3, local)
     got_qkv = got_qkv.transpose(2, 1, 0, 3).reshape(3, strip, nc * local)
     return (

time: 919 us -> 805 us (0.88)
  local copies, waits for them, and re-layouts: 84.1 us -> 41.8 us
  Pallas kernels: 690 us -> 665 us
  starting transfers between devices: 35.8 us -> 19.5 us
  other arithmetic: 42.2 us -> 27.2 us
  waiting for transfers between devices: 10 us -> 0.01 us
    pallas_call x1, Pallas kernels: 188 us -> 150 us  [finish(): pl.pallas_call(functools.partial(final_kernel, nz, nc), out_shape=[jax.Sh...]
    pallas_call x1, Pallas kernels: 176 us -> 143 us  [dispatch(): pl.pallas_call(functools.partial(dispatch_kernel, nz, nc), out_shape=[jax...]
    convert_element_type x2 -> x0, local copies, waits for them, and re-layouts: 30.4 us -> none  [one_chip(): dw_experts = dw_experts.reshape(strip, 3, E, ffn).astype(f32)]
    pallas_call x1, Pallas kernels: 143 us -> 166 us  [give_back(): pl.pallas_call(functools.partial(return_kernel, nz, nc), out_shape=[jax.S...]
    pallas_call x1 -> x3, Pallas kernels: 73.7 us -> 96.2 us  [the longest x1 74.6 us: experts(): pl.pallas_call(functools.partial(experts_kernel, nz, nc), out_shape=[jax....]
    all_to_all x3 -> x2, starting transfers between devices: 35.2 us -> 19.5 us  [exchange(): return lax.all_to_all(value, axes, split_axis=0, concat_axis=0, tiled=True)]
    dynamic_slice x1 -> x0, local copies, waits for them, and re-layouts: 10.6 us -> none  [one_chip(): lax.dynamic_slice_in_dim(w_experts, c * nz, nz, 2).transpose(2, 1, 0, 3)]
    ppermute x2 -> x0, waiting for transfers between devices: 10 us -> none  [swap(): return lax.ppermute(value, 'tp', [(0, 1), (1, 0)])]
  transfers between devices with their start and end apart: 5 -> 2, of which waited for: 1 -> 0; matrix products, arithmetic and copies ran while one was open for 11% -> 11% of each run, Pallas kernels for 56% -> 37%
where the time goes in v4:
time: 805 us; the launch traced here: 800 us
  Pallas kernels  665 us (83%)
  matrix products  45.3 us (6%)
  local copies, waits for them, and re-layouts  41.8 us (5%)
  other arithmetic  27.2 us (3%)
  starting transfers between devices  19.5 us (2%)
    pallas_call x1, Pallas kernels, give_back(): pl.pallas_call(functools.partial(return_kernel, nz, nc), out_shape=[jax.S...  166 us
    pallas_call x1, Pallas kernels, finish(): pl.pallas_call(functools.partial(final_kernel, nz, nc), out_shape=[jax.Sh...  150 us
    pallas_call x1, Pallas kernels, dispatch(): pl.pallas_call(functools.partial(dispatch_kernel, nz, nc), out_shape=[jax...  143 us
    pallas_call x1, Pallas kernels, load(): pl.pallas_call(functools.partial(load_kernel, nz, nc), out_shape=[jax.Sha...  110 us
    pallas_call x1, Pallas kernels, experts(): pl.pallas_call(functools.partial(experts_kernel, nz, nc), out_shape=[jax....  74.6 us
    unnamed x76, local copies, waits for them, and re-layouts  21.1 us
    all_to_all x2, starting transfers between devices, exchange(): return lax.all_to_all(value, axes, split_axis=0, concat_axis=0, tiled=True)  19.5 us
  transfers between devices with their start and end apart: 2, of which 0 were waited for; matrix products, arithmetic and copies ran while one was open for 11% of the time, Pallas kernels for 37%

profile of v4, /device:TPU:15, one launch (start us, length us, event | category | flops | bytes accessed | tf_op | source)
XLA Modules:
  0.0 799.8 jit_solution(18045248700481413702)
XLA Ops:
  2.5 2.8 concatenate.34
  5.3 1.2 copy-done
  6.6 1.2 copy-done.2
  7.8 1.2 copy-done.6
  9.0 1.2 copy-done.7
  10.2 109.7 %shard_map.220 = (bf16[1024,2048]{1,0:T(8,128)(2,1)}, bf16[4,512,768]{2,1,0:T(8,128)(2,1)}, bf16[4,256,512]{2,1,0:T(8,128)(2,1)S(1)}, bf16[4,80,128]{2,1,0:T(8,1...) custom-call(bf16[256,2048]{1,0:T(8,128)(2,1)S(1)} %bitcast.147, ...), custom_call_target="tpu_custom_call" | custom-call | tf_op jit(solution)/shard_map/pallas_call | solution.py:702
  119.9 12.2 %shard_map.221 = (bf16[4,2,512,512]{3,2,1,0:T(8,128)(2,1)S(1)}, bf16[4,512,512]{2,1,0:T(8,128)(2,1)S(1)}) custom-call(bf16[512,3,16,512]{3,2,1,0:T(8,128)(2,1)} %src), custom_call_target="tpu_custom_call" | custom-call | tf_op jit(solution)/shard_map/pallas_call | solution.py:1098
  132.1 2.0 copy-done.1
  134.1 1.3 copy-done.5
  135.5 13.0 %all-to-all-start = ((bf16[4,2,512,512]{3,2,1,0:T(8,128)(2,1)}), bf16[4,2,512,512]{3,2,1,0:T(8,128)(2,1)}, u32[]{:S(2)}, u32[]{:S(2)}) async-start(bf16[4,2,512,512]{3,2,1,0:T(8,128)(2,1)} %copy-done.1), calls=%async_computation | async-start | bytes 8388608 | tf_op jit(solution)/shard_map/all_to_all | solution.py:413
  149.1 1.3 copy.93
  151.0 1.1 copy.96
  155.2 1.1 broadcast_multiply_fusion.2
  156.3 3.1 fusion.2
  159.4 3.8 fusion.30
  164.7 1.3 multiply_reduce_fusion.1
  166.0 1.4 fusion.5
  167.4 2.0 copy-done.8
  169.4 2.5 fusion.18
  172.0 3.3 convolution_convert_fusion
  175.2 142.8 %shard_map.222 = (f32[128,2048]{1,0:T(8,128)}, bf16[128,2048]{1,0:T(8,128)(2,1)}, f32[128,128]{1,0:T(8,128)}, bf16[4,2,144,2048]{3,2,1,0:T(8,128)(2,1)}, bf16[4,...) custom-call(bf16[4,2,128,2048]{3,2,1,0:T(8,128)(2,1)} %bitcast.154, bf16[256,2048]{1,0:T(8,128)(2,1)} %bitcast.145, ...), custom_call_target="tpu_custom_call" | custom-call | tf_op jit(solution)/shard_map/pallas_call | solution.py:857
  318.0 74.6 %shard_map.223 = (bf16[1152,2048]{1,0:T(8,128)(2,1)}, bf16[1152,2048]{1,0:T(8,128)(2,1)}, bf16[1152,256]{1,0:T(8,128)(2,1)}, bf16[16,3,128,512]{3,2,1,0:T(8,128)(2,1)}, bf16[16,3,128,512]{3,2,1,0:T(8,128)(2,1)}) custom-call(bf16[1152,2048]{1,0:T(8,128)(2,1)} %bitcast.168, bf16[1152,2048]{1,0:T(8,128)(2,1)} %bitcast.166, bf16[1152,256]{1,0:T(8,128)(2,1)} %bitcast.185, ...), custom_call_target="tpu_custom_call" | custom-call | tf_op jit(solution)/shard_map/pallas_call | solution.py:1042
  392.7 4.4 add_convert_fusion.1.early
  397.1 4.3 add_convert_fusion
  401.3 165.7 %shard_map.224 = (bf16[128,128]{1,0:T(8,128)(2,1)}, f32[8,2048]{1,0:T(8,128)}, f32[128,2048]{1,0:T(8,128)}, bf16[4,2,128,2048]{3,2,1,0:T(8,128)(2,1)}, bf16[16,1,128,512]{3,2,1,0:T(8,128)(2,1)}) custom-call(bf16[4,2,144,2048]{3,2,1,0:T(8,128)(2,1)} %bitcast.165, bf16[4,2,144,256]{3,2,1,0:T(8,128)(2,1)} %bitcast.186, ...), custom_call_target="tpu_custom_call" | custom-call | tf_op jit(solution)/shard_map/pallas_call | solution.py:1362
  567.0 6.5 all-to-all-start.1
  573.5 3.8 convolution_convert_fusion.4
  577.3 5.2 multiply_reduce_fusion
  583.4 2.5 multiply_convert_fusion
  587.1 1.6 broadcast_multiply_fusion
  589.7 1.8 multiply_reduce_fusion.3
  591.7 2.3 fusion.51
  594.0 1.5 concatenate.41
  595.6 4.6 convolution_convert_fusion.3
  600.2 2.3 copy.102
  602.5 2.3 copy.103
  604.8 1.3 concatenate.45.small
  606.2 2.0 fusion.24
  608.2 2.0 fusion.25
  610.2 5.3 fusion.26
  615.6 5.3 convolution_convert_fusion.1
  620.9 5.5 convolution_convert_fusion.2
  626.4 150.2 %shard_map.225 = (bf16[256,2048]{1,0:T(8,128)(2,1)}, bf16[4,128,768]{2,1,0:T(8,128)(2,1)}, bf16[4,256,128]{2,1,0:T(8,128)(2,1)}, f32[24,128]{1,0:T(8,128)}, bf16[256,1024]{1,0:T(8,128)(2,1)}) custom-call(bf16[4,2,128,2048]{3,2,1,0:T(8,128)(2,1)} %bitcast.172, bf16[256,2048]{1,0:T(8,128)(2,1)} %bitcast.146, f32[1,2048]{1,0:T(1,128)} %bitcast.196, ...), custom_call_target="tpu_custom_call" | custom-call | tf_op jit(solution)/shard_map/pallas_call | solution.py:1637
  776.6 2.6 copy.105
  779.2 2.4 fusion.57
  781.6 2.0 copy.106
  783.7 1.0 copy.107
  788.4 9.4 %shard_map.226 = f32[128,3,16,512]{3,2,1,0:T(8,128)} custom-call(bf16[16,1,128,512]{3,2,1,0:T(8,128)(2,1)S(1)} %copy-done.4, bf16[16,2,128,512]{3,2,1,0:T(8,128)(2,1)} %all-to-all-done.1.rest), custom_call_target="tpu_custom_call" | custom-call | tf_op jit(solution)/shard_map/pallas_call | solution.py:1132
  (113 shorter events, 16.5 us)
Async XLA Ops:
  5.3 1.2 copy-start
  6.6 1.2 copy-start.2
  7.8 1.2 copy-start.6
  9.0 1.2 copy-start.7
  119.9 31.1 %copy-start.3 = (bf16[2,576,256]{2,1,0:T(8,128)(2,1)}, bf16[2,576,256]{2,1,0:T(8,128)(2,1)S(1)}, u32[]{:S(2)}) copy-start(bf16[2,576,256]{2,1,0:T(8,128)(2,1)S(1)} %get-tuple-element.56.pick) | copy-start | bytes 1769476
  132.1 2.0 copy-start.1
  134.1 1.3 copy-start.5
  135.5 182.5 %all-to-all-start = ((bf16[4,2,512,512]{3,2,1,0:T(8,128)(2,1)}), bf16[4,2,512,512]{3,2,1,0:T(8,128)(2,1)}, u32[]{:S(2)}, u32[]{:S(2)}) async-start(bf16[4,2,512,512]{3,2,1,0:T(8,128)(2,1)} %copy-done.1), calls=%async_computation | async-start | bytes 8388608 | tf_op jit(solution)/shard_map/all_to_all | solution.py:413
  152.1 7.3 copy-start.15
  152.1 7.3 copy-start.28
  164.6 1.3 copy-start.9
  164.7 1.3 copy-start.12
  166.0 3.4 copy-start.8
  169.4 2.6 copy-start.14
  171.9 3.3 copy-start.21
  392.7 4.4 copy-start.11
  567.0 221.4 %all-to-all-start.1 = ((bf16[16,2,128,512]{3,2,1,0:T(8,128)(2,1)}), bf16[16,2,128,512]{3,2,1,0:T(8,128)(2,1)}, u32[]{:S(2)}, u32[]{:S(2)}) async-start(bf16[16,2,128,512]{3,2,1,0:T(8,128)(2,1)} %add_convert_fusion), calls=%async_computation.1 | async-start | bytes 8388608 | tf_op jit(solution)/shard_map/all_to_all | solution.py:413
  577.2 5.2 copy-start.19
  577.3 5.2 slice-start
  577.3 6.1 slice-start.1
  583.3 2.5 copy-start.10
  585.8 1.0 copy-start.13
  585.9 1.2 copy-start.18
  588.6 1.0 copy-start.17
  589.7 2.0 copy-start.26
  589.7 5.9 copy-start.25
  606.2 4.0 copy-start.20
  610.1 5.5 copy-start.29
  615.6 5.3 copy-start.16
  776.6 9.0 %copy-start.27 = (f32[24,128]{1,0:T(8,128)S(1)}, f32[24,128]{1,0:T(8,128)}, u32[]{:S(2)}) copy-start(f32[24,128]{1,0:T(8,128)} %get-tuple-element.81) | copy-start | bytes 36868
  776.6 10.9 %copy-start.24 = (bf16[4,256,128]{2,1,0:T(8,128)(2,1)S(1)}, bf16[4,256,128]{2,1,0:T(8,128)(2,1)}, u32[]{:S(2)}) copy-start(bf16[4,256,128]{2,1,0:T(8,128)(2,1)} %get-tuple-element.80) | copy-start | bytes 786436
  779.2 9.1 %copy-start.4 = (bf16[16,1,128,512]{3,2,1,0:T(8,128)(2,1)S(1)}, bf16[16,1,128,512]{3,2,1,0:T(8,128)(2,1)}, u32[]{:S(2)}) copy-start(bf16[16,1,128,512]{3,2,1,0:T(8,128)(2,1)} %get-tuple-element.82.gate) | copy-start | bytes 6291460
  788.4 9.4 %copy-start.23 = (bf16[256,1024]{1,0:T(8,128)(2,1)S(1)}, bf16[256,1024]{1,0:T(8,128)(2,1)}, u32[]{:S(2)}) copy-start(bf16[256,1024]{1,0:T(8,128)(2,1)} %get-tuple-element.77) | copy-start | bytes 1572868
  788.4 10.2 %copy-start.22 = (bf16[256,2048]{1,0:T(8,128)(2,1)S(1)}, bf16[256,2048]{1,0:T(8,128)(2,1)}, u32[]{:S(2)}) copy-start(bf16[256,2048]{1,0:T(8,128)(2,1)} %get-tuple-element.78) | copy-start | bytes 3145732

commit v5 on v4

--- a/solution.py
+++ b/solution.py
@@ -567,12 +567,70 @@
     pl.when(shard // 2 != t)(give)
 
 
+def selector(nz, src, pair, third, held, pair_out, third_out, in_sem, pair_sem, third_sem):
+    c = lax.axis_index("ctx")
+    tile = 16
+    count = src.shape[2]
+    height = held.shape[1]
+    bands = src.shape[0] // height
+
+    def take(b):
+        slot = lax.rem(b, 2)
+        return pltpu.make_async_copy(
+            src.at[pl.ds(pl.multiple_of(b * height, height), height)], held.at[slot], in_sem.at[slot]
+        )
+
+    def put(b):
+        slot = lax.rem(b, 2)
+        at = pl.ds(pl.multiple_of(b * height, height), height)
+        return (
+            pltpu.make_async_copy(pair_out.at[slot], pair.at[:, :, at], pair_sem.at[slot]),
+            pltpu.make_async_copy(third_out.at[slot], third.at[:, at], third_sem.at[slot]),
+        )
+
+    def pick_band(b):
+        slot = lax.rem(b, 2)
+        take(b).wait()
+        pl.when(b + 1 < bands)(lambda: take(b + 1).start())
+
+        @pl.when(b >= 2)
+        def _():
+            for copy in put(b - 2):
+                copy.wait()
+
+        row = lax.broadcasted_iota(jnp.int32, (nz * tile, tile * count), 0)
+        column = lax.broadcasted_iota(jnp.int32, (nz * tile, tile * count), 1)
+        hit = column == lax.rem(row, tile) * count + c * nz + row // tile
+        hit = jnp.where(hit, 1.0, 0.0).astype(jnp.bfloat16)
+        for n in range(height // tile):
+            at = pl.ds(n * tile, tile)
+            for k in range(3):
+                value = held[slot, n * tile : (n + 1) * tile, k].reshape(tile * count, -1)
+                value = jnp.dot(hit, value, preferred_element_type=jnp.float32).astype(jnp.bfloat16)
+                value = value.reshape(nz, tile, -1)
+                if k == 1:
+                    third_out[slot, :, at, :] = value
+                else:
+                    pair_out[slot, :, k // 2, at, :] = value
+        for copy in put(b):
+            copy.start()
+
+    def close():
+        for b in (bands - 2, bands - 1):
+            for copy in put(b):
+                copy.wait()
+
+    pick_band.close = close
+    return take, pick_band, bands
+
+
 def load_kernel(
-    nz, nc, tok, cot, wq, wk, wv, wo, small, rank,
-    x_all, w_qkv, w_o, small_all, rank_line, rank_seq, pick, cot_in,
+    nz, nc, tok, cot, wq, wk, wv, wo, small, rank, w_experts,
+    x_all, w_qkv, w_o, small_all, rank_line, rank_seq, pick, cot_in, pair, third,
     cot_line, cot_two, cot_send,
     own_sem, line_send, line_recv, w_send, w_recv, tok_send, tok_recv, pass_send, pass_recv,
     rank_send, rank_recv, keep_sem, give_send, give_recv, cot_s, cot_r, cot_own,
+    sel_in, sel_pair, sel_third, sel_s, sel_p, sel_t,
 ):
     z, c, t = places()
     block = tok.shape[0]
@@ -597,6 +655,8 @@
     ]
     for copy in own:
         copy.start()
+    take, pick_band, bands = selector(nz, w_experts, pair, third, sel_in, sel_pair, sel_third, sel_s, sel_p, sel_t)
+    take(0).start()
     greet(nz, nc, False)
 
     def band(source, core):
@@ -646,7 +706,11 @@
     def ignore(shard):
         pass
 
-    line_gather(nz, (w_qkv, w_o), w_send, w_recv, ignore, send_cotangent)
+    def select_some(step):
+        pl.loop(bands * (0, 1, 3)[step] // 4, bands * (1, 3, 4)[step] // 4)(pick_band)
+
+    line_gather(nz, (w_qkv, w_o), w_send, w_recv, ignore, send_cotangent, select_some)
+    pick_band.close()
     for step in range(1, nc):
         source = ring(c, -step, nc)
         token_copy(step - 1, source, source).wait_recv()
@@ -681,11 +745,12 @@
     remote(line.at[0], two.at[slot, other], give_recv.at[slot], give_recv.at[slot], tp=1 - t).wait_recv()
 
 
-def load(tok, cot, wq, wk, wv, wo, small, rank, most):
+def load(tok, cot, wq, wk, wv, wo, small, rank, w_experts, most):
     nz, nc = lax.axis_size("fsdp"), lax.axis_size("ctx")
     block, width = tok.shape
     deep, local = wq.shape[0], wq.shape[1] // nc
     rows = block // 2
+    count, ffn = w_experts.shape[2:]
     dma = pltpu.SemaphoreType.DMA
     bf16, f32 = jnp.bfloat16, jnp.float32
     shapes = [
@@ -697,13 +762,16 @@
         ((nc,) + rank.shape, f32),
         ((2, nc * most, block), bf16),
         ((nc, 2, most, width), bf16),
+        ((nz, 2, deep, ffn), bf16),
+        ((nz, deep, ffn), bf16),
     ]
     hbm = pl.BlockSpec(memory_space=pl.ANY)
+    height = 32
     return pl.pallas_call(
         functools.partial(load_kernel, nz, nc),
         out_shape=[jax.ShapeDtypeStruct(shape, kind) for shape, kind in shapes],
-        in_specs=[hbm] * 8,
-        out_specs=[pl.BlockSpec(memory_space=pltpu.VMEM)] * 7 + [hbm],
+        in_specs=[hbm] * 9,
+        out_specs=[pl.BlockSpec(memory_space=pltpu.VMEM)] * 7 + [hbm] * 3,
         scratch_shapes=[
             pltpu.VMEM((nz, rows, width), bf16),
             pltpu.VMEM((2, block, width), bf16),
@@ -712,11 +780,15 @@
             dma((2, nz - 1, 3)), dma((2, nz - 1, 3)), dma((2, nz - 1, 2)), dma((2, nz - 1, 2)),
             dma((nc - 1,)), dma((nc - 1,)), dma((nc - 1,)), dma((nc - 1,)), dma((nc - 1,)), dma((nc - 1,)),
             dma((2,)), dma((2,)), dma((2,)), dma((2, nc - 1)), dma((2, nc - 1)), dma((2,)),
+            pltpu.VMEM((2, height, 3, count, ffn), bf16),
+            pltpu.VMEM((2, nz, 2, height, ffn), bf16),
+            pltpu.VMEM((2, nz, height, ffn), bf16),
+            dma((2,)), dma((2,)), dma((2,)),
         ],
         compiler_params=pltpu.CompilerParams(
             collective_id=0, has_side_effects=True, vmem_limit_bytes=48 * 2**20
         ),
-    )(tok, cot, wq, wk, wv, wo, small, rank)
+    )(tok, cot, wq, wk, wv, wo, small, rank, w_experts)
 
 
 def dispatch_kernel(
@@ -890,9 +962,9 @@
 
 
 def experts_kernel(
-    nz, nc, x_hbm, cot_hbm, gates, pair_hbm, third_hbm, y, r, pair_out, own_grad, other_grad,
-    x, cot, w, weight, pair, gate, up, out_grad, hid, gg, gu, stage,
-    sem, swap_s, swap_r, stage_sem, give_sem, got_sem,
+    nz, nc, x_hbm, cot_hbm, gates, pair_hbm, third_hbm, y, r, pair_out, hid, gg, gu,
+    x, cot, w, weight, pair, gate, up, out_grad,
+    sem, swap_s, swap_r,
 ):
     z, c, t = places()
     f32, bf16 = jnp.float32, jnp.bfloat16
@@ -988,56 +1060,18 @@
         y[:, full] = back(hid, 1).astype(bf16)
         r[:, full] = (back(gg, 0) + back(gu, 2)).astype(bf16)
 
-    strip = stage.shape[4]
-    count = span // strip
-
-    def flush(n):
-        slot = lax.rem(n, 2)
-        at = pl.ds(pl.multiple_of(n * count, count), count)
-        return (
-            pltpu.make_async_copy(stage.at[slot, 0], own_grad.at[at], stage_sem.at[slot]),
-            remote(stage.at[slot, 1], other_grad.at[at], give_sem.at[slot], got_sem, tp=1 - t),
-        )
-
-    def flushed(n):
-        keep, give = flush(n)
-        keep.wait()
-        give.wait_send()
-
-    @pl.loop(0, width // span)
-    def _(n):
-        full = pl.ds(pl.multiple_of(n * span, span), span)
-        slot = lax.rem(n, 2)
-
-        @pl.when(n >= 2)
-        def _():
-            flushed(n - 2)
-
-        for k, (rows, grads) in enumerate(((x, gg), (x, gu), (cot, hid))):
-            value = lax.dot_general(
-                rows[:, full], grads[...], (((0,), (0,)), ((), ())), preferred_element_type=f32
-            ).astype(bf16)
-            for half in range(2):
-                for i in range(count):
-                    stage[slot, half, i, k] = value[i * strip : (i + 1) * strip, half * ffn : (half + 1) * ffn]
-        for copy in flush(n):
-            copy.start()
-
-    flushed(width // span - 2)
-    flushed(width // span - 1)
-    remote(other_grad, other_grad, got_sem, got_sem, tp=1 - t).wait_recv()
     for copy in swaps:
         copy.wait_send()
 
 
-def experts(x, cot, gates, pair, third, strip):
+def experts(x, cot, gates, pair, third):
     bf16, f32 = jnp.bfloat16, jnp.float32
     nz, nc = lax.axis_size("fsdp"), lax.axis_size("ctx")
     tall, width = x.shape
     deep, ffn = third.shape[1:]
     vmem = pl.BlockSpec(memory_space=pltpu.VMEM)
     hbm = pl.BlockSpec(memory_space=pl.ANY)
-    grads = jax.ShapeDtypeStruct((width // strip, 3, strip, ffn), bf16)
+    inner = jax.ShapeDtypeStruct((tall, 2 * ffn), bf16)
     dma = pltpu.SemaphoreType.DMA
     return pl.pallas_call(
         functools.partial(experts_kernel, nz, nc),
@@ -1045,11 +1079,12 @@
             jax.ShapeDtypeStruct((tall, width), bf16),
             jax.ShapeDtypeStruct((tall, width), bf16),
             jax.ShapeDtypeStruct((tall, 256), bf16),
-            grads,
-            grads,
+            inner,
+            inner,
+            inner,
         ],
         in_specs=[hbm, hbm, vmem, hbm, hbm],
-        out_specs=[vmem, vmem, vmem, hbm, hbm],
+        out_specs=[vmem] * 6,
         scratch_shapes=[
             pltpu.VMEM((tall, width), bf16),
             pltpu.VMEM((tall, width), bf16),
@@ -1059,56 +1094,12 @@
             pltpu.VMEM((tall, 256), f32),
             pltpu.VMEM((tall, 256), f32),
             pltpu.VMEM((tall, 256), f32),
-            pltpu.VMEM((tall, 2 * ffn), bf16),
-            pltpu.VMEM((tall, 2 * ffn), bf16),
-            pltpu.VMEM((tall, 2 * ffn), bf16),
-            pltpu.VMEM((2, 2, 256 // strip, 3, strip, ffn), bf16),
-            dma((4,)), dma((2,)), dma((2,)), dma((2,)), dma((2,)), dma,
+            dma((4,)), dma((2,)), dma((2,)),
         ],
         compiler_params=pltpu.CompilerParams(
             collective_id=4, has_side_effects=True, vmem_limit_bytes=60 * 2**20
         ),
     )(x, cot, gates, pair, third)
-
-
-def select_kernel(nz, src, pair, third):
-    c = lax.axis_index("ctx")
-    tile = 16
-    count = src.shape[2]
-    row = lax.broadcasted_iota(jnp.int32, (nz * tile, tile * count), 0)
-    column = lax.broadcasted_iota(jnp.int32, (nz * tile, tile * count), 1)
-    hit = column == lax.rem(row, tile) * count + c * nz + row // tile
-    hit = jnp.where(hit, 1.0, 0.0).astype(jnp.bfloat16)
-    for n in range(src.shape[0] // tile):
-        at = pl.ds(n * tile, tile)
-        for k in range(3):
-            value = src[n * tile : (n + 1) * tile, k].reshape(tile * count, -1)
-            value = jnp.dot(hit, value, preferred_element_type=jnp.float32).astype(jnp.bfloat16)
-            value = value.reshape(nz, tile, -1)
-            if k == 1:
-                third[:, at, :] = value
-            else:
-                pair[:, k // 2, at, :] = value
-
-
-def select(w_experts, nz):
-    deep, kinds, count, ffn = w_experts.shape
-    band = 64
-    bf16 = jnp.bfloat16
-    return pl.pallas_call(
-        functools.partial(select_kernel, nz),
-        grid=(deep // band,),
-        out_shape=[
-            jax.ShapeDtypeStruct((nz, 2, deep, ffn), bf16),
-            jax.ShapeDtypeStruct((nz, deep, ffn), bf16),
-        ],
-        in_specs=[pl.BlockSpec((band, kinds, count, ffn), lambda i: (i, 0, 0, 0))],
-        out_specs=[
-            pl.BlockSpec((nz, 2, band, ffn), lambda i: (0, 0, i, 0)),
-            pl.BlockSpec((nz, band, ffn), lambda i: (0, i, 0)),
-        ],
-        compiler_params=pltpu.CompilerParams(vmem_limit_bytes=40 * 2**20),
-    )(w_experts)
 
 
 def place_kernel(nz, nc, gate, rest, out):
@@ -1268,8 +1259,10 @@
 
 
 def return_kernel(
-    nz, nc, r, g, early, pick_t, residual, probs, kept, router, gain, cot,
-    logits_grad, gain_grad, residual_grad, attn_grad, early_got, *scratch,
+    nz, nc, r, g, x_hbm, cot_hbm, hid_hbm, gg_hbm, gu_hbm, pick_t, residual, probs, kept, router, gain, cot,
+    logits_grad, gain_grad, residual_grad, attn_grad, early_got, own_grad, other_grad,
+    x, cot_rows, hid, gg, gu, stage, early, early_sib,
+    load_sem, keep_sem, give_sem, got_sem, first_s, first_r, *scratch,
 ):
     z, c, t = places()
     f32, bf16 = jnp.float32, jnp.bfloat16
@@ -1280,7 +1273,14 @@
     begin, process, join, done = collector(nz, nc, pick_t, items, scratch[10:18])
     here = z * nc + c
     keep_early = pltpu.make_async_copy(early.at[here], early_got.at[here], early_own)
-    keep_early.start()
+    loads = [
+        pltpu.make_async_copy(src, dst, load_sem.at[k])
+        for k, (src, dst) in enumerate(
+            ((x_hbm, x), (gg_hbm, gg), (gu_hbm, gu), (cot_hbm, cot_rows), (hid_hbm, hid))
+        )
+    ]
+    for copy in loads:
+        copy.start()
     greet(nz, nc, True, True)
     chips = nz * nc
     steps = [(i, j) for i in range(nz) for j in range(nc) if i or j]
@@ -1289,10 +1289,62 @@
         return remote(early.at[target], early_got.at[source], early_s.at[n], early_r.at[n], fsdp=fsdp, ctx=ctx)
 
     begin(0)
+    begin(1)
+    for copy in loads:
+        copy.wait()
+
+    span = 256
+    ffn = stage.shape[5]
+    strip = stage.shape[4]
+    per = span // strip
+    bands = width // span
+
+    def flush(n):
+        slot = lax.rem(n, 2)
+        at = pl.ds(pl.multiple_of(n * per, per), per)
+        return (
+            pltpu.make_async_copy(stage.at[slot, 0, :, pl.ds(1, 2)], own_grad.at[at], keep_sem.at[slot]),
+            remote(stage.at[slot, 1, :, pl.ds(1, 2)], other_grad.at[at], give_sem.at[slot], got_sem, tp=1 - t),
+            remote(stage.at[slot, 1, :, 0], early_sib.at[at], first_s.at[slot], first_r, tp=1 - t),
+        )
+
+    def flushed(n):
+        keep, give, first = flush(n)
+        keep.wait()
+        give.wait_send()
+        first.wait_send()
+
+    @pl.loop(0, bands)
+    def _(n):
+        full = pl.ds(pl.multiple_of(n * span, span), span)
+        slot = lax.rem(n, 2)
+        pl.when(n >= 2)(lambda: flushed(n - 2))
+        for k, (rows_in, grads) in enumerate(((x, gg), (x, gu), (cot_rows, hid))):
+            value = lax.dot_general(
+                rows_in[:, full], grads[...], (((0,), (0,)), ((), ())), preferred_element_type=f32
+            ).astype(bf16)
+            for i in range(per):
+                piece = value[i * strip : (i + 1) * strip]
+                if k == 0:
+                    early[n * per + i] = piece[:, :ffn]
+                else:
+                    stage[slot, 0, i, k] = piece[:, :ffn]
+                stage[slot, 1, i, k] = piece[:, ffn:]
+        for copy in flush(n):
+            copy.start()
+
+    flushed(bands - 2)
+    flushed(bands - 1)
+    remote(early_sib, early_sib, first_r, first_r, tp=1 - t).wait_recv()
+
+    @pl.loop(0, chips)
+    def _(n):
+        early[n] = (early[n].astype(f32) + early_sib[n].astype(f32)).astype(bf16)
+
+    keep_early.start()
     for n, (i, j) in enumerate(steps):
         zz, cc = ring(z, i, nz), ring(c, j, nc)
         early_copy(n, here, zz * nc + cc, zz, cc).start()
-    begin(1)
     for turn in range(2):
         process(turn)
     join()
@@ -1349,9 +1401,10 @@
         copy.wait_recv()
         copy.wait_send()
     keep_early.wait()
-
-
-def give_back(r, g, early, pick_t, residual, probs, kept, router, gain, cot):
+    remote(other_grad, other_grad, got_sem, got_sem, tp=1 - t).wait_recv()
+
+
+def give_back(r, g, x, cot_rows, hid, gg, gu, pick_t, residual, probs, kept, router, gain, cot):
     nz, nc = lax.axis_size("fsdp"), lax.axis_size("ctx")
     rows, width = residual.shape
     dma = pltpu.SemaphoreType.DMA
@@ -1359,6 +1412,9 @@
     vmem = pl.BlockSpec(memory_space=pltpu.VMEM)
     hbm = pl.BlockSpec(memory_space=pl.ANY)
     bufs, sems = collector_scratch(nz, nc, r.shape[2], rows, (width, 256))
+    chips = nz * nc
+    strip, ffn = width // chips, hid.shape[1] // 2
+    tall = x.shape[0]
     return pl.pallas_call(
         functools.partial(return_kernel, nz, nc),
         out_shape=[
@@ -1366,18 +1422,31 @@
             jax.ShapeDtypeStruct((8, width), f32),
             jax.ShapeDtypeStruct((rows, width), f32),
             jax.ShapeDtypeStruct((nc, 2, rows, width), bf16),
-            jax.ShapeDtypeStruct(early.shape, bf16),
+            jax.ShapeDtypeStruct((chips, strip, ffn), bf16),
+            jax.ShapeDtypeStruct((chips, 2, strip, ffn), bf16),
+            jax.ShapeDtypeStruct((chips, 2, strip, ffn), bf16),
         ],
-        in_specs=[hbm] * 3 + [vmem] * 7,
-        out_specs=[vmem] * 4 + [hbm],
-        scratch_shapes=bufs
+        in_specs=[hbm] * 7 + [vmem] * 7,
+        out_specs=[vmem] * 4 + [hbm] * 3,
+        scratch_shapes=[
+            pltpu.VMEM((tall, width), bf16),
+            pltpu.VMEM((tall, width), bf16),
+            pltpu.VMEM((tall, 2 * ffn), bf16),
+            pltpu.VMEM((tall, 2 * ffn), bf16),
+            pltpu.VMEM((tall, 2 * ffn), bf16),
+            pltpu.VMEM((2, 2, 256 // strip, 3, strip, ffn), bf16),
+            pltpu.VMEM((chips, strip, ffn), bf16),
+            pltpu.VMEM((chips, strip, ffn), bf16),
+            dma((5,)), dma((2,)), dma((2,)), dma, dma((2,)), dma,
+        ]
+        + bufs
         + sems
         + [dma((nc,)), dma((nc,)), dma((nc,)), dma((nc,))]
         + [dma((nz * nc - 1,)), dma((nz * nc - 1,)), dma],
         compiler_params=pltpu.CompilerParams(
-            collective_id=2, has_side_effects=True, vmem_limit_bytes=56 * 2**20
+            collective_id=2, has_side_effects=True, vmem_limit_bytes=60 * 2**20
         ),
-    )(r, g, early, pick_t, residual, probs, kept, router, gain, cot)
+    )(r, g, x, cot_rows, hid, gg, gu, pick_t, residual, probs, kept, router, gain, cot)
 
 
 def final_kernel(
@@ -1712,8 +1781,8 @@
     named = jnp.any(routes[0][:, :, None] == ids, 1)
     below = jnp.tril(jnp.ones((block, block), bf16), -1)
     rank = jnp.where(named, dot(below, named.astype(bf16)), -1.0).T
-    x_rows, w_qkv, w_o, small, _, rank_seq, pick, cot_rows = load(
-        tokens[0], cotangent[0], w_query, w_key, w_value, w_out, small, rank, most
+    x_rows, w_qkv, w_o, small, _, rank_seq, pick, cot_rows, pair, third = load(
+        tokens[0], cotangent[0], w_query, w_key, w_value, w_out, small, rank, w_experts, most
     )
     w_qkv = w_qkv.reshape(width, 3 * local)
     w_o = w_o.transpose(1, 0, 2).reshape(local, width)
@@ -1726,8 +1795,6 @@
     query_gain = small[:, at : at + part].reshape(-1).astype(f32)
     key_gain = small[:, at + part : at + 2 * part].reshape(-1).astype(f32)
 
-    w_experts, w_qkv = lax.optimization_barrier((w_experts, w_qkv))
-    pair, third = select(w_experts, nz)
     pair = exchange(pair, "fsdp")
 
     counts = jnp.sum((rank_seq >= 0).astype(f32), 2)
@@ -1769,17 +1836,19 @@
     cot_rows = cot_rows.reshape(nc * 2 * most, width)
     chips = nz * nc
     strip = width // chips
-    out_rows, back_rows, pair_rows, own_grad, other_grad = experts(
-        x_in, cot_rows, g_in.reshape(nc * 2 * most, -1), pair, third, strip
-    )
-    early = 1
-    dw_gate = (own_grad[:, :early].astype(f32) + other_grad[:, :early].astype(f32)).astype(bf16)
+    out_rows, back_rows, pair_rows, hid, gg, gu = experts(
+        x_in, cot_rows, g_in.reshape(nc * 2 * most, -1), pair, third
+    )
     shape = (nc, 2, most, -1)
     pick_t = pick.transpose(0, 2, 1)
-    grad_logits, dgain_moe, grad_residual, grad_attn, dw_gate = give_back(
+    grad_logits, dgain_moe, grad_residual, grad_attn, dw_gate, own_grad, other_grad = give_back(
         back_rows.reshape(shape),
         pair_rows.reshape(shape),
-        dw_gate,
+        x_in,
+        cot_rows,
+        hid,
+        gg,
+        gu,
         pick_t,
         residual,
         router_probs,
@@ -1791,7 +1860,7 @@
 
     dw_router = dot_tn(normed_two, grad_logits[:, :E])
     dgain_moe = jnp.sum(dgain_moe, 0)
-    dw_rest = (own_grad[:, early:].astype(f32) + other_grad[:, early:].astype(f32)).astype(bf16)
+    dw_rest = (own_grad.astype(f32) + other_grad.astype(f32)).astype(bf16)
     dw_rest, grad_attn = lax.optimization_barrier((dw_rest, grad_attn))
     dw_rest = exchange(dw_rest, ("fsdp", "ctx"))
     grad_attn = grad_attn.reshape(tall, width)
@@ -1842,7 +1911,7 @@
         pick_t,
         residual,
     )
-    dw_experts = lay_out(dw_gate, dw_rest, nz, nc)
+    dw_experts = lay_out(dw_gate[:, None], dw_rest, nz, nc)
     got_qkv = got_qkv.astype(f32).reshape(nc, strip, 3, local)
     got_qkv = got_qkv.transpose(2, 1, 0, 3).reshape(3, strip, nc * local)
     return (

time: 805 us -> 780 us (0.969)
  Pallas kernels: 665 us -> 642 us
    pallas_call x1, Pallas kernels: 74.6 us -> 56.8 us  [experts(): pl.pallas_call(functools.partial(experts_kernel, nz, nc), out_shape=[jax....]
    pallas_call x1, Pallas kernels: 166 us -> 178 us  [give_back(): pl.pallas_call(functools.partial(return_kernel, nz, nc), out_shape=[jax.S...]
    pallas_call x1 -> x0, Pallas kernels: 12.2 us -> none  [select(): pl.pallas_call(functools.partial(select_kernel, nz), grid=(deep // band,)...]
    unnamed x76 -> x70, local copies, waits for them, and re-layouts: 21.1 us -> 17.7 us
  transfers between devices with their start and end apart: 2 -> 2, of which waited for: 0 -> 0; matrix products, arithmetic and copies ran while one was open for 11% -> 12% of each run, Pallas kernels for 37% -> 37%
where the time goes in v5:
time: 780 us; the launch traced here: 775 us
  Pallas kernels  642 us (82%)
  matrix products  45.1 us (6%)
  local copies, waits for them, and re-layouts  43.1 us (6%)
  other arithmetic  25.8 us (3%)
  starting transfers between devices  17.6 us (2%)
    pallas_call x1, Pallas kernels, give_back(): pl.pallas_call(functools.partial(return_kernel, nz, nc), out_shape=[jax.S...  178 us
    pallas_call x1, Pallas kernels, finish(): pl.pallas_call(functools.partial(final_kernel, nz, nc), out_shape=[jax.Sh...  149 us
    pallas_call x1, Pallas kernels, dispatch(): pl.pallas_call(functools.partial(dispatch_kernel, nz, nc), out_shape=[jax...  138 us
    pallas_call x1, Pallas kernels, load(): pl.pallas_call(functools.partial(load_kernel, nz, nc), out_shape=[jax.Sha...  110 us
    pallas_call x1, Pallas kernels, experts(): pl.pallas_call(functools.partial(experts_kernel, nz, nc), out_shape=[jax....  56.8 us
    unnamed x70, local copies, waits for them, and re-layouts  17.7 us
    all_to_all x2, starting transfers between devices, exchange(): return lax.all_to_all(value, axes, split_axis=0, concat_axis=0, tiled=True)  17.6 us
  transfers between devices with their start and end apart: 2, of which 0 were waited for; matrix products, arithmetic and copies ran while one was open for 12% of the time, Pallas kernels for 37%

profile of v5, /device:TPU:15, one launch (start us, length us, event | category | flops | bytes accessed | tf_op | source)
XLA Modules:
  0.0 775.3 jit_solution(3766568845157350379)
XLA Ops:
  2.5 2.8 concatenate.34
  5.3 1.2 copy-done
  6.6 1.2 copy-done.1
  7.8 1.2 copy-done.4
  9.0 1.2 copy-done.5
  10.2 109.9 %shard_map.220 = (bf16[1024,2048]{1,0:T(8,128)(2,1)}, bf16[4,512,768]{2,1,0:T(8,128)(2,1)}, bf16[4,256,512]{2,1,0:T(8,128)(2,1)S(1)}, bf16[4,80,128]{2,1,0:T(8,1...) custom-call(bf16[256,2048]{1,0:T(8,128)(2,1)S(1)} %bitcast.155, ...), custom_call_target="tpu_custom_call" | custom-call | tf_op jit(solution)/shard_map/pallas_call | solution.py:770
  120.2 13.1 %all-to-all-start = ((bf16[4,2,512,512]{3,2,1,0:T(8,128)(2,1)}), bf16[4,2,512,512]{3,2,1,0:T(8,128)(2,1)}, u32[]{:S(2)}, u32[]{:S(2)}) async-start(bf16[4,2,512,512]{3,2,1,0:T(8,128)(2,1)} %get-tuple-element.52), calls=%async_computation | async-start | bytes 8388608 | tf_op jit(solution)/shard_map/all_to_all | solution.py:413
  133.5 1.0 multiply_cosine_fusion
  134.7 4.6 copy.93
  139.5 1.3 copy.97
  141.4 1.1 copy.100
  144.6 1.2 broadcast_multiply_fusion.2
  145.8 3.1 fusion.2
  148.9 3.5 fusion.9
  153.8 1.3 multiply_reduce_fusion.1
  155.2 1.4 fusion.5
  156.6 2.0 copy-done.6
  158.6 2.5 fusion.20
  161.1 3.3 convolution_convert_fusion
  164.4 138.3 %shard_map.221 = (f32[128,2048]{1,0:T(8,128)}, bf16[128,2048]{1,0:T(8,128)(2,1)}, f32[128,128]{1,0:T(8,128)}, bf16[4,2,144,2048]{3,2,1,0:T(8,128)(2,1)}, bf16[4,...) custom-call(bf16[4,2,128,2048]{3,2,1,0:T(8,128)(2,1)} %bitcast.163, bf16[256,2048]{1,0:T(8,128)(2,1)} %bitcast.153, ...), custom_call_target="tpu_custom_call" | custom-call | tf_op jit(solution)/shard_map/pallas_call | solution.py:929
  302.8 56.8 %shard_map.222 = (bf16[1152,2048]{1,0:T(8,128)(2,1)}, bf16[1152,2048]{1,0:T(8,128)(2,1)}, bf16[1152,256]{1,0:T(8,128)(2,1)}, bf16[1152,1024]{1,0:T(8,128)(2,1)},...) custom-call(bf16[1152,2048]{1,0:T(8,128)(2,1)} %bitcast.166, bf16[1152,2048]{1,0:T(8,128)(2,1)} %bitcast.164, ...), custom_call_target="tpu_custom_call" | custom-call | tf_op jit(solution)/shard_map/pallas_call | solution.py:1076
  359.6 178.4 %shard_map.223 = (bf16[128,128]{1,0:T(8,128)(2,1)}, f32[8,2048]{1,0:T(8,128)}, f32[128,2048]{1,0:T(8,128)}, bf16[4,2,128,2048]{3,2,1,0:T(8,128)(2,1)}, bf16[16,1...) custom-call(bf16[4,2,144,2048]{3,2,1,0:T(8,128)(2,1)} %bitcast.172, ...), custom_call_target="tpu_custom_call" | custom-call | tf_op jit(solution)/shard_map/pallas_call | solution.py:1418
  538.0 7.2 add_convert_fusion
  545.1 4.6 all-to-all-start.1
  549.7 3.8 convolution_convert_fusion.4
  553.5 5.2 multiply_reduce_fusion
  559.6 2.5 multiply_convert_fusion
  563.3 1.6 broadcast_multiply_fusion
  565.9 1.8 multiply_reduce_fusion.3
  568.0 2.4 fusion.52
  570.3 1.5 concatenate.41
  571.9 4.6 convolution_convert_fusion.3
  576.5 2.3 copy.106
  578.7 2.3 copy.107
  581.1 1.3 concatenate.45.small
  582.4 2.0 fusion.26
  584.5 2.0 fusion.27
  586.4 5.3 fusion.28
  591.9 5.3 convolution_convert_fusion.1
  597.2 5.5 convolution_convert_fusion.2
  602.7 149.4 %shard_map.224 = (bf16[256,2048]{1,0:T(8,128)(2,1)}, bf16[4,128,768]{2,1,0:T(8,128)(2,1)}, bf16[4,256,128]{2,1,0:T(8,128)(2,1)}, f32[24,128]{1,0:T(8,128)}, bf16[256,1024]{1,0:T(8,128)(2,1)}) custom-call(bf16[4,2,128,2048]{3,2,1,0:T(8,128)(2,1)} %bitcast.176, bf16[256,2048]{1,0:T(8,128)(2,1)} %bitcast.154, f32[1,2048]{1,0:T(1,128)} %bitcast.203, ...), custom_call_target="tpu_custom_call" | custom-call | tf_op jit(solution)/shard_map/pallas_call | solution.py:1706
  752.1 2.6 copy.109
  754.7 2.4 fusion.58
  757.1 2.0 copy.110
  759.2 1.0 copy.111
  760.2 1.0 copy.112
  763.9 9.4 %shard_map.225 = f32[128,3,16,512]{3,2,1,0:T(8,128)} custom-call(bf16[16,1,128,512]{3,2,1,0:T(8,128)(2,1)S(1)} %bitcast.158, bf16[16,2,128,512]{3,2,1,0:T(8,128)(2,1)} %all-to-all-done.1.rest), custom_call_target="tpu_custom_call" | custom-call | tf_op jit(solution)/shard_map/pallas_call | solution.py:1123
  774.1 1.0 copy.151
  (106 shorter events, 13.6 us)
Async XLA Ops:
  5.3 1.2 copy-start
  6.6 1.2 copy-start.1
  7.8 1.2 copy-start.4
  9.0 1.2 copy-start.5
  120.2 21.2 %copy-start.2 = (bf16[2,576,256]{2,1,0:T(8,128)(2,1)}, bf16[2,576,256]{2,1,0:T(8,128)(2,1)S(1)}, u32[]{:S(2)}) copy-start(bf16[2,576,256]{2,1,0:T(8,128)(2,1)S(1)} %get-tuple-element.55.pick) | copy-start | bytes 1769476
  120.2 182.6 %all-to-all-start = ((bf16[4,2,512,512]{3,2,1,0:T(8,128)(2,1)}), bf16[4,2,512,512]{3,2,1,0:T(8,128)(2,1)}, u32[]{:S(2)}, u32[]{:S(2)}) async-start(bf16[4,2,512,512]{3,2,1,0:T(8,128)(2,1)} %get-tuple-element.52), calls=%async_computation | async-start | bytes 8388608 | tf_op jit(solution)/shard_map/all_to_all | solution.py:413
  142.5 6.4 copy-start.12
  142.5 6.4 copy-start.15
  153.8 1.3 copy-start.7
  153.8 1.3 copy-start.9
  155.2 3.4 copy-start.6
  158.6 2.6 copy-start.11
  161.1 3.3 copy-start.20
  545.1 218.7 %all-to-all-start.1 = ((bf16[16,2,128,512]{3,2,1,0:T(8,128)(2,1)}), bf16[16,2,128,512]{3,2,1,0:T(8,128)(2,1)}, u32[]{:S(2)}, u32[]{:S(2)}) async-start(bf16[16,2,128,512]{3,2,1,0:T(8,128)(2,1)} %add_convert_fusion), calls=%async_computation.1 | async-start | bytes 8388608 | tf_op jit(solution)/shard_map/all_to_all | solution.py:413
  553.5 5.2 copy-start.18
  553.5 5.2 slice-start
  553.5 6.1 slice-start.1
  559.6 2.5 copy-start.8
  562.1 1.0 copy-start.10
  562.1 1.2 copy-start.17
  564.9 1.0 copy-start.16
  565.9 2.0 copy-start.25
  565.9 5.9 copy-start.24
  582.4 4.0 copy-start.19
  586.4 5.5 copy-start.14
  591.9 5.3 copy-start.13
  752.1 9.0 %copy-start.26 = (f32[24,128]{1,0:T(8,128)S(1)}, f32[24,128]{1,0:T(8,128)}, u32[]{:S(2)}) copy-start(f32[24,128]{1,0:T(8,128)} %get-tuple-element.83) | copy-start | bytes 36868
  752.1 10.9 %copy-start.23 = (bf16[4,256,128]{2,1,0:T(8,128)(2,1)S(1)}, bf16[4,256,128]{2,1,0:T(8,128)(2,1)}, u32[]{:S(2)}) copy-start(bf16[4,256,128]{2,1,0:T(8,128)(2,1)} %get-tuple-element.82) | copy-start | bytes 786436
  754.7 9.1 %copy-start.3 = (bf16[16,128,512]{2,1,0:T(8,128)(2,1)S(1)}, bf16[16,128,512]{2,1,0:T(8,128)(2,1)}, u32[]{:S(2)}) copy-start(bf16[16,128,512]{2,1,0:T(8,128)(2,1)} %get-tuple-element.84) | copy-start | bytes 6291460
  763.9 9.4 %copy-start.22 = (bf16[256,1024]{1,0:T(8,128)(2,1)S(1)}, bf16[256,1024]{1,0:T(8,128)(2,1)}, u32[]{:S(2)}) copy-start(bf16[256,1024]{1,0:T(8,128)(2,1)} %get-tuple-element.79) | copy-start | bytes 1572868
  763.9 10.2 %copy-start.21 = (bf16[256,2048]{1,0:T(8,128)(2,1)S(1)}, bf16[256,2048]{1,0:T(8,128)(2,1)}, u32[]{:S(2)}) copy-start(bf16[256,2048]{1,0:T(8,128)(2,1)} %get-tuple-element.80) | copy-start | bytes 3145732

commit v6 on v5

--- a/solution.py
+++ b/solution.py
@@ -962,16 +962,16 @@
 
 
 def experts_kernel(
-    nz, nc, x_hbm, cot_hbm, gates, pair_hbm, third_hbm, y, r, pair_out, hid, gg, gu,
-    x, cot, w, weight, pair, gate, up, out_grad,
-    sem, swap_s, swap_r,
+    nz, nc, x_hbm, cot_hbm, gates, pair_hbm, third_hbm, y_hbm, r_hbm, pair_out, hid_hbm, gg_hbm, gu_hbm,
+    x, cot, w, weight, pair, gate, up, out_grad, y, r, hid, gg, gu,
+    sem, swap_s, swap_r, out_sem, inner_sem,
 ):
     z, c, t = places()
     f32, bf16 = jnp.float32, jnp.bfloat16
     width, tall = x.shape[1], x.shape[0]
     deep, ffn = w.shape[3], w.shape[4]
     span = 256
-    chunk = 48
+    chunk = 288
     copies = [
         pltpu.make_async_copy(cot_hbm, cot, sem.at[0]),
         pltpu.make_async_copy(pair_hbm, w.at[0, :, pl.ds(0, 2)], sem.at[1]),
@@ -1000,7 +1000,7 @@
         value = jnp.where((lane == mine) | (lane == mine + 128), value, 0.0)
         weight[rows, :] = jnp.sum(value, 1, keepdims=True)
 
-    for copy in copies:
+    for copy in copies[:2]:
         copy.wait()
     per = ffn // span
 
@@ -1012,6 +1012,12 @@
             return jnp.dot(rows[...], w[half, :, k, :, at].reshape(width, span), preferred_element_type=f32)
 
         out_grad[...] = times(cot, 1)
+
+        @pl.when(n == 0)
+        def _():
+            for copy in copies[2:]:
+                copy.wait()
+
         gate[...] = times(x, 0)
         up[...] = times(x, 2)
 
@@ -1041,7 +1047,20 @@
         out = jnp.where(lane == mine, high, jnp.where(lane == mine + 128, value - high, 0.0))
         pair_out[rows, :] = out.astype(bf16)
 
+    inner = [
+        pltpu.make_async_copy(src, dst, inner_sem.at[k])
+        for k, (src, dst) in enumerate(((hid, hid_hbm), (gg, gg_hbm), (gu, gu_hbm)))
+    ]
+    for copy in inner:
+        copy.start()
     per_deep = deep // span
+
+    def leave(n):
+        full = pl.ds(pl.multiple_of(n * span, span), span)
+        return (
+            pltpu.make_async_copy(y.at[:, full], y_hbm.at[:, full], out_sem.at[0, n]),
+            pltpu.make_async_copy(r.at[:, full], r_hbm.at[:, full], out_sem.at[1, n]),
+        )
 
     @pl.loop(0, width // span)
     def _(n):
@@ -1059,7 +1078,14 @@
 
         y[:, full] = back(hid, 1).astype(bf16)
         r[:, full] = (back(gg, 0) + back(gu, 2)).astype(bf16)
-
+        for copy in leave(n):
+            copy.start()
+
+    for n in range(width // span):
+        for copy in leave(n):
+            copy.wait()
+    for copy in inner:
+        copy.wait()
     for copy in swaps:
         copy.wait_send()
 
@@ -1084,7 +1110,7 @@
             inner,
         ],
         in_specs=[hbm, hbm, vmem, hbm, hbm],
-        out_specs=[vmem] * 6,
+        out_specs=[hbm, hbm, vmem, hbm, hbm, hbm],
         scratch_shapes=[
             pltpu.VMEM((tall, width), bf16),
             pltpu.VMEM((tall, width), bf16),
@@ -1094,7 +1120,12 @@
             pltpu.VMEM((tall, 256), f32),
             pltpu.VMEM((tall, 256), f32),
             pltpu.VMEM((tall, 256), f32),
-            dma((4,)), dma((2,)), dma((2,)),
+            pltpu.VMEM((tall, width), bf16),
+            pltpu.VMEM((tall, width), bf16),
+            pltpu.VMEM((tall, 2 * ffn), bf16),
+            pltpu.VMEM((tall, 2 * ffn), bf16),
+            pltpu.VMEM((tall, 2 * ffn), bf16),
+            dma((4,)), dma((2,)), dma((2,)), dma((2, width // 256)), dma((3,)),
         ],
         compiler_params=pltpu.CompilerParams(
             collective_id=4, has_side_effects=True, vmem_limit_bytes=60 * 2**20
@@ -1341,10 +1372,6 @@
     def _(n):
         early[n] = (early[n].astype(f32) + early_sib[n].astype(f32)).astype(bf16)
 
-    keep_early.start()
-    for n, (i, j) in enumerate(steps):
-        zz, cc = ring(z, i, nz), ring(c, j, nc)
-        early_copy(n, here, zz * nc + cc, zz, cc).start()
     for turn in range(2):
         process(turn)
     join()
@@ -1384,6 +1411,10 @@
     for step in range(1, nc):
         row_copy(step, c, ring(c, step, nc)).start()
     pass_copy(0, c, t).start()
+    keep_early.start()
+    for n, (i, j) in enumerate(steps):
+        zz, cc = ring(z, i, nz), ring(c, j, nc)
+        early_copy(n, here, zz * nc + cc, zz, cc).start()
     for step in range(1, nc):
         source = ring(c, -step, nc)
         row_copy(step, source, source).wait_recv()

time: 780 us -> 753 us (0.965)
  Pallas kernels: 642 us -> 603 us
  matrix products: 45.1 us -> 55.7 us
    pallas_call x1, Pallas kernels: 178 us -> 162 us  [give_back(): pl.pallas_call(functools.partial(return_kernel, nz, nc), out_shape=[jax.S...]
    pallas_call x1, Pallas kernels: 56.8 us -> 45 us  [experts(): pl.pallas_call(functools.partial(experts_kernel, nz, nc), out_shape=[jax....]
    pallas_call x1, Pallas kernels: 138 us -> 128 us  [dispatch(): pl.pallas_call(functools.partial(dispatch_kernel, nz, nc), out_shape=[jax...]
    dot_general x1, matrix products: 2.54 us -> 13.2 us  [one_chip(): jnp.einsum('hqk,khd->qhd', attn_probs.astype(bf16), values, preferred_ele...]
  transfers between devices with their start and end apart: 2 -> 2, of which waited for: 0 -> 0; matrix products, arithmetic and copies ran while one was open for 12% -> 14% of each run, Pallas kernels for 37% -> 37%
where the time goes in v6:
time: 753 us; the launch traced here: 748 us
  Pallas kernels  603 us (80%)
  matrix products  55.7 us (7%)
  local copies, waits for them, and re-layouts  43.1 us (6%)
  other arithmetic  25.8 us (3%)
  starting transfers between devices  19.6 us (3%)
    pallas_call x1, Pallas kernels, give_back(): pl.pallas_call(functools.partial(return_kernel, nz, nc), out_shape=[jax.S...  162 us
    pallas_call x1, Pallas kernels, finish(): pl.pallas_call(functools.partial(final_kernel, nz, nc), out_shape=[jax.Sh...  148 us
    pallas_call x1, Pallas kernels, dispatch(): pl.pallas_call(functools.partial(dispatch_kernel, nz, nc), out_shape=[jax...  128 us
    pallas_call x1, Pallas kernels, load(): pl.pallas_call(functools.partial(load_kernel, nz, nc), out_shape=[jax.Sha...  110 us
    pallas_call x1, Pallas kernels, experts(): pl.pallas_call(functools.partial(experts_kernel, nz, nc), out_shape=[jax....  45 us
    all_to_all x2, starting transfers between devices, exchange(): return lax.all_to_all(value, axes, split_axis=0, concat_axis=0, tiled=True)  19.6 us
    unnamed x70, local copies, waits for them, and re-layouts  17.7 us
  transfers between devices with their start and end apart: 2, of which 0 were waited for; matrix products, arithmetic and copies ran while one was open for 14% of the time, Pallas kernels for 37%

profile of v6, /device:TPU:15, one launch (start us, length us, event | category | flops | bytes accessed | tf_op | source)
XLA Modules:
  0.0 748.3 jit_solution(12863890351360077130)
XLA Ops:
  2.5 2.8 concatenate.34
  5.3 1.2 copy-done
  6.6 1.2 copy-done.1
  7.8 1.2 copy-done.4
  9.0 1.2 copy-done.5
  10.2 109.9 %shard_map.220 = (bf16[1024,2048]{1,0:T(8,128)(2,1)}, bf16[4,512,768]{2,1,0:T(8,128)(2,1)}, bf16[4,256,512]{2,1,0:T(8,128)(2,1)S(1)}, bf16[4,80,128]{2,1,0:T(8,1...) custom-call(bf16[256,2048]{1,0:T(8,128)(2,1)S(1)} %bitcast.155, ...), custom_call_target="tpu_custom_call" | custom-call | tf_op jit(solution)/shard_map/pallas_call | solution.py:770
  120.2 13.2 %all-to-all-start = ((bf16[4,2,512,512]{3,2,1,0:T(8,128)(2,1)}), bf16[4,2,512,512]{3,2,1,0:T(8,128)(2,1)}, u32[]{:S(2)}, u32[]{:S(2)}) async-start(bf16[4,2,512,512]{3,2,1,0:T(8,128)(2,1)} %get-tuple-element.52), calls=%async_computation | async-start | bytes 8388608 | tf_op jit(solution)/shard_map/all_to_all | solution.py:413
  133.6 1.0 multiply_cosine_fusion
  134.8 4.6 copy.93
  139.6 1.3 copy.97
  141.6 1.1 copy.100
  144.7 1.2 broadcast_multiply_fusion.2
  146.0 3.1 fusion.2
  149.1 3.5 fusion.9
  154.0 1.3 multiply_reduce_fusion.1
  155.3 1.4 fusion.5
  156.7 2.0 copy-done.6
  158.7 13.2 %fusion.20 = bf16[2,128,1024]{2,1,0:T(8,128)(2,1)S(1)} fusion(f32[2,1024,1024]{1,2,0:T(8,128)S(1)} %get-tuple-element.177, f32[2,1024]{1,0:T(2,128)S(1)} %fusion.5, f32[2,1024]{1,0:T(2,128)S(1)} %get-tuple-element.176, f32[1024,3,2,128]{0,3,2,1:T(8,128)S(1)} %fusion.9), kind=kOutput, calls=%fused_computation.35 | convolution fusion | flops 545521664 | bytes 9453568 | tf_op jit(solution)/shard_map/hqk,khd->qhd/dot_general | solution.py:1857
  171.9 3.3 convolution_convert_fusion
  175.2 127.7 %shard_map.221 = (f32[128,2048]{1,0:T(8,128)}, bf16[128,2048]{1,0:T(8,128)(2,1)}, f32[128,128]{1,0:T(8,128)}, bf16[4,2,144,2048]{3,2,1,0:T(8,128)(2,1)}, bf16[4,...) custom-call(bf16[4,2,128,2048]{3,2,1,0:T(8,128)(2,1)} %bitcast.163, bf16[256,2048]{1,0:T(8,128)(2,1)} %bitcast.153, ...), custom_call_target="tpu_custom_call" | custom-call | tf_op jit(solution)/shard_map/pallas_call | solution.py:929
  303.0 45.0 %shard_map.222 = (bf16[1152,2048]{1,0:T(8,128)(2,1)}, bf16[1152,2048]{1,0:T(8,128)(2,1)}, bf16[1152,256]{1,0:T(8,128)(2,1)}, bf16[1152,1024]{1,0:T(8,128)(2,1)},...) custom-call(bf16[1152,2048]{1,0:T(8,128)(2,1)} %bitcast.166, bf16[1152,2048]{1,0:T(8,128)(2,1)} %bitcast.164, ...), custom_call_target="tpu_custom_call" | custom-call | tf_op jit(solution)/shard_map/pallas_call | solution.py:1102
  348.0 162.5 %shard_map.223 = (bf16[128,128]{1,0:T(8,128)(2,1)}, f32[8,2048]{1,0:T(8,128)}, f32[128,2048]{1,0:T(8,128)}, bf16[4,2,128,2048]{3,2,1,0:T(8,128)(2,1)}, bf16[16,1...) custom-call(bf16[4,2,144,2048]{3,2,1,0:T(8,128)(2,1)} %bitcast.172, ...), custom_call_target="tpu_custom_call" | custom-call | tf_op jit(solution)/shard_map/pallas_call | solution.py:1449
  510.5 7.2 add_convert_fusion
  517.6 6.4 all-to-all-start.1
  524.0 3.8 convolution_convert_fusion.4
  527.8 5.2 multiply_reduce_fusion
  533.9 2.5 multiply_convert_fusion
  537.6 1.6 broadcast_multiply_fusion
  540.3 1.8 multiply_reduce_fusion.3
  542.3 2.4 fusion.52
  544.6 1.5 concatenate.41
  546.2 4.6 convolution_convert_fusion.3
  550.8 2.3 copy.106
  553.1 2.3 copy.107
  555.4 1.3 concatenate.45.small
  556.8 2.0 fusion.26
  558.8 2.0 fusion.27
  560.8 5.3 fusion.28
  566.2 5.2 convolution_convert_fusion.1
  571.4 5.5 convolution_convert_fusion.2
  577.0 148.2 %shard_map.224 = (bf16[256,2048]{1,0:T(8,128)(2,1)}, bf16[4,128,768]{2,1,0:T(8,128)(2,1)}, bf16[4,256,128]{2,1,0:T(8,128)(2,1)}, f32[24,128]{1,0:T(8,128)}, bf16[256,1024]{1,0:T(8,128)(2,1)}) custom-call(bf16[4,2,128,2048]{3,2,1,0:T(8,128)(2,1)} %bitcast.176, bf16[256,2048]{1,0:T(8,128)(2,1)} %bitcast.154, f32[1,2048]{1,0:T(1,128)} %bitcast.203, ...), custom_call_target="tpu_custom_call" | custom-call | tf_op jit(solution)/shard_map/pallas_call | solution.py:1737
  725.2 2.6 copy.109
  727.8 2.4 fusion.58
  730.2 2.0 copy.110
  732.2 1.0 copy.111
  733.2 1.0 copy.112
  736.9 9.4 %shard_map.225 = f32[128,3,16,512]{3,2,1,0:T(8,128)} custom-call(bf16[16,1,128,512]{3,2,1,0:T(8,128)(2,1)S(1)} %bitcast.158, bf16[16,2,128,512]{3,2,1,0:T(8,128)(2,1)} %all-to-all-done.1.rest), custom_call_target="tpu_custom_call" | custom-call | tf_op jit(solution)/shard_map/pallas_call | solution.py:1154
  747.1 1.0 copy.151
  (106 shorter events, 13.6 us)
Async XLA Ops:
  5.3 1.2 copy-start
  6.6 1.2 copy-start.1
  7.8 1.2 copy-start.4
  9.0 1.2 copy-start.5
  120.2 21.4 %copy-start.2 = (bf16[2,576,256]{2,1,0:T(8,128)(2,1)}, bf16[2,576,256]{2,1,0:T(8,128)(2,1)S(1)}, u32[]{:S(2)}) copy-start(bf16[2,576,256]{2,1,0:T(8,128)(2,1)S(1)} %get-tuple-element.55.pick) | copy-start | bytes 1769476
  120.2 182.8 %all-to-all-start = ((bf16[4,2,512,512]{3,2,1,0:T(8,128)(2,1)}), bf16[4,2,512,512]{3,2,1,0:T(8,128)(2,1)}, u32[]{:S(2)}, u32[]{:S(2)}) async-start(bf16[4,2,512,512]{3,2,1,0:T(8,128)(2,1)} %get-tuple-element.52), calls=%async_computation | async-start | bytes 8388608 | tf_op jit(solution)/shard_map/all_to_all | solution.py:413
  142.7 6.4 copy-start.12
  142.7 6.4 copy-start.15
  154.0 1.3 copy-start.7
  154.0 1.3 copy-start.9
  155.3 3.4 copy-start.6
  158.7 13.2 %copy-start.11 = (bf16[256,4,512]{0,2,1:T(8,128)(2,1)S(1)}, bf16[256,4,512]{0,2,1:T(8,128)(2,1)}, u32[]{:S(2)}) copy-start(bf16[256,4,512]{0,2,1:T(8,128)(2,1)} %copy.97) | copy-start | bytes 3145732
  171.9 3.3 copy-start.20
  517.6 219.3 %all-to-all-start.1 = ((bf16[16,2,128,512]{3,2,1,0:T(8,128)(2,1)}), bf16[16,2,128,512]{3,2,1,0:T(8,128)(2,1)}, u32[]{:S(2)}, u32[]{:S(2)}) async-start(bf16[16,2,128,512]{3,2,1,0:T(8,128)(2,1)} %add_convert_fusion), calls=%async_computation.1 | async-start | bytes 8388608 | tf_op jit(solution)/shard_map/all_to_all | solution.py:413
  527.8 5.2 copy-start.18
  527.8 5.2 slice-start
  527.8 6.1 slice-start.1
  533.9 2.5 copy-start.8
  536.4 1.0 copy-start.10
  536.4 1.2 copy-start.17
  539.2 1.0 copy-start.16
  540.3 2.0 copy-start.25
  540.3 5.9 copy-start.24
  556.8 4.0 copy-start.19
  560.8 5.5 copy-start.14
  566.2 5.2 copy-start.13
  725.2 9.0 %copy-start.26 = (f32[24,128]{1,0:T(8,128)S(1)}, f32[24,128]{1,0:T(8,128)}, u32[]{:S(2)}) copy-start(f32[24,128]{1,0:T(8,128)} %get-tuple-element.83) | copy-start | bytes 36868
  725.2 10.9 %copy-start.23 = (bf16[4,256,128]{2,1,0:T(8,128)(2,1)S(1)}, bf16[4,256,128]{2,1,0:T(8,128)(2,1)}, u32[]{:S(2)}) copy-start(bf16[4,256,128]{2,1,0:T(8,128)(2,1)} %get-tuple-element.82) | copy-start | bytes 786436
  727.8 9.1 %copy-start.3 = (bf16[16,128,512]{2,1,0:T(8,128)(2,1)S(1)}, bf16[16,128,512]{2,1,0:T(8,128)(2,1)}, u32[]{:S(2)}) copy-start(bf16[16,128,512]{2,1,0:T(8,128)(2,1)} %get-tuple-element.84) | copy-start | bytes 6291460
  736.9 9.4 %copy-start.22 = (bf16[256,1024]{1,0:T(8,128)(2,1)S(1)}, bf16[256,1024]{1,0:T(8,128)(2,1)}, u32[]{:S(2)}) copy-start(bf16[256,1024]{1,0:T(8,128)(2,1)} %get-tuple-element.79) | copy-start | bytes 1572868
  736.9 10.2 %copy-start.21 = (bf16[256,2048]{1,0:T(8,128)(2,1)S(1)}, bf16[256,2048]{1,0:T(8,128)(2,1)}, u32[]{:S(2)}) copy-start(bf16[256,2048]{1,0:T(8,128)(2,1)} %get-tuple-element.80) | copy-start | bytes 3145732

commit v7 on v6

--- a/solution.py
+++ b/solution.py
@@ -626,11 +626,11 @@
 
 def load_kernel(
     nz, nc, tok, cot, wq, wk, wv, wo, small, rank, w_experts,
-    x_all, w_qkv, w_o, small_all, rank_line, rank_seq, pick, cot_in, pair, third,
+    x_all, w_qkv, w_o, small_all, rank_line, rank_seq, pick, cot_in, pair, third, middle,
     cot_line, cot_two, cot_send,
     own_sem, line_send, line_recv, w_send, w_recv, tok_send, tok_recv, pass_send, pass_recv,
     rank_send, rank_recv, keep_sem, give_send, give_recv, cot_s, cot_r, cot_own,
-    sel_in, sel_pair, sel_third, sel_s, sel_p, sel_t,
+    sel_in, sel_pair, sel_third, sel_s, sel_p, sel_t, mid_s, mid_r,
 ):
     z, c, t = places()
     block = tok.shape[0]
@@ -706,11 +706,17 @@
     def ignore(shard):
         pass
 
+    partner = nz - 1 - z
+    centre = (z == nz // 2 - 1) | (z == nz // 2)
+    middle_copy = remote(third.at[partner], middle, mid_s, mid_r, fsdp=partner)
+
     def select_some(step):
         pl.loop(bands * (0, 1, 3)[step] // 4, bands * (1, 3, 4)[step] // 4)(pick_band)
+        if step == 2:
+            pick_band.close()
+            pl.when(centre)(lambda: middle_copy.start())
 
     line_gather(nz, (w_qkv, w_o), w_send, w_recv, ignore, send_cotangent, select_some)
-    pick_band.close()
     for step in range(1, nc):
         source = ring(c, -step, nc)
         token_copy(step - 1, source, source).wait_recv()
@@ -732,6 +738,11 @@
         own_copy(slot).wait()
         wait_given(slot, t, rows, cot_line, cot_two, give_send, give_recv)
 
+    @pl.when(centre)
+    def _():
+        middle_copy.wait_recv()
+        middle_copy.wait_send()
+
 
 def wait_given(slot, t, rows, line, two, give_send, give_recv):
     band = pl.ds(pl.multiple_of(t * rows, rows), rows)
@@ -764,6 +775,7 @@
         ((nc, 2, most, width), bf16),
         ((nz, 2, deep, ffn), bf16),
         ((nz, deep, ffn), bf16),
+        ((deep, ffn), bf16),
     ]
     hbm = pl.BlockSpec(memory_space=pl.ANY)
     height = 32
@@ -771,7 +783,7 @@
         functools.partial(load_kernel, nz, nc),
         out_shape=[jax.ShapeDtypeStruct(shape, kind) for shape, kind in shapes],
         in_specs=[hbm] * 9,
-        out_specs=[pl.BlockSpec(memory_space=pltpu.VMEM)] * 7 + [hbm] * 3,
+        out_specs=[pl.BlockSpec(memory_space=pltpu.VMEM)] * 7 + [hbm] * 4,
         scratch_shapes=[
             pltpu.VMEM((nz, rows, width), bf16),
             pltpu.VMEM((2, block, width), bf16),
@@ -783,7 +795,7 @@
             pltpu.VMEM((2, height, 3, count, ffn), bf16),
             pltpu.VMEM((2, nz, 2, height, ffn), bf16),
             pltpu.VMEM((2, nz, height, ffn), bf16),
-            dma((2,)), dma((2,)), dma((2,)),
+            dma((2,)), dma((2,)), dma((2,)), dma, dma,
         ],
         compiler_params=pltpu.CompilerParams(
             collective_id=0, has_side_effects=True, vmem_limit_bytes=48 * 2**20
@@ -792,12 +804,12 @@
 
 
 def dispatch_kernel(
-    nz, nc, part, tok, gain, router, kept, pick, third,
+    nz, nc, part, tok, gain, router, kept, pick, third, middle,
     residual, normed, probs, x_in, g_in, third_got,
     sib, rs_send, rs_recv, n_line, g_line, n_two, g_two, x_send, g_send,
     sib_s, sib_r, rs_s, rs_r, line_send, line_recv, keep_sem, give_send, give_recv,
     gkeep_sem, ggive_send, ggive_recv, x_s, x_r, g_s, g_r, own_sem,
-    third_s, third_r, third_own,
+    third_s, third_r, third_own, mid_own,
 ):
     z, c, t = places()
     f32, bf16 = jnp.float32, jnp.bfloat16
@@ -806,6 +818,13 @@
     greet(nz, nc, True)
     keep_third = pltpu.make_async_copy(third.at[z], third_got.at[z], third_own)
     keep_third.start()
+    partner = nz - 1 - z
+    centre = (z == nz // 2 - 1) | (z == nz // 2)
+    keep_middle = pltpu.make_async_copy(middle, third_got.at[partner], mid_own)
+    pl.when(centre)(lambda: keep_middle.start())
+
+    def still(other):
+        return jnp.logical_not(centre & (other == partner))
 
     def third_copy(step, source, target):
         return remote(third.at[target], third_got.at[source], third_s.at[step], third_r.at[step], fsdp=target)
@@ -894,7 +913,7 @@
     line_gather(nz, (n_line, g_line), line_send, line_recv, arrived, None, near)
     near(nz - 1)
     for step in range(1, nz):
-        third_copy(step - 1, z, ring(z, step, nz)).start()
+        pl.when(still(ring(z, step, nz)))(lambda: third_copy(step - 1, z, ring(z, step, nz)).start())
     line_sent(nz, (n_line, g_line), line_send, line_recv)
     for slot in range(2):
         wait_given(slot, t, rows, n_line, n_two, give_send, give_recv)
@@ -912,12 +931,13 @@
         sib_copy(step).wait_send()
     for step in range(1, nz):
         source = ring(z, -step, nz)
-        third_copy(step - 1, source, source).wait_recv()
-        third_copy(step - 1, source, source).wait_send()
+        pl.when(still(source))(lambda: third_copy(step - 1, source, source).wait_recv())
+        pl.when(still(ring(z, step, nz)))(lambda: third_copy(step - 1, source, source).wait_send())
     keep_third.wait()
-
-
-def dispatch(part, tok, gain, router, kept, pick, third):
+    pl.when(centre)(lambda: keep_middle.wait())
+
+
+def dispatch(part, tok, gain, router, kept, pick, third, middle):
     nz, nc = lax.axis_size("fsdp"), lax.axis_size("ctx")
     rows, width = part.shape[2], part.shape[3]
     block = rows * 2
@@ -936,7 +956,7 @@
             jax.ShapeDtypeStruct((nc, 2, most, 256), bf16),
             jax.ShapeDtypeStruct(third.shape, bf16),
         ],
-        in_specs=[vmem] * 6 + [hbm],
+        in_specs=[vmem] * 6 + [hbm] * 2,
         out_specs=[vmem] * 3 + [hbm] * 3,
         scratch_shapes=[
             pltpu.VMEM((nc, rows, width), bf16),
@@ -953,12 +973,12 @@
             dma((2,)), dma((2,)), dma((2,)), dma((2,)), dma((2,)), dma((2,)),
             dma((2, nc - 1)), dma((2, nc - 1)), dma((2, nc - 1)), dma((2, nc - 1)),
             dma((2, 2)),
-            dma((nz - 1,)), dma((nz - 1,)), dma,
+            dma((nz - 1,)), dma((nz - 1,)), dma, dma,
         ],
         compiler_params=pltpu.CompilerParams(
             collective_id=1, has_side_effects=True, vmem_limit_bytes=56 * 2**20
         ),
-    )(part, tok, gain, router, kept, pick, third)
+    )(part, tok, gain, router, kept, pick, third, middle)
 
 
 def experts_kernel(
@@ -1134,7 +1154,7 @@
 
 
 def place_kernel(nz, nc, gate, rest, out):
-    tile = gate.shape[2]
+    tile = rest.shape[1]
     count = nz * nc
     row = lax.broadcasted_iota(jnp.int32, (tile * count, tile * count), 0)
     column = lax.broadcasted_iota(jnp.int32, (tile * count, tile * count), 1)
@@ -1142,22 +1162,21 @@
     hit = column == (lax.rem(expert, nz) * nc + expert // nz) * tile + row // count
     hit = jnp.where(hit, 1.0, 0.0).astype(jnp.bfloat16)
     for k in range(3):
-        early = gate.shape[1]
-        value = (gate[:, k] if k < early else rest[:, k - early]).reshape(count * tile, -1)
+        value = (gate[k] if k < 2 else rest[...]).reshape(count * tile, -1)
         value = jnp.dot(hit, value, preferred_element_type=jnp.float32)
         out[:, k] = value.reshape(tile, count, -1)
 
 
 def lay_out(gate, rest, nz, nc):
-    count, _, strip, ffn = gate.shape
+    count, strip, ffn = rest.shape
     tile = 16
     return pl.pallas_call(
         functools.partial(place_kernel, nz, nc),
         grid=(strip // tile,),
         out_shape=jax.ShapeDtypeStruct((strip, 3, count, ffn), jnp.float32),
         in_specs=[
-            pl.BlockSpec((count, src.shape[1], tile, ffn), lambda i: (0, 0, i, 0))
-            for src in (gate, rest)
+            pl.BlockSpec((2, count, tile, ffn), lambda i: (0, 0, i, 0)),
+            pl.BlockSpec((count, tile, ffn), lambda i: (0, i, 0)),
         ],
         out_specs=pl.BlockSpec((tile, 3, count, ffn), lambda i: (i, 0, 0, 0)),
         compiler_params=pltpu.CompilerParams(vmem_limit_bytes=40 * 2**20),
@@ -1293,7 +1312,7 @@
     nz, nc, r, g, x_hbm, cot_hbm, hid_hbm, gg_hbm, gu_hbm, pick_t, residual, probs, kept, router, gain, cot,
     logits_grad, gain_grad, residual_grad, attn_grad, early_got, own_grad, other_grad,
     x, cot_rows, hid, gg, gu, stage, early, early_sib,
-    load_sem, keep_sem, give_sem, got_sem, first_s, first_r, *scratch,
+    load_sem, keep_sem, give_sem, got_sem, *scratch,
 ):
     z, c, t = places()
     f32, bf16 = jnp.float32, jnp.bfloat16
@@ -1303,7 +1322,9 @@
     items = ((r,) + scratch[:5], (g,) + scratch[5:10])
     begin, process, join, done = collector(nz, nc, pick_t, items, scratch[10:18])
     here = z * nc + c
-    keep_early = pltpu.make_async_copy(early.at[here], early_got.at[here], early_own)
+    def keep_early(kind):
+        return pltpu.make_async_copy(early.at[kind, here], early_got.at[kind, here], early_own.at[kind])
+
     loads = [
         pltpu.make_async_copy(src, dst, load_sem.at[k])
         for k, (src, dst) in enumerate(
@@ -1316,62 +1337,79 @@
     chips = nz * nc
     steps = [(i, j) for i in range(nz) for j in range(nc) if i or j]
 
-    def early_copy(n, source, target, fsdp, ctx):
-        return remote(early.at[target], early_got.at[source], early_s.at[n], early_r.at[n], fsdp=fsdp, ctx=ctx)
+    def early_copy(kind, n, source, target, fsdp, ctx):
+        return remote(
+            early.at[kind, target], early_got.at[kind, source], early_s.at[kind, n], early_r.at[kind, n],
+            fsdp=fsdp, ctx=ctx,
+        )
+
+    def send_early(kind):
+        keep_early(kind).start()
+        for n, (i, j) in enumerate(steps):
+            zz, cc = ring(z, i, nz), ring(c, j, nc)
+            early_copy(kind, n, here, zz * nc + cc, zz, cc).start()
 
     begin(0)
     begin(1)
-    for copy in loads:
-        copy.wait()
 
     span = 256
-    ffn = stage.shape[5]
-    strip = stage.shape[4]
+    strip, ffn = stage.shape[3], stage.shape[4]
     per = span // strip
     bands = width // span
 
-    def flush(n):
-        slot = lax.rem(n, 2)
-        at = pl.ds(pl.multiple_of(n * per, per), per)
-        return (
-            pltpu.make_async_copy(stage.at[slot, 0, :, pl.ds(1, 2)], own_grad.at[at], keep_sem.at[slot]),
-            remote(stage.at[slot, 1, :, pl.ds(1, 2)], other_grad.at[at], give_sem.at[slot], got_sem, tp=1 - t),
-            remote(stage.at[slot, 1, :, 0], early_sib.at[at], first_s.at[slot], first_r, tp=1 - t),
-        )
-
-    def flushed(n):
-        keep, give, first = flush(n)
-        keep.wait()
-        give.wait_send()
-        first.wait_send()
-
-    @pl.loop(0, bands)
-    def _(n):
-        full = pl.ds(pl.multiple_of(n * span, span), span)
-        slot = lax.rem(n, 2)
-        pl.when(n >= 2)(lambda: flushed(n - 2))
-        for k, (rows_in, grads) in enumerate(((x, gg), (x, gu), (cot_rows, hid))):
+    def gradients(kind, rows_in, grads):
+        last = kind == 2
+
+        def flush(n):
+            slot = lax.rem(n, 2)
+            at = pl.ds(pl.multiple_of(n * per, per), per)
+            target = other_grad.at[at] if last else early_sib.at[kind, at]
+            give = remote(stage.at[slot, 1], target, give_sem.at[slot], got_sem.at[kind], tp=1 - t)
+            if not last:
+                return (give,)
+            return (give, pltpu.make_async_copy(stage.at[slot, 0], own_grad.at[at], keep_sem.at[slot]))
+
+        def flushed(n):
+            copies = flush(n)
+            copies[0].wait_send()
+            for copy in copies[1:]:
+                copy.wait()
+
+        @pl.loop(0, bands)
+        def _(n):
+            full = pl.ds(pl.multiple_of(n * span, span), span)
+            slot = lax.rem(n, 2)
+            pl.when(n >= 2)(lambda: flushed(n - 2))
             value = lax.dot_general(
                 rows_in[:, full], grads[...], (((0,), (0,)), ((), ())), preferred_element_type=f32
             ).astype(bf16)
             for i in range(per):
                 piece = value[i * strip : (i + 1) * strip]
-                if k == 0:
-                    early[n * per + i] = piece[:, :ffn]
+                if last:
+                    stage[slot, 0, i] = piece[:, :ffn]
                 else:
-                    stage[slot, 0, i, k] = piece[:, :ffn]
-                stage[slot, 1, i, k] = piece[:, ffn:]
-        for copy in flush(n):
-            copy.start()
-
-    flushed(bands - 2)
-    flushed(bands - 1)
-    remote(early_sib, early_sib, first_r, first_r, tp=1 - t).wait_recv()
-
-    @pl.loop(0, chips)
-    def _(n):
-        early[n] = (early[n].astype(f32) + early_sib[n].astype(f32)).astype(bf16)
-
+                    early[kind, n * per + i] = piece[:, :ffn]
+                stage[slot, 1, i] = piece[:, ffn:]
+            for copy in flush(n):
+                copy.start()
+
+        flushed(bands - 2)
+        flushed(bands - 1)
+        if not last:
+            remote(early_sib.at[kind], early_sib.at[kind], got_sem.at[kind], got_sem.at[kind], tp=1 - t).wait_recv()
+
+            @pl.loop(0, chips)
+            def _(n):
+                early[kind, n] = (early[kind, n].astype(f32) + early_sib[kind, n].astype(f32)).astype(bf16)
+
+    loads[0].wait()
+    loads[1].wait()
+    gradients(0, x, gg)
+    send_early(0)
+    for copy in loads[2:]:
+        copy.wait()
+    gradients(1, x, gu)
+    gradients(2, cot_rows, hid)
     for turn in range(2):
         process(turn)
     join()
@@ -1411,10 +1449,7 @@
     for step in range(1, nc):
         row_copy(step, c, ring(c, step, nc)).start()
     pass_copy(0, c, t).start()
-    keep_early.start()
-    for n, (i, j) in enumerate(steps):
-        zz, cc = ring(z, i, nz), ring(c, j, nc)
-        early_copy(n, here, zz * nc + cc, zz, cc).start()
+    send_early(1)
     for step in range(1, nc):
         source = ring(c, -step, nc)
         row_copy(step, source, source).wait_recv()
@@ -1426,13 +1461,14 @@
         if step:
             row_copy(step, c, source).wait_send()
     done()
-    for n, (i, j) in enumerate(steps):
-        zz, cc = ring(z, -i, nz), ring(c, -j, nc)
-        copy = early_copy(n, zz * nc + cc, zz * nc + cc, zz, cc)
-        copy.wait_recv()
-        copy.wait_send()
-    keep_early.wait()
-    remote(other_grad, other_grad, got_sem, got_sem, tp=1 - t).wait_recv()
+    for kind in range(2):
+        for n, (i, j) in enumerate(steps):
+            zz, cc = ring(z, -i, nz), ring(c, -j, nc)
+            copy = early_copy(kind, n, zz * nc + cc, zz * nc + cc, zz, cc)
+            copy.wait_recv()
+            copy.wait_send()
+        keep_early(kind).wait()
+    remote(other_grad, other_grad, got_sem.at[2], got_sem.at[2], tp=1 - t).wait_recv()
 
 
 def give_back(r, g, x, cot_rows, hid, gg, gu, pick_t, residual, probs, kept, router, gain, cot):
@@ -1453,9 +1489,9 @@
             jax.ShapeDtypeStruct((8, width), f32),
             jax.ShapeDtypeStruct((rows, width), f32),
             jax.ShapeDtypeStruct((nc, 2, rows, width), bf16),
+            jax.ShapeDtypeStruct((2, chips, strip, ffn), bf16),
             jax.ShapeDtypeStruct((chips, strip, ffn), bf16),
-            jax.ShapeDtypeStruct((chips, 2, strip, ffn), bf16),
-            jax.ShapeDtypeStruct((chips, 2, strip, ffn), bf16),
+            jax.ShapeDtypeStruct((chips, strip, ffn), bf16),
         ],
         in_specs=[hbm] * 7 + [vmem] * 7,
         out_specs=[vmem] * 4 + [hbm] * 3,
@@ -1465,15 +1501,15 @@
             pltpu.VMEM((tall, 2 * ffn), bf16),
             pltpu.VMEM((tall, 2 * ffn), bf16),
             pltpu.VMEM((tall, 2 * ffn), bf16),
-            pltpu.VMEM((2, 2, 256 // strip, 3, strip, ffn), bf16),
-            pltpu.VMEM((chips, strip, ffn), bf16),
-            pltpu.VMEM((chips, strip, ffn), bf16),
-            dma((5,)), dma((2,)), dma((2,)), dma, dma((2,)), dma,
+            pltpu.VMEM((2, 2, 256 // strip, strip, ffn), bf16),
+            pltpu.VMEM((2, chips, strip, ffn), bf16),
+            pltpu.VMEM((2, chips, strip, ffn), bf16),
+            dma((5,)), dma((2,)), dma((2,)), dma((3,)),
         ]
         + bufs
         + sems
         + [dma((nc,)), dma((nc,)), dma((nc,)), dma((nc,))]
-        + [dma((nz * nc - 1,)), dma((nz * nc - 1,)), dma],
+        + [dma((2, nz * nc - 1)), dma((2, nz * nc - 1)), dma((2,))],
         compiler_params=pltpu.CompilerParams(
             collective_id=2, has_side_effects=True, vmem_limit_bytes=60 * 2**20
         ),
@@ -1776,6 +1812,196 @@
     )(part, tok, gain, residual_grad, dw, dwo, small, y, pick_t, residual)
 
 
+def attention_kernel(
+    scale, x, gain, w_qkv, tables, gains, w_o,
+    normed, proj, queries, keys, values, context, part,
+):
+    f32, bf16 = jnp.float32, jnp.bfloat16
+    tall, local = queries.shape
+    width = x.shape[1]
+    heads = local // HD
+    small, chunk, span = 32, 256, 256
+
+    @pl.loop(0, tall // small)
+    def _(n):
+        rows = pl.ds(pl.multiple_of(n * small, small), small)
+        value = x[rows, :].astype(f32)
+        inv = lax.rsqrt(jnp.mean(value * value, -1, keepdims=True) + EPS)
+        normed[rows, :] = (value * inv * gain[...]).astype(bf16)
+
+    @pl.loop(0, 3 * local // span)
+    def _(n):
+        at = pl.ds(pl.multiple_of(n * span, span), span)
+        proj[:, at] = jnp.dot(normed[...], w_qkv[:, at], preferred_element_type=f32)
+
+    @pl.loop(0, tall // chunk)
+    def _(n):
+        rows = pl.ds(pl.multiple_of(n * chunk, chunk), chunk)
+        cos, sin = tables[rows, pl.ds(0, HD)], tables[rows, pl.ds(HD, HD)]
+        for head in range(heads):
+            at = pl.ds(head * HD, HD)
+            for kind, out in enumerate((queries, keys)):
+                value = proj[rows, pl.ds(kind * local + head * HD, HD)]
+                inv = lax.rsqrt(jnp.mean(value * value, -1, keepdims=True) + EPS)
+                value = value * inv * gains[pl.ds(kind, 1), :]
+                out[rows, at] = (value * cos - pltpu.roll(value, HD // 2, 1) * sin).astype(bf16)
+        values[rows, :] = proj[rows, pl.ds(2 * local, local)].astype(bf16)
+
+    @pl.loop(0, tall // chunk)
+    def _(n):
+        rows = pl.ds(pl.multiple_of(n * chunk, chunk), chunk)
+        for head in range(heads):
+            at = pl.ds(head * HD, HD)
+            scores = lax.dot_general(
+                queries[rows, at], keys[:, at], (((1,), (1,)), ((), ())), preferred_element_type=f32
+            ) * scale
+            raised = jnp.exp(scores - jnp.max(scores, -1, keepdims=True))
+            probs = (raised / jnp.sum(raised, -1, keepdims=True)).astype(bf16)
+            context[rows, at] = jnp.dot(probs, values[:, at], preferred_element_type=f32).astype(bf16)
+
+    @pl.loop(0, width // span)
+    def _(n):
+        at = pl.ds(pl.multiple_of(n * span, span), span)
+        part[:, at] = jnp.dot(context[...], w_o[:, at], preferred_element_type=f32).astype(bf16)
+
+
+def attention(x, gain, w_qkv, tables, gains, w_o):
+    bf16, f32 = jnp.bfloat16, jnp.float32
+    tall, width = x.shape
+    local = w_o.shape[0]
+    vmem = pl.BlockSpec(memory_space=pltpu.VMEM)
+    shapes = [
+        ((tall, width), bf16),
+        ((tall, 3 * local), f32),
+        ((tall, local), bf16),
+        ((tall, local), bf16),
+        ((tall, local), bf16),
+        ((tall, local), bf16),
+        ((tall, width), bf16),
+    ]
+    return pl.pallas_call(
+        functools.partial(attention_kernel, 1.0 / math.sqrt(HD)),
+        out_shape=[jax.ShapeDtypeStruct(shape, kind) for shape, kind in shapes],
+        in_specs=[vmem] * 6,
+        out_specs=[vmem] * 7,
+        compiler_params=pltpu.CompilerParams(vmem_limit_bytes=56 * 2**20),
+    )(x, gain, w_qkv, tables, gains, w_o)
+
+
+def attention_back_kernel(
+    scale, *refs,
+):
+    sources, refs = refs[:11], refs[11:]
+    part, dw, dwo, q_sum, k_sum = refs[:5]
+    held, refs = refs[5:16], refs[16:]
+    grad_ctx, gq, gk, gv, grads, sem = refs
+    grad_attn, w_o, queries, keys, values, proj, tables, gains, context, normed, w_qkv = held
+    f32, bf16 = jnp.float32, jnp.bfloat16
+    tall, local = queries.shape
+    heads = local // HD
+    width = grad_attn.shape[1]
+    copies = [pltpu.make_async_copy(src, dst, sem.at[k]) for k, (src, dst) in enumerate(zip(sources, held))]
+    for copy in copies:
+        copy.start()
+    for copy in copies[:5]:
+        copy.wait()
+
+    def nt(left, right):
+        return lax.dot_general(left, right, (((1,), (1,)), ((), ())), preferred_element_type=f32)
+
+    def tn(left, right):
+        return lax.dot_general(left, right, (((0,), (0,)), ((), ())), preferred_element_type=f32)
+
+    grad_ctx[...] = nt(grad_attn[...], w_o[...]).astype(bf16)
+    gk[...] = jnp.zeros_like(gk)
+    gv[...] = jnp.zeros_like(gv)
+    q_sum[...] = jnp.zeros_like(q_sum)
+    k_sum[...] = jnp.zeros_like(k_sum)
+    chunk = 256
+
+    @pl.loop(0, tall // chunk)
+    def _(n):
+        rows = pl.ds(pl.multiple_of(n * chunk, chunk), chunk)
+        for head in range(heads):
+            at = pl.ds(head * HD, HD)
+            q, k, v, g = queries[rows, at], keys[:, at], values[:, at], grad_ctx[rows, at]
+            scores = nt(q, k) * scale
+            raised = jnp.exp(scores - jnp.max(scores, -1, keepdims=True))
+            probs = raised / jnp.sum(raised, -1, keepdims=True)
+            grad_probs = nt(g, v)
+            inner = jnp.sum(probs * grad_probs, -1, keepdims=True)
+            grad_scores = (probs * (grad_probs - inner)).astype(bf16)
+            gq[rows, at] = jnp.dot(grad_scores, k, preferred_element_type=f32) * scale
+            gk[:, at] += tn(grad_scores, q)
+            gv[:, at] += tn(probs.astype(bf16), g)
+
+    for copy in copies[5:8]:
+        copy.wait()
+
+    @pl.loop(0, tall // chunk)
+    def _(n):
+        rows = pl.ds(pl.multiple_of(n * chunk, chunk), chunk)
+        cos, sin = tables[rows, pl.ds(0, HD)], tables[rows, pl.ds(HD, HD)]
+        for head in range(heads):
+            for kind, total in enumerate((q_sum, k_sum)):
+                at = pl.ds(head * HD, HD)
+                column = pl.ds(kind * local + head * HD, HD)
+                grad = gq[rows, at] if kind == 0 else gk[rows, at] * scale
+                grad = grad * cos + pltpu.roll(grad, HD // 2, 1) * sin
+                value = proj[rows, column]
+                inv = lax.rsqrt(jnp.mean(value * value, -1, keepdims=True) + EPS)
+                total[...] += jnp.sum((grad * value * inv).reshape(chunk // 8, 8, HD), 0)
+                weighted = grad * gains[pl.ds(kind, 1), :]
+                inner = jnp.sum(weighted * value, -1, keepdims=True)
+                out = inv * weighted - value * (inv * inv * inv) * inner / HD
+                grads[rows, column] = out.astype(bf16)
+        grads[rows, pl.ds(2 * local, local)] = gv[rows, :].astype(bf16)
+
+    for copy in copies[8:]:
+        copy.wait()
+    span = 256
+    strip = dwo.shape[2]
+
+    @pl.loop(0, width // span)
+    def _(n):
+        full = pl.ds(pl.multiple_of(n * span, span), span)
+        dw[full, :] = tn(normed[:, full], grads[...]).astype(bf16)
+        part[:, full] = nt(grads[...], w_qkv[full, :]).astype(bf16)
+        value = tn(context[...], grad_attn[:, full]).astype(bf16)
+        for i in range(span // strip):
+            dwo[n * (span // strip) + i] = value[:, i * strip : (i + 1) * strip]
+
+
+def attention_back(grad_attn, w_o, queries, keys, values, proj, tables, gains, context, normed, w_qkv, strip):
+    bf16, f32 = jnp.bfloat16, jnp.float32
+    tall, width = grad_attn.shape
+    local = queries.shape[1]
+    vmem = pl.BlockSpec(memory_space=pltpu.VMEM)
+    sources = (grad_attn, w_o, queries, keys, values, proj, tables, gains, context, normed, w_qkv)
+    return pl.pallas_call(
+        functools.partial(attention_back_kernel, 1.0 / math.sqrt(HD)),
+        out_shape=[
+            jax.ShapeDtypeStruct((tall, width), bf16),
+            jax.ShapeDtypeStruct((width, 3 * local), bf16),
+            jax.ShapeDtypeStruct((width // strip, local, strip), bf16),
+            jax.ShapeDtypeStruct((8, HD), f32),
+            jax.ShapeDtypeStruct((8, HD), f32),
+        ],
+        in_specs=[pl.BlockSpec(memory_space=pl.ANY)] * len(sources),
+        out_specs=[vmem] * 5,
+        scratch_shapes=[pltpu.VMEM(source.shape, source.dtype) for source in sources]
+        + [
+            pltpu.VMEM((tall, local), bf16),
+            pltpu.VMEM((tall, local), f32),
+            pltpu.VMEM((tall, local), f32),
+            pltpu.VMEM((tall, local), f32),
+            pltpu.VMEM((tall, 3 * local), bf16),
+            pltpu.SemaphoreType.DMA((len(sources),)),
+        ],
+        compiler_params=pltpu.CompilerParams(vmem_limit_bytes=60 * 2**20),
+    )(*sources)
+
+
 def one_chip(
     tokens,
     w_query,
@@ -1812,7 +2038,7 @@
     named = jnp.any(routes[0][:, :, None] == ids, 1)
     below = jnp.tril(jnp.ones((block, block), bf16), -1)
     rank = jnp.where(named, dot(below, named.astype(bf16)), -1.0).T
-    x_rows, w_qkv, w_o, small, _, rank_seq, pick, cot_rows, pair, third = load(
+    x_rows, w_qkv, w_o, small, _, rank_seq, pick, cot_rows, pair, third, middle = load(
         tokens[0], cotangent[0], w_query, w_key, w_value, w_out, small, rank, w_experts, most
     )
     w_qkv = w_qkv.reshape(width, 3 * local)
@@ -1833,34 +2059,20 @@
     kept = ((rank >= 0) & (rank + earlier[:, None] < CAP)).astype(f32).T
     kept = lax.dynamic_slice_in_dim(kept, t * rows, rows, 0)
 
-    x_rows = x_rows.astype(f32)
-    place = jnp.arange(tall, dtype=jnp.int32)
     half_dim = HD // 2
     inv_freq = jnp.exp(jnp.arange(half_dim, dtype=f32) * (-2.0 * math.log(ROPE_BASE) / HD))
-    angles = place.astype(f32)[:, None] * inv_freq[None, :]
-    cos_full = jnp.concatenate([jnp.cos(angles)] * 2, -1)[:, None, :]
-    sin_full = jnp.concatenate([jnp.sin(angles)] * 2, -1)[:, None, :]
-    normed_one = (x_rows * rms_scale(x_rows) * attn_gain).astype(bf16)
-    proj = dot(normed_one, w_qkv).reshape(tall, 3, local // HD, HD)
-    query_heads, key_heads = proj[:, 0], proj[:, 1]
-    values = proj[:, 2].astype(bf16)
-    query_inv, key_inv = rms_scale(query_heads), rms_scale(key_heads)
-    queries = apply_rope(query_heads * query_inv * query_gain, cos_full, sin_full).astype(bf16)
-    keys = apply_rope(key_heads * key_inv * key_gain, cos_full, sin_full).astype(bf16)
-    score_scale = 1.0 / math.sqrt(HD)
-    scores = jnp.einsum("qhd,khd->hqk", queries, keys, preferred_element_type=f32) * score_scale
-    maximum = jnp.max(scores, -1, keepdims=True)
-    exp_scores = jnp.exp(scores - maximum)
-    denominator = jnp.sum(exp_scores, -1, keepdims=True)
-    attn_probs = exp_scores / denominator
-    log_total = maximum + jnp.log(denominator)
-    context = jnp.einsum("hqk,khd->qhd", attn_probs.astype(bf16), values, preferred_element_type=f32)
-    context = context.astype(bf16).reshape(tall, local)
-    attn_part = dot(context, w_o).astype(bf16).reshape(nc, 2, rows, width)
+    angles = jnp.arange(tall, dtype=jnp.int32).astype(f32)[:, None] * inv_freq[None, :]
+    cosines, sines = jnp.cos(angles), jnp.sin(angles)
+    tables = jnp.concatenate([cosines, cosines, sines, -sines], 1)
+    gains = jnp.pad(jnp.stack([query_gain, key_gain]), ((0, 6), (0, 0)))
+    normed_one, proj, queries, keys, values, context, attn_part = attention(
+        x_rows, attn_gain[None], w_qkv, tables, gains, w_o
+    )
+    attn_part = attn_part.reshape(nc, 2, rows, width)
     kept_wide = jnp.pad(kept, ((0, 0), (0, 128 - E)))
     router_wide = jnp.pad(router, ((0, 128 - E), (0, 0)))
     residual, normed_two, router_probs, x_in, g_in, third = dispatch(
-        attn_part, tokens[0], moe_gain[None], router_wide, kept_wide, pick, third
+        attn_part, tokens[0], moe_gain[None], router_wide, kept_wide, pick, third, middle
     )
     pair, x_in = lax.optimization_barrier((pair, x_in))
     x_in = x_in.reshape(nc * 2 * most, width)
@@ -1896,27 +2108,22 @@
     dw_rest = exchange(dw_rest, ("fsdp", "ctx"))
     grad_attn = grad_attn.reshape(tall, width)
 
-    dw_out = dot_tn(context, grad_attn).astype(bf16)
-    grad_context = dot_nt(grad_attn, w_o).astype(bf16).reshape(tall, -1, HD)
-    scores = jnp.einsum("qhd,khd->hqk", queries, keys, preferred_element_type=f32) * score_scale
-    attn_probs = jnp.exp(scores - log_total)
-    grad_probs = jnp.einsum("qhd,khd->hqk", grad_context, values, preferred_element_type=f32)
-    grad_scores = attn_probs * (grad_probs - jnp.sum(attn_probs * grad_probs, -1, keepdims=True))
-    grad_scores = grad_scores.astype(bf16)
-    grad_queries = jnp.einsum("hqk,khd->qhd", grad_scores, keys, preferred_element_type=f32) * score_scale
-    grad_keys = jnp.einsum("hqk,qhd->khd", grad_scores, queries, preferred_element_type=f32) * score_scale
-    grad_values = jnp.einsum(
-        "hqk,qhd->khd", attn_probs.astype(bf16), grad_context, preferred_element_type=f32
-    ).astype(bf16)
-    grad_qnormed = rope_back(grad_queries, cos_full, sin_full)
-    grad_knormed = rope_back(grad_keys, cos_full, sin_full)
-    dgain_query = jnp.sum(grad_qnormed * query_heads * query_inv, (0, 1))
-    dgain_key = jnp.sum(grad_knormed * key_heads * key_inv, (0, 1))
-    grad_qproj = norm_back(grad_qnormed, query_heads, query_inv, query_gain).astype(bf16)
-    grad_kproj = norm_back(grad_knormed, key_heads, key_inv, key_gain).astype(bf16)
-    grad_proj = jnp.stack([grad_qproj, grad_kproj, grad_values], 1).reshape(tall, 3 * local)
-    dw_qkv = dot_tn(normed_one, grad_proj).astype(bf16)
-    grad_normed_part = dot_nt(grad_proj, w_qkv).astype(bf16).reshape(nc, 2, rows, width)
+    grad_normed_part, dw_qkv, dw_out, dgain_query, dgain_key = attention_back(
+        grad_attn,
+        w_o,
+        queries,
+        keys,
+        values,
+        proj,
+        tables,
+        gains,
+        context,
+        normed_one,
+        w_qkv,
+        strip,
+    )
+    dgain_query, dgain_key = jnp.sum(dgain_query, 0), jnp.sum(dgain_key, 0)
+    grad_normed_part = grad_normed_part.reshape(nc, 2, rows, width)
     head_part = HD // chips
     heads = [dgain_query.reshape(chips, 1, head_part), dgain_key.reshape(chips, 1, head_part)]
     heads = jnp.pad(jnp.concatenate(heads, 2), ((0, 0), (0, 0), (0, strip - 2 * head_part)))
@@ -1936,13 +2143,13 @@
         attn_gain[None],
         grad_residual,
         dw_qkv.reshape(nz, nc, strip, 3 * local),
-        dw_out.reshape(local, nz, nc, strip).transpose(1, 2, 0, 3),
+        dw_out.reshape(nz, nc, local, strip),
         sums,
         out_rows.reshape(shape),
         pick_t,
         residual,
     )
-    dw_experts = lay_out(dw_gate[:, None], dw_rest, nz, nc)
+    dw_experts = lay_out(dw_gate, dw_rest, nz, nc)
     got_qkv = got_qkv.astype(f32).reshape(nc, strip, 3, local)
     got_qkv = got_qkv.transpose(2, 1, 0, 3).reshape(3, strip, nc * local)
     return (

time: 753 us -> 734 us (0.975)
  Pallas kernels: 603 us -> 668 us
  matrix products: 55.7 us -> 1.6 us
  other arithmetic: 25.8 us -> 11.5 us
  local copies, waits for them, and re-layouts: 43.1 us -> 29.9 us
    pallas_call x0 -> x2, Pallas kernels: none -> 55.6 us  [the longest x1 28.5 us: attention_back(): pl.pallas_call(functools.partial(attention_back_kernel, 1.0 / math.sqrt(H...]
    dot_general x8 -> x0, matrix products: 36.2 us -> none  [the longest x1 13.2 us: one_chip(): jnp.einsum('hqk,khd->qhd', attn_probs.astype(bf16), values, preferred_ele...]
    pallas_call x1, Pallas kernels: 162 us -> 176 us  [give_back(): pl.pallas_call(functools.partial(return_kernel, nz, nc), out_shape=[jax.S...]
    dot_general x3 -> x1, matrix products: 12.5 us -> 1.38 us  [dot_tn(): lax.dot_general(left, right, (((0,), (0,)), ((), ())), preferred_element_...]
    pallas_call x1, Pallas kernels: 148 us -> 138 us  [finish(): pl.pallas_call(functools.partial(final_kernel, nz, nc), out_shape=[jax.Sh...]
    unnamed x70 -> x35, local copies, waits for them, and re-layouts: 17.7 us -> 15.1 us
  transfers between devices with their start and end apart: 2 -> 2, of which waited for: 0 -> 0; matrix products, arithmetic and copies ran while one was open for 14% -> 3% of each run, Pallas kernels for 37% -> 44%
where the time goes in v7:
time: 734 us; the launch traced here: 733 us
  Pallas kernels  668 us (91%)
  local copies, waits for them, and re-layouts  29.9 us (4%)
  starting transfers between devices  20.9 us (3%)
  other arithmetic  11.5 us (2%)
    pallas_call x1, Pallas kernels, give_back(): pl.pallas_call(functools.partial(return_kernel, nz, nc), out_shape=[jax.S...  176 us
    pallas_call x1, Pallas kernels, finish(): pl.pallas_call(functools.partial(final_kernel, nz, nc), out_shape=[jax.Sh...  138 us
    pallas_call x1, Pallas kernels, dispatch(): pl.pallas_call(functools.partial(dispatch_kernel, nz, nc), out_shape=[jax...  129 us
    pallas_call x1, Pallas kernels, load(): pl.pallas_call(functools.partial(load_kernel, nz, nc), out_shape=[jax.Sha...  110 us
    pallas_call x1, Pallas kernels, experts(): pl.pallas_call(functools.partial(experts_kernel, nz, nc), out_shape=[jax....  51.5 us
    pallas_call x1, Pallas kernels, attention_back(): pl.pallas_call(functools.partial(attention_back_kernel, 1.0 / math.sqrt(H...  28.5 us
    pallas_call x1, Pallas kernels, attention(): pl.pallas_call(functools.partial(attention_kernel, 1.0 / math.sqrt(HD)),...  27.2 us
    all_to_all x2, starting transfers between devices, exchange(): return lax.all_to_all(value, axes, split_axis=0, concat_axis=0, tiled=True)  20.9 us
  transfers between devices with their start and end apart: 2, of which 0 were waited for; matrix products, arithmetic and copies ran while one was open for 3% of the time, Pallas kernels for 44%

profile of v7, /device:TPU:15, one launch (start us, length us, event | category | flops | bytes accessed | tf_op | source)
XLA Modules:
  0.0 732.5 jit_solution(9862123321848026388)
XLA Ops:
  0.7 0.7 fusion.4
  1.4 0.1 copy.60
  1.5 0.2 convolution_select_fusion
  1.8 0.7 copy.84
  2.5 2.8 concatenate.19
  5.3 1.2 copy-done
  6.6 1.2 copy-done.1
  7.8 1.2 copy-done.4
  9.0 110.3 %shard_map.220 = (bf16[1024,2048]{1,0:T(8,128)(2,1)}, bf16[4,512,768]{2,1,0:T(8,128)(2,1)}, bf16[4,256,512]{2,1,0:T(8,128)(2,1)S(1)}, bf16[4,80,128]{2,1,0:T(8,1...) custom-call(bf16[256,2048]{1,0:T(8,128)(2,1)S(1)} %bitcast.70, ...), custom_call_target="tpu_custom_call" | custom-call | tf_op jit(solution)/shard_map/pallas_call | solution.py:782
  119.3 0.8 copy-done.5
  120.1 12.7 %all-to-all-start = ((bf16[4,2,512,512]{3,2,1,0:T(8,128)(2,1)}), bf16[4,2,512,512]{3,2,1,0:T(8,128)(2,1)}, u32[]{:S(2)}, u32[]{:S(2)}) async-start(bf16[4,2,512,512]{3,2,1,0:T(8,128)(2,1)} %get-tuple-element.62), calls=%async_computation | async-start | bytes 8388608 | tf_op jit(solution)/shard_map/all_to_all | solution.py:413
  133.1 0.6 copy.86
  133.7 1.1 copy.83
  134.9 0.6 copy.87
  135.5 1.1 copy.67
  136.6 0.1 convert_reduce_fusion
  136.7 0.1 select_reduce_fusion
  136.8 0.6 pad.26.kept
  137.4 0.8 pad.25.router
  138.3 0.6 fusion.13.gains.refs_7_
  138.9 1.9 multiply_cosine_fusion
  140.8 1.4 pad_maximum_fusion.tables.refs_6_
  142.2 27.2 %shard_map.221 = (bf16[1024,2048]{1,0:T(8,128)(2,1)}, f32[1024,768]{1,0:T(8,128)}, bf16[1024,256]{1,0:T(8,128)(2,1)}, bf16[1024,256]{1,0:T(8,128)(2,1)}, bf16[10...) custom-call(bf16[1024,2048]{1,0:T(8,128)(2,1)} %get-tuple-element.63.x, ...), custom_call_target="tpu_custom_call" | custom-call | tf_op jit(solution)/shard_map/pallas_call | solution.py:1882
  169.4 129.1 %shard_map.222 = (f32[128,2048]{1,0:T(8,128)}, bf16[128,2048]{1,0:T(8,128)(2,1)}, f32[128,128]{1,0:T(8,128)}, bf16[4,2,144,2048]{3,2,1,0:T(8,128)(2,1)}, bf16[4,...) custom-call(bf16[4,2,128,2048]{3,2,1,0:T(8,128)(2,1)} %bitcast.89, bf16[256,2048]{1,0:T(8,128)(2,1)} %bitcast.68, ...), custom_call_target="tpu_custom_call" | custom-call | tf_op jit(solution)/shard_map/pallas_call | solution.py:949
  298.5 51.5 %shard_map.223 = (bf16[1152,2048]{1,0:T(8,128)(2,1)}, bf16[1152,2048]{1,0:T(8,128)(2,1)}, bf16[1152,256]{1,0:T(8,128)(2,1)}, bf16[1152,1024]{1,0:T(8,128)(2,1)},...) custom-call(bf16[1152,2048]{1,0:T(8,128)(2,1)} %bitcast.77, bf16[1152,2048]{1,0:T(8,128)(2,1)} %bitcast.75, ...), custom_call_target="tpu_custom_call" | custom-call | tf_op jit(solution)/shard_map/pallas_call | solution.py:1122
  350.1 176.2 %shard_map.224 = (bf16[128,128]{1,0:T(8,128)(2,1)}, f32[8,2048]{1,0:T(8,128)}, f32[128,2048]{1,0:T(8,128)}, bf16[4,2,128,2048]{3,2,1,0:T(8,128)(2,1)}, bf16[2,16...) custom-call(bf16[4,2,144,2048]{3,2,1,0:T(8,128)(2,1)} %bitcast.87, ...), custom_call_target="tpu_custom_call" | custom-call | tf_op jit(solution)/shard_map/pallas_call | solution.py:1485
  526.3 4.3 add_convert_fusion
  530.5 8.1 %all-to-all-start.1 = ((bf16[16,128,512]{2,1,0:T(8,128)(2,1)}), bf16[16,128,512]{2,1,0:T(8,128)(2,1)S(1)}, u32[]{:S(2)}, u32[]{:S(2)}) async-start(bf16[16,128,512]{2,1,0:T(8,128)(2,1)} %add_convert_fusion), calls=%async_computation.1 | async-start | bytes 4194304 | tf_op jit(solution)/shard_map/all_to_all | solution.py:413
  538.7 28.5 %shard_map.225 = (bf16[1024,2048]{1,0:T(8,128)(2,1)}, bf16[2048,768]{1,0:T(8,128)(2,1)}, bf16[16,256,128]{2,1,0:T(8,128)(2,1)}, f32[8,128]{1,0:T(8,128)}, f32[8,128]{1,0:T(8,128)}) custom-call(bf16[1024,2048]{1,0:T(8,128)(2,1)} %bitcast.88, bf16[256,2048]{1,0:T(8,128)(2,1)} %bitcast.82, bf16[1024,256]{1,0:T(8,128)(2,1)} %get-tuple-element.89.refs_2_, ...), custom_call_target="tpu_custom_call" | custom-call | tf_op jit(solution)/shard_map/pallas_call | solution.py:1981
  567.1 0.7 reduce_sum.48
  567.9 0.7 reduce_sum.49
  568.7 1.4 fusion.8
  570.1 0.3 concatenate.21
  570.6 1.3 concatenate.25.small
  571.9 138.2 %shard_map.226 = (bf16[256,2048]{1,0:T(8,128)(2,1)}, bf16[4,128,768]{2,1,0:T(8,128)(2,1)}, bf16[4,256,128]{2,1,0:T(8,128)(2,1)}, f32[24,128]{1,0:T(8,128)}, bf16[256,1024]{1,0:T(8,128)(2,1)}) custom-call(bf16[4,2,128,2048]{3,2,1,0:T(8,128)(2,1)} %bitcast.90, bf16[256,2048]{1,0:T(8,128)(2,1)} %bitcast.69, f32[1,2048]{1,0:T(1,128)} %bitcast.106, ...), custom_call_target="tpu_custom_call" | custom-call | tf_op jit(solution)/shard_map/pallas_call | solution.py:1773
  710.2 2.6 copy.69
  712.8 2.3 fusion.16
  715.0 2.0 copy.70
  717.1 1.0 copy.71
  718.1 1.0 copy.72
  719.1 0.7 copy.73
  719.8 0.5 slice_bitcast_fusion
  720.3 0.6 slice_bitcast_fusion.1
  720.9 0.8 bitcast_convert_fusion
  721.8 2.2 copy-done.2
  724.0 6.8 shard_map.227
  730.8 0.8 copy.94
  731.6 1.0 copy.95
  (43 shorter events, 0.8 us)
Async XLA Ops:
  5.3 1.2 copy-start
  6.6 1.2 copy-start.1
  7.8 1.2 copy-start.4
  119.3 0.8 copy-start.5
  120.1 15.4 %copy-start.3 = (bf16[2,576,256]{2,1,0:T(8,128)(2,1)}, bf16[2,576,256]{2,1,0:T(8,128)(2,1)S(1)}, u32[]{:S(2)}) copy-start(bf16[2,576,256]{2,1,0:T(8,128)(2,1)S(1)} %get-tuple-element.69.pick) | copy-start | bytes 1769476
  120.1 178.4 %all-to-all-start = ((bf16[4,2,512,512]{3,2,1,0:T(8,128)(2,1)}), bf16[4,2,512,512]{3,2,1,0:T(8,128)(2,1)}, u32[]{:S(2)}, u32[]{:S(2)}) async-start(bf16[4,2,512,512]{3,2,1,0:T(8,128)(2,1)} %get-tuple-element.62), calls=%async_computation | async-start | bytes 8388608 | tf_op jit(solution)/shard_map/all_to_all | solution.py:413
  530.5 191.2 %all-to-all-start.1 = ((bf16[16,128,512]{2,1,0:T(8,128)(2,1)}), bf16[16,128,512]{2,1,0:T(8,128)(2,1)S(1)}, u32[]{:S(2)}, u32[]{:S(2)}) async-start(bf16[16,128,512]{2,1,0:T(8,128)(2,1)} %add_convert_fusion), calls=%async_computation.1 | async-start | bytes 4194304 | tf_op jit(solution)/shard_map/all_to_all | solution.py:413
  538.7 30.1 %copy-start.10 = (bf16[128,128]{1,0:T(8,128)(2,1)S(1)}, bf16[128,128]{1,0:T(8,128)(2,1)}, u32[]{:S(2)}) copy-start(bf16[128,128]{1,0:T(8,128)(2,1)} %get-tuple-element.100) | copy-start | bytes 98308
  538.7 31.8 %copy-start.9 = (f32[8,2048]{1,0:T(8,128)S(1)}, f32[8,2048]{1,0:T(8,128)}, u32[]{:S(2)}) copy-start(f32[8,2048]{1,0:T(8,128)} %get-tuple-element.101) | copy-start | bytes 196612
  710.2 8.9 %copy-start.11 = (f32[24,128]{1,0:T(8,128)S(1)}, f32[24,128]{1,0:T(8,128)}, u32[]{:S(2)}) copy-start(f32[24,128]{1,0:T(8,128)} %get-tuple-element.109) | copy-start | bytes 36868
  710.2 10.7 %copy-start.8 = (bf16[4,256,128]{2,1,0:T(8,128)(2,1)S(1)}, bf16[4,256,128]{2,1,0:T(8,128)(2,1)}, u32[]{:S(2)}) copy-start(bf16[4,256,128]{2,1,0:T(8,128)(2,1)} %get-tuple-element.108) | copy-start | bytes 786436
  721.8 2.2 copy-start.2
  724.0 6.8 copy-start.7
  724.0 7.6 %copy-start.6 = (bf16[256,2048]{1,0:T(8,128)(2,1)S(1)}, bf16[256,2048]{1,0:T(8,128)(2,1)}, u32[]{:S(2)}) copy-start(bf16[256,2048]{1,0:T(8,128)(2,1)} %get-tuple-element.106) | copy-start | bytes 3145732

commit v8 on v7

--- a/solution.py
+++ b/solution.py
@@ -798,7 +798,7 @@
             dma((2,)), dma((2,)), dma((2,)), dma, dma,
         ],
         compiler_params=pltpu.CompilerParams(
-            collective_id=0, has_side_effects=True, vmem_limit_bytes=48 * 2**20
+            collective_id=0, has_side_effects=True, vmem_limit_bytes=60 * 2**20
         ),
     )(tok, cot, wq, wk, wv, wo, small, rank, w_experts)
 
@@ -1310,7 +1310,7 @@
 
 def return_kernel(
     nz, nc, r, g, x_hbm, cot_hbm, hid_hbm, gg_hbm, gu_hbm, pick_t, residual, probs, kept, router, gain, cot,
-    logits_grad, gain_grad, residual_grad, attn_grad, early_got, own_grad, other_grad,
+    logits_grad, gain_grad, residual_grad, attn_grad, early_got, rest,
     x, cot_rows, hid, gg, gu, stage, early, early_sib,
     load_sem, keep_sem, give_sem, got_sem, *scratch,
 ):
@@ -1353,54 +1353,37 @@
     begin(1)
 
     span = 256
-    strip, ffn = stage.shape[3], stage.shape[4]
+    strip, ffn = stage.shape[2], stage.shape[3]
     per = span // strip
     bands = width // span
 
     def gradients(kind, rows_in, grads):
-        last = kind == 2
-
         def flush(n):
             slot = lax.rem(n, 2)
             at = pl.ds(pl.multiple_of(n * per, per), per)
-            target = other_grad.at[at] if last else early_sib.at[kind, at]
-            give = remote(stage.at[slot, 1], target, give_sem.at[slot], got_sem.at[kind], tp=1 - t)
-            if not last:
-                return (give,)
-            return (give, pltpu.make_async_copy(stage.at[slot, 0], own_grad.at[at], keep_sem.at[slot]))
-
-        def flushed(n):
-            copies = flush(n)
-            copies[0].wait_send()
-            for copy in copies[1:]:
-                copy.wait()
+            return remote(stage.at[slot], early_sib.at[kind, at], give_sem.at[slot], got_sem.at[kind], tp=1 - t)
 
         @pl.loop(0, bands)
         def _(n):
             full = pl.ds(pl.multiple_of(n * span, span), span)
             slot = lax.rem(n, 2)
-            pl.when(n >= 2)(lambda: flushed(n - 2))
+            pl.when(n >= 2)(lambda: flush(n - 2).wait_send())
             value = lax.dot_general(
                 rows_in[:, full], grads[...], (((0,), (0,)), ((), ())), preferred_element_type=f32
             ).astype(bf16)
             for i in range(per):
                 piece = value[i * strip : (i + 1) * strip]
-                if last:
-                    stage[slot, 0, i] = piece[:, :ffn]
-                else:
-                    early[kind, n * per + i] = piece[:, :ffn]
-                stage[slot, 1, i] = piece[:, ffn:]
-            for copy in flush(n):
-                copy.start()
-
-        flushed(bands - 2)
-        flushed(bands - 1)
-        if not last:
-            remote(early_sib.at[kind], early_sib.at[kind], got_sem.at[kind], got_sem.at[kind], tp=1 - t).wait_recv()
-
-            @pl.loop(0, chips)
-            def _(n):
-                early[kind, n] = (early[kind, n].astype(f32) + early_sib[kind, n].astype(f32)).astype(bf16)
+                early[kind, n * per + i] = piece[:, :ffn]
+                stage[slot, i] = piece[:, ffn:]
+            flush(n).start()
+
+        flush(bands - 2).wait_send()
+        flush(bands - 1).wait_send()
+        remote(early_sib.at[kind], early_sib.at[kind], got_sem.at[kind], got_sem.at[kind], tp=1 - t).wait_recv()
+
+        @pl.loop(0, chips)
+        def _(n):
+            early[kind, n] = (early[kind, n].astype(f32) + early_sib[kind, n].astype(f32)).astype(bf16)
 
     loads[0].wait()
     loads[1].wait()
@@ -1410,6 +1393,8 @@
         copy.wait()
     gradients(1, x, gu)
     gradients(2, cot_rows, hid)
+    keep_rest = pltpu.make_async_copy(early.at[2], rest, keep_sem)
+    keep_rest.start()
     for turn in range(2):
         process(turn)
     join()
@@ -1468,7 +1453,7 @@
             copy.wait_recv()
             copy.wait_send()
         keep_early(kind).wait()
-    remote(other_grad, other_grad, got_sem.at[2], got_sem.at[2], tp=1 - t).wait_recv()
+    keep_rest.wait()
 
 
 def give_back(r, g, x, cot_rows, hid, gg, gu, pick_t, residual, probs, kept, router, gain, cot):
@@ -1491,20 +1476,19 @@
             jax.ShapeDtypeStruct((nc, 2, rows, width), bf16),
             jax.ShapeDtypeStruct((2, chips, strip, ffn), bf16),
             jax.ShapeDtypeStruct((chips, strip, ffn), bf16),
-            jax.ShapeDtypeStruct((chips, strip, ffn), bf16),
         ],
         in_specs=[hbm] * 7 + [vmem] * 7,
-        out_specs=[vmem] * 4 + [hbm] * 3,
+        out_specs=[vmem] * 4 + [hbm] * 2,
         scratch_shapes=[
             pltpu.VMEM((tall, width), bf16),
             pltpu.VMEM((tall, width), bf16),
             pltpu.VMEM((tall, 2 * ffn), bf16),
             pltpu.VMEM((tall, 2 * ffn), bf16),
             pltpu.VMEM((tall, 2 * ffn), bf16),
-            pltpu.VMEM((2, 2, 256 // strip, strip, ffn), bf16),
-            pltpu.VMEM((2, chips, strip, ffn), bf16),
-            pltpu.VMEM((2, chips, strip, ffn), bf16),
-            dma((5,)), dma((2,)), dma((2,)), dma((3,)),
+            pltpu.VMEM((2, 256 // strip, strip, ffn), bf16),
+            pltpu.VMEM((3, chips, strip, ffn), bf16),
+            pltpu.VMEM((3, chips, strip, ffn), bf16),
+            dma((5,)), dma, dma((2,)), dma((3,)),
         ]
         + bufs
         + sems
@@ -1518,8 +1502,8 @@
 
 def final_kernel(
     nz, nc, part, tok, gain, residual_grad, dw, dwo, small, y, pick_t, residual,
-    tokens_grad, dw_out, dwo_out, small_out, layer,
-    sib, rs_send, rs_recv, tok_grad, gain_acc, dw_up, dw_down, dwo_up, dwo_down, dw_to, dwo_to,
+    tokens_grad, q_out, k_out, v_out, o_out, small_out, layer,
+    dw_out, dwo_out, sib, rs_send, rs_recv, tok_grad, gain_acc, dw_up, dw_down, dwo_up, dwo_down, dw_to, dwo_to,
     dw_next, dwo_next, small_line, small_plane, small_sib, small_a, small_b,
     sib_s, sib_r, rs_s, rs_r, line_s, line_r, to_s, to_r, tg_s, tg_r, sm_s, sm_r, sp_s, sp_r, ss_s, ss_r,
     layer_send, lay_s, lay_r, *scratch,
@@ -1735,6 +1719,12 @@
             remote(
                 src.at[c], dst.at[source], to_s.at[k, step - 1], to_r.at[k, step - 1], ctx=source
             ).wait_recv()
+    local = o_out.shape[0] // nc
+    for source in range(nc):
+        at = slice(source * local, (source + 1) * local)
+        for k, out in enumerate((q_out, k_out, v_out)):
+            out[:, at] = dw_out[source, :, k * local : (k + 1) * local].astype(f32)
+        o_out[at, :] = dwo_out[source].astype(f32)
     grad_copy(1 - t).wait_recv()
     grad_copy(t).wait_send()
     layer_copy(1 - t).wait_recv()
@@ -1774,14 +1764,18 @@
         functools.partial(final_kernel, nz, nc),
         out_shape=[
             jax.ShapeDtypeStruct((2 * rows, width), bf16),
-            jax.ShapeDtypeStruct(one, bf16),
-            jax.ShapeDtypeStruct(two, bf16),
+            jax.ShapeDtypeStruct((one[1], nc * two[1]), f32),
+            jax.ShapeDtypeStruct((one[1], nc * two[1]), f32),
+            jax.ShapeDtypeStruct((one[1], nc * two[1]), f32),
+            jax.ShapeDtypeStruct((nc * two[1], two[2]), f32),
             jax.ShapeDtypeStruct(tiny, f32),
             jax.ShapeDtypeStruct((2 * rows, width // 2), bf16),
         ],
         in_specs=[vmem] * 7 + [pl.BlockSpec(memory_space=pl.ANY)] + [vmem] * 2,
-        out_specs=[vmem] * 5,
+        out_specs=[vmem] * 7,
         scratch_shapes=[
+            pltpu.VMEM(one, bf16),
+            pltpu.VMEM(two, bf16),
             pltpu.VMEM((nc, rows, width), bf16),
             pltpu.VMEM((nc - 1, rows, width), bf16),
             pltpu.VMEM((nc - 1, rows, width), bf16),
@@ -2084,7 +2078,7 @@
     )
     shape = (nc, 2, most, -1)
     pick_t = pick.transpose(0, 2, 1)
-    grad_logits, dgain_moe, grad_residual, grad_attn, dw_gate, own_grad, other_grad = give_back(
+    grad_logits, dgain_moe, grad_residual, grad_attn, dw_gate, dw_rest = give_back(
         back_rows.reshape(shape),
         pair_rows.reshape(shape),
         x_in,
@@ -2103,7 +2097,6 @@
 
     dw_router = dot_tn(normed_two, grad_logits[:, :E])
     dgain_moe = jnp.sum(dgain_moe, 0)
-    dw_rest = (own_grad.astype(f32) + other_grad.astype(f32)).astype(bf16)
     dw_rest, grad_attn = lax.optimization_barrier((dw_rest, grad_attn))
     dw_rest = exchange(dw_rest, ("fsdp", "ctx"))
     grad_attn = grad_attn.reshape(tall, width)
@@ -2137,7 +2130,7 @@
         ],
         1,
     ).reshape(nz, nc, 24, strip)
-    tokens_grad, got_qkv, got_out, sums, layer_out = finish(
+    tokens_grad, dw_query, dw_key, dw_value, dw_out, sums, layer_out = finish(
         grad_normed_part,
         tokens[0],
         attn_gain[None],
@@ -2150,15 +2143,13 @@
         residual,
     )
     dw_experts = lay_out(dw_gate, dw_rest, nz, nc)
-    got_qkv = got_qkv.astype(f32).reshape(nc, strip, 3, local)
-    got_qkv = got_qkv.transpose(2, 1, 0, 3).reshape(3, strip, nc * local)
     return (
         layer_out[None],
         tokens_grad[None],
-        got_qkv[0],
-        got_qkv[1],
-        got_qkv[2],
-        got_out.astype(f32).reshape(nc * local, strip),
+        dw_query,
+        dw_key,
+        dw_value,
+        dw_out,
         sums[E + 1],
         sums[E + 2, :head_part],
         sums[E + 2, head_part : 2 * head_part],

time: 734 us -> 725 us (0.988)
    unnamed x35 -> x38, local copies, waits for them, and re-layouts: 15.1 us -> 9.83 us
  transfers between devices with their start and end apart: 2 -> 2, of which waited for: 0 -> 0; matrix products, arithmetic and copies ran while one was open for 3% -> 3% of each run, Pallas kernels for 44% -> 45%
where the time goes in v8:
time: 725 us; the launch traced here: 724 us
  Pallas kernels  672 us (93%)
  local copies, waits for them, and re-layouts  23.2 us (3%)
  starting transfers between devices  19.6 us (3%)
    pallas_call x1, Pallas kernels, give_back(): pl.pallas_call(functools.partial(return_kernel, nz, nc), out_shape=[jax.S...  179 us
    pallas_call x1, Pallas kernels, finish(): pl.pallas_call(functools.partial(final_kernel, nz, nc), out_shape=[jax.Sh...  139 us
    pallas_call x1, Pallas kernels, dispatch(): pl.pallas_call(functools.partial(dispatch_kernel, nz, nc), out_shape=[jax...  129 us
    pallas_call x1, Pallas kernels, load(): pl.pallas_call(functools.partial(load_kernel, nz, nc), out_shape=[jax.Sha...  111 us
    pallas_call x1, Pallas kernels, experts(): pl.pallas_call(functools.partial(experts_kernel, nz, nc), out_shape=[jax....  51.5 us
    pallas_call x1, Pallas kernels, attention_back(): pl.pallas_call(functools.partial(attention_back_kernel, 1.0 / math.sqrt(H...  28.4 us
    pallas_call x1, Pallas kernels, attention(): pl.pallas_call(functools.partial(attention_kernel, 1.0 / math.sqrt(HD)),...  27.1 us
    all_to_all x2, starting transfers between devices, exchange(): return lax.all_to_all(value, axes, split_axis=0, concat_axis=0, tiled=True)  19.6 us
  transfers between devices with their start and end apart: 2, of which 0 were waited for; matrix products, arithmetic and copies ran while one was open for 3% of the time, Pallas kernels for 45%

profile of v8, /device:TPU:15, one launch (start us, length us, event | category | flops | bytes accessed | tf_op | source)
XLA Modules:
  0.0 723.8 jit_solution(17383208254910062760)
XLA Ops:
  0.7 0.7 fusion.4
  1.4 0.1 copy.49
  1.5 0.2 convolution_select_fusion
  1.7 0.7 copy.51.rank
  2.4 0.7 copy.69
  3.1 2.8 concatenate.19
  5.9 0.6 pad_bitcast_fusion.small
  6.5 111.3 %shard_map.220 = (bf16[1024,2048]{1,0:T(8,128)(2,1)}, bf16[4,512,768]{2,1,0:T(8,128)(2,1)}, bf16[4,256,512]{2,1,0:T(8,128)(2,1)}, bf16[4,80,128]{2,1,0:T(8,128)(...) custom-call(bf16[256,2048]{1,0:T(8,128)(2,1)} %bitcast.67, ...), custom_call_target="tpu_custom_call" | custom-call | tf_op jit(solution)/shard_map/pallas_call | solution.py:782
  117.9 13.2 %all-to-all-start = ((bf16[4,2,512,512]{3,2,1,0:T(8,128)(2,1)}), bf16[4,2,512,512]{3,2,1,0:T(8,128)(2,1)}, u32[]{:S(2)}, u32[]{:S(2)}) async-start(bf16[4,2,512,512]{3,2,1,0:T(8,128)(2,1)} %get-tuple-element.63), calls=%async_computation | async-start | bytes 8388608 | tf_op jit(solution)/shard_map/all_to_all | solution.py:413
  131.2 0.1 convert_element_type.81
  131.2 0.1 convert_element_type.82
  131.3 0.6 copy.71
  131.9 1.1 copy.68
  133.1 0.6 copy.72
  133.7 1.1 copy.56
  134.8 0.1 convert_reduce_fusion
  134.9 0.1 select_reduce_fusion
  135.0 0.6 pad.26.kept
  135.6 0.8 pad.25.router
  136.5 0.6 fusion.13.gains.refs_7_
  137.1 1.9 multiply_cosine_fusion
  139.0 1.4 pad_maximum_fusion.tables.refs_6_
  140.4 27.1 %shard_map.221 = (bf16[1024,2048]{1,0:T(8,128)(2,1)}, f32[1024,768]{1,0:T(8,128)}, bf16[1024,256]{1,0:T(8,128)(2,1)}, bf16[1024,256]{1,0:T(8,128)(2,1)}, bf16[10...) custom-call(bf16[1024,2048]{1,0:T(8,128)(2,1)} %get-tuple-element.64.x, ...), custom_call_target="tpu_custom_call" | custom-call | tf_op jit(solution)/shard_map/pallas_call | solution.py:1876
  167.6 129.1 %shard_map.222 = (f32[128,2048]{1,0:T(8,128)}, bf16[128,2048]{1,0:T(8,128)(2,1)}, f32[128,128]{1,0:T(8,128)}, bf16[4,2,144,2048]{3,2,1,0:T(8,128)(2,1)}, bf16[4,...) custom-call(bf16[4,2,128,2048]{3,2,1,0:T(8,128)(2,1)} %bitcast.77, bf16[256,2048]{1,0:T(8,128)(2,1)} %bitcast.68, ...), custom_call_target="tpu_custom_call" | custom-call | tf_op jit(solution)/shard_map/pallas_call | solution.py:949
  296.7 51.5 %shard_map.223 = (bf16[1152,2048]{1,0:T(8,128)(2,1)}, bf16[1152,2048]{1,0:T(8,128)(2,1)}, bf16[1152,256]{1,0:T(8,128)(2,1)}, bf16[1152,1024]{1,0:T(8,128)(2,1)},...) custom-call(bf16[1152,2048]{1,0:T(8,128)(2,1)} %bitcast.61, bf16[1152,2048]{1,0:T(8,128)(2,1)} %bitcast.59, ...), custom_call_target="tpu_custom_call" | custom-call | tf_op jit(solution)/shard_map/pallas_call | solution.py:1122
  348.3 178.8 %shard_map.224 = (bf16[128,128]{1,0:T(8,128)(2,1)}, f32[8,2048]{1,0:T(8,128)}, f32[128,2048]{1,0:T(8,128)}, bf16[4,2,128,2048]{3,2,1,0:T(8,128)(2,1)}, bf16[2,16...) custom-call(bf16[4,2,144,2048]{3,2,1,0:T(8,128)(2,1)} %bitcast.73, bf16[4,2,144,256]{3,2,1,0:T(8,128)(2,1)} %bitcast.84, ...), custom_call_target="tpu_custom_call" | custom-call | tf_op jit(solution)/shard_map/pallas_call | solution.py:1470
  527.0 6.5 all-to-all-start.1
  533.5 28.4 %shard_map.225 = (bf16[1024,2048]{1,0:T(8,128)(2,1)}, bf16[2048,768]{1,0:T(8,128)(2,1)}, bf16[16,256,128]{2,1,0:T(8,128)(2,1)}, f32[8,128]{1,0:T(8,128)}, f32[8,128]{1,0:T(8,128)}) custom-call(bf16[1024,2048]{1,0:T(8,128)(2,1)} %bitcast.74, bf16[256,2048]{1,0:T(8,128)(2,1)} %bitcast.66, bf16[1024,256]{1,0:T(8,128)(2,1)} %get-tuple-element.89.refs_2_, ...), custom_call_target="tpu_custom_call" | custom-call | tf_op jit(solution)/shard_map/pallas_call | solution.py:1975
  561.9 0.7 reduce_sum.48
  562.6 0.1 reshape.182
  562.7 0.7 reduce_sum.49
  563.4 0.1 reshape.183
  563.5 1.4 fusion.8
  564.9 0.3 concatenate.21
  565.4 1.3 concatenate.25.small
  566.7 139.1 %shard_map.226 = (bf16[256,2048]{1,0:T(8,128)(2,1)}, f32[128,1024]{1,0:T(8,128)}, f32[128,1024]{1,0:T(8,128)}, f32[128,1024]{1,0:T(8,128)}, f32[1024,128]{1,0:T(...) custom-call(bf16[4,2,128,2048]{3,2,1,0:T(8,128)(2,1)} %bitcast.78, bf16[256,2048]{1,0:T(8,128)(2,1)} %bitcast.69, ...), custom_call_target="tpu_custom_call" | custom-call | tf_op jit(solution)/shard_map/pallas_call | solution.py:1763
  705.8 0.7 slice.43
  706.6 0.7 copy.58
  707.2 1.3 slice_bitcast_fusion
  708.5 1.3 slice_bitcast_fusion.1
  709.8 2.2 copy-done
  712.0 6.8 shard_map.227
  718.8 0.8 copy.83
  719.6 1.0 copy.84
  720.6 0.8 copy.85
  721.4 0.8 copy.86
  722.2 0.8 copy.87
  723.0 0.8 copy.88
  (42 shorter events, 0.4 us)
Async XLA Ops:
  117.8 13.2 %copy-start.9 = (bf16[4,80,128]{2,1,0:T(8,128)(2,1)S(1)}, bf16[4,80,128]{2,1,0:T(8,128)(2,1)}, u32[]{:S(2)}) copy-start(bf16[4,80,128]{2,1,0:T(8,128)(2,1)} %get-tuple-element.65) | copy-start | bytes 245764
  117.8 14.1 %copy-start.2 = (bf16[4,256,512]{2,1,0:T(8,128)(2,1)S(1)}, bf16[4,256,512]{2,1,0:T(8,128)(2,1)}, u32[]{:S(2)}) copy-start(bf16[4,256,512]{2,1,0:T(8,128)(2,1)} %get-tuple-element.67) | copy-start | bytes 3145732
  117.8 15.9 %copy-start.1 = (bf16[2,576,256]{2,1,0:T(8,128)(2,1)S(1)}, bf16[2,576,256]{2,1,0:T(8,128)(2,1)}, u32[]{:S(2)}) copy-start(bf16[2,576,256]{2,1,0:T(8,128)(2,1)} %get-tuple-element.70.pick) | copy-start | bytes 1769476
  117.8 17.0 %copy-start.11 = (f32[4,16,256]{2,1,0:T(8,128)S(1)}, f32[4,16,256]{2,1,0:T(8,128)}, u32[]{:S(2)}) copy-start(f32[4,16,256]{2,1,0:T(8,128)} %get-tuple-element.69) | copy-start | bytes 196612
  117.9 178.9 %all-to-all-start = ((bf16[4,2,512,512]{3,2,1,0:T(8,128)(2,1)}), bf16[4,2,512,512]{3,2,1,0:T(8,128)(2,1)}, u32[]{:S(2)}, u32[]{:S(2)}) async-start(bf16[4,2,512,512]{3,2,1,0:T(8,128)(2,1)} %get-tuple-element.63), calls=%async_computation | async-start | bytes 8388608 | tf_op jit(solution)/shard_map/all_to_all | solution.py:413
  527.0 182.8 %all-to-all-start.1 = ((bf16[16,128,512]{2,1,0:T(8,128)(2,1)}), bf16[16,128,512]{2,1,0:T(8,128)(2,1)S(1)}, u32[]{:S(2)}, u32[]{:S(2)}) async-start(bf16[16,128,512]{2,1,0:T(8,128)(2,1)} %get-tuple-element.113), calls=%async_computation.1 | async-start | bytes 4194304 | tf_op jit(solution)/shard_map/all_to_all | solution.py:413
  533.5 30.0 %copy-start.12 = (bf16[128,128]{1,0:T(8,128)(2,1)S(1)}, bf16[128,128]{1,0:T(8,128)(2,1)}, u32[]{:S(2)}) copy-start(bf16[128,128]{1,0:T(8,128)(2,1)} %get-tuple-element.100) | copy-start | bytes 98308
  533.5 31.7 %copy-start.10 = (f32[8,2048]{1,0:T(8,128)S(1)}, f32[8,2048]{1,0:T(8,128)}, u32[]{:S(2)}) copy-start(f32[8,2048]{1,0:T(8,128)} %get-tuple-element.101) | copy-start | bytes 196612
  709.8 2.2 copy-start
  712.0 6.8 copy-start.8
  712.0 7.6 %copy-start.3 = (bf16[256,2048]{1,0:T(8,128)(2,1)S(1)}, bf16[256,2048]{1,0:T(8,128)(2,1)}, u32[]{:S(2)}) copy-start(bf16[256,2048]{1,0:T(8,128)(2,1)} %get-tuple-element.106) | copy-start | bytes 3145732
  712.0 8.6 %copy-start.7 = (f32[128,1024]{1,0:T(8,128)S(1)}, f32[128,1024]{1,0:T(8,128)}, u32[]{:S(2)}) copy-start(f32[128,1024]{1,0:T(8,128)} %get-tuple-element.187) | copy-start | bytes 1572868
  718.8 2.6 copy-start.6
  718.8 3.4 copy-start.5
  718.8 4.2 copy-start.4

commit v9 on v8

--- a/solution.py
+++ b/solution.py
@@ -584,8 +584,8 @@
         slot = lax.rem(b, 2)
         at = pl.ds(pl.multiple_of(b * height, height), height)
         return (
-            pltpu.make_async_copy(pair_out.at[slot], pair.at[:, :, at], pair_sem.at[slot]),
-            pltpu.make_async_copy(third_out.at[slot], third.at[:, at], third_sem.at[slot]),
+            pltpu.make_async_copy(pair_out.at[slot], pair.at[:, at], pair_sem.at[slot]),
+            pltpu.make_async_copy(third_out.at[slot], third.at[:, :, at], third_sem.at[slot]),
         )
 
     def pick_band(b):
@@ -608,10 +608,10 @@
                 value = held[slot, n * tile : (n + 1) * tile, k].reshape(tile * count, -1)
                 value = jnp.dot(hit, value, preferred_element_type=jnp.float32).astype(jnp.bfloat16)
                 value = value.reshape(nz, tile, -1)
-                if k == 1:
-                    third_out[slot, :, at, :] = value
+                if k == 2:
+                    pair_out[slot, :, at, :] = value
                 else:
-                    pair_out[slot, :, k // 2, at, :] = value
+                    third_out[slot, k, :, at, :] = value
         for copy in put(b):
             copy.start()
 
@@ -708,7 +708,7 @@
 
     partner = nz - 1 - z
     centre = (z == nz // 2 - 1) | (z == nz // 2)
-    middle_copy = remote(third.at[partner], middle, mid_s, mid_r, fsdp=partner)
+    middle_copy = remote(third.at[:, partner], middle, mid_s, mid_r, fsdp=partner)
 
     def select_some(step):
         pl.loop(bands * (0, 1, 3)[step] // 4, bands * (1, 3, 4)[step] // 4)(pick_band)
@@ -773,9 +773,9 @@
         ((nc,) + rank.shape, f32),
         ((2, nc * most, block), bf16),
         ((nc, 2, most, width), bf16),
-        ((nz, 2, deep, ffn), bf16),
         ((nz, deep, ffn), bf16),
-        ((deep, ffn), bf16),
+        ((2, nz, deep, ffn), bf16),
+        ((2, deep, ffn), bf16),
     ]
     hbm = pl.BlockSpec(memory_space=pl.ANY)
     height = 32
@@ -793,8 +793,8 @@
             dma((nc - 1,)), dma((nc - 1,)), dma((nc - 1,)), dma((nc - 1,)), dma((nc - 1,)), dma((nc - 1,)),
             dma((2,)), dma((2,)), dma((2,)), dma((2, nc - 1)), dma((2, nc - 1)), dma((2,)),
             pltpu.VMEM((2, height, 3, count, ffn), bf16),
-            pltpu.VMEM((2, nz, 2, height, ffn), bf16),
             pltpu.VMEM((2, nz, height, ffn), bf16),
+            pltpu.VMEM((2, 2, nz, height, ffn), bf16),
             dma((2,)), dma((2,)), dma((2,)), dma, dma,
         ],
         compiler_params=pltpu.CompilerParams(
@@ -816,18 +816,26 @@
     rows, width = residual.shape
     most = x_in.shape[2]
     greet(nz, nc, True)
-    keep_third = pltpu.make_async_copy(third.at[z], third_got.at[z], third_own)
+    keep_third = pltpu.make_async_copy(third.at[:, z], third_got.at[:, z], third_own)
     keep_third.start()
     partner = nz - 1 - z
     centre = (z == nz // 2 - 1) | (z == nz // 2)
-    keep_middle = pltpu.make_async_copy(middle, third_got.at[partner], mid_own)
+    keep_middle = pltpu.make_async_copy(middle, third_got.at[:, partner], mid_own)
     pl.when(centre)(lambda: keep_middle.start())
 
     def still(other):
         return jnp.logical_not(centre & (other == partner))
 
-    def third_copy(step, source, target):
-        return remote(third.at[target], third_got.at[source], third_s.at[step], third_r.at[step], fsdp=target)
+    def third_copy(kind, step, source, target):
+        return remote(
+            third.at[kind, target], third_got.at[kind, source], third_s.at[kind, step], third_r.at[kind, step],
+            fsdp=target,
+        )
+
+    def send_third(kind):
+        for step in range(1, nz):
+            target = ring(z, step, nz)
+            pl.when(still(target))(lambda: third_copy(kind, step - 1, z, target).start())
 
     def sib_copy(q):
         return remote(part.at[q, 1 - t], sib.at[q], sib_s.at[q], sib_r.at[q], tp=1 - t)
@@ -854,6 +862,7 @@
             src.at[slot, pl.ds(pl.multiple_of(c * most, 16), most)], dst.at[c, slot], own_sem.at[k, slot]
         )
 
+    send_third(0)
     sib_copy(c).wait_recv()
     for step in range(1, nc):
         rs_copy(step - 1, c, c).wait_recv()
@@ -912,8 +921,7 @@
 
     line_gather(nz, (n_line, g_line), line_send, line_recv, arrived, None, near)
     near(nz - 1)
-    for step in range(1, nz):
-        pl.when(still(ring(z, step, nz)))(lambda: third_copy(step - 1, z, ring(z, step, nz)).start())
+    send_third(1)
     line_sent(nz, (n_line, g_line), line_send, line_recv)
     for slot in range(2):
         wait_given(slot, t, rows, n_line, n_two, give_send, give_recv)
@@ -931,8 +939,9 @@
         sib_copy(step).wait_send()
     for step in range(1, nz):
         source = ring(z, -step, nz)
-        pl.when(still(source))(lambda: third_copy(step - 1, source, source).wait_recv())
-        pl.when(still(ring(z, step, nz)))(lambda: third_copy(step - 1, source, source).wait_send())
+        for kind in range(2):
+            pl.when(still(source))(lambda: third_copy(kind, step - 1, source, source).wait_recv())
+            pl.when(still(ring(z, step, nz)))(lambda: third_copy(kind, step - 1, source, source).wait_send())
     keep_third.wait()
     pl.when(centre)(lambda: keep_middle.wait())
 
@@ -973,7 +982,7 @@
             dma((2,)), dma((2,)), dma((2,)), dma((2,)), dma((2,)), dma((2,)),
             dma((2, nc - 1)), dma((2, nc - 1)), dma((2, nc - 1)), dma((2, nc - 1)),
             dma((2, 2)),
-            dma((nz - 1,)), dma((nz - 1,)), dma, dma,
+            dma((2, nz - 1)), dma((2, nz - 1)), dma, dma,
         ],
         compiler_params=pltpu.CompilerParams(
             collective_id=1, has_side_effects=True, vmem_limit_bytes=56 * 2**20
@@ -994,9 +1003,10 @@
     chunk = 288
     copies = [
         pltpu.make_async_copy(cot_hbm, cot, sem.at[0]),
-        pltpu.make_async_copy(pair_hbm, w.at[0, :, pl.ds(0, 2)], sem.at[1]),
+        pltpu.make_async_copy(pair_hbm, w.at[0, :, 1], sem.at[1]),
         pltpu.make_async_copy(x_hbm, x, sem.at[2]),
-        pltpu.make_async_copy(third_hbm, w.at[0, :, 2], sem.at[3]),
+        pltpu.make_async_copy(third_hbm.at[0], w.at[0, :, 0], sem.at[3]),
+        pltpu.make_async_copy(third_hbm.at[1], w.at[0, :, 2], sem.at[4]),
     ]
     for copy in copies:
         copy.start()
@@ -1004,8 +1014,9 @@
     pl.semaphore_signal(barrier, inc=1, device_id=dict(tp=1 - t), device_id_type=MESH)
     pl.semaphore_wait(barrier, 1)
     swaps = [
-        remote(pair_hbm, w.at[1, :, pl.ds(0, 2)], swap_s.at[0], swap_r.at[0], tp=1 - t),
-        remote(third_hbm, w.at[1, :, 2], swap_s.at[1], swap_r.at[1], tp=1 - t),
+        remote(pair_hbm, w.at[1, :, 1], swap_s.at[0], swap_r.at[0], tp=1 - t),
+        remote(third_hbm.at[0], w.at[1, :, 0], swap_s.at[1], swap_r.at[1], tp=1 - t),
+        remote(third_hbm.at[1], w.at[1, :, 2], swap_s.at[2], swap_r.at[2], tp=1 - t),
     ]
     for copy in swaps:
         copy.start()
@@ -1114,7 +1125,7 @@
     bf16, f32 = jnp.bfloat16, jnp.float32
     nz, nc = lax.axis_size("fsdp"), lax.axis_size("ctx")
     tall, width = x.shape
-    deep, ffn = third.shape[1:]
+    deep, ffn = third.shape[2:]
     vmem = pl.BlockSpec(memory_space=pltpu.VMEM)
     hbm = pl.BlockSpec(memory_space=pl.ANY)
     inner = jax.ShapeDtypeStruct((tall, 2 * ffn), bf16)
@@ -1145,7 +1156,7 @@
             pltpu.VMEM((tall, 2 * ffn), bf16),
             pltpu.VMEM((tall, 2 * ffn), bf16),
             pltpu.VMEM((tall, 2 * ffn), bf16),
-            dma((4,)), dma((2,)), dma((2,)), dma((2, width // 256)), dma((3,)),
+            dma((5,)), dma((3,)), dma((3,)), dma((2, width // 256)), dma((3,)),
         ],
         compiler_params=pltpu.CompilerParams(
             collective_id=4, has_side_effects=True, vmem_limit_bytes=60 * 2**20

time: 725 us -> 715 us (0.986)
  Pallas kernels: 672 us -> 661 us
    pallas_call x1, Pallas kernels: 129 us -> 121 us  [dispatch(): pl.pallas_call(functools.partial(dispatch_kernel, nz, nc), out_shape=[jax...]
  transfers between devices with their start and end apart: 2 -> 2, of which waited for: 0 -> 0; matrix products, arithmetic and copies ran while one was open for 3% -> 3% of each run, Pallas kernels for 45% -> 44%
where the time goes in v9:
time: 715 us; the launch traced here: 714 us
  Pallas kernels  661 us (92%)
  local copies, waits for them, and re-layouts  25.7 us (4%)
  starting transfers between devices  18.3 us (3%)
    pallas_call x1, Pallas kernels, give_back(): pl.pallas_call(functools.partial(return_kernel, nz, nc), out_shape=[jax.S...  176 us
    pallas_call x1, Pallas kernels, finish(): pl.pallas_call(functools.partial(final_kernel, nz, nc), out_shape=[jax.Sh...  140 us
    pallas_call x1, Pallas kernels, dispatch(): pl.pallas_call(functools.partial(dispatch_kernel, nz, nc), out_shape=[jax...  121 us
    pallas_call x1, Pallas kernels, load(): pl.pallas_call(functools.partial(load_kernel, nz, nc), out_shape=[jax.Sha...  111 us
    pallas_call x1, Pallas kernels, experts(): pl.pallas_call(functools.partial(experts_kernel, nz, nc), out_shape=[jax....  49.2 us
    pallas_call x1, Pallas kernels, attention_back(): pl.pallas_call(functools.partial(attention_back_kernel, 1.0 / math.sqrt(H...  28.4 us
    pallas_call x1, Pallas kernels, attention(): pl.pallas_call(functools.partial(attention_kernel, 1.0 / math.sqrt(HD)),...  27.1 us
    all_to_all x2, starting transfers between devices, exchange(): return lax.all_to_all(value, axes, split_axis=0, concat_axis=0, tiled=True)  18.3 us
  transfers between devices with their start and end apart: 2, of which 0 were waited for; matrix products, arithmetic and copies ran while one was open for 3% of the time, Pallas kernels for 44%

profile of v9, /device:TPU:15, one launch (start us, length us, event | category | flops | bytes accessed | tf_op | source)
XLA Modules:
  0.0 713.8 jit_solution(12359180880925309037)
XLA Ops:
  0.7 0.7 fusion.4
  1.4 0.1 copy.49
  1.5 0.2 convolution_select_fusion
  1.7 0.7 copy.51.rank
  2.4 0.7 copy.69
  3.1 2.8 concatenate.19
  5.9 0.6 pad_bitcast_fusion.small
  6.5 111.5 %shard_map.220 = (bf16[1024,2048]{1,0:T(8,128)(2,1)}, bf16[4,512,768]{2,1,0:T(8,128)(2,1)}, bf16[4,256,512]{2,1,0:T(8,128)(2,1)}, bf16[4,80,128]{2,1,0:T(8,128)(...) custom-call(bf16[256,2048]{1,0:T(8,128)(2,1)} %bitcast.67, ...), custom_call_target="tpu_custom_call" | custom-call | tf_op jit(solution)/shard_map/pallas_call | solution.py:782
  118.0 11.9 %all-to-all-start = ((bf16[4,512,512]{2,1,0:T(8,128)(2,1)}), bf16[4,512,512]{2,1,0:T(8,128)(2,1)S(1)}, u32[]{:S(2)}, u32[]{:S(2)}) async-start(bf16[4,512,512]{2,1,0:T(8,128)(2,1)} %get-tuple-element.63), calls=%async_computation | async-start | bytes 4194304 | tf_op jit(solution)/shard_map/all_to_all | solution.py:413
  130.1 0.1 convert_element_type.81
  130.2 0.1 convert_element_type.82
  130.3 0.6 copy.71
  130.9 2.3 copy.68
  133.2 0.6 copy.72
  133.9 1.1 copy.56
  135.0 0.1 convert_reduce_fusion
  135.1 0.1 select_reduce_fusion
  135.2 0.6 pad.26.kept
  135.8 0.8 pad.25.router
  136.7 0.6 fusion.13.gains.refs_7_
  137.3 1.9 multiply_cosine_fusion
  139.2 1.4 pad_maximum_fusion.tables.refs_6_
  140.6 27.1 %shard_map.221 = (bf16[1024,2048]{1,0:T(8,128)(2,1)}, f32[1024,768]{1,0:T(8,128)}, bf16[1024,256]{1,0:T(8,128)(2,1)}, bf16[1024,256]{1,0:T(8,128)(2,1)}, bf16[10...) custom-call(bf16[1024,2048]{1,0:T(8,128)(2,1)} %get-tuple-element.64.x, ...), custom_call_target="tpu_custom_call" | custom-call | tf_op jit(solution)/shard_map/pallas_call | solution.py:1887
  167.7 121.2 %shard_map.222 = (f32[128,2048]{1,0:T(8,128)}, bf16[128,2048]{1,0:T(8,128)(2,1)}, f32[128,128]{1,0:T(8,128)}, bf16[4,2,144,2048]{3,2,1,0:T(8,128)(2,1)}, bf16[4,...) custom-call(bf16[4,2,128,2048]{3,2,1,0:T(8,128)(2,1)} %bitcast.77, bf16[256,2048]{1,0:T(8,128)(2,1)} %bitcast.68, ...), custom_call_target="tpu_custom_call" | custom-call | tf_op jit(solution)/shard_map/pallas_call | solution.py:958
  289.0 1.3 copy-done.1
  290.3 49.2 %shard_map.223 = (bf16[1152,2048]{1,0:T(8,128)(2,1)}, bf16[1152,2048]{1,0:T(8,128)(2,1)}, bf16[1152,256]{1,0:T(8,128)(2,1)}, bf16[1152,1024]{1,0:T(8,128)(2,1)},...) custom-call(bf16[1152,2048]{1,0:T(8,128)(2,1)} %bitcast.61, bf16[1152,2048]{1,0:T(8,128)(2,1)} %bitcast.59, ...), custom_call_target="tpu_custom_call" | custom-call | tf_op jit(solution)/shard_map/pallas_call | solution.py:1133
  339.5 176.4 %shard_map.224 = (bf16[128,128]{1,0:T(8,128)(2,1)}, f32[8,2048]{1,0:T(8,128)}, f32[128,2048]{1,0:T(8,128)}, bf16[4,2,128,2048]{3,2,1,0:T(8,128)(2,1)}, bf16[2,16...) custom-call(bf16[4,2,144,2048]{3,2,1,0:T(8,128)(2,1)} %bitcast.73, bf16[4,2,144,256]{3,2,1,0:T(8,128)(2,1)} %bitcast.84, ...), custom_call_target="tpu_custom_call" | custom-call | tf_op jit(solution)/shard_map/pallas_call | solution.py:1481
  516.0 6.4 all-to-all-start.1
  522.4 28.4 %shard_map.225 = (bf16[1024,2048]{1,0:T(8,128)(2,1)}, bf16[2048,768]{1,0:T(8,128)(2,1)}, bf16[16,256,128]{2,1,0:T(8,128)(2,1)}, f32[8,128]{1,0:T(8,128)}, f32[8,128]{1,0:T(8,128)}) custom-call(bf16[1024,2048]{1,0:T(8,128)(2,1)} %bitcast.74, bf16[256,2048]{1,0:T(8,128)(2,1)} %bitcast.66, bf16[1024,256]{1,0:T(8,128)(2,1)} %get-tuple-element.89.refs_2_, ...), custom_call_target="tpu_custom_call" | custom-call | tf_op jit(solution)/shard_map/pallas_call | solution.py:1986
  550.8 0.7 reduce_sum.48
  551.5 0.1 reshape.182
  551.6 0.7 reduce_sum.49
  552.4 1.4 fusion.8
  553.8 0.3 concatenate.21
  554.2 1.3 concatenate.25.small
  555.5 140.3 %shard_map.226 = (bf16[256,2048]{1,0:T(8,128)(2,1)}, f32[128,1024]{1,0:T(8,128)}, f32[128,1024]{1,0:T(8,128)}, f32[128,1024]{1,0:T(8,128)}, f32[1024,128]{1,0:T(...) custom-call(bf16[4,2,128,2048]{3,2,1,0:T(8,128)(2,1)} %bitcast.78, bf16[256,2048]{1,0:T(8,128)(2,1)} %bitcast.69, ...), custom_call_target="tpu_custom_call" | custom-call | tf_op jit(solution)/shard_map/pallas_call | solution.py:1774
  695.8 0.7 slice.43
  696.6 0.7 copy.58
  697.3 1.3 slice_bitcast_fusion
  698.5 1.3 slice_bitcast_fusion.1
  699.8 2.2 copy-done
  702.0 6.8 shard_map.227
  708.9 0.8 copy.83
  709.7 1.0 copy.84
  710.6 0.8 copy.85
  711.4 0.8 copy.86
  712.2 0.8 copy.87
  713.0 0.8 copy.88
  (42 shorter events, 0.5 us)
Async XLA Ops:
  118.0 12.0 %copy-start.9 = (bf16[4,80,128]{2,1,0:T(8,128)(2,1)S(1)}, bf16[4,80,128]{2,1,0:T(8,128)(2,1)}, u32[]{:S(2)}) copy-start(bf16[4,80,128]{2,1,0:T(8,128)(2,1)} %get-tuple-element.65) | copy-start | bytes 245764
  118.0 15.8 %copy-start.2 = (bf16[2,576,256]{2,1,0:T(8,128)(2,1)S(1)}, bf16[2,576,256]{2,1,0:T(8,128)(2,1)}, u32[]{:S(2)}) copy-start(bf16[2,576,256]{2,1,0:T(8,128)(2,1)} %get-tuple-element.70.pick) | copy-start | bytes 1769476
  118.0 16.9 %copy-start.11 = (f32[4,16,256]{2,1,0:T(8,128)S(1)}, f32[4,16,256]{2,1,0:T(8,128)}, u32[]{:S(2)}) copy-start(f32[4,16,256]{2,1,0:T(8,128)} %get-tuple-element.69) | copy-start | bytes 196612
  118.0 170.9 %all-to-all-start = ((bf16[4,512,512]{2,1,0:T(8,128)(2,1)}), bf16[4,512,512]{2,1,0:T(8,128)(2,1)S(1)}, u32[]{:S(2)}, u32[]{:S(2)}) async-start(bf16[4,512,512]{2,1,0:T(8,128)(2,1)} %get-tuple-element.63), calls=%async_computation | async-start | bytes 4194304 | tf_op jit(solution)/shard_map/all_to_all | solution.py:413
  289.0 1.3 copy-start.1
  516.0 183.8 %all-to-all-start.1 = ((bf16[16,128,512]{2,1,0:T(8,128)(2,1)}), bf16[16,128,512]{2,1,0:T(8,128)(2,1)S(1)}, u32[]{:S(2)}, u32[]{:S(2)}) async-start(bf16[16,128,512]{2,1,0:T(8,128)(2,1)} %get-tuple-element.113), calls=%async_computation.1 | async-start | bytes 4194304 | tf_op jit(solution)/shard_map/all_to_all | solution.py:413
  522.4 30.0 %copy-start.12 = (bf16[128,128]{1,0:T(8,128)(2,1)S(1)}, bf16[128,128]{1,0:T(8,128)(2,1)}, u32[]{:S(2)}) copy-start(bf16[128,128]{1,0:T(8,128)(2,1)} %get-tuple-element.100) | copy-start | bytes 98308
  522.4 31.7 %copy-start.10 = (f32[8,2048]{1,0:T(8,128)S(1)}, f32[8,2048]{1,0:T(8,128)}, u32[]{:S(2)}) copy-start(f32[8,2048]{1,0:T(8,128)} %get-tuple-element.101) | copy-start | bytes 196612
  699.8 2.2 copy-start
  702.0 6.8 copy-start.8
  702.0 7.6 %copy-start.3 = (bf16[256,2048]{1,0:T(8,128)(2,1)S(1)}, bf16[256,2048]{1,0:T(8,128)(2,1)}, u32[]{:S(2)}) copy-start(bf16[256,2048]{1,0:T(8,128)(2,1)} %get-tuple-element.106) | copy-start | bytes 3145732
  702.0 8.6 %copy-start.7 = (f32[128,1024]{1,0:T(8,128)S(1)}, f32[128,1024]{1,0:T(8,128)}, u32[]{:S(2)}) copy-start(f32[128,1024]{1,0:T(8,128)} %get-tuple-element.187) | copy-start | bytes 1572868
  708.8 2.6 copy-start.6
  708.8 3.4 copy-start.5
  708.8 4.2 copy-start.4

commit v10 on v9

--- a/solution.py
+++ b/solution.py
@@ -1000,7 +1000,7 @@
     width, tall = x.shape[1], x.shape[0]
     deep, ffn = w.shape[3], w.shape[4]
     span = 256
-    chunk = 288
+    chunk = 576
     copies = [
         pltpu.make_async_copy(cot_hbm, cot, sem.at[0]),
         pltpu.make_async_copy(pair_hbm, w.at[0, :, 1], sem.at[1]),
@@ -1346,7 +1346,7 @@
         copy.start()
     greet(nz, nc, True, True)
     chips = nz * nc
-    steps = [(i, j) for i in range(nz) for j in range(nc) if i or j]
+    steps = [(i, j) for i in (*range(1, nz), 0) for j in range(nc) if i or j]
 
     def early_copy(kind, n, source, target, fsdp, ctx):
         return remote(

time: 715 us -> 714 us (level)
  no operation moved by 1% of the time
where the time goes in v10:
time: 714 us; the launch traced here: 713 us
  Pallas kernels  658 us (92%)
  local copies, waits for them, and re-layouts  25.7 us (4%)
  starting transfers between devices  19.9 us (3%)
    pallas_call x1, Pallas kernels, give_back(): pl.pallas_call(functools.partial(return_kernel, nz, nc), out_shape=[jax.S...  177 us
    pallas_call x1, Pallas kernels, finish(): pl.pallas_call(functools.partial(final_kernel, nz, nc), out_shape=[jax.Sh...  139 us
    pallas_call x1, Pallas kernels, dispatch(): pl.pallas_call(functools.partial(dispatch_kernel, nz, nc), out_shape=[jax...  121 us
    pallas_call x1, Pallas kernels, load(): pl.pallas_call(functools.partial(load_kernel, nz, nc), out_shape=[jax.Sha...  111 us
    pallas_call x1, Pallas kernels, experts(): pl.pallas_call(functools.partial(experts_kernel, nz, nc), out_shape=[jax....  48.2 us
    pallas_call x1, Pallas kernels, attention_back(): pl.pallas_call(functools.partial(attention_back_kernel, 1.0 / math.sqrt(H...  28.4 us
    pallas_call x1, Pallas kernels, attention(): pl.pallas_call(functools.partial(attention_kernel, 1.0 / math.sqrt(HD)),...  27.1 us
    all_to_all x2, starting transfers between devices, exchange(): return lax.all_to_all(value, axes, split_axis=0, concat_axis=0, tiled=True)  19.9 us
  transfers between devices with their start and end apart: 2, of which 0 were waited for; matrix products, arithmetic and copies ran while one was open for 3% of the time, Pallas kernels for 44%

profile of v10, /device:TPU:15, one launch (start us, length us, event | category | flops | bytes accessed | tf_op | source)
XLA Modules:
  0.0 712.9 jit_solution(16003919647070467671)
XLA Ops:
  0.7 0.7 fusion.4
  1.4 0.1 copy.49
  1.5 0.2 convolution_select_fusion
  1.7 0.7 copy.51.rank
  2.4 0.7 copy.69
  3.1 2.8 concatenate.19
  5.9 0.6 pad_bitcast_fusion.small
  6.5 111.5 %shard_map.220 = (bf16[1024,2048]{1,0:T(8,128)(2,1)}, bf16[4,512,768]{2,1,0:T(8,128)(2,1)}, bf16[4,256,512]{2,1,0:T(8,128)(2,1)}, bf16[4,80,128]{2,1,0:T(8,128)(...) custom-call(bf16[256,2048]{1,0:T(8,128)(2,1)} %bitcast.67, ...), custom_call_target="tpu_custom_call" | custom-call | tf_op jit(solution)/shard_map/pallas_call | solution.py:782
  118.0 11.9 %all-to-all-start = ((bf16[4,512,512]{2,1,0:T(8,128)(2,1)}), bf16[4,512,512]{2,1,0:T(8,128)(2,1)S(1)}, u32[]{:S(2)}, u32[]{:S(2)}) async-start(bf16[4,512,512]{2,1,0:T(8,128)(2,1)} %get-tuple-element.63), calls=%async_computation | async-start | bytes 4194304 | tf_op jit(solution)/shard_map/all_to_all | solution.py:413
  130.1 0.1 convert_element_type.81
  130.2 0.1 convert_element_type.82
  130.3 0.6 copy.71
  130.9 2.3 copy.68
  133.2 0.6 copy.72
  133.9 1.1 copy.56
  135.0 0.1 convert_reduce_fusion
  135.1 0.1 select_reduce_fusion
  135.2 0.6 pad.26.kept
  135.8 0.8 pad.25.router
  136.7 0.6 fusion.13.gains.refs_7_
  137.3 1.9 multiply_cosine_fusion
  139.2 1.4 pad_maximum_fusion.tables.refs_6_
  140.6 27.1 %shard_map.221 = (bf16[1024,2048]{1,0:T(8,128)(2,1)}, f32[1024,768]{1,0:T(8,128)}, bf16[1024,256]{1,0:T(8,128)(2,1)}, bf16[1024,256]{1,0:T(8,128)(2,1)}, bf16[10...) custom-call(bf16[1024,2048]{1,0:T(8,128)(2,1)} %get-tuple-element.64.x, ...), custom_call_target="tpu_custom_call" | custom-call | tf_op jit(solution)/shard_map/pallas_call | solution.py:1887
  167.7 121.2 %shard_map.222 = (f32[128,2048]{1,0:T(8,128)}, bf16[128,2048]{1,0:T(8,128)(2,1)}, f32[128,128]{1,0:T(8,128)}, bf16[4,2,144,2048]{3,2,1,0:T(8,128)(2,1)}, bf16[4,...) custom-call(bf16[4,2,128,2048]{3,2,1,0:T(8,128)(2,1)} %bitcast.77, bf16[256,2048]{1,0:T(8,128)(2,1)} %bitcast.68, ...), custom_call_target="tpu_custom_call" | custom-call | tf_op jit(solution)/shard_map/pallas_call | solution.py:958
  289.0 1.3 copy-done.1
  290.3 48.2 %shard_map.223 = (bf16[1152,2048]{1,0:T(8,128)(2,1)}, bf16[1152,2048]{1,0:T(8,128)(2,1)}, bf16[1152,256]{1,0:T(8,128)(2,1)}, bf16[1152,1024]{1,0:T(8,128)(2,1)},...) custom-call(bf16[1152,2048]{1,0:T(8,128)(2,1)} %bitcast.61, bf16[1152,2048]{1,0:T(8,128)(2,1)} %bitcast.59, ...), custom_call_target="tpu_custom_call" | custom-call | tf_op jit(solution)/shard_map/pallas_call | solution.py:1133
  338.5 176.6 %shard_map.224 = (bf16[128,128]{1,0:T(8,128)(2,1)}, f32[8,2048]{1,0:T(8,128)}, f32[128,2048]{1,0:T(8,128)}, bf16[4,2,128,2048]{3,2,1,0:T(8,128)(2,1)}, bf16[2,16...) custom-call(bf16[4,2,144,2048]{3,2,1,0:T(8,128)(2,1)} %bitcast.73, bf16[4,2,144,256]{3,2,1,0:T(8,128)(2,1)} %bitcast.84, ...), custom_call_target="tpu_custom_call" | custom-call | tf_op jit(solution)/shard_map/pallas_call | solution.py:1481
  515.1 7.9 %all-to-all-start.1 = ((bf16[16,128,512]{2,1,0:T(8,128)(2,1)}), bf16[16,128,512]{2,1,0:T(8,128)(2,1)S(1)}, u32[]{:S(2)}, u32[]{:S(2)}) async-start(bf16[16,128,512]{2,1,0:T(8,128)(2,1)} %get-tuple-element.113), calls=%async_computation.1 | async-start | bytes 4194304 | tf_op jit(solution)/shard_map/all_to_all | solution.py:413
  523.1 28.4 %shard_map.225 = (bf16[1024,2048]{1,0:T(8,128)(2,1)}, bf16[2048,768]{1,0:T(8,128)(2,1)}, bf16[16,256,128]{2,1,0:T(8,128)(2,1)}, f32[8,128]{1,0:T(8,128)}, f32[8,128]{1,0:T(8,128)}) custom-call(bf16[1024,2048]{1,0:T(8,128)(2,1)} %bitcast.74, bf16[256,2048]{1,0:T(8,128)(2,1)} %bitcast.66, bf16[1024,256]{1,0:T(8,128)(2,1)} %get-tuple-element.89.refs_2_, ...), custom_call_target="tpu_custom_call" | custom-call | tf_op jit(solution)/shard_map/pallas_call | solution.py:1986
  551.5 0.7 reduce_sum.48
  552.3 0.7 reduce_sum.49
  553.0 0.1 reshape.183
  553.1 1.4 fusion.8
  554.5 0.3 concatenate.21
  554.9 1.3 concatenate.25.small
  556.2 138.7 %shard_map.226 = (bf16[256,2048]{1,0:T(8,128)(2,1)}, f32[128,1024]{1,0:T(8,128)}, f32[128,1024]{1,0:T(8,128)}, f32[128,1024]{1,0:T(8,128)}, f32[1024,128]{1,0:T(...) custom-call(bf16[4,2,128,2048]{3,2,1,0:T(8,128)(2,1)} %bitcast.78, bf16[256,2048]{1,0:T(8,128)(2,1)} %bitcast.69, ...), custom_call_target="tpu_custom_call" | custom-call | tf_op jit(solution)/shard_map/pallas_call | solution.py:1774
  694.9 0.7 slice.43
  695.7 0.7 copy.58
  696.4 1.3 slice_bitcast_fusion
  697.6 1.3 slice_bitcast_fusion.1
  698.9 2.2 copy-done
  701.1 6.8 shard_map.227
  708.0 0.8 copy.83
  708.8 1.0 copy.84
  709.7 0.8 copy.85
  710.5 0.8 copy.86
  711.3 0.8 copy.87
  712.1 0.8 copy.88
  (42 shorter events, 0.5 us)
Async XLA Ops:
  118.0 12.0 %copy-start.9 = (bf16[4,80,128]{2,1,0:T(8,128)(2,1)S(1)}, bf16[4,80,128]{2,1,0:T(8,128)(2,1)}, u32[]{:S(2)}) copy-start(bf16[4,80,128]{2,1,0:T(8,128)(2,1)} %get-tuple-element.65) | copy-start | bytes 245764
  118.0 15.8 %copy-start.2 = (bf16[2,576,256]{2,1,0:T(8,128)(2,1)S(1)}, bf16[2,576,256]{2,1,0:T(8,128)(2,1)}, u32[]{:S(2)}) copy-start(bf16[2,576,256]{2,1,0:T(8,128)(2,1)} %get-tuple-element.70.pick) | copy-start | bytes 1769476
  118.0 16.9 %copy-start.11 = (f32[4,16,256]{2,1,0:T(8,128)S(1)}, f32[4,16,256]{2,1,0:T(8,128)}, u32[]{:S(2)}) copy-start(f32[4,16,256]{2,1,0:T(8,128)} %get-tuple-element.69) | copy-start | bytes 196612
  118.0 170.9 %all-to-all-start = ((bf16[4,512,512]{2,1,0:T(8,128)(2,1)}), bf16[4,512,512]{2,1,0:T(8,128)(2,1)S(1)}, u32[]{:S(2)}, u32[]{:S(2)}) async-start(bf16[4,512,512]{2,1,0:T(8,128)(2,1)} %get-tuple-element.63), calls=%async_computation | async-start | bytes 4194304 | tf_op jit(solution)/shard_map/all_to_all | solution.py:413
  289.0 1.3 copy-start.1
  515.1 183.8 %all-to-all-start.1 = ((bf16[16,128,512]{2,1,0:T(8,128)(2,1)}), bf16[16,128,512]{2,1,0:T(8,128)(2,1)S(1)}, u32[]{:S(2)}, u32[]{:S(2)}) async-start(bf16[16,128,512]{2,1,0:T(8,128)(2,1)} %get-tuple-element.113), calls=%async_computation.1 | async-start | bytes 4194304 | tf_op jit(solution)/shard_map/all_to_all | solution.py:413
  523.1 30.0 %copy-start.12 = (bf16[128,128]{1,0:T(8,128)(2,1)S(1)}, bf16[128,128]{1,0:T(8,128)(2,1)}, u32[]{:S(2)}) copy-start(bf16[128,128]{1,0:T(8,128)(2,1)} %get-tuple-element.100) | copy-start | bytes 98308
  523.1 31.7 %copy-start.10 = (f32[8,2048]{1,0:T(8,128)S(1)}, f32[8,2048]{1,0:T(8,128)}, u32[]{:S(2)}) copy-start(f32[8,2048]{1,0:T(8,128)} %get-tuple-element.101) | copy-start | bytes 196612
  698.9 2.2 copy-start
  701.1 6.8 copy-start.8
  701.1 7.6 %copy-start.3 = (bf16[256,2048]{1,0:T(8,128)(2,1)S(1)}, bf16[256,2048]{1,0:T(8,128)(2,1)}, u32[]{:S(2)}) copy-start(bf16[256,2048]{1,0:T(8,128)(2,1)} %get-tuple-element.106) | copy-start | bytes 3145732
  701.1 8.6 %copy-start.7 = (f32[128,1024]{1,0:T(8,128)S(1)}, f32[128,1024]{1,0:T(8,128)}, u32[]{:S(2)}) copy-start(f32[128,1024]{1,0:T(8,128)} %get-tuple-element.187) | copy-start | bytes 1572868
  707.9 2.6 copy-start.6
  707.9 3.4 copy-start.5
  707.9 4.2 copy-start.4
